TPU v7x, 32 devices: a whole 2x2x4 slice. The times are simulated.
32 devices in a mesh: ctx: 8 (over z, y), head: 4 (over x, core).
Axes of the slice: x: 2, y: 2, z: 4, core: 2. Of those that a mesh axis runs over, the one named last changes fastest.
Arguments:
- queries: bfloat16 [1536, 8192], P(('ctx', 'head')), may hold values from -16 to 16
- keys: bfloat16 [1536, 1024], P(('ctx', 'head')), may hold values from -16 to 16
- values: bfloat16 [1536, 1024], P(('ctx', 'head')), may hold values from -6 to 6
- segment_ids: int32 [8, 1536], P('head', 'ctx'), may hold values from 0 to 95, as said below
- grad_out: bfloat16 [1536, 8192], P(('ctx', 'head')), may hold values from -6 to 6
Outputs:
- grad_queries: bfloat16 [1536, 8192], P('ctx', 'head')
- grad_keys: bfloat16 [1536, 1024], P('ctx', 'head')
- grad_values: bfloat16 [1536, 1024], P('ctx', 'head')
Inputs may be any that keep to these rules, and one draw needn't show every extreme that they name: `segment_ids`: for each KV head and each aligned block of 192 tokens the ids start at 0 at the block's first token, never fall, and rise by at most one from token to token; for each KV head some block uses every id up to 95.
All inputs are finite; a program needn't handle non-finite values.
Results may differ from a plain program's by a relative error of at most 0.015.
Values may be sent and summed in bfloat16 or wider, within the bound.
No kernel may reach another device: no remote copies, remote signals or barrier semaphores. Data moves between devices by JAX's collectives and lax.ppermute only.
A program may use at most 64 MiB of HBM per device.

v0:
```python
import jax
import jax.numpy as jnp
import numpy as np
from jax import lax
from jax.sharding import PartitionSpec as P

QH = 64
KVH = 8
HD = 128
SLOT_DEV = 96


masked_score = -1e30


def block_group(shards, per_shard):
    block_width = max(1, min(shards, 512 // per_shard))
    while shards % block_width:
        block_width = block_width - 1
    return block_width


def slot_mask(first_slot, block_rows, live_block, row_shards, row_segments):
    slot_index = first_slot + jnp.arange(block_rows, dtype=jnp.int32)
    slot_owner = slot_index // SLOT_DEV
    slot_place = slot_index % SLOT_DEV
    earlier = slot_owner[None, None, :] < row_shards[:, None, None]
    same = (slot_owner[None, None, :] == row_shards[:, None, None]) & (
        slot_place[None, None, :] < row_segments[:, :, None]
    )
    visible = (live_block.T[None, :, :] > 0) & (earlier | same)
    return visible[:, :, None, :]


def local(queries, keys, values, segment_ids, grad_out):
    queries, keys, values, grad_out = (
        lax.all_to_all(queries, "head", split_axis=1, concat_axis=0, tiled=True),
        lax.all_to_all(keys, "head", split_axis=1, concat_axis=0, tiled=True),
        lax.all_to_all(values, "head", split_axis=1, concat_axis=0, tiled=True),
        lax.all_to_all(grad_out, "head", split_axis=1, concat_axis=0, tiled=True),
    )
    tokens = queries.shape[0]
    kv_heads = keys.shape[1] // HD
    group_size = QH // KVH
    score_scale = HD ** (-0.5)
    shards = lax.axis_size("ctx")
    own_shard = lax.axis_index("ctx")
    slot_picks = segment_ids[:, :, None] == jnp.arange(SLOT_DEV, dtype=jnp.int32)[None, None, :]
    onehot = slot_picks.astype(jnp.bfloat16)
    counts = jnp.sum(slot_picks.astype(jnp.int32), axis=1)
    slot_sizes = jnp.maximum(counts, 1).astype(jnp.float32).T[:, :, None]
    key_sums = jnp.einsum(
        "gts,tgd->sgd",
        onehot,
        keys.reshape(tokens, kv_heads, HD),
        preferred_element_type=jnp.float32,
    )
    value_sums = jnp.einsum(
        "gts,tgd->sgd",
        onehot,
        values.reshape(tokens, kv_heads, HD),
        preferred_element_type=jnp.float32,
    )
    slot_rows = jnp.stack(
        [
            (key_sums / slot_sizes).astype(jnp.bfloat16),
            (value_sums / slot_sizes).astype(jnp.bfloat16),
        ],
        axis=2,
    )
    slot_rows = slot_rows.reshape(SLOT_DEV, kv_heads * 2 * HD)
    slot_live = (counts.T > 0).astype(jnp.bfloat16)
    gathered, live_flags = (
        lax.all_gather(slot_rows, "ctx", axis=0, tiled=True),
        lax.all_gather(slot_live, "ctx", axis=0, tiled=True),
    )
    gathered = gathered.reshape(-1, kv_heads, 2, HD)
    total_slots = gathered.shape[0]
    block_width = block_group(shards, SLOT_DEV)
    slot_block = block_width * SLOT_DEV
    slot_blocks = shards // block_width
    query_rows, key_rows, value_rows, cotangent_rows = (queries, keys, values, grad_out)
    row_segment = segment_ids.T
    row_shard = jnp.full((tokens,), own_shard, jnp.int32)
    pair_list = [(0, slot_part) for slot_part in range(slot_blocks)]
    query_heads = query_rows.reshape(tokens, kv_heads, group_size, HD)
    cotangent_heads = cotangent_rows.reshape(tokens, kv_heads, group_size, HD)
    key_heads = key_rows.reshape(tokens, kv_heads, HD)
    value_heads = value_rows.reshape(tokens, kv_heads, HD)
    own_scores = score_scale * jnp.einsum(
        "rghd,rgd->rgh", query_heads, key_heads, preferred_element_type=jnp.float32
    )
    own_grad_probs = jnp.einsum(
        "rghd,rgd->rgh", cotangent_heads, value_heads, preferred_element_type=jnp.float32
    )
    query_table = jnp.asarray(np.array([entry[0] for entry in pair_list], np.int32))
    slot_table = jnp.asarray(np.array([entry[1] for entry in pair_list], np.int32))
    pair_count = len(pair_list)

    def tile_inputs(first_slot, row_shards):
        slots_block = lax.dynamic_slice_in_dim(gathered, first_slot, slot_block, 0)
        live_block = lax.dynamic_slice_in_dim(live_flags, first_slot, slot_block, 0)
        key_block = slots_block[:, :, 0]
        value_block = slots_block[:, :, 1]
        visible = slot_mask(first_slot, slot_block, live_block, row_shards, row_segment)
        scores = score_scale * jnp.einsum(
            "rghd,sgd->rghs", query_heads, key_block, preferred_element_type=jnp.float32
        )
        return (query_heads, cotangent_heads, key_block, value_block, visible, scores)

    def visit_pair(pair_index, carried, update_fn):
        first_row = query_table[pair_index] * tokens
        first_slot = slot_table[pair_index] * slot_block
        needed = first_slot // SLOT_DEV <= jnp.max(row_shard)

        def run_tile(state):
            return update_fn(state, first_row, first_slot, row_shard)

        def keep_state(state):
            return state

        return lax.cond(needed, run_tile, keep_state, carried)

    def sweep(update_fn, initial):

        def loop_body(pair_index, carried):
            return visit_pair(pair_index, carried, update_fn)

        return lax.fori_loop(0, pair_count, loop_body, initial)

    ones_start = jnp.ones_like(own_scores)

    def stat_update(carried, first_row, first_slot, row_shards):
        maxima, totals = carried
        query_block, cotangent_block, key_block, value_block, visible, scores = tile_inputs(
            first_slot, row_shards
        )
        new_max = jnp.maximum(maxima, jnp.max(jnp.where(visible, scores, masked_score), axis=3))
        weights = jnp.exp(jnp.where(visible, scores - new_max[..., None], masked_score))
        new_totals = totals * jnp.exp(maxima - new_max) + jnp.sum(weights, axis=3)
        return (new_max, new_totals)

    maxima, totals = sweep(stat_update, (own_scores, ones_start))

    def delta_update(carried, first_row, first_slot, row_shards):
        query_block, cotangent_block, key_block, value_block, visible, scores = tile_inputs(
            first_slot, row_shards
        )
        probabilities = (
            jnp.exp(jnp.where(visible, scores - maxima[..., None], masked_score))
            / totals[..., None]
        )
        grad_probs = jnp.einsum(
            "rghd,sgd->rghs", cotangent_block, value_block, preferred_element_type=jnp.float32
        )
        return carried + jnp.sum(probabilities * grad_probs, axis=3)

    start_probs = jnp.exp(own_scores - maxima) / totals
    deltas = sweep(delta_update, start_probs * own_grad_probs)

    def grad_update(carried, first_row, first_slot, row_shards):
        query_grad, slot_grad = carried
        query_block, cotangent_block, key_block, value_block, visible, scores = tile_inputs(
            first_slot, row_shards
        )
        probabilities = (
            jnp.exp(jnp.where(visible, scores - maxima[..., None], masked_score))
            / totals[..., None]
        )
        grad_probs = jnp.einsum(
            "rghd,sgd->rghs", cotangent_block, value_block, preferred_element_type=jnp.float32
        )
        grad_scores = probabilities * (grad_probs - deltas[..., None])
        low_grads = grad_scores.astype(jnp.bfloat16)
        low_probs = probabilities.astype(jnp.bfloat16)
        query_part = score_scale * jnp.einsum(
            "rghs,sgd->rghd", low_grads, key_block, preferred_element_type=jnp.float32
        )
        key_part = score_scale * jnp.einsum(
            "rghs,rghd->sgd", low_grads, query_block, preferred_element_type=jnp.float32
        )
        value_part = jnp.einsum(
            "rghs,rghd->sgd", low_probs, cotangent_block, preferred_element_type=jnp.float32
        )
        query_grad = query_grad + query_part
        slot_old = lax.dynamic_slice_in_dim(slot_grad, first_slot, slot_block, 0)
        slot_grad = lax.dynamic_update_slice_in_dim(
            slot_grad, slot_old + jnp.stack([key_part, value_part], axis=2), first_slot, 0
        )
        return (query_grad, slot_grad)

    query_zero = jnp.zeros((tokens, kv_heads, group_size, HD), jnp.float32)
    slot_zero = jnp.zeros((total_slots, kv_heads, 2, HD), jnp.float32)
    query_grad, slot_grad = sweep(grad_update, (query_zero, slot_zero))
    own_probs = jnp.exp(own_scores - maxima) / totals
    own_grad_scores = own_probs * (own_grad_probs - deltas)
    query_full = query_grad + score_scale * own_grad_scores[..., None] * key_heads[:, :, None, :]
    own_key_grads = score_scale * jnp.sum(own_grad_scores[..., None] * query_heads, axis=2)
    own_value_grads = jnp.sum(own_probs[..., None] * cotangent_heads, axis=2)
    query_flat = query_full.reshape(tokens, kv_heads * group_size * HD)
    own_key_flat = own_key_grads.reshape(tokens, kv_heads * HD)
    own_value_flat = own_value_grads.reshape(tokens, kv_heads * HD)
    slot_terms = slot_grad.reshape(total_slots, kv_heads * 2 * HD)
    slot_total = lax.psum_scatter(
        slot_terms.astype(jnp.bfloat16), "ctx", scatter_dimension=0, tiled=True
    ).astype(jnp.float32)
    slot_total = slot_total.reshape(SLOT_DEV, kv_heads, 2, HD)
    slot_spread = jnp.einsum(
        "gts,sgcd->tgcd",
        slot_picks.astype(jnp.float32),
        slot_total,
        precision=lax.Precision.HIGHEST,
    )
    token_sizes = jnp.sum(jnp.where(slot_picks, counts[:, None, :], 0), axis=2).T.astype(
        jnp.float32
    )
    grad_keys = slot_spread[:, :, 0] / token_sizes[..., None] + own_key_flat.reshape(
        tokens, kv_heads, HD
    )
    grad_values = slot_spread[:, :, 1] / token_sizes[..., None] + own_value_flat.reshape(
        tokens, kv_heads, HD
    )
    return (
        query_flat.astype(jnp.bfloat16),
        grad_keys.astype(jnp.bfloat16).reshape(tokens, kv_heads * HD),
        grad_values.astype(jnp.bfloat16).reshape(tokens, kv_heads * HD),
    )


def solution(mesh):
    return jax.shard_map(
        local,
        mesh=mesh,
        in_specs=(
            P(("ctx", "head"), None),
            P(("ctx", "head"), None),
            P(("ctx", "head"), None),
            P("head", "ctx"),
            P(("ctx", "head"), None),
        ),
        out_specs=(P("ctx", "head"), P("ctx", "head"), P("ctx", "head")),
        check_vma=False,
    )
```

profile of v0, /device:TPU:0, one launch (start us, length us, event | category | flops | bytes accessed | tf_op | source)
XLA Modules:
  0.0 233.4 jit_solution(15196201795948508610)
XLA Ops:
  7.2 1.5 copy.147
  8.7 4.2 %all-to-all-start = ((bf16[48,4,256]{2,0,1:T(8,128)(2,1)}), bf16[48,4,256]{2,0,1:T(8,128)(2,1)S(1)}, u32[]{:S(2)}, u32[]{:S(2)}) async-start(bf16[48,4,256]{2,0,1:T(8,128)(2,1)} %bitcast.228), calls=%async_computation | async-start | bytes 196608 | tf_op jit(solution)/shard_map/all_to_all | solution.py:38
  14.7 1.5 copy.146
  17.2 3.3 %all-to-all-start.1 = ((bf16[48,4,256]{2,0,1:T(8,128)(2,1)}), bf16[48,4,256]{2,0,1:T(8,128)(2,1)S(1)}, u32[]{:S(2)}, u32[]{:S(2)}) async-start(bf16[48,4,256]{2,0,1:T(8,128)(2,1)} %bitcast.227), calls=%async_computation.1 | async-start | bytes 196608 | tf_op jit(solution)/shard_map/all_to_all | solution.py:39
  20.6 21.2 %all-gather = bf16[8,96,2]{1,2,0:T(2,128)(2,1)S(1)} all-gather(bf16[1,96,2]{1,2,0:T(2,128)(2,1)S(1)} %fusion.65), channel_id=1, replica_groups=mesh['ctx'=8,'head'=4] {'ctx'}, dimensions={0}, use_global_device_ids=true | all-gather | bytes 3456 | tf_op jit(solution)/shard_map/all_gather | solution.py:75
  42.0 2.1 copy.145
  44.1 2.1 copy.144
  46.2 3.5 %all-to-all-start.2 = ((bf16[48,4,2048]{2,0,1:T(8,128)(2,1)}), bf16[48,4,2048]{2,0,1:T(8,128)(2,1)S(1)}, u32[]{:S(2)}, u32[]{:S(2)}) async-start(bf16[48,4,2048]{2,0,1:T(8,128)(2,1)} %bitcast.226), calls=%async_computation.2 | async-start | bytes 1572864 | tf_op jit(solution)/shard_map/all_to_all | solution.py:37
  50.6 10.7 %all-to-all-done.2 = bf16[48,4,2048]{2,0,1:T(8,128)(2,1)S(1)} async-done(((bf16[48,4,2048]{2,0,1:T(8,128)(2,1)}), bf16[48,4,2048]{2,0,1:T(8,128)(2,1)S(1)}, u32[]{:S(2)}, u32[]{:S(2)}) %all-to-all-start.2) | async-done | bytes 786464 | tf_op jit(solution)/shard_map/all_to_all | solution.py:37
  61.3 3.5 %all-to-all-start.3 = ((bf16[48,4,2048]{2,0,1:T(8,128)(2,1)}), bf16[48,4,2048]{2,0,1:T(8,128)(2,1)S(1)}, u32[]{:S(2)}, u32[]{:S(2)}) async-start(bf16[48,4,2048]{2,0,1:T(8,128)(2,1)} %bitcast.225), calls=%async_computation.3 | async-start | bytes 1572864 | tf_op jit(solution)/shard_map/all_to_all | solution.py:40
  64.9 32.0 %all_gather.6 = bf16[768,512]{1,0:T(8,128)(2,1)S(1)} all-gather(bf16[96,512]{1,0:T(8,128)(2,1)S(1)} %reshape.320), channel_id=1, replica_groups=mesh['ctx'=8,'head'=4] {'ctx'}, dimensions={0}, use_global_device_ids=true | all-gather | bytes 884736 | tf_op jit(solution)/shard_map/all_gather | solution.py:74
  99.4 2.2 fusion.68
  102.6 6.0 %while.58 = (s32[]{:T(128)}, f32[192,2,8]{0,2,1:T(8,128)S(1)}, f32[192,2,8]{0,2,1:T(8,128)S(1)}, s32[2]{0:T(128)S(1)}, s32[]{:T(128)}, /*index=5*/bf16[768,2]{0,...) while((s32[]{:T(128)}, f32[192,2,8]{0,2,1:T(8,128)S(1)}, ...), condition=%wide.region_6.7_spmd.clone.clone, body=%wide.region_1.6_spmd.clone.clone.sunk | while | flops 310852608 | bytes 11031967 | solution.py:129
  103.9 3.4 %conditional.12 = ((f32[192,2,8]{0,2,1:T(8,128)S(1)}, f32[192,2,8]{0,2,1:T(8,128)S(1)})) conditional(s32[]{:T(128)} %convert_element_type.151, (f32[192,2,8]{0,2,1:T(8,128)S(1)}, f32[192,2,8]{0,2,1:T(8,128)S(1)}) %tuple.177, (s32[]{:T(128)}, bf16[768,2]{0,1:T(2,128)(2,1)S(1)}, s32[]{:T(128)}, s32[192,2]{0,1:T(2,128)S(1)}, ...), branch_computations={%region_2.2_spmd, %region_3.0_spmd} | conditional | flops 310852608 | bytes 11031630 | solution.py:122
  104.3 1.2 fusion.6
  105.5 1.9 fusion.9
  109.6 1.3 copy.121
  111.1 2.2 fusion.69
  115.2 6.2 %while.59 = (s32[]{:T(128)}, f32[192,2,8]{0,2,1:T(8,128)S(1)}, s32[2]{0:T(128)S(1)}, s32[]{:T(128)}, bf16[768,2]{0,1:T(2,128)(2,1)S(1)}, /*index=5*/s32[192,2]{0...) while((s32[]{:T(128)}, f32[192,2,8]{0,2,1:T(8,128)S(1)}, ...), condition=%wide.region_11.12_spmd.clone.clone, body=%wide.region_7.11_spmd.clone.clone.sunk | while | flops 611656704 | bytes 11789747 | solution.py:129
  116.4 3.7 %conditional.13 = (f32[192,2,8]{0,2,1:T(8,128)S(1)}) conditional(s32[]{:T(128)} %convert_element_type.152, f32[192,2,8]{0,2,1:T(8,128)S(1)} %get-tuple-element.1583, (s32[]{:T(128)}, bf16[768,2]{0,1:T(2,128)(2,1)S(1)}, s32[]{:T(128)}, s32[192,2]{0,1:T(2,128)S(1)}, bf16[768,2,2,128]{3,0,1,2:T(8,128)(2,1)S(1)}, ...), branch_computations={%region_8.8_spmd, %region_9.10_spmd} | conditional | flops 611656704 | bytes 11789394 | solution.py:122
  117.6 2.5 %fusion.17 = f32[192,2,8]{0,2,1:T(8,128)S(1)} fusion(f32[2,384,192,8]{1,2,3,0:T(8,128)S(1)} %fusion.21, f32[192,2,8]{0,2,1:T(8,128)S(1)} %get-tuple-element.899, f32[192,2,8]{0,2,1:T(8,128)S(1)} %get-tuple-element.898, pred[192,2,384]{2,0,1:T(8,128)(4,1)S(1)} %or_and_fusion.1, bf16[192,2,8,128]{3,0,2,1:T(8,128)(2,1)S(1)} %get-tuple-element.900, ...), kind=kOutput, calls=%fused_computation.27 | convolution fusion | flops 309064704 | bytes 5894152 | tf_op jit(solution)/shard_map/while/body/eval_jaxpr/cond/branch_1_fun/rghd,sgd->rghs/dot_general | solution.py:153
  121.4 1.2 broadcast_in_dim.79
  122.7 1.3 broadcast_in_dim.78
  124.0 16.5 %while.60 = (s32[]{:T(128)}, f32[192,2,8,128]{3,0,2,1:T(8,128)}, f32[768,2,2,128]{3,0,1,2:T(8,128)}, s32[2]{0:T(128)S(1)}, s32[]{:T(128)}, /*index=5*/bf16[768,2...) while((s32[]{:T(128)}, f32[192,2,8,128]{3,0,2,1:T(8,128)}, ...), condition=%wide.region_15.16_spmd.clone.clone, body=%wide.region_12.15_spmd.clone.clone.sunk | while | flops 1521263616 | bytes 33187328 | solution.py:129
  125.2 13.8 %conditional.14 = ((f32[192,2,8,128]{3,0,2,1:T(8,128)}, f32[768,2,2,128]{3,0,1,2:T(8,128)})) conditional(s32[]{:T(128)} %convert_element_type.153, (f32[192,2,8,128]{3,0,2,1:T(8,128)}, f32[768,2,2,128]{3,0,1,2:T(8,128)}) %tuple.182, (s32[]{:T(128)}, bf16[768,2,2,128]{3,0,1,2:T(8,128)(2,1)S(1)}, bf16[768,2]{0,1:T(2,128)(2,1)S(1)}, s32[]{:T(128)}, ...), branch_computations={%region_13.13_spmd, %region_14.14_spmd} | conditional | flops 1521263616 | bytes 33186926 | solution.py:122
  125.6 1.7 fusion.33
  130.6 3.4 %bitcast_add_fusion = f32[192,2,8,128]{3,0,2,1:T(8,128)} fusion(f32[192,2,8,128]{3,0,2,1:T(8,128)} %get-tuple-element.914, bf16[192,2,8,384]{3,0,2,1:T(8,128)(2,1)S(1)} %fusion.30, bf16[768,2,2,128]{3,0,1,2:T(8,128)(2,1)S(1)} %get-tuple-element.915, s32[]{:T(128)S(6)} %select_n.130), kind=kOutput, calls=%fused_computation.59 | convolution fusion | flops 302776320 | bytes 5701636 | tf_op jit(solution)/shard_map/while/body/eval_jaxpr/cond/branch_1_fun/rghs,sgd->rghd/dot_general | solution.py:176
  134.0 1.3 maximum_add_fusion
  135.2 3.8 %dynamic_update_slice.2 = f32[768,2,2,128]{3,0,1,2:T(8,128)} dynamic-update-slice(f32[768,2,2,128]{3,0,1,2:T(8,128)} %get-tuple-element.925, f32[384,2,2,128]{3,0,1,2:T(8,128)S(1)} %maximum_add_fusion, s32[]{:T(128)S(6)} %select_n.130, s32[]{:T(128)} %constant.284.clone, s32[]{:T(128)} %constant.284.clone, s32[]{:T(128)} %constant.284.clone) | dynamic-update-slice | bytes 1572868 | tf_op jit(solution)/shard_map/while/body/eval_jaxpr/cond/branch_1_fun/dynamic_update_slice | solution.py:187
  140.5 1.7 copy.90
  143.6 1.9 add_convert_fusion
  148.4 75.4 %reduce-scatter.4.cloned.1.call-done = bf16[96,512]{1,0:T(8,128)(2,1)} async-done(((bf16[768,512]{1,0:T(8,128)(2,1)}), bf16[96,512]{1,0:T(8,128)(2,1)}) %reduce-scatter.4.cloned.1.call-update) | async-done | bytes 98320
  (93 shorter events, 25.8 us)
Async XLA Ops:
  7.2 42.6 %copy-start.6 = (s32[2,192]{1,0:T(2,128)S(1)}, s32[2,192]{1,0:T(2,128)}, u32[]{:S(2)}) copy-start(s32[2,192]{1,0:T(2,128)} %param.21) | copy-start | bytes 4612
  8.7 8.5 %all-to-all-start = ((bf16[48,4,256]{2,0,1:T(8,128)(2,1)}), bf16[48,4,256]{2,0,1:T(8,128)(2,1)S(1)}, u32[]{:S(2)}, u32[]{:S(2)}) async-start(bf16[48,4,256]{2,0,1:T(8,128)(2,1)} %bitcast.228), calls=%async_computation | async-start | bytes 196608 | tf_op jit(solution)/shard_map/all_to_all | solution.py:38
  17.2 29.0 %all-to-all-start.1 = ((bf16[48,4,256]{2,0,1:T(8,128)(2,1)}), bf16[48,4,256]{2,0,1:T(8,128)(2,1)S(1)}, u32[]{:S(2)}, u32[]{:S(2)}) async-start(bf16[48,4,256]{2,0,1:T(8,128)(2,1)} %bitcast.227), calls=%async_computation.1 | async-start | bytes 196608 | tf_op jit(solution)/shard_map/all_to_all | solution.py:39
  46.2 15.1 %all-to-all-start.2 = ((bf16[48,4,2048]{2,0,1:T(8,128)(2,1)}), bf16[48,4,2048]{2,0,1:T(8,128)(2,1)S(1)}, u32[]{:S(2)}, u32[]{:S(2)}) async-start(bf16[48,4,2048]{2,0,1:T(8,128)(2,1)} %bitcast.226), calls=%async_computation.2 | async-start | bytes 1572864 | tf_op jit(solution)/shard_map/all_to_all | solution.py:37
  61.3 47.3 %all-to-all-start.3 = ((bf16[48,4,2048]{2,0,1:T(8,128)(2,1)}), bf16[48,4,2048]{2,0,1:T(8,128)(2,1)S(1)}, u32[]{:S(2)}, u32[]{:S(2)}) async-start(bf16[48,4,2048]{2,0,1:T(8,128)(2,1)} %bitcast.225), calls=%async_computation.3 | async-start | bytes 1572864 | tf_op jit(solution)/shard_map/all_to_all | solution.py:40
  64.8 159.0 %reduce-scatter.4.cloned.1.call-start = ((), (), s32[]{:S(2)}) async-start(), calls=%async_computation.5 | async-start | bytes 884736
  99.1 3.5 %copy-start = (bf16[24,8,16,128]{3,2,1,0:T(8,128)(2,1)}, bf16[24,8,16,128]{3,2,1,0:T(8,128)(2,1)S(1)}, u32[]{:S(2)}) copy-start(bf16[24,8,16,128]{3,2,1,0:T(8,128)(2,1)S(1)} %copy.120) | copy-start | bytes 2359300
  108.7 0.9 copy-start.4
  110.9 4.3 %copy-start.2 = (bf16[24,8,16,128]{3,2,1,0:T(8,128)(2,1)}, bf16[24,8,16,128]{3,2,1,0:T(8,128)(2,1)S(1)}, u32[]{:S(2)}) copy-start(bf16[24,8,16,128]{3,2,1,0:T(8,128)(2,1)S(1)} %copy.121) | copy-start | bytes 2359300
  142.2 4.9 %copy-start.1 = (bf16[24,8,16,128]{3,2,1,0:T(8,128)(2,1)S(1)}, bf16[24,8,16,128]{3,2,1,0:T(8,128)(2,1)}, u32[]{:S(2)}) copy-start(bf16[24,8,16,128]{3,2,1,0:T(8,128)(2,1)} %copy-done) | copy-start | bytes 2359300
  142.2 5.6 %copy-start.3 = (bf16[24,8,16,128]{3,2,1,0:T(8,128)(2,1)S(1)}, bf16[24,8,16,128]{3,2,1,0:T(8,128)(2,1)}, u32[]{:S(2)}) copy-start(bf16[24,8,16,128]{3,2,1,0:T(8,128)(2,1)} %copy-done.2) | copy-start | bytes 2359300
  142.2 5.6 %copy-start.5 = (f32[192,2,8]{2,1,0:T(2,128)S(1)}, f32[192,2,8]{2,1,0:T(2,128)}, u32[]{:S(2)}) copy-start(f32[192,2,8]{2,1,0:T(2,128)} %copy.97) | copy-start | bytes 36868
Sparse Core Ops, SparseCore 0:
  143.5 80.2 reduce-scatter.3
where the time goes:
time: 235 us; the launch traced here: 233 us
  waiting for transfers between devices  87.1 us (37%)
  blocking collectives  53.2 us (23%)
  local copies, waits for them, and re-layouts  31.5 us (13%)
  matrix products  18.1 us (8%)
  starting transfers between devices  14.5 us (6%)
  between operations  14.4 us (6%)
  other arithmetic  9.87 us (4%)
  loops' own time  4.58 us (2%)
    unnamed x2, waiting for transfers between devices  75.4 us
    all_gather x1, blocking collectives, local(): lax.all_gather(slot_rows, 'ctx', axis=0, tiled=True)  32 us
    all_gather x1, blocking collectives, local(): lax.all_gather(slot_live, 'ctx', axis=0, tiled=True)  21.2 us
    all_to_all x1, waiting for transfers between devices, local(): lax.all_to_all(queries, 'head', split_axis=1, concat_axis=0, tiled=True)  10.7 us
    unnamed x23, local copies, waits for them, and re-layouts  6.46 us
  transfers between devices with their start and end apart: 5, of which 3 were waited for; matrix products, arithmetic and copies ran while one was open for 10% of the time, Pallas kernels for 0%

commit v1 on v0

v1 whole, which is shorter than its diff:
```python
import functools

import jax
import jax.numpy as jnp
from jax import lax
from jax.experimental import pallas as pl
from jax.experimental.pallas import tpu as pltpu
from jax.sharding import PartitionSpec as P

QH = 64
KVH = 8
HD = 128
SLOT_DEV = 96
GROUP = QH // KVH
SCALE = HD ** (-0.5)
LOG2E = 1.4426950408889634
DEAD = 1024.0
HIDDEN = 2.0**96
PAIR = 2


def nt(a, b):
    return lax.dot_general(a, b, (((1,), (1,)), ((), ())), preferred_element_type=jnp.float32)


def nn(a, b):
    return lax.dot_general(a, b, (((1,), (0,)), ((), ())), preferred_element_type=jnp.float32)


def tn(a, b):
    return lax.dot_general(a, b, (((0,), (0,)), ((), ())), preferred_element_type=jnp.float32)


def slot_picks(seg_row, tokens):
    return lax.broadcasted_iota(jnp.int32, (SLOT_DEV, tokens), 0) == seg_row


def merge_kernel(seg_ref, kv_ref, out_ref):
    kv_heads, tokens = seg_ref.shape
    for g in range(kv_heads):
        picks = slot_picks(seg_ref[g : g + 1, :], tokens).astype(jnp.float32)
        counts = jnp.sum(picks, axis=1, keepdims=True)
        sums = nn(picks.astype(jnp.bfloat16), kv_ref[:, g * 2 * HD : (g + 1) * 2 * HD])
        rows = sums / jnp.maximum(counts, 1.0)
        is_key = lax.broadcasted_iota(jnp.int32, rows.shape, 1) < HD
        rows = jnp.where((counts == 0.0) & is_key, DEAD, rows)
        out_ref[:, g * 2 * HD : (g + 1) * 2 * HD] = rows.astype(jnp.bfloat16)


def attend_kernel(g, steps, place_ref, seg_ref, segcol_ref, kvtok_ref, qo_ref, *refs):
    blocks = refs[: 2 * steps]
    dq_ref, near_ref, far_ref, own_ref, kx, vx, kt = refs[2 * steps :]
    tokens = kvtok_ref.shape[0]
    slots = 2 * steps * SLOT_DEV
    outer = place_ref[0]
    inner = place_ref[1]
    base = g * 2 * HD
    lane = lax.broadcasted_iota(jnp.int32, (SLOT_DEV, HD), 1)
    row = lax.broadcasted_iota(jnp.int32, (SLOT_DEV, HD), 0)
    for r, block in enumerate(blocks):
        rows = pl.ds(r * SLOT_DEV, SLOT_DEV)
        key = block[:, base : base + HD].astype(jnp.float32)
        if r == 0:
            extra = jnp.where(lane == row, 1.0, 0.0)
        else:
            step = r % steps
            if step == 0:
                there = inner == 1
            else:
                there = outer >= step
            hide = (key[:, 0:1] > 100.0) | jnp.logical_not(there)
            extra = jnp.where(hide & (lane >= SLOT_DEV), -HIDDEN, 0.0)
        key = jnp.where(key > 100.0, 0.0, key)
        kx[rows, 0:HD] = key.astype(jnp.bfloat16)
        kx[rows, HD : 2 * HD] = extra.astype(jnp.bfloat16)
        vx[rows, :] = block[:, base + HD : base + 2 * HD]
    kx[slots : slots + tokens, 0:HD] = kvtok_ref[:, base : base + HD]
    kx[slots : slots + tokens, HD : 2 * HD] = jnp.zeros((tokens, HD), jnp.bfloat16)
    vx[slots : slots + tokens, :] = kvtok_ref[:, base + HD : base + 2 * HD]
    kt[...] = kx[:, 0:HD].astype(jnp.float32).T.astype(jnp.bfloat16)

    qlane = lax.broadcasted_iota(jnp.int32, (tokens, HD), 1)
    late = (qlane >= segcol_ref[:, g : g + 1]) & (qlane < SLOT_DEV)
    qe = jnp.where(late, -HIDDEN, jnp.where(qlane == SLOT_DEV, 1.0, 0.0)).astype(jnp.bfloat16)
    qe = jnp.concatenate([qe] * PAIR, axis=0)
    width = PAIR * tokens
    eye_row = lax.broadcasted_iota(jnp.int32, (tokens, width), 0)
    eye_lane = lax.broadcasted_iota(jnp.int32, (tokens, width), 1)
    eye = eye_row == lax.rem(eye_lane, tokens)
    factor = SCALE * LOG2E

    dk = None
    dv = None
    for first in range(0, GROUP, PAIR):
        q2 = jnp.concatenate(
            [qo_ref[:, (first + i) * HD : (first + i + 1) * HD] for i in range(PAIR)], axis=0
        )
        o2 = jnp.concatenate(
            [
                qo_ref[:, (GROUP + first + i) * HD : (GROUP + first + i + 1) * HD]
                for i in range(PAIR)
            ],
            axis=0,
        )
        scores = nt(kx[...], jnp.concatenate([q2, qe], axis=1))
        own_score = jnp.sum(jnp.where(eye, scores[slots:], 0.0), axis=0, keepdims=True)
        scores = scores[:slots]
        top = jnp.maximum(jnp.max(scores, axis=0, keepdims=True), own_score)
        weights = jnp.exp2((scores - top) * factor)
        own_weight = jnp.exp2((own_score - top) * factor)
        inverse = 1.0 / (jnp.sum(weights, axis=0, keepdims=True) + own_weight)
        probs = weights * inverse
        own_prob = own_weight * inverse
        grad_probs = nt(vx[...], o2)
        own_grad_prob = jnp.sum(jnp.where(eye, grad_probs[slots:], 0.0), axis=0, keepdims=True)
        grad_probs = grad_probs[:slots]
        delta = jnp.sum(probs * grad_probs, axis=0, keepdims=True) + own_prob * own_grad_prob
        grad_scores = probs * (grad_probs - delta)
        own_grad_score = own_prob * (own_grad_prob - delta)
        low_probs = jnp.concatenate(
            [probs.astype(jnp.bfloat16), jnp.where(eye, own_prob, 0.0).astype(jnp.bfloat16)], axis=0
        )
        low_grads = jnp.concatenate(
            [
                grad_scores.astype(jnp.bfloat16),
                jnp.where(eye, own_grad_score, 0.0).astype(jnp.bfloat16),
            ],
            axis=0,
        )
        dv_part = nn(low_probs, o2)
        dk_part = nn(low_grads, q2)
        dv = dv_part if dv is None else dv + dv_part
        dk = dk_part if dk is None else dk + dk_part
        dq = (SCALE * nn(kt[...], low_grads)).T.astype(jnp.bfloat16)
        for i in range(PAIR):
            dq_ref[:, (first + i) * HD : (first + i + 1) * HD] = dq[i * tokens : (i + 1) * tokens]
    dk = dk * SCALE
    half = steps * SLOT_DEV
    near_ref[:, 0:HD] = dk[:half].astype(near_ref.dtype)
    near_ref[:, HD : 2 * HD] = dv[:half].astype(near_ref.dtype)
    far_ref[:, 0:HD] = dk[half:slots].astype(far_ref.dtype)
    far_ref[:, HD : 2 * HD] = dv[half:slots].astype(far_ref.dtype)
    own_ref[:, 0:HD] = dk[slots:]
    own_ref[:, HD : 2 * HD] = dv[slots:]


def spread_kernel(steps, seg_ref, *refs):
    kv_heads, tokens = seg_ref.shape
    gk_ref, gv_ref = refs[-2:]
    per_head = steps + 1
    for g in range(kv_heads):
        parts = refs[g * per_head : (g + 1) * per_head]
        total = parts[0][...].astype(jnp.float32)
        for part in parts[1:steps]:
            total = total + part[...].astype(jnp.float32)
        picks = slot_picks(seg_ref[g : g + 1, :], tokens).astype(jnp.float32)
        counts = jnp.sum(picks, axis=1, keepdims=True)
        total = total / jnp.maximum(counts, 1.0)
        high = total.astype(jnp.bfloat16)
        low = (total - high.astype(jnp.float32)).astype(jnp.bfloat16)
        picks = picks.astype(jnp.bfloat16)
        spread = tn(picks, high) + tn(picks, low) + parts[steps][...]
        gk_ref[:, g * HD : (g + 1) * HD] = spread[:, 0:HD].astype(jnp.bfloat16)
        gv_ref[:, g * HD : (g + 1) * HD] = spread[:, HD : 2 * HD].astype(jnp.bfloat16)


def vmem_spec():
    return pl.BlockSpec(memory_space=pltpu.VMEM)


def smem_spec():
    return pl.BlockSpec(memory_space=pltpu.SMEM)


def params():
    return pltpu.CompilerParams(vmem_limit_bytes=28 * 2**20)


def local(queries, keys, values, segment_ids, grad_out):
    rows = queries.shape[0]
    heads = lax.axis_size("head")
    tokens = rows * heads
    kv_heads = KVH // heads
    shards = lax.axis_size("ctx")
    steps = shards // 2
    me = lax.axis_index("ctx")
    place = jnp.stack([me // 2, me % 2]).astype(jnp.int32)
    swap = [(c, c ^ 1) for c in range(shards)]

    kv = jnp.stack(
        [keys.reshape(rows, heads, kv_heads, HD), values.reshape(rows, heads, kv_heads, HD)], axis=3
    )
    kv = lax.all_to_all(
        kv.reshape(rows, heads * kv_heads * 2 * HD), "head", split_axis=1, concat_axis=0, tiled=True
    )
    q_parts = queries.reshape(rows, heads, kv_heads, GROUP * HD)
    o_parts = grad_out.reshape(rows, heads, kv_heads, GROUP * HD)
    qo = []
    for g in range(kv_heads):
        both = jnp.concatenate([q_parts[:, :, g], o_parts[:, :, g]], axis=2)
        qo.append(
            lax.all_to_all(
                both.reshape(rows, heads * 2 * GROUP * HD),
                "head",
                split_axis=1,
                concat_axis=0,
                tiled=True,
            )
        )

    merged = pl.pallas_call(
        merge_kernel,
        out_shape=jax.ShapeDtypeStruct((SLOT_DEV, kv_heads * 2 * HD), jnp.bfloat16),
        in_specs=[vmem_spec(), vmem_spec()],
        out_specs=vmem_spec(),
        compiler_params=params(),
        name="merge",
    )(segment_ids, kv)

    near = [merged]
    for k in range(1, steps):
        near.append(lax.ppermute(merged, "ctx", [(c, c + 2 * k) for c in range(shards - 2 * k)]))
    far = [lax.ppermute(block, "ctx", swap) for block in near]
    blocks = near + far

    seg_col = segment_ids.T
    slots = shards * SLOT_DEV
    half = steps * SLOT_DEV
    dq = []
    spread_args = []
    for g in range(kv_heads):
        dq_g, near_g, far_g, own_g = pl.pallas_call(
            functools.partial(attend_kernel, g, steps),
            out_shape=(
                jax.ShapeDtypeStruct((tokens, GROUP * HD), jnp.bfloat16),
                jax.ShapeDtypeStruct((half, 2 * HD), jnp.float32),
                jax.ShapeDtypeStruct((half, 2 * HD), jnp.bfloat16),
                jax.ShapeDtypeStruct((tokens, 2 * HD), jnp.float32),
            ),
            in_specs=[smem_spec()] + [vmem_spec()] * (4 + shards),
            out_specs=[vmem_spec()] * 4,
            scratch_shapes=[
                pltpu.VMEM((slots + tokens, 2 * HD), jnp.bfloat16),
                pltpu.VMEM((slots + tokens, HD), jnp.bfloat16),
                pltpu.VMEM((HD, slots + tokens), jnp.bfloat16),
            ],
            compiler_params=params(),
            cost_estimate=pl.CostEstimate(
                flops=10 * tokens * GROUP * (slots + tokens) * HD,
                bytes_accessed=4 * 2**20,
                transcendentals=tokens * GROUP * slots,
            ),
            name="attend",
        )(place, segment_ids, seg_col, kv, qo[g], *blocks)
        dq.append(dq_g)
        sums = near_g + lax.ppermute(far_g, "ctx", swap).astype(jnp.float32)
        low_sums = sums.astype(jnp.bfloat16)
        spread_args.append(sums[:SLOT_DEV])
        for k in range(1, steps):
            part = low_sums[k * SLOT_DEV : (k + 1) * SLOT_DEV]
            spread_args.append(
                lax.ppermute(part, "ctx", [(c, c - 2 * k) for c in range(2 * k, shards)])
            )
        spread_args.append(own_g)

    grad_keys, grad_values = pl.pallas_call(
        functools.partial(spread_kernel, steps),
        out_shape=(jax.ShapeDtypeStruct((tokens, kv_heads * HD), jnp.bfloat16),) * 2,
        in_specs=[vmem_spec()] * (1 + len(spread_args)),
        out_specs=[vmem_spec()] * 2,
        compiler_params=params(),
        name="spread",
    )(segment_ids, *spread_args)
    return jnp.concatenate(dq, axis=1), grad_keys, grad_values


def solution(mesh):
    return jax.shard_map(
        local,
        mesh=mesh,
        in_specs=(
            P(("ctx", "head"), None),
            P(("ctx", "head"), None),
            P(("ctx", "head"), None),
            P("head", "ctx"),
            P(("ctx", "head"), None),
        ),
        out_specs=(P("ctx", "head"), P("ctx", "head"), P("ctx", "head")),
        check_vma=False,
    )
```

time: 235 us -> 90.5 us (0.39)
  waiting for transfers between devices: 87.1 us -> 24.2 us
  blocking collectives: 53.2 us -> 0 us
  starting transfers between devices: 14.5 us -> 35.6 us
  local copies, waits for them, and re-layouts: 31.5 us -> 11.6 us
  matrix products: 18.1 us -> 0 us
  Pallas kernels: 0 us -> 14.2 us
  between operations: 14.4 us -> 0.95 us
  other arithmetic: 9.87 us -> 3.3 us
  loops' own time: 4.58 us -> 0 us
    unnamed x2 -> x0, waiting for transfers between devices: 75.4 us -> none
    all_gather x2 -> x0, blocking collectives: 53.2 us -> none  [the longest x1 32 us: local(): lax.all_gather(slot_rows, 'ctx', axis=0, tiled=True)]
    ppermute x0 -> x15, starting transfers between devices: none -> 24.4 us  [the longest x3 10.1 us: local(): lax.ppermute(merged, 'ctx', [(c, c + 2 * k) for c in range(shards - 2 * k)])]
    dot_general x13 -> x0, matrix products: 18.1 us -> none  [the longest x3 3.69 us: tile_inputs(): jnp.einsum('rghd,sgd->rghs', query_heads, key_block, preferred_element_ty...]
    ppermute x0 -> x15, waiting for transfers between devices: none -> 14.4 us  [the longest x6 6.69 us: local(): lax.ppermute(part, 'ctx', [(c, c - 2 * k) for c in range(2 * k, shards)])]
    pallas_call x0 -> x4, Pallas kernels: none -> 14.2 us  [the longest x2 13 us: local(): pl.pallas_call(functools.partial(attend_kernel, g, steps), out_shape=(jax...]
    all_to_all x4 -> x1, local copies, waits for them, and re-layouts: 7.29 us -> 0.76 us  [local(): lax.all_to_all(kv.reshape(rows, heads * kv_heads * 2 * HD), 'head', split...]
    reduce_sum x5 -> x0, other arithmetic: 4.83 us -> none  [the longest x1 1.86 us: stat_update(): new_totals = totals * jnp.exp(maxima - new_max) + jnp.sum(weights, axis=3)]
  transfers between devices with their start and end apart: 5 -> 18, of which waited for: 3 -> 9; matrix products, arithmetic and copies ran while one was open for 10% -> 10% of each run, Pallas kernels for 0% -> 15%
where the time goes in v1:
time: 90.5 us; the launch traced here: 89.8 us
  starting transfers between devices  35.6 us (39%)
  waiting for transfers between devices  24.2 us (27%)
  Pallas kernels  14.2 us (16%)
  local copies, waits for them, and re-layouts  11.6 us (13%)
  other arithmetic  3.3 us (4%)
  between operations  0.95 us (1%)
    pallas_call x2, Pallas kernels, local(): pl.pallas_call(functools.partial(attend_kernel, g, steps), out_shape=(jax...  13 us
    ppermute x3, starting transfers between devices, local(): lax.ppermute(merged, 'ctx', [(c, c + 2 * k) for c in range(shards - 2 * k)])  10.1 us
    all_to_all x2, waiting for transfers between devices, local(): lax.all_to_all(both.reshape(rows, heads * 2 * GROUP * HD), 'head', split_...  9.83 us
    ppermute x6, starting transfers between devices, local(): lax.ppermute(part, 'ctx', [(c, c - 2 * k) for c in range(2 * k, shards)])  7.75 us
    all_to_all x2, starting transfers between devices, local(): lax.all_to_all(both.reshape(rows, heads * 2 * GROUP * HD), 'head', split_...  6.99 us
    ppermute x6, waiting for transfers between devices, local(): lax.ppermute(part, 'ctx', [(c, c - 2 * k) for c in range(2 * k, shards)])  6.69 us
    ppermute x4, waiting for transfers between devices, local(): far = [lax.ppermute(block, 'ctx', swap) for block in near]  6.52 us
    ppermute x4, starting transfers between devices, local(): far = [lax.ppermute(block, 'ctx', swap) for block in near]  4.39 us
  transfers between devices with their start and end apart: 18, of which 9 were waited for; matrix products, arithmetic and copies ran while one was open for 10% of the time, Pallas kernels for 15%

profile of v1, /device:TPU:0, one launch (start us, length us, event | category | flops | bytes accessed | tf_op | source)
XLA Modules:
  0.0 89.8 jit_solution(3494890808341721177)
XLA Ops:
  1.6 0.9 %stack_reshape.6 = bf16[48,4,2,1,128]{4,2,1,0,3:T(2,128)(2,1)S(1)} reshape(bf16[48,1024]{1,0:T(8,128)(2,1)} %param.6) | data formatting | bytes 196608 | tf_op jit(solution)/shard_map/stack;reshape | solution.py:190
  3.9 4.2 %all-to-all-start = ((bf16[48,4,512]{2,0,1:T(8,128)(2,1)}), bf16[48,4,512]{2,0,1:T(8,128)(2,1)S(1)}, u32[]{:S(2)}, u32[]{:S(2)}) async-start(bf16[48,4,512]{2,0,1:T(8,128)(2,1)} %all_to_all.38), calls=%async_computation | async-start | bytes 393216 | tf_op jit(solution)/shard_map/all_to_all | solution.py:193
  8.7 1.9 %fusion.3 = (bf16[48,4,1,1024]{3,2,1,0:T(2,128)(2,1)S(1)}, bf16[48,4,1,1024]{3,2,1,0:T(2,128)(2,1)S(1)}) fusion(bf16[48,4,2,1024]{3,2,1,0:T(2,128)(2,1)S(1)} %reshape.28), kind=kLoop, calls=%fused_computation.14 | loop fusion | bytes 1572864 | tf_op jit(solution)/shard_map/slice | solution.py:200
  11.2 1.1 %fusion.2 = (bf16[48,4,1,1024]{3,2,1,0:T(2,128)(2,1)S(1)}, bf16[48,4,1,1024]{3,2,1,0:T(2,128)(2,1)S(1)}) fusion(bf16[48,4,2,1024]{3,2,1,0:T(2,128)(2,1)S(1)} %reshape.27), kind=kLoop, calls=%fused_computation.13 | loop fusion | bytes 1572864 | tf_op jit(solution)/shard_map/slice | solution.py:200
  13.1 1.0 %pad_maximum_fusion = bf16[48,4,2048]{2,0,1:T(8,128)(2,1)} fusion(bf16[48,4,1024]{2,0,1:T(8,128)(2,1)S(1)} %get-tuple-element.39, bf16[48,4,1024]{2,0,1:T(8,128)(2,1)S(1)} %get-tuple-element.40), kind=kLoop, calls=%fused_computation | loop fusion | flops 1572864 | bytes 1572864 | tf_op jit(solution)/shard_map/concatenate | solution.py:200
  14.1 3.5 %all-to-all-start.1 = ((bf16[48,4,2048]{2,0,1:T(8,128)(2,1)}), bf16[48,4,2048]{2,0,1:T(8,128)(2,1)S(1)}, u32[]{:S(2)}, u32[]{:S(2)}) async-start(bf16[48,4,2048]{2,0,1:T(8,128)(2,1)} %pad_maximum_fusion), calls=%async_computation.1 | async-start | bytes 1572864 | tf_op jit(solution)/shard_map/all_to_all | solution.py:202
  18.4 0.9 %pad_maximum_fusion.1 = bf16[48,4,2048]{2,0,1:T(8,128)(2,1)} fusion(bf16[48,4,1024]{2,0,1:T(8,128)(2,1)S(1)} %get-tuple-element.37, bf16[48,4,1024]{2,0,1:T(8,128)(2,1)S(1)} %get-tuple-element.38), kind=kLoop, calls=%fused_computation.1 | loop fusion | flops 1572864 | bytes 1572864 | tf_op jit(solution)/shard_map/concatenate | solution.py:200
  19.4 9.8 %all-to-all-done.1 = bf16[48,4,2048]{2,0,1:T(8,128)(2,1)S(1)} async-done(((bf16[48,4,2048]{2,0,1:T(8,128)(2,1)}), bf16[48,4,2048]{2,0,1:T(8,128)(2,1)S(1)}, u32[]{:S(2)}, u32[]{:S(2)}) %all-to-all-start.1) | async-done | bytes 786464 | tf_op jit(solution)/shard_map/all_to_all | solution.py:202
  29.2 3.5 %all-to-all-start.2 = ((bf16[48,4,2048]{2,0,1:T(8,128)(2,1)}), bf16[48,4,2048]{2,0,1:T(8,128)(2,1)S(1)}, u32[]{:S(2)}, u32[]{:S(2)}) async-start(bf16[48,4,2048]{2,0,1:T(8,128)(2,1)} %pad_maximum_fusion.1), calls=%async_computation.2 | async-start | bytes 1572864 | tf_op jit(solution)/shard_map/all_to_all | solution.py:202
  32.9 4.1 %collective-permute-start = (bf16[96,512]{1,0:T(8,128)(2,1)S(1)}, bf16[96,512]{1,0:T(8,128)(2,1)S(1)}, u32[]{:S(2)}, u32[]{:S(2)}) collective-permute-start(bf16[96,512]{1,0:T(8,128)(2,1)S(1)} %merge.1.refs_0_), channel_id=1, source_target_pairs={{0,8},{4,12},{8,16},{12,20},{16,24},{20,28},{1,9},{5,13},{9,17},{1... | collective-permute-start | bytes 294920 | tf_op jit(solution)/shard_map/ppermute | solution.py:222
  37.0 4.5 %collective-permute-start.1 = (bf16[96,512]{1,0:T(8,128)(2,1)S(1)}, bf16[96,512]{1,0:T(8,128)(2,1)S(1)}, u32[]{:S(2)}, u32[]{:S(2)}) collective-permute-start(bf16[96,512]{1,0:T(8,128)(2,1)S(1)} %merge.1.refs_0_), channel_id=1, source_target_pairs={{0,16},{4,20},{8,24},{12,28},{1,17},{5,21},{9,25},{13,29},{2,18},{... | collective-permute-start | bytes 294920 | tf_op jit(solution)/shard_map/ppermute | solution.py:222
  41.5 1.5 %collective-permute-start.2 = (bf16[96,512]{1,0:T(8,128)(2,1)S(1)}, bf16[96,512]{1,0:T(8,128)(2,1)S(1)}, u32[]{:S(2)}, u32[]{:S(2)}) collective-permute-start(bf16[96,512]{1,0:T(8,128)(2,1)S(1)} %merge.1.refs_0_), channel_id=1, source_target_pairs={{0,24},{4,28},{1,25},{5,29},{2,26},{6,30},{3,27},{7,31}} | collective-permute-start | bytes 294920 | tf_op jit(solution)/shard_map/ppermute | solution.py:222
  43.2 1.6 %collective-permute-start.3 = (bf16[96,512]{1,0:T(8,128)(2,1)S(1)}, bf16[96,512]{1,0:T(8,128)(2,1)S(1)}, u32[]{:S(2)}, u32[]{:S(2)}) collective-permute-start(bf16[96,512]{1,0:T(8,128)(2,1)S(1)} %merge.1.refs_0_), channel_id=1, source_target_pairs={{0,4},{4,0},{8,12},{12,8},{16,20},{20,16},{24,28},{28,24},{1,5},{5... | collective-permute-start | bytes 294920 | tf_op jit(solution)/shard_map/ppermute | solution.py:223
  45.3 1.5 %collective-permute-start.5 = (bf16[96,512]{1,0:T(8,128)(2,1)S(1)}, bf16[96,512]{1,0:T(8,128)(2,1)S(1)}, u32[]{:S(2)}, u32[]{:S(2)}) collective-permute-start(bf16[96,512]{1,0:T(8,128)(2,1)S(1)} %collective-permute-done.1.refs_2_), channel_id=1, source_target_pairs={{0,4},{4,0},{8,12},{12,8},{16,20},{20,16},{24,28},{28,24},{1,5},{5... | collective-permute-start | bytes 294920 | tf_op jit(solution)/shard_map/ppermute | solution.py:223
  47.6 1.1 %collective-permute-done.3.refs_4_ = bf16[96,512]{1,0:T(8,128)(2,1)S(1)} collective-permute-done((bf16[96,512]{1,0:T(8,128)(2,1)S(1)}, bf16[96,512]{1,0:T(8,128)(2,1)S(1)}, u32[]{:S(2)}, u32[]{:S(2)}) %collective-permute-start.3) | collective-permute-done | bytes 98336 | tf_op jit(solution)/shard_map/ppermute | solution.py:223
  48.7 2.1 %collective-permute-done.4.refs_5_ = bf16[96,512]{1,0:T(8,128)(2,1)S(1)} collective-permute-done((bf16[96,512]{1,0:T(8,128)(2,1)S(1)}, bf16[96,512]{1,0:T(8,128)(2,1)S(1)}, u32[]{:S(2)}, u32[]{:S(2)}) %collective-permute-start.4) | collective-permute-done | bytes 98336 | tf_op jit(solution)/shard_map/ppermute | solution.py:223
  50.8 2.1 %collective-permute-done.5.refs_6_ = bf16[96,512]{1,0:T(8,128)(2,1)S(1)} collective-permute-done((bf16[96,512]{1,0:T(8,128)(2,1)S(1)}, bf16[96,512]{1,0:T(8,128)(2,1)S(1)}, u32[]{:S(2)}, u32[]{:S(2)}) %collective-permute-start.5) | collective-permute-done | bytes 98336 | tf_op jit(solution)/shard_map/ppermute | solution.py:223
  52.9 1.2 %collective-permute-done.6.refs_7_ = bf16[96,512]{1,0:T(8,128)(2,1)S(1)} collective-permute-done((bf16[96,512]{1,0:T(8,128)(2,1)S(1)}, bf16[96,512]{1,0:T(8,128)(2,1)S(1)}, u32[]{:S(2)}, u32[]{:S(2)}) %collective-permute-start.6) | collective-permute-done | bytes 98336 | tf_op jit(solution)/shard_map/ppermute | solution.py:223
  54.2 6.5 %attend.2 = (bf16[192,1024]{1,0:T(8,128)(2,1)S(1)}, f32[384,256]{1,0:T(8,128)S(1)}, bf16[384,256]{1,0:T(8,128)(2,1)S(1)}, f32[192,256]{1,0:T(8,128)S(1)}) custom-call(s32[2]{0:T(128)S(1)} %pad_add_fusion.place_ref, s32[2,192]{1,0:T(2,128)S(1)} %copy-done, s32[192,2]{1,0:T(8,128)S(1)} %bitcast.27, bf16[192,512]{1,0:T(8,128)(2,1)S(1)} %bitcast.25, ...), custom_call_target="tpu_custom_call" | custom-call | flops 1887436800 | bytes 4194304 | tf_op jit(solution)/shard_map/attend/pallas_call | solution.py:232
  60.7 1.6 %collective-permute-start.7 = (bf16[384,256]{1,0:T(8,128)(2,1)S(1)}, bf16[384,256]{1,0:T(8,128)(2,1)S(1)}, u32[]{:S(2)}, u32[]{:S(2)}) collective-permute-start(bf16[384,256]{1,0:T(8,128)(2,1)S(1)} %get-tuple-element.16), channel_id=1, source_target_pairs={{0,4},{4,0},{8,12},{12,8},{16,20},{20,16},{24,28},{28,24},{1,5},{5... | collective-permute-start | bytes 589832 | tf_op jit(solution)/shard_map/ppermute | solution.py:256
  64.9 6.5 %attend.3 = (bf16[192,1024]{1,0:T(8,128)(2,1)S(1)}, f32[384,256]{1,0:T(8,128)S(1)}, bf16[384,256]{1,0:T(8,128)(2,1)S(1)}, f32[192,256]{1,0:T(8,128)S(1)}) custom-call(s32[2]{0:T(128)S(1)} %pad_add_fusion.place_ref, s32[2,192]{1,0:T(2,128)S(1)} %copy-done, s32[192,2]{1,0:T(8,128)S(1)} %bitcast.28, bf16[192,512]{1,0:T(8,128)(2,1)S(1)} %bitcast.26, ...), custom_call_target="tpu_custom_call" | custom-call | flops 1887436800 | bytes 4194304 | tf_op jit(solution)/shard_map/attend/pallas_call | solution.py:232
  72.1 1.3 %collective-permute-start.8 = (bf16[96,256]{1,0:T(8,128)(2,1)S(1)}, bf16[96,256]{1,0:T(8,128)(2,1)S(1)}, u32[]{:S(2)}, u32[]{:S(2)}) collective-permute-start(bf16[96,256]{1,0:T(8,128)(2,1)S(1)} %get-tuple-element.36), channel_id=1, source_target_pairs={{8,0},{12,4},{16,8},{20,12},{24,16},{28,20},{9,1},{13,5},{17,9},{2... | collective-permute-start | bytes 147464 | tf_op jit(solution)/shard_map/ppermute | solution.py:262
  73.4 1.3 %collective-permute-start.9 = (bf16[96,256]{1,0:T(8,128)(2,1)S(1)}, bf16[96,256]{1,0:T(8,128)(2,1)S(1)}, u32[]{:S(2)}, u32[]{:S(2)}) collective-permute-start(bf16[96,256]{1,0:T(8,128)(2,1)S(1)} %get-tuple-element.35), channel_id=1, source_target_pairs={{16,0},{20,4},{24,8},{28,12},{17,1},{21,5},{25,9},{29,13},{18,2},{... | collective-permute-start | bytes 147464 | tf_op jit(solution)/shard_map/ppermute | solution.py:262
  74.7 1.3 %collective-permute-start.10 = (bf16[96,256]{1,0:T(8,128)(2,1)S(1)}, bf16[96,256]{1,0:T(8,128)(2,1)S(1)}, u32[]{:S(2)}, u32[]{:S(2)}) collective-permute-start(bf16[96,256]{1,0:T(8,128)(2,1)S(1)} %get-tuple-element.34), channel_id=1, source_target_pairs={{24,0},{28,4},{25,1},{29,5},{26,2},{30,6},{27,3},{31,7}} | collective-permute-start | bytes 147464 | tf_op jit(solution)/shard_map/ppermute | solution.py:262
  76.0 1.2 %collective-permute-done.11 = bf16[384,256]{1,0:T(8,128)(2,1)S(1)} collective-permute-done((bf16[384,256]{1,0:T(8,128)(2,1)S(1)}, bf16[384,256]{1,0:T(8,128)(2,1)S(1)}, u32[]{:S(2)}, u32[]{:S(2)}) %collective-permute-start.11) | collective-permute-done | bytes 196640 | tf_op jit(solution)/shard_map/ppermute | solution.py:256
  77.2 1.3 %collective-permute-start.12 = (bf16[96,256]{1,0:T(8,128)(2,1)S(1)}, bf16[96,256]{1,0:T(8,128)(2,1)S(1)}, u32[]{:S(2)}, u32[]{:S(2)}) collective-permute-start(bf16[96,256]{1,0:T(8,128)(2,1)S(1)} %get-tuple-element.33), channel_id=1, source_target_pairs={{8,0},{12,4},{16,8},{20,12},{24,16},{28,20},{9,1},{13,5},{17,9},{2... | collective-permute-start | bytes 147464 | tf_op jit(solution)/shard_map/ppermute | solution.py:262
  78.5 1.3 %collective-permute-start.13 = (bf16[96,256]{1,0:T(8,128)(2,1)S(1)}, bf16[96,256]{1,0:T(8,128)(2,1)S(1)}, u32[]{:S(2)}, u32[]{:S(2)}) collective-permute-start(bf16[96,256]{1,0:T(8,128)(2,1)S(1)} %get-tuple-element.32), channel_id=1, source_target_pairs={{16,0},{20,4},{24,8},{28,12},{17,1},{21,5},{25,9},{29,13},{18,2},{... | collective-permute-start | bytes 147464 | tf_op jit(solution)/shard_map/ppermute | solution.py:262
  79.8 1.3 %collective-permute-start.14 = (bf16[96,256]{1,0:T(8,128)(2,1)S(1)}, bf16[96,256]{1,0:T(8,128)(2,1)S(1)}, u32[]{:S(2)}, u32[]{:S(2)}) collective-permute-start(bf16[96,256]{1,0:T(8,128)(2,1)S(1)} %get-tuple-element.31), channel_id=1, source_target_pairs={{24,0},{28,4},{25,1},{29,5},{26,2},{30,6},{27,3},{31,7}} | collective-permute-start | bytes 147464 | tf_op jit(solution)/shard_map/ppermute | solution.py:262
  82.1 1.9 %collective-permute-done.10.refs_3_ = bf16[96,256]{1,0:T(8,128)(2,1)S(1)} collective-permute-done((bf16[96,256]{1,0:T(8,128)(2,1)S(1)}, bf16[96,256]{1,0:T(8,128)(2,1)S(1)}, u32[]{:S(2)}, u32[]{:S(2)}) %collective-permute-start.10) | collective-permute-done | bytes 49184 | tf_op jit(solution)/shard_map/ppermute | solution.py:262
  84.0 1.8 %collective-permute-done.13.refs_7_ = bf16[96,256]{1,0:T(8,128)(2,1)S(1)} collective-permute-done((bf16[96,256]{1,0:T(8,128)(2,1)S(1)}, bf16[96,256]{1,0:T(8,128)(2,1)S(1)}, u32[]{:S(2)}, u32[]{:S(2)}) %collective-permute-start.13) | collective-permute-done | bytes 49184 | tf_op jit(solution)/shard_map/ppermute | solution.py:262
  85.8 3.0 %collective-permute-done.14.refs_8_ = bf16[96,256]{1,0:T(8,128)(2,1)S(1)} collective-permute-done((bf16[96,256]{1,0:T(8,128)(2,1)S(1)}, bf16[96,256]{1,0:T(8,128)(2,1)S(1)}, u32[]{:S(2)}, u32[]{:S(2)}) %collective-permute-start.14) | collective-permute-done | bytes 49184 | tf_op jit(solution)/shard_map/ppermute | solution.py:262
  88.8 1.0 %spread.1 = (bf16[192,256]{1,0:T(8,128)(2,1)}, bf16[192,256]{1,0:T(8,128)(2,1)}) custom-call(s32[2,192]{1,0:T(2,128)S(1)} %copy-done, f32[96,256]{1,0:T(8,128)S(1)} %slice.52.refs_0_, bf16[96,256]{1,0:T(8,128)(2,1)S(1)} %collective-permute-done.8.refs_1_, bf16[96,256]{1,0:T(8,128)(2,1)S(1)} %collective-permute-done.9.refs_2_, ...), custom_call_target="tpu_custom_call" | custom-call | tf_op jit(solution)/shard_map/spread/pallas_call | solution.py:266
  (48 shorter events, 11.2 us)
Async XLA Ops:
  2.5 5.6 %copy-start.7 = (bf16[48,8192]{1,0:T(8,128)(2,1)S(1)}, bf16[48,8192]{1,0:T(8,128)(2,1)}, u32[]{:S(2)}) copy-start(bf16[48,8192]{1,0:T(8,128)(2,1)} %param.9) | copy-start | bytes 2359300
  3.9 10.2 %all-to-all-start = ((bf16[48,4,512]{2,0,1:T(8,128)(2,1)}), bf16[48,4,512]{2,0,1:T(8,128)(2,1)S(1)}, u32[]{:S(2)}, u32[]{:S(2)}) async-start(bf16[48,4,512]{2,0,1:T(8,128)(2,1)} %all_to_all.38), calls=%async_computation | async-start | bytes 393216 | tf_op jit(solution)/shard_map/all_to_all | solution.py:193
  8.7 1.9 %copy-start.8 = (bf16[48,8192]{1,0:T(8,128)(2,1)S(1)}, bf16[48,8192]{1,0:T(8,128)(2,1)}, u32[]{:S(2)}) copy-start(bf16[48,8192]{1,0:T(8,128)(2,1)} %param.5) | copy-start | bytes 2359300
  14.1 15.1 %all-to-all-start.1 = ((bf16[48,4,2048]{2,0,1:T(8,128)(2,1)}), bf16[48,4,2048]{2,0,1:T(8,128)(2,1)S(1)}, u32[]{:S(2)}, u32[]{:S(2)}) async-start(bf16[48,4,2048]{2,0,1:T(8,128)(2,1)} %pad_maximum_fusion), calls=%async_computation.1 | async-start | bytes 1572864 | tf_op jit(solution)/shard_map/all_to_all | solution.py:202
  19.4 13.3 %copy-start = (s32[2,192]{1,0:T(2,128)S(1)}, s32[2,192]{1,0:T(2,128)}, u32[]{:S(2)}) copy-start(s32[2,192]{1,0:T(2,128)} %seg_ref.7) | copy-start | bytes 4612
  29.2 33.0 %all-to-all-start.2 = ((bf16[48,4,2048]{2,0,1:T(8,128)(2,1)}), bf16[48,4,2048]{2,0,1:T(8,128)(2,1)S(1)}, u32[]{:S(2)}, u32[]{:S(2)}) async-start(bf16[48,4,2048]{2,0,1:T(8,128)(2,1)} %pad_maximum_fusion.1), calls=%async_computation.2 | async-start | bytes 1572864 | tf_op jit(solution)/shard_map/all_to_all | solution.py:202
  32.9 11.8 %collective-permute-start = (bf16[96,512]{1,0:T(8,128)(2,1)S(1)}, bf16[96,512]{1,0:T(8,128)(2,1)S(1)}, u32[]{:S(2)}, u32[]{:S(2)}) collective-permute-start(bf16[96,512]{1,0:T(8,128)(2,1)S(1)} %merge.1.refs_0_), channel_id=1, source_target_pairs={{0,8},{4,12},{8,16},{12,20},{16,24},{20,28},{1,9},{5,13},{9,17},{1... | collective-permute-start | bytes 294920 | tf_op jit(solution)/shard_map/ppermute | solution.py:222
  37.0 8.2 %collective-permute-start.1 = (bf16[96,512]{1,0:T(8,128)(2,1)S(1)}, bf16[96,512]{1,0:T(8,128)(2,1)S(1)}, u32[]{:S(2)}, u32[]{:S(2)}) collective-permute-start(bf16[96,512]{1,0:T(8,128)(2,1)S(1)} %merge.1.refs_0_), channel_id=1, source_target_pairs={{0,16},{4,20},{8,24},{12,28},{1,17},{5,21},{9,25},{13,29},{2,18},{... | collective-permute-start | bytes 294920 | tf_op jit(solution)/shard_map/ppermute | solution.py:222
  41.5 5.3 %collective-permute-start.2 = (bf16[96,512]{1,0:T(8,128)(2,1)S(1)}, bf16[96,512]{1,0:T(8,128)(2,1)S(1)}, u32[]{:S(2)}, u32[]{:S(2)}) collective-permute-start(bf16[96,512]{1,0:T(8,128)(2,1)S(1)} %merge.1.refs_0_), channel_id=1, source_target_pairs={{0,24},{4,28},{1,25},{5,29},{2,26},{6,30},{3,27},{7,31}} | collective-permute-start | bytes 294920 | tf_op jit(solution)/shard_map/ppermute | solution.py:222
  43.2 5.6 %collective-permute-start.3 = (bf16[96,512]{1,0:T(8,128)(2,1)S(1)}, bf16[96,512]{1,0:T(8,128)(2,1)S(1)}, u32[]{:S(2)}, u32[]{:S(2)}) collective-permute-start(bf16[96,512]{1,0:T(8,128)(2,1)S(1)} %merge.1.refs_0_), channel_id=1, source_target_pairs={{0,4},{4,0},{8,12},{12,8},{16,20},{20,16},{24,28},{28,24},{1,5},{5... | collective-permute-start | bytes 294920 | tf_op jit(solution)/shard_map/ppermute | solution.py:223
  44.7 6.1 %collective-permute-start.4 = (bf16[96,512]{1,0:T(8,128)(2,1)S(1)}, bf16[96,512]{1,0:T(8,128)(2,1)S(1)}, u32[]{:S(2)}, u32[]{:S(2)}) collective-permute-start(bf16[96,512]{1,0:T(8,128)(2,1)S(1)} %collective-permute-done.refs_1_), channel_id=1, source_target_pairs={{0,4},{4,0},{8,12},{12,8},{16,20},{20,16},{24,28},{28,24},{1,5},{5... | collective-permute-start | bytes 294920 | tf_op jit(solution)/shard_map/ppermute | solution.py:223
  45.3 7.7 %collective-permute-start.5 = (bf16[96,512]{1,0:T(8,128)(2,1)S(1)}, bf16[96,512]{1,0:T(8,128)(2,1)S(1)}, u32[]{:S(2)}, u32[]{:S(2)}) collective-permute-start(bf16[96,512]{1,0:T(8,128)(2,1)S(1)} %collective-permute-done.1.refs_2_), channel_id=1, source_target_pairs={{0,4},{4,0},{8,12},{12,8},{16,20},{20,16},{24,28},{28,24},{1,5},{5... | collective-permute-start | bytes 294920 | tf_op jit(solution)/shard_map/ppermute | solution.py:223
  46.8 7.4 %collective-permute-start.6 = (bf16[96,512]{1,0:T(8,128)(2,1)S(1)}, bf16[96,512]{1,0:T(8,128)(2,1)S(1)}, u32[]{:S(2)}, u32[]{:S(2)}) collective-permute-start(bf16[96,512]{1,0:T(8,128)(2,1)S(1)} %collective-permute-done.2.refs_3_), channel_id=1, source_target_pairs={{0,4},{4,0},{8,12},{12,8},{16,20},{20,16},{24,28},{28,24},{1,5},{5... | collective-permute-start | bytes 294920 | tf_op jit(solution)/shard_map/ppermute | solution.py:223
  50.8 9.8 %copy-start.1 = (bf16[96,512]{1,0:T(8,128)(2,1)}, bf16[96,512]{1,0:T(8,128)(2,1)S(1)}, u32[]{:S(2)}) copy-start(bf16[96,512]{1,0:T(8,128)(2,1)S(1)} %collective-permute-done.4.refs_5_) | copy-start | bytes 294916
  52.9 7.7 %copy-start.3 = (bf16[96,512]{1,0:T(8,128)(2,1)}, bf16[96,512]{1,0:T(8,128)(2,1)S(1)}, u32[]{:S(2)}) copy-start(bf16[96,512]{1,0:T(8,128)(2,1)S(1)} %collective-permute-done.5.refs_6_) | copy-start | bytes 294916
  54.2 6.5 %copy-start.5 = (bf16[96,512]{1,0:T(8,128)(2,1)}, bf16[96,512]{1,0:T(8,128)(2,1)S(1)}, u32[]{:S(2)}) copy-start(bf16[96,512]{1,0:T(8,128)(2,1)S(1)} %collective-permute-done.6.refs_7_) | copy-start | bytes 294916
  60.7 11.3 %collective-permute-start.7 = (bf16[384,256]{1,0:T(8,128)(2,1)S(1)}, bf16[384,256]{1,0:T(8,128)(2,1)S(1)}, u32[]{:S(2)}, u32[]{:S(2)}) collective-permute-start(bf16[384,256]{1,0:T(8,128)(2,1)S(1)} %get-tuple-element.16), channel_id=1, source_target_pairs={{0,4},{4,0},{8,12},{12,8},{16,20},{20,16},{24,28},{28,24},{1,5},{5... | collective-permute-start | bytes 589832 | tf_op jit(solution)/shard_map/ppermute | solution.py:256
  62.2 0.9 copy-start.2
  63.1 0.9 copy-start.4
  64.0 0.9 copy-start.6
  71.4 5.7 %collective-permute-start.11 = (bf16[384,256]{1,0:T(8,128)(2,1)S(1)}, bf16[384,256]{1,0:T(8,128)(2,1)S(1)}, u32[]{:S(2)}, u32[]{:S(2)}) collective-permute-start(bf16[384,256]{1,0:T(8,128)(2,1)S(1)} %get-tuple-element.19), channel_id=1, source_target_pairs={{0,4},{4,0},{8,12},{12,8},{16,20},{20,16},{24,28},{28,24},{1,5},{5... | collective-permute-start | bytes 589832 | tf_op jit(solution)/shard_map/ppermute | solution.py:256
  72.1 7.8 %collective-permute-start.8 = (bf16[96,256]{1,0:T(8,128)(2,1)S(1)}, bf16[96,256]{1,0:T(8,128)(2,1)S(1)}, u32[]{:S(2)}, u32[]{:S(2)}) collective-permute-start(bf16[96,256]{1,0:T(8,128)(2,1)S(1)} %get-tuple-element.36), channel_id=1, source_target_pairs={{8,0},{12,4},{16,8},{20,12},{24,16},{28,20},{9,1},{13,5},{17,9},{2... | collective-permute-start | bytes 147464 | tf_op jit(solution)/shard_map/ppermute | solution.py:262
  73.4 8.7 %collective-permute-start.9 = (bf16[96,256]{1,0:T(8,128)(2,1)S(1)}, bf16[96,256]{1,0:T(8,128)(2,1)S(1)}, u32[]{:S(2)}, u32[]{:S(2)}) collective-permute-start(bf16[96,256]{1,0:T(8,128)(2,1)S(1)} %get-tuple-element.35), channel_id=1, source_target_pairs={{16,0},{20,4},{24,8},{28,12},{17,1},{21,5},{25,9},{29,13},{18,2},{... | collective-permute-start | bytes 147464 | tf_op jit(solution)/shard_map/ppermute | solution.py:262
  74.7 9.3 %collective-permute-start.10 = (bf16[96,256]{1,0:T(8,128)(2,1)S(1)}, bf16[96,256]{1,0:T(8,128)(2,1)S(1)}, u32[]{:S(2)}, u32[]{:S(2)}) collective-permute-start(bf16[96,256]{1,0:T(8,128)(2,1)S(1)} %get-tuple-element.34), channel_id=1, source_target_pairs={{24,0},{28,4},{25,1},{29,5},{26,2},{30,6},{27,3},{31,7}} | collective-permute-start | bytes 147464 | tf_op jit(solution)/shard_map/ppermute | solution.py:262
  77.2 6.8 %collective-permute-start.12 = (bf16[96,256]{1,0:T(8,128)(2,1)S(1)}, bf16[96,256]{1,0:T(8,128)(2,1)S(1)}, u32[]{:S(2)}, u32[]{:S(2)}) collective-permute-start(bf16[96,256]{1,0:T(8,128)(2,1)S(1)} %get-tuple-element.33), channel_id=1, source_target_pairs={{8,0},{12,4},{16,8},{20,12},{24,16},{28,20},{9,1},{13,5},{17,9},{2... | collective-permute-start | bytes 147464 | tf_op jit(solution)/shard_map/ppermute | solution.py:262
  78.5 7.3 %collective-permute-start.13 = (bf16[96,256]{1,0:T(8,128)(2,1)S(1)}, bf16[96,256]{1,0:T(8,128)(2,1)S(1)}, u32[]{:S(2)}, u32[]{:S(2)}) collective-permute-start(bf16[96,256]{1,0:T(8,128)(2,1)S(1)} %get-tuple-element.32), channel_id=1, source_target_pairs={{16,0},{20,4},{24,8},{28,12},{17,1},{21,5},{25,9},{29,13},{18,2},{... | collective-permute-start | bytes 147464 | tf_op jit(solution)/shard_map/ppermute | solution.py:262
  79.8 9.0 %collective-permute-start.14 = (bf16[96,256]{1,0:T(8,128)(2,1)S(1)}, bf16[96,256]{1,0:T(8,128)(2,1)S(1)}, u32[]{:S(2)}, u32[]{:S(2)}) collective-permute-start(bf16[96,256]{1,0:T(8,128)(2,1)S(1)} %get-tuple-element.31), channel_id=1, source_target_pairs={{24,0},{28,4},{25,1},{29,5},{26,2},{30,6},{27,3},{31,7}} | collective-permute-start | bytes 147464 | tf_op jit(solution)/shard_map/ppermute | solution.py:262

commit v2 on v1

v2 whole, which is shorter than its diff:
```python
import functools

import jax
import jax.numpy as jnp
from jax import lax
from jax.experimental import pallas as pl
from jax.experimental.pallas import tpu as pltpu
from jax.sharding import PartitionSpec as P

QH = 64
KVH = 8
HD = 128
SLOT_DEV = 96
GROUP = QH // KVH
GW = GROUP * HD
SCALE = HD ** (-0.5)
LOG2E = 1.4426950408889634
DEAD = 1024.0
HIDDEN = 2.0**96
NEAR = 4


def nt(a, b):
    return lax.dot_general(a, b, (((1,), (1,)), ((), ())), preferred_element_type=jnp.float32)


def nn(a, b):
    return lax.dot_general(a, b, (((1,), (0,)), ((), ())), preferred_element_type=jnp.float32)


def tn(a, b):
    return lax.dot_general(a, b, (((0,), (0,)), ((), ())), preferred_element_type=jnp.float32)


def slot_picks(seg_row, tokens):
    return lax.broadcasted_iota(jnp.int32, (SLOT_DEV, tokens), 0) == seg_row


def lanes(start, size):
    return pl.ds(pl.multiple_of(start, HD), size)


def pack_kv_kernel(kv_heads, place_ref, key_ref, value_ref, *out_refs):
    me = place_ref[1]
    for m, out in enumerate(out_refs):
        other = lax.bitwise_xor(me, m)
        for g in range(kv_heads):
            start = (other * kv_heads + g) * HD
            out[:, 2 * g * HD : (2 * g + 1) * HD] = key_ref[:, lanes(start, HD)]
            out[:, (2 * g + 1) * HD : (2 * g + 2) * HD] = value_ref[:, lanes(start, HD)]


def pack_qo_kernel(kv_heads, heads, place_ref, q_ref, o_ref, *refs):
    outs, sems = refs[:-1], refs[-1]
    me = place_ref[1]
    copies = []
    for g in range(kv_heads):
        for m in range(1, heads):
            start = (lax.bitwise_xor(me, m) * kv_heads + g) * GW
            out = outs[g * (heads - 1) + m - 1]
            for part, source in enumerate((q_ref, o_ref)):
                copies.append(
                    pltpu.make_async_copy(
                        source.at[:, lanes(start, GW)],
                        out.at[:, part * GW : (part + 1) * GW],
                        sems.at[len(copies)],
                    )
                )
    for copy in copies:
        copy.start()
    for copy in copies:
        copy.wait()


def merge_kernel(heads, place_ref, seg_ref, *refs):
    pieces, outs, whole = refs[:heads], refs[heads:-1], refs[-1]
    tokens = seg_ref.shape[1]
    rows = tokens // heads
    me = place_ref[1]
    for m, piece in enumerate(pieces):
        start = pl.multiple_of(lax.bitwise_xor(me, m) * rows, 16)
        whole[pl.ds(start, rows), :] = piece[...]
    for g, out in enumerate(outs):
        picks = slot_picks(seg_ref[g : g + 1, :], tokens).astype(jnp.float32)
        counts = jnp.sum(picks, axis=1, keepdims=True)
        sums = nn(picks.astype(jnp.bfloat16), whole[:, g * 2 * HD : (g + 1) * 2 * HD])
        merged = sums / jnp.maximum(counts, 1.0)
        is_key = lax.broadcasted_iota(jnp.int32, merged.shape, 1) < HD
        out[...] = jnp.where((counts == 0.0) & is_key, DEAD, merged).astype(jnp.bfloat16)


def attend_kernel(g, order, heads, place_ref, segcol_ref, q_ref, o_ref, *refs):
    shards = len(order)
    kv_pieces, refs = refs[:heads], refs[heads:]
    qo_pieces, refs = refs[: heads - 1], refs[heads - 1 :]
    blocks, refs = refs[:shards], refs[shards:]
    dq_ref, own_ref, refs = refs[0], refs[1], refs[2:]
    term_refs, (kx, vx, kt, mine, sems) = refs[:-5], refs[-5:]
    rows = kv_pieces[0].shape[0]
    slots = shards * SLOT_DEV
    shard = place_ref[0]
    me = place_ref[1]
    start = (me * kv_pieces[0].shape[1] // (2 * HD) + g) * GW
    copies = [
        pltpu.make_async_copy(
            source.at[:, lanes(start, GW)], mine.at[:, part * GW : (part + 1) * GW], sems.at[part]
        )
        for part, source in enumerate((q_ref, o_ref))
    ]
    for copy in copies:
        copy.start()

    lane = lax.broadcasted_iota(jnp.int32, (SLOT_DEV, HD), 1)
    row = lax.broadcasted_iota(jnp.int32, (SLOT_DEV, HD), 0)
    for r, (m, block) in enumerate(zip(order, blocks)):
        at = pl.ds(r * SLOT_DEV, SLOT_DEV)
        key = block[:, 0:HD].astype(jnp.float32)
        if m == 0:
            extra = jnp.where(lane == row, 1.0, 0.0)
        else:
            hide = (key[:, 0:1] > 100.0) | (lax.bitwise_xor(shard, m) > shard)
            extra = jnp.where(hide & (lane >= SLOT_DEV), -HIDDEN, 0.0)
        kx[at, 0:HD] = jnp.where(key > 100.0, 0.0, key).astype(jnp.bfloat16)
        kx[at, HD : 2 * HD] = extra.astype(jnp.bfloat16)
        vx[at, :] = block[:, HD : 2 * HD]
    kx[slots : slots + rows, HD : 2 * HD] = jnp.zeros((rows, HD), jnp.bfloat16)
    kt[...] = kx[0:slots, 0:HD].astype(jnp.float32).T.astype(jnp.bfloat16)

    width = GROUP * rows
    qlane = lax.broadcasted_iota(jnp.int32, (rows, HD), 1)
    eye_row = lax.broadcasted_iota(jnp.int32, (rows, width), 0)
    eye_lane = lax.broadcasted_iota(jnp.int32, (rows, width), 1)
    eye = eye_row == lax.rem(eye_lane, rows)
    factor = SCALE * LOG2E
    for copy in copies:
        copy.wait()

    dk = None
    dv = None
    for m in range(heads):
        qo = mine if m == 0 else qo_pieces[m - 1]
        at = pl.ds(pl.multiple_of(lax.bitwise_xor(me, m) * rows, 16), rows)
        own_key = kv_pieces[m][:, 2 * g * HD : (2 * g + 1) * HD]
        kx[slots : slots + rows, 0:HD] = own_key
        vx[slots : slots + rows, :] = kv_pieces[m][:, (2 * g + 1) * HD : (2 * g + 2) * HD]
        late = (qlane >= segcol_ref[at, g : g + 1]) & (qlane < SLOT_DEV)
        qe = jnp.where(late, -HIDDEN, jnp.where(qlane == SLOT_DEV, 1.0, 0.0)).astype(jnp.bfloat16)
        q2 = jnp.concatenate([qo[:, h * HD : (h + 1) * HD] for h in range(GROUP)], axis=0)
        o2 = jnp.concatenate([qo[:, GW + h * HD : GW + (h + 1) * HD] for h in range(GROUP)], axis=0)
        qx = jnp.concatenate([q2, jnp.concatenate([qe] * GROUP, axis=0)], axis=1)
        scores = nt(kx[...], qx)
        own_score = jnp.sum(jnp.where(eye, scores[slots:], 0.0), axis=0, keepdims=True)
        scores = scores[:slots]
        top = jnp.maximum(jnp.max(scores, axis=0, keepdims=True), own_score)
        weights = jnp.exp2((scores - top) * factor)
        own_weight = jnp.exp2((own_score - top) * factor)
        inverse = 1.0 / (jnp.sum(weights, axis=0, keepdims=True) + own_weight)
        probs = weights * inverse
        own_prob = own_weight * inverse
        grad_probs = nt(vx[...], o2)
        own_grad_prob = jnp.sum(jnp.where(eye, grad_probs[slots:], 0.0), axis=0, keepdims=True)
        grad_probs = grad_probs[:slots]
        delta = jnp.sum(probs * grad_probs, axis=0, keepdims=True) + own_prob * own_grad_prob
        low_grads = (probs * (grad_probs - delta)).astype(jnp.bfloat16)
        low_probs = probs.astype(jnp.bfloat16)
        own_grad_score = own_prob * (own_grad_prob - delta)
        own_low_probs = jnp.where(eye, own_prob, 0.0).astype(jnp.bfloat16)
        own_low_grads = jnp.where(eye, own_grad_score, 0.0).astype(jnp.bfloat16)
        dv_part = nn(low_probs, o2)
        dk_part = nn(low_grads, q2)
        dv = dv_part if dv is None else dv + dv_part
        dk = dk_part if dk is None else dk + dk_part
        own_ref[at, 0:HD] = SCALE * nn(own_low_grads, q2)
        own_ref[at, HD : 2 * HD] = nn(own_low_probs, o2)
        dq = nn(kt[...], low_grads) + tn(own_key, own_low_grads)
        dq = (SCALE * dq).T.astype(jnp.bfloat16)
        for h in range(GROUP):
            dq_ref[at, h * HD : (h + 1) * HD] = dq[h * rows : (h + 1) * rows]
    dk = dk * SCALE
    span = slots // len(term_refs)
    for m, term in enumerate(term_refs):
        part = slice(m * span, (m + 1) * span)
        term[:, 0:HD] = dk[part].astype(term.dtype)
        term[:, HD : 2 * HD] = dv[part].astype(term.dtype)


def spread_kernel(parts_per_head, seg_ref, *refs):
    kv_heads, tokens = seg_ref.shape
    gk_ref, gv_ref = refs[-2:]
    for g in range(kv_heads):
        parts = refs[g * parts_per_head : (g + 1) * parts_per_head]
        total = parts[0][...].astype(jnp.float32)
        for part in parts[1:-1]:
            total = total + part[...].astype(jnp.float32)
        picks = slot_picks(seg_ref[g : g + 1, :], tokens).astype(jnp.float32)
        counts = jnp.sum(picks, axis=1, keepdims=True)
        total = total / jnp.maximum(counts, 1.0)
        high = total.astype(jnp.bfloat16)
        low = (total - high.astype(jnp.float32)).astype(jnp.bfloat16)
        picks = picks.astype(jnp.bfloat16)
        spread = tn(picks, high) + tn(picks, low) + parts[-1][...]
        gk_ref[:, g * HD : (g + 1) * HD] = spread[:, 0:HD].astype(jnp.bfloat16)
        gv_ref[:, g * HD : (g + 1) * HD] = spread[:, HD : 2 * HD].astype(jnp.bfloat16)


def in_vmem(count):
    return [pl.BlockSpec(memory_space=pltpu.VMEM)] * count


def in_smem():
    return [pl.BlockSpec(memory_space=pltpu.SMEM)]


def anywhere(count):
    return [pl.BlockSpec(memory_space=pl.ANY)] * count


def params():
    return pltpu.CompilerParams(vmem_limit_bytes=28 * 2**20)


def shape(*dims, dtype=jnp.bfloat16):
    return jax.ShapeDtypeStruct(dims, dtype)


def swap(x, axis, size, m):
    return lax.ppermute(x, axis, [(i, i ^ m) for i in range(size)])


def local(queries, keys, values, segment_ids, grad_out):
    rows = queries.shape[0]
    heads = lax.axis_size("head")
    tokens = rows * heads
    kv_heads = KVH // heads
    shards = lax.axis_size("ctx")
    place = jnp.stack([lax.axis_index("ctx"), lax.axis_index("head")]).astype(jnp.int32)
    near = min(NEAR, shards)
    far = shards // near
    order = [m + near * h for m in range(near) for h in range(far)]

    kv_out = pl.pallas_call(
        functools.partial(pack_kv_kernel, kv_heads),
        out_shape=[shape(rows, kv_heads * 2 * HD)] * heads,
        in_specs=in_smem() + in_vmem(2),
        out_specs=in_vmem(heads),
        compiler_params=params(),
        name="pack_kv",
    )(place, keys, values)
    kv = [kv_out[0]] + [swap(kv_out[m], "head", heads, m) for m in range(1, heads)]

    qo_out = pl.pallas_call(
        functools.partial(pack_qo_kernel, kv_heads, heads),
        out_shape=[shape(rows, 2 * GW)] * (kv_heads * (heads - 1)),
        in_specs=in_smem() + anywhere(2),
        out_specs=in_vmem(kv_heads * (heads - 1)),
        scratch_shapes=[pltpu.SemaphoreType.DMA((2 * kv_heads * (heads - 1),))],
        compiler_params=params(),
        name="pack_qo",
    )(place, queries, grad_out)
    qo = [
        [swap(qo_out[g * (heads - 1) + m - 1], "head", heads, m) for m in range(1, heads)]
        for g in range(kv_heads)
    ]

    merged = pl.pallas_call(
        functools.partial(merge_kernel, heads),
        out_shape=[shape(SLOT_DEV, 2 * HD)] * kv_heads,
        in_specs=in_smem() + in_vmem(1 + heads),
        out_specs=in_vmem(kv_heads),
        scratch_shapes=[pltpu.VMEM((tokens, kv_heads * 2 * HD), jnp.bfloat16)],
        compiler_params=params(),
        name="merge",
    )(place, segment_ids, *kv)

    seg_col = segment_ids.T
    slots = shards * SLOT_DEV
    span = far * SLOT_DEV
    dq = []
    spread_args = []
    for g in range(kv_heads):
        held = {0: merged[g]}
        for h in range(1, far):
            held[near * h] = swap(merged[g], "ctx", shards, near * h)
        for h in range(far):
            for m in range(1, near):
                held[near * h + m] = swap(held[near * h], "ctx", shards, m)
        outs = pl.pallas_call(
            functools.partial(attend_kernel, g, order, heads),
            out_shape=[shape(tokens, GW), shape(tokens, 2 * HD, dtype=jnp.float32)]
            + [shape(span, 2 * HD, dtype=jnp.float32)]
            + [shape(span, 2 * HD)] * (near - 1),
            in_specs=in_smem()
            + in_vmem(1)
            + anywhere(2)
            + in_vmem(heads + heads - 1 + shards),
            out_specs=in_vmem(2 + near),
            scratch_shapes=[
                pltpu.VMEM((slots + rows, 2 * HD), jnp.bfloat16),
                pltpu.VMEM((slots + rows, HD), jnp.bfloat16),
                pltpu.VMEM((HD, slots), jnp.bfloat16),
                pltpu.VMEM((rows, 2 * GW), jnp.bfloat16),
                pltpu.SemaphoreType.DMA((2,)),
            ],
            compiler_params=params(),
            cost_estimate=pl.CostEstimate(
                flops=10 * tokens * GROUP * (slots + rows) * HD,
                bytes_accessed=4 * 2**20,
                transcendentals=tokens * GROUP * slots,
            ),
            name="attend",
        )(place, seg_col, queries, grad_out, *kv, *qo[g], *[held[m] for m in order])
        dq.append(outs[0])
        sums = outs[2]
        for m in range(1, near):
            sums = sums + swap(outs[2 + m], "ctx", shards, m).astype(jnp.float32)
        spread_args.append(sums[:SLOT_DEV])
        for h in range(1, far):
            part = sums[h * SLOT_DEV : (h + 1) * SLOT_DEV].astype(jnp.bfloat16)
            spread_args.append(swap(part, "ctx", shards, near * h))
        spread_args.append(outs[1])

    grad_keys, grad_values = pl.pallas_call(
        functools.partial(spread_kernel, far + 1),
        out_shape=[shape(tokens, kv_heads * HD)] * 2,
        in_specs=in_vmem(1 + len(spread_args)),
        out_specs=in_vmem(2),
        compiler_params=params(),
        name="spread",
    )(segment_ids, *spread_args)
    return jnp.concatenate(dq, axis=1), grad_keys, grad_values


def solution(mesh):
    return jax.shard_map(
        local,
        mesh=mesh,
        in_specs=(
            P(("ctx", "head"), None),
            P(("ctx", "head"), None),
            P(("ctx", "head"), None),
            P("head", "ctx"),
            P(("ctx", "head"), None),
        ),
        out_specs=(P("ctx", "head"), P("ctx", "head"), P("ctx", "head")),
        check_vma=False,
    )
```

time: 90.5 us -> 86.4 us (0.955)
  waiting for transfers between devices: 24.2 us -> 14.6 us
  local copies, waits for them, and re-layouts: 11.6 us -> 17.4 us
  Pallas kernels: 14.2 us -> 17.6 us
  other arithmetic: 3.3 us -> 1.11 us
  starting transfers between devices: 35.6 us -> 34.1 us
    unnamed x19 -> x65, local copies, waits for them, and re-layouts: 2.82 us -> 17.4 us
    all_to_all x3 -> x0, starting transfers between devices: 11.2 us -> none  [the longest x2 6.99 us: local(): lax.all_to_all(both.reshape(rows, heads * 2 * GROUP * HD), 'head', split_...]
    all_to_all x3 -> x0, waiting for transfers between devices: 9.83 us -> none  [the longest x2 9.83 us: local(): lax.all_to_all(both.reshape(rows, heads * 2 * GROUP * HD), 'head', split_...]
    ppermute x15 -> x31, starting transfers between devices: 24.4 us -> 34.1 us  [swap(): return lax.ppermute(x, axis, [(i, i ^ m) for i in range(size)])]
    pallas_call x4 -> x6, Pallas kernels: 14.2 us -> 17.6 us  [the longest x2 13.6 us: local(): pl.pallas_call(functools.partial(attend_kernel, g, order, heads), out_sha...]
    slice x4 -> x2, local copies, waits for them, and re-layouts: 3 us -> 0.02 us  [local(): part = sums[h * SLOT_DEV:(h + 1) * SLOT_DEV].astype(jnp.bfloat16)]
    another operation x3 -> x0, local copies, waits for them, and re-layouts: 2.19 us -> none  [local(): jnp.stack([keys.reshape(rows, heads, kv_heads, HD), values.reshape(rows,...]
    concatenate x2 -> x0, other arithmetic: 1.9 us -> none  [local(): both = jnp.concatenate([q_parts[:, :, g], o_parts[:, :, g]], axis=2)]
  transfers between devices with their start and end apart: 18 -> 31, of which waited for: 9 -> 9; matrix products, arithmetic and copies ran while one was open for 10% -> 1% of each run, Pallas kernels for 15% -> 18%
where the time goes in v2:
time: 86.4 us; the launch traced here: 85.6 us
  starting transfers between devices  34.1 us (39%)
  Pallas kernels  17.6 us (20%)
  local copies, waits for them, and re-layouts  17.4 us (20%)
  waiting for transfers between devices  14.6 us (17%)
  other arithmetic  1.11 us (1%)
    ppermute x31, starting transfers between devices, swap(): return lax.ppermute(x, axis, [(i, i ^ m) for i in range(size)])  34.1 us
    unnamed x65, local copies, waits for them, and re-layouts  17.4 us
    ppermute x31, waiting for transfers between devices, swap(): return lax.ppermute(x, axis, [(i, i ^ m) for i in range(size)])  14.6 us
    pallas_call x2, Pallas kernels, local(): pl.pallas_call(functools.partial(attend_kernel, g, order, heads), out_sha...  13.6 us
  transfers between devices with their start and end apart: 31, of which 9 were waited for; matrix products, arithmetic and copies ran while one was open for 1% of the time, Pallas kernels for 18%

profile of v2, /device:TPU:0, one launch (start us, length us, event | category | flops | bytes accessed | tf_op | source)
XLA Modules:
  0.0 85.6 jit_solution(16884587991316335584)
XLA Ops:
  0.7 0.9 %copy-done.4 = bf16[48,1024]{1,0:T(8,128)(2,1)S(1)} copy-done((bf16[48,1024]{1,0:T(8,128)(2,1)S(1)}, bf16[48,1024]{1,0:T(8,128)(2,1)}, u32[]{:S(2)}) %copy-start.4) | copy-done | bytes 98328
  1.6 0.9 %copy-done.5 = bf16[48,1024]{1,0:T(8,128)(2,1)S(1)} copy-done((bf16[48,1024]{1,0:T(8,128)(2,1)S(1)}, bf16[48,1024]{1,0:T(8,128)(2,1)}, u32[]{:S(2)}) %copy-start.5) | copy-done | bytes 98328
  3.6 2.6 %collective-permute-start.1 = (bf16[48,512]{1,0:T(8,128)(2,1)S(1)}, bf16[48,512]{1,0:T(8,128)(2,1)S(1)}, u32[]{:S(2)}, u32[]{:S(2)}) collective-permute-start(bf16[48,512]{1,0:T(8,128)(2,1)S(1)} %get-tuple-element.31), channel_id=1, source_target_pairs={{0,2},{1,3},{2,0},{3,1},{4,6},{5,7},{6,4},{7,5},{8,10},{9,11},{10,... | collective-permute-start | bytes 147464 | tf_op jit(solution)/shard_map/ppermute | solution.py:227
  6.3 2.3 %collective-permute-done.1.refs_2_ = bf16[48,512]{1,0:T(8,128)(2,1)S(1)} collective-permute-done((bf16[48,512]{1,0:T(8,128)(2,1)S(1)}, bf16[48,512]{1,0:T(8,128)(2,1)S(1)}, u32[]{:S(2)}, u32[]{:S(2)}) %collective-permute-start.1) | collective-permute-done | bytes 49184 | tf_op jit(solution)/shard_map/ppermute | solution.py:227
  8.5 1.4 %collective-permute-done.2.refs_3_ = bf16[48,512]{1,0:T(8,128)(2,1)S(1)} collective-permute-done((bf16[48,512]{1,0:T(8,128)(2,1)S(1)}, bf16[48,512]{1,0:T(8,128)(2,1)S(1)}, u32[]{:S(2)}, u32[]{:S(2)}) %collective-permute-start.2) | collective-permute-done | bytes 49184 | tf_op jit(solution)/shard_map/ppermute | solution.py:227
  11.3 2.6 %collective-permute-start.16 = (bf16[96,256]{1,0:T(8,128)(2,1)S(1)}, bf16[96,256]{1,0:T(8,128)(2,1)S(1)}, u32[]{:S(2)}, u32[]{:S(2)}) collective-permute-start(bf16[96,256]{1,0:T(8,128)(2,1)S(1)} %get-tuple-element.41.refs_7_), channel_id=1, source_target_pairs={{0,16},{4,20},{8,24},{12,28},{16,0},{20,4},{24,8},{28,12},{1,17},{... | collective-permute-start | bytes 147464 | tf_op jit(solution)/shard_map/ppermute | solution.py:227
  14.0 1.5 %collective-permute-start.17 = (bf16[96,256]{1,0:T(8,128)(2,1)S(1)}, bf16[96,256]{1,0:T(8,128)(2,1)S(1)}, u32[]{:S(2)}, u32[]{:S(2)}) collective-permute-start(bf16[96,256]{1,0:T(8,128)(2,1)S(1)} %get-tuple-element.41.refs_7_), channel_id=1, source_target_pairs={{0,4},{4,0},{8,12},{12,8},{16,20},{20,16},{24,28},{28,24},{1,5},{5... | collective-permute-start | bytes 147464 | tf_op jit(solution)/shard_map/ppermute | solution.py:227
  15.5 1.6 %collective-permute-start.19 = (bf16[96,256]{1,0:T(8,128)(2,1)S(1)}, bf16[96,256]{1,0:T(8,128)(2,1)S(1)}, u32[]{:S(2)}, u32[]{:S(2)}) collective-permute-start(bf16[96,256]{1,0:T(8,128)(2,1)S(1)} %get-tuple-element.41.refs_7_), channel_id=1, source_target_pairs={{0,8},{4,12},{8,0},{12,4},{16,24},{20,28},{24,16},{28,20},{1,9},{5... | collective-permute-start | bytes 147464 | tf_op jit(solution)/shard_map/ppermute | solution.py:227
  17.8 2.5 %collective-permute-start.11 = (bf16[96,256]{1,0:T(8,128)(2,1)S(1)}, bf16[96,256]{1,0:T(8,128)(2,1)S(1)}, u32[]{:S(2)}, u32[]{:S(2)}) collective-permute-start(bf16[96,256]{1,0:T(8,128)(2,1)S(1)} %get-tuple-element.36.refs_7_), channel_id=1, source_target_pairs={{0,12},{4,8},{8,4},{12,0},{16,28},{20,24},{24,20},{28,16},{1,13},{... | collective-permute-start | bytes 147464 | tf_op jit(solution)/shard_map/ppermute | solution.py:227
  20.3 1.1 %copy-done = bf16[48,8192]{1,0:T(8,128)(2,1)S(1)} copy-done((bf16[48,8192]{1,0:T(8,128)(2,1)S(1)}, bf16[48,8192]{1,0:T(8,128)(2,1)}, u32[]{:S(2)}) %copy-start) | copy-done | bytes 786456
  21.5 1.1 %copy-done.2 = bf16[48,8192]{1,0:T(8,128)(2,1)S(1)} copy-done((bf16[48,8192]{1,0:T(8,128)(2,1)S(1)}, bf16[48,8192]{1,0:T(8,128)(2,1)}, u32[]{:S(2)}) %copy-start.2) | copy-done | bytes 786456
  22.6 1.6 %pack_qo.1 = (bf16[48,2048]{1,0:T(8,128)(2,1)S(1)}, bf16[48,2048]{1,0:T(8,128)(2,1)S(1)}, bf16[48,2048]{1,0:T(8,128)(2,1)S(1)}, bf16[48,2048]{1,0:T(8,128)(2,1)S...) custom-call(s32[2]{0:T(128)S(1)} %pad_add_fusion.place_ref, bf16[48,8192]{1,0:T(8,128)(2,1)S(1)} %copy-done, ...), custom_call_target="tpu_custom_call" | custom-call | tf_op jit(solution)/shard_map/pack_qo/pallas_call | solution.py:251
  25.5 1.0 %collective-permute-start.14 = (bf16[48,2048]{1,0:T(8,128)(2,1)}, bf16[48,2048]{1,0:T(8,128)(2,1)S(1)}, u32[]{:S(2)}, u32[]{:S(2)}) collective-permute-start(bf16[48,2048]{1,0:T(8,128)(2,1)} %get-tuple-element.39), channel_id=1, source_target_pairs={{0,2},{1,3},{2,0},{3,1},{4,6},{5,7},{6,4},{7,5},{8,10},{9,11},{10,... | collective-permute-start | bytes 589832 | tf_op jit(solution)/shard_map/ppermute | solution.py:227
  29.5 2.5 %collective-permute-done.7.refs_9_ = bf16[96,256]{1,0:T(8,128)(2,1)S(1)} collective-permute-done((bf16[96,256]{1,0:T(8,128)(2,1)S(1)}, bf16[96,256]{1,0:T(8,128)(2,1)S(1)}, u32[]{:S(2)}, u32[]{:S(2)}) %collective-permute-start.7) | collective-permute-done | bytes 49184 | tf_op jit(solution)/shard_map/ppermute | solution.py:227
  34.2 2.5 %collective-permute-done.18.refs_10_ = bf16[96,256]{1,0:T(8,128)(2,1)S(1)} collective-permute-done((bf16[96,256]{1,0:T(8,128)(2,1)S(1)}, bf16[96,256]{1,0:T(8,128)(2,1)S(1)}, u32[]{:S(2)}, u32[]{:S(2)}) %collective-permute-start.18) | collective-permute-done | bytes 49184 | tf_op jit(solution)/shard_map/ppermute | solution.py:227
  38.5 1.5 %collective-permute-start.10 = (bf16[96,256]{1,0:T(8,128)(2,1)S(1)}, bf16[96,256]{1,0:T(8,128)(2,1)S(1)}, u32[]{:S(2)}, u32[]{:S(2)}) collective-permute-start(bf16[96,256]{1,0:T(8,128)(2,1)S(1)} %collective-permute-done.6.refs_8_), channel_id=1, source_target_pairs={{0,8},{4,12},{8,0},{12,4},{16,24},{20,28},{24,16},{28,20},{1,9},{5... | collective-permute-start | bytes 147464 | tf_op jit(solution)/shard_map/ppermute | solution.py:227
  40.0 2.4 %collective-permute-done.22.refs_14_ = bf16[96,256]{1,0:T(8,128)(2,1)S(1)} collective-permute-done((bf16[96,256]{1,0:T(8,128)(2,1)S(1)}, bf16[96,256]{1,0:T(8,128)(2,1)S(1)}, u32[]{:S(2)}, u32[]{:S(2)}) %collective-permute-start.22) | collective-permute-done | bytes 49184 | tf_op jit(solution)/shard_map/ppermute | solution.py:227
  43.6 1.0 %collective-permute-start.4 = (bf16[48,2048]{1,0:T(8,128)(2,1)S(1)}, bf16[48,2048]{1,0:T(8,128)(2,1)}, u32[]{:S(2)}, u32[]{:S(2)}) collective-permute-start(bf16[48,2048]{1,0:T(8,128)(2,1)S(1)} %get-tuple-element.34), channel_id=1, source_target_pairs={{0,2},{1,3},{2,0},{3,1},{4,6},{5,7},{6,4},{7,5},{8,10},{9,11},{10,... | collective-permute-start | bytes 589832 | tf_op jit(solution)/shard_map/ppermute | solution.py:227
  44.6 0.9 %collective-permute-start.5 = (bf16[48,2048]{1,0:T(8,128)(2,1)S(1)}, bf16[48,2048]{1,0:T(8,128)(2,1)}, u32[]{:S(2)}, u32[]{:S(2)}) collective-permute-start(bf16[48,2048]{1,0:T(8,128)(2,1)S(1)} %get-tuple-element.35), channel_id=1, source_target_pairs={{0,3},{1,2},{2,1},{3,0},{4,7},{5,6},{6,5},{7,4},{8,11},{9,10},{10,... | collective-permute-start | bytes 589832 | tf_op jit(solution)/shard_map/ppermute | solution.py:227
  45.6 1.2 %collective-permute-start.12 = (bf16[96,256]{1,0:T(8,128)(2,1)S(1)}, bf16[96,256]{1,0:T(8,128)(2,1)S(1)}, u32[]{:S(2)}, u32[]{:S(2)}) collective-permute-start(bf16[96,256]{1,0:T(8,128)(2,1)S(1)} %collective-permute-done.6.refs_8_), channel_id=1, source_target_pairs={{0,12},{4,8},{8,4},{12,0},{16,28},{20,24},{24,20},{28,16},{1,13},{... | collective-permute-start | bytes 147464 | tf_op jit(solution)/shard_map/ppermute | solution.py:227
  54.0 6.5 %attend.3 = (bf16[192,1024]{1,0:T(8,128)(2,1)S(1)}, f32[192,256]{1,0:T(8,128)S(1)}, f32[192,256]{1,0:T(8,128)S(1)}, bf16[192,256]{1,0:T(8,128)(2,1)S(1)}, bf16[1...) custom-call(s32[2]{0:T(128)S(1)} %pad_add_fusion.place_ref, s32[192,2]{1,0:T(8,128)S(1)} %bitcast.3, ...), custom_call_target="tpu_custom_call" | custom-call | flops 1604321280 | bytes 4194304 | tf_op jit(solution)/shard_map/attend/pallas_call | solution.py:287
  60.5 1.3 %collective-permute-start.27 = (bf16[192,256]{1,0:T(8,128)(2,1)S(1)}, bf16[192,256]{1,0:T(8,128)(2,1)S(1)}, u32[]{:S(2)}, u32[]{:S(2)}) collective-permute-start(bf16[192,256]{1,0:T(8,128)(2,1)S(1)} %get-tuple-element.49), channel_id=1, source_target_pairs={{0,4},{4,0},{8,12},{12,8},{16,20},{20,16},{24,28},{28,24},{1,5},{5... | collective-permute-start | bytes 294920 | tf_op jit(solution)/shard_map/ppermute | solution.py:227
  62.6 1.5 %collective-permute-start.29 = (bf16[192,256]{1,0:T(8,128)(2,1)S(1)}, bf16[192,256]{1,0:T(8,128)(2,1)S(1)}, u32[]{:S(2)}, u32[]{:S(2)}) collective-permute-start(bf16[192,256]{1,0:T(8,128)(2,1)S(1)} %get-tuple-element.51), channel_id=1, source_target_pairs={{0,12},{4,8},{8,4},{12,0},{16,28},{20,24},{24,20},{28,16},{1,13},{... | collective-permute-start | bytes 294920 | tf_op jit(solution)/shard_map/ppermute | solution.py:227
  64.1 7.1 %attend.2 = (bf16[192,1024]{1,0:T(8,128)(2,1)S(1)}, f32[192,256]{1,0:T(8,128)S(1)}, f32[192,256]{1,0:T(8,128)S(1)}, bf16[192,256]{1,0:T(8,128)(2,1)S(1)}, bf16[1...) custom-call(s32[2]{0:T(128)S(1)} %pad_add_fusion.place_ref, s32[192,2]{1,0:T(8,128)S(1)} %bitcast.4, ...), custom_call_target="tpu_custom_call" | custom-call | flops 1604321280 | bytes 4194304 | tf_op jit(solution)/shard_map/attend/pallas_call | solution.py:287
  71.3 1.3 %collective-permute-start.23 = (bf16[192,256]{1,0:T(8,128)(2,1)S(1)}, bf16[192,256]{1,0:T(8,128)(2,1)S(1)}, u32[]{:S(2)}, u32[]{:S(2)}) collective-permute-start(bf16[192,256]{1,0:T(8,128)(2,1)S(1)} %get-tuple-element.44), channel_id=1, source_target_pairs={{0,4},{4,0},{8,12},{12,8},{16,20},{20,16},{24,28},{28,24},{1,5},{5... | collective-permute-start | bytes 294920 | tf_op jit(solution)/shard_map/ppermute | solution.py:227
  73.4 1.5 %collective-permute-start.25 = (bf16[192,256]{1,0:T(8,128)(2,1)S(1)}, bf16[192,256]{1,0:T(8,128)(2,1)S(1)}, u32[]{:S(2)}, u32[]{:S(2)}) collective-permute-start(bf16[192,256]{1,0:T(8,128)(2,1)S(1)} %get-tuple-element.46), channel_id=1, source_target_pairs={{0,12},{4,8},{8,4},{12,0},{16,28},{20,24},{24,20},{28,16},{1,13},{... | collective-permute-start | bytes 294920 | tf_op jit(solution)/shard_map/ppermute | solution.py:227
  74.9 2.6 %collective-permute-start.30 = (bf16[96,256]{1,0:T(8,128)(2,1)S(1)}, bf16[96,256]{1,0:T(8,128)(2,1)S(1)}, u32[]{:S(2)}, u32[]{:S(2)}) collective-permute-start(bf16[96,256]{1,0:T(8,128)(2,1)S(1)} %slice.24), channel_id=1, source_target_pairs={{0,16},{4,20},{8,24},{12,28},{16,0},{20,4},{24,8},{28,12},{1,17},{... | collective-permute-start | bytes 147464 | tf_op jit(solution)/shard_map/ppermute | solution.py:227
  78.3 1.2 %collective-permute-done.25 = bf16[192,256]{1,0:T(8,128)(2,1)S(1)} collective-permute-done((bf16[192,256]{1,0:T(8,128)(2,1)S(1)}, bf16[192,256]{1,0:T(8,128)(2,1)S(1)}, u32[]{:S(2)}, u32[]{:S(2)}) %collective-permute-start.25) | collective-permute-done | bytes 98336 | tf_op jit(solution)/shard_map/ppermute | solution.py:227
  79.6 2.6 %collective-permute-start.26 = (bf16[96,256]{1,0:T(8,128)(2,1)S(1)}, bf16[96,256]{1,0:T(8,128)(2,1)S(1)}, u32[]{:S(2)}, u32[]{:S(2)}) collective-permute-start(bf16[96,256]{1,0:T(8,128)(2,1)S(1)} %slice.25), channel_id=1, source_target_pairs={{0,16},{4,20},{8,24},{12,28},{16,0},{20,4},{24,8},{28,12},{1,17},{... | collective-permute-start | bytes 147464 | tf_op jit(solution)/shard_map/ppermute | solution.py:227
  82.2 0.9 %pad_maximum_fusion = bf16[192,2048]{1,0:T(8,128)(2,1)} fusion(bf16[192,1024]{1,0:T(8,128)(2,1)S(1)} %get-tuple-element.42, bf16[192,1024]{1,0:T(8,128)(2,1)S(1)} %get-tuple-element.37), kind=kLoop, calls=%fused_computation | loop fusion | flops 1572864 | bytes 1572864 | tf_op jit(solution)/shard_map/concatenate | solution.py:330
  83.2 1.4 %collective-permute-done.26.refs_1_ = bf16[96,256]{1,0:T(8,128)(2,1)S(1)} collective-permute-done((bf16[96,256]{1,0:T(8,128)(2,1)S(1)}, bf16[96,256]{1,0:T(8,128)(2,1)S(1)}, u32[]{:S(2)}, u32[]{:S(2)}) %collective-permute-start.26) | collective-permute-done | bytes 49184 | tf_op jit(solution)/shard_map/ppermute | solution.py:227
  84.6 1.0 %spread.1 = (bf16[192,256]{1,0:T(8,128)(2,1)}, bf16[192,256]{1,0:T(8,128)(2,1)}) custom-call(s32[2,192]{1,0:T(2,128)S(1)} %copy-done.7, f32[96,256]{1,0:T(8,128)S(1)} %slice.18.refs_0_, bf16[96,256]{1,0:T(8,128)(2,1)S(1)} %collective-permute-done.26.refs_1_, f32[192,256]{1,0:T(8,128)S(1)} %get-tuple-element.47.refs_2_, f32[96,256]{1,0:T(8,128)S(1)} %slice.20.refs_3_, ...), custom_call_target="tpu_custom_call" | custom-call | tf_op jit(solution)/shard_map/spread/pallas_call | solution.py:322
  (109 shorter events, 22.7 us)
Async XLA Ops:
  3.1 3.2 %collective-permute-start = (bf16[48,512]{1,0:T(8,128)(2,1)S(1)}, bf16[48,512]{1,0:T(8,128)(2,1)S(1)}, u32[]{:S(2)}, u32[]{:S(2)}) collective-permute-start(bf16[48,512]{1,0:T(8,128)(2,1)S(1)} %get-tuple-element.30), channel_id=1, source_target_pairs={{0,1},{1,0},{2,3},{3,2},{4,5},{5,4},{6,7},{7,6},{8,9},{9,8},{10,11... | collective-permute-start | bytes 147464 | tf_op jit(solution)/shard_map/ppermute | solution.py:227
  3.6 4.9 %collective-permute-start.1 = (bf16[48,512]{1,0:T(8,128)(2,1)S(1)}, bf16[48,512]{1,0:T(8,128)(2,1)S(1)}, u32[]{:S(2)}, u32[]{:S(2)}) collective-permute-start(bf16[48,512]{1,0:T(8,128)(2,1)S(1)} %get-tuple-element.31), channel_id=1, source_target_pairs={{0,2},{1,3},{2,0},{3,1},{4,6},{5,7},{6,4},{7,5},{8,10},{9,11},{10,... | collective-permute-start | bytes 147464 | tf_op jit(solution)/shard_map/ppermute | solution.py:227
  6.2 3.7 %collective-permute-start.2 = (bf16[48,512]{1,0:T(8,128)(2,1)S(1)}, bf16[48,512]{1,0:T(8,128)(2,1)S(1)}, u32[]{:S(2)}, u32[]{:S(2)}) collective-permute-start(bf16[48,512]{1,0:T(8,128)(2,1)S(1)} %get-tuple-element.32), channel_id=1, source_target_pairs={{0,3},{1,2},{2,1},{3,0},{4,7},{5,6},{6,5},{7,4},{8,11},{9,10},{10,... | collective-permute-start | bytes 147464 | tf_op jit(solution)/shard_map/ppermute | solution.py:227
  11.3 6.5 %collective-permute-start.16 = (bf16[96,256]{1,0:T(8,128)(2,1)S(1)}, bf16[96,256]{1,0:T(8,128)(2,1)S(1)}, u32[]{:S(2)}, u32[]{:S(2)}) collective-permute-start(bf16[96,256]{1,0:T(8,128)(2,1)S(1)} %get-tuple-element.41.refs_7_), channel_id=1, source_target_pairs={{0,16},{4,20},{8,24},{12,28},{16,0},{20,4},{24,8},{28,12},{1,17},{... | collective-permute-start | bytes 147464 | tf_op jit(solution)/shard_map/ppermute | solution.py:227
  14.0 10.3 %collective-permute-start.17 = (bf16[96,256]{1,0:T(8,128)(2,1)S(1)}, bf16[96,256]{1,0:T(8,128)(2,1)S(1)}, u32[]{:S(2)}, u32[]{:S(2)}) collective-permute-start(bf16[96,256]{1,0:T(8,128)(2,1)S(1)} %get-tuple-element.41.refs_7_), channel_id=1, source_target_pairs={{0,4},{4,0},{8,12},{12,8},{16,20},{20,16},{24,28},{28,24},{1,5},{5... | collective-permute-start | bytes 147464 | tf_op jit(solution)/shard_map/ppermute | solution.py:227
  15.5 9.4 %collective-permute-start.19 = (bf16[96,256]{1,0:T(8,128)(2,1)S(1)}, bf16[96,256]{1,0:T(8,128)(2,1)S(1)}, u32[]{:S(2)}, u32[]{:S(2)}) collective-permute-start(bf16[96,256]{1,0:T(8,128)(2,1)S(1)} %get-tuple-element.41.refs_7_), channel_id=1, source_target_pairs={{0,8},{4,12},{8,0},{12,4},{16,24},{20,28},{24,16},{28,20},{1,9},{5... | collective-permute-start | bytes 147464 | tf_op jit(solution)/shard_map/ppermute | solution.py:227
  17.1 9.4 %collective-permute-start.21 = (bf16[96,256]{1,0:T(8,128)(2,1)S(1)}, bf16[96,256]{1,0:T(8,128)(2,1)S(1)}, u32[]{:S(2)}, u32[]{:S(2)}) collective-permute-start(bf16[96,256]{1,0:T(8,128)(2,1)S(1)} %get-tuple-element.41.refs_7_), channel_id=1, source_target_pairs={{0,12},{4,8},{8,4},{12,0},{16,28},{20,24},{24,20},{28,16},{1,13},{... | collective-permute-start | bytes 147464 | tf_op jit(solution)/shard_map/ppermute | solution.py:227
  17.4 10.5 %collective-permute-start.6 = (bf16[96,256]{1,0:T(8,128)(2,1)S(1)}, bf16[96,256]{1,0:T(8,128)(2,1)S(1)}, u32[]{:S(2)}, u32[]{:S(2)}) collective-permute-start(bf16[96,256]{1,0:T(8,128)(2,1)S(1)} %get-tuple-element.36.refs_7_), channel_id=1, source_target_pairs={{0,16},{4,20},{8,24},{12,28},{16,0},{20,4},{24,8},{28,12},{1,17},{... | collective-permute-start | bytes 147464 | tf_op jit(solution)/shard_map/ppermute | solution.py:227
  17.8 10.7 %collective-permute-start.11 = (bf16[96,256]{1,0:T(8,128)(2,1)S(1)}, bf16[96,256]{1,0:T(8,128)(2,1)S(1)}, u32[]{:S(2)}, u32[]{:S(2)}) collective-permute-start(bf16[96,256]{1,0:T(8,128)(2,1)S(1)} %get-tuple-element.36.refs_7_), channel_id=1, source_target_pairs={{0,12},{4,8},{8,4},{12,0},{16,28},{20,24},{24,20},{28,16},{1,13},{... | collective-permute-start | bytes 147464 | tf_op jit(solution)/shard_map/ppermute | solution.py:227
  22.6 25.0 %copy-start.3 = (bf16[48,8192]{1,0:T(8,128)(2,1)S(1)}, bf16[48,8192]{1,0:T(8,128)(2,1)}, u32[]{:S(2)}) copy-start(bf16[48,8192]{1,0:T(8,128)(2,1)} %o_ref.5) | copy-start | bytes 2359300
  24.9 19.7 %collective-permute-start.13 = (bf16[48,2048]{1,0:T(8,128)(2,1)S(1)}, bf16[48,2048]{1,0:T(8,128)(2,1)S(1)}, u32[]{:S(2)}, u32[]{:S(2)}) collective-permute-start(bf16[48,2048]{1,0:T(8,128)(2,1)S(1)} %get-tuple-element.38), channel_id=1, source_target_pairs={{0,1},{1,0},{2,3},{3,2},{4,5},{5,4},{6,7},{7,6},{8,9},{9,8},{10,11... | collective-permute-start | bytes 589832 | tf_op jit(solution)/shard_map/ppermute | solution.py:227
  25.5 20.1 %collective-permute-start.14 = (bf16[48,2048]{1,0:T(8,128)(2,1)}, bf16[48,2048]{1,0:T(8,128)(2,1)S(1)}, u32[]{:S(2)}, u32[]{:S(2)}) collective-permute-start(bf16[48,2048]{1,0:T(8,128)(2,1)} %get-tuple-element.39), channel_id=1, source_target_pairs={{0,2},{1,3},{2,0},{3,1},{4,6},{5,7},{6,4},{7,5},{8,10},{9,11},{10,... | collective-permute-start | bytes 589832 | tf_op jit(solution)/shard_map/ppermute | solution.py:227
  27.1 19.7 %collective-permute-start.15 = (bf16[48,2048]{1,0:T(8,128)(2,1)S(1)}, bf16[48,2048]{1,0:T(8,128)(2,1)S(1)}, u32[]{:S(2)}, u32[]{:S(2)}) collective-permute-start(bf16[48,2048]{1,0:T(8,128)(2,1)S(1)} %get-tuple-element.40), channel_id=1, source_target_pairs={{0,3},{1,2},{2,1},{3,0},{4,7},{5,6},{6,5},{7,4},{8,11},{9,10},{10,... | collective-permute-start | bytes 589832 | tf_op jit(solution)/shard_map/ppermute | solution.py:227
  28.0 4.1 %collective-permute-start.7 = (bf16[96,256]{1,0:T(8,128)(2,1)S(1)}, bf16[96,256]{1,0:T(8,128)(2,1)S(1)}, u32[]{:S(2)}, u32[]{:S(2)}) collective-permute-start(bf16[96,256]{1,0:T(8,128)(2,1)S(1)} %get-tuple-element.36.refs_7_), channel_id=1, source_target_pairs={{0,4},{4,0},{8,12},{12,8},{16,20},{20,16},{24,28},{28,24},{1,5},{5... | collective-permute-start | bytes 147464 | tf_op jit(solution)/shard_map/ppermute | solution.py:227
  29.1 4.1 %collective-permute-start.9 = (bf16[96,256]{1,0:T(8,128)(2,1)S(1)}, bf16[96,256]{1,0:T(8,128)(2,1)S(1)}, u32[]{:S(2)}, u32[]{:S(2)}) collective-permute-start(bf16[96,256]{1,0:T(8,128)(2,1)S(1)} %get-tuple-element.36.refs_7_), channel_id=1, source_target_pairs={{0,8},{4,12},{8,0},{12,4},{16,24},{20,28},{24,16},{28,20},{1,9},{5... | collective-permute-start | bytes 147464 | tf_op jit(solution)/shard_map/ppermute | solution.py:227
  32.7 4.1 %collective-permute-start.18 = (bf16[96,256]{1,0:T(8,128)(2,1)S(1)}, bf16[96,256]{1,0:T(8,128)(2,1)S(1)}, u32[]{:S(2)}, u32[]{:S(2)}) collective-permute-start(bf16[96,256]{1,0:T(8,128)(2,1)S(1)} %collective-permute-done.16.refs_8_), channel_id=1, source_target_pairs={{0,4},{4,0},{8,12},{12,8},{16,20},{20,16},{24,28},{28,24},{1,5},{5... | collective-permute-start | bytes 147464 | tf_op jit(solution)/shard_map/ppermute | solution.py:227
  33.8 4.1 %collective-permute-start.20 = (bf16[96,256]{1,0:T(8,128)(2,1)S(1)}, bf16[96,256]{1,0:T(8,128)(2,1)S(1)}, u32[]{:S(2)}, u32[]{:S(2)}) collective-permute-start(bf16[96,256]{1,0:T(8,128)(2,1)S(1)} %collective-permute-done.16.refs_8_), channel_id=1, source_target_pairs={{0,8},{4,12},{8,0},{12,4},{16,24},{20,28},{24,16},{28,20},{1,9},{5... | collective-permute-start | bytes 147464 | tf_op jit(solution)/shard_map/ppermute | solution.py:227
  37.4 5.0 %collective-permute-start.22 = (bf16[96,256]{1,0:T(8,128)(2,1)S(1)}, bf16[96,256]{1,0:T(8,128)(2,1)S(1)}, u32[]{:S(2)}, u32[]{:S(2)}) collective-permute-start(bf16[96,256]{1,0:T(8,128)(2,1)S(1)} %collective-permute-done.16.refs_8_), channel_id=1, source_target_pairs={{0,12},{4,8},{8,4},{12,0},{16,28},{20,24},{24,20},{28,16},{1,13},{... | collective-permute-start | bytes 147464 | tf_op jit(solution)/shard_map/ppermute | solution.py:227
  38.5 4.5 %collective-permute-start.10 = (bf16[96,256]{1,0:T(8,128)(2,1)S(1)}, bf16[96,256]{1,0:T(8,128)(2,1)S(1)}, u32[]{:S(2)}, u32[]{:S(2)}) collective-permute-start(bf16[96,256]{1,0:T(8,128)(2,1)S(1)} %collective-permute-done.6.refs_8_), channel_id=1, source_target_pairs={{0,8},{4,12},{8,0},{12,4},{16,24},{20,28},{24,16},{28,20},{1,9},{5... | collective-permute-start | bytes 147464 | tf_op jit(solution)/shard_map/ppermute | solution.py:227
  43.0 19.6 %collective-permute-start.3 = (bf16[48,2048]{1,0:T(8,128)(2,1)S(1)}, bf16[48,2048]{1,0:T(8,128)(2,1)S(1)}, u32[]{:S(2)}, u32[]{:S(2)}) collective-permute-start(bf16[48,2048]{1,0:T(8,128)(2,1)S(1)} %get-tuple-element.33), channel_id=1, source_target_pairs={{0,1},{1,0},{2,3},{3,2},{4,5},{5,4},{6,7},{7,6},{8,9},{9,8},{10,11... | collective-permute-start | bytes 589832 | tf_op jit(solution)/shard_map/ppermute | solution.py:227
  43.6 20.5 %collective-permute-start.4 = (bf16[48,2048]{1,0:T(8,128)(2,1)S(1)}, bf16[48,2048]{1,0:T(8,128)(2,1)}, u32[]{:S(2)}, u32[]{:S(2)}) collective-permute-start(bf16[48,2048]{1,0:T(8,128)(2,1)S(1)} %get-tuple-element.34), channel_id=1, source_target_pairs={{0,2},{1,3},{2,0},{3,1},{4,6},{5,7},{6,4},{7,5},{8,10},{9,11},{10,... | collective-permute-start | bytes 589832 | tf_op jit(solution)/shard_map/ppermute | solution.py:227
  44.6 19.5 %collective-permute-start.5 = (bf16[48,2048]{1,0:T(8,128)(2,1)S(1)}, bf16[48,2048]{1,0:T(8,128)(2,1)}, u32[]{:S(2)}, u32[]{:S(2)}) collective-permute-start(bf16[48,2048]{1,0:T(8,128)(2,1)S(1)} %get-tuple-element.35), channel_id=1, source_target_pairs={{0,3},{1,2},{2,1},{3,0},{4,7},{5,6},{6,5},{7,4},{8,11},{9,10},{10,... | collective-permute-start | bytes 589832 | tf_op jit(solution)/shard_map/ppermute | solution.py:227
  45.6 14.9 %collective-permute-start.12 = (bf16[96,256]{1,0:T(8,128)(2,1)S(1)}, bf16[96,256]{1,0:T(8,128)(2,1)S(1)}, u32[]{:S(2)}, u32[]{:S(2)}) collective-permute-start(bf16[96,256]{1,0:T(8,128)(2,1)S(1)} %collective-permute-done.6.refs_8_), channel_id=1, source_target_pairs={{0,12},{4,8},{8,4},{12,0},{16,28},{20,24},{24,20},{28,16},{1,13},{... | collective-permute-start | bytes 147464 | tf_op jit(solution)/shard_map/ppermute | solution.py:227
  46.8 15.0 %collective-permute-start.8 = (bf16[96,256]{1,0:T(8,128)(2,1)S(1)}, bf16[96,256]{1,0:T(8,128)(2,1)S(1)}, u32[]{:S(2)}, u32[]{:S(2)}) collective-permute-start(bf16[96,256]{1,0:T(8,128)(2,1)S(1)} %collective-permute-done.6.refs_8_), channel_id=1, source_target_pairs={{0,4},{4,0},{8,12},{12,8},{16,20},{20,16},{24,28},{28,24},{1,5},{5... | collective-permute-start | bytes 147464 | tf_op jit(solution)/shard_map/ppermute | solution.py:227
  60.5 12.8 %collective-permute-start.27 = (bf16[192,256]{1,0:T(8,128)(2,1)S(1)}, bf16[192,256]{1,0:T(8,128)(2,1)S(1)}, u32[]{:S(2)}, u32[]{:S(2)}) collective-permute-start(bf16[192,256]{1,0:T(8,128)(2,1)S(1)} %get-tuple-element.49), channel_id=1, source_target_pairs={{0,4},{4,0},{8,12},{12,8},{16,20},{20,16},{24,28},{28,24},{1,5},{5... | collective-permute-start | bytes 294920 | tf_op jit(solution)/shard_map/ppermute | solution.py:227
  61.8 13.0 %collective-permute-start.28 = (bf16[192,256]{1,0:T(8,128)(2,1)S(1)}, bf16[192,256]{1,0:T(8,128)(2,1)S(1)}, u32[]{:S(2)}, u32[]{:S(2)}) collective-permute-start(bf16[192,256]{1,0:T(8,128)(2,1)S(1)} %get-tuple-element.50), channel_id=1, source_target_pairs={{0,8},{4,12},{8,0},{12,4},{16,24},{20,28},{24,16},{28,20},{1,9},{5... | collective-permute-start | bytes 294920 | tf_op jit(solution)/shard_map/ppermute | solution.py:227
  62.6 12.2 %collective-permute-start.29 = (bf16[192,256]{1,0:T(8,128)(2,1)S(1)}, bf16[192,256]{1,0:T(8,128)(2,1)S(1)}, u32[]{:S(2)}, u32[]{:S(2)}) collective-permute-start(bf16[192,256]{1,0:T(8,128)(2,1)S(1)} %get-tuple-element.51), channel_id=1, source_target_pairs={{0,12},{4,8},{8,4},{12,0},{16,28},{20,24},{24,20},{28,16},{1,13},{... | collective-permute-start | bytes 294920 | tf_op jit(solution)/shard_map/ppermute | solution.py:227
  71.3 6.3 %collective-permute-start.23 = (bf16[192,256]{1,0:T(8,128)(2,1)S(1)}, bf16[192,256]{1,0:T(8,128)(2,1)S(1)}, u32[]{:S(2)}, u32[]{:S(2)}) collective-permute-start(bf16[192,256]{1,0:T(8,128)(2,1)S(1)} %get-tuple-element.44), channel_id=1, source_target_pairs={{0,4},{4,0},{8,12},{12,8},{16,20},{20,16},{24,28},{28,24},{1,5},{5... | collective-permute-start | bytes 294920 | tf_op jit(solution)/shard_map/ppermute | solution.py:227
  72.6 5.7 %collective-permute-start.24 = (bf16[192,256]{1,0:T(8,128)(2,1)S(1)}, bf16[192,256]{1,0:T(8,128)(2,1)S(1)}, u32[]{:S(2)}, u32[]{:S(2)}) collective-permute-start(bf16[192,256]{1,0:T(8,128)(2,1)S(1)} %get-tuple-element.45), channel_id=1, source_target_pairs={{0,8},{4,12},{8,0},{12,4},{16,24},{20,28},{24,16},{28,20},{1,9},{5... | collective-permute-start | bytes 294920 | tf_op jit(solution)/shard_map/ppermute | solution.py:227
  73.4 6.1 %collective-permute-start.25 = (bf16[192,256]{1,0:T(8,128)(2,1)S(1)}, bf16[192,256]{1,0:T(8,128)(2,1)S(1)}, u32[]{:S(2)}, u32[]{:S(2)}) collective-permute-start(bf16[192,256]{1,0:T(8,128)(2,1)S(1)} %get-tuple-element.46), channel_id=1, source_target_pairs={{0,12},{4,8},{8,4},{12,0},{16,28},{20,24},{24,20},{28,16},{1,13},{... | collective-permute-start | bytes 294920 | tf_op jit(solution)/shard_map/ppermute | solution.py:227
  74.9 8.3 %collective-permute-start.30 = (bf16[96,256]{1,0:T(8,128)(2,1)S(1)}, bf16[96,256]{1,0:T(8,128)(2,1)S(1)}, u32[]{:S(2)}, u32[]{:S(2)}) collective-permute-start(bf16[96,256]{1,0:T(8,128)(2,1)S(1)} %slice.24), channel_id=1, source_target_pairs={{0,16},{4,20},{8,24},{12,28},{16,0},{20,4},{24,8},{28,12},{1,17},{... | collective-permute-start | bytes 147464 | tf_op jit(solution)/shard_map/ppermute | solution.py:227
  79.6 5.1 %collective-permute-start.26 = (bf16[96,256]{1,0:T(8,128)(2,1)S(1)}, bf16[96,256]{1,0:T(8,128)(2,1)S(1)}, u32[]{:S(2)}, u32[]{:S(2)}) collective-permute-start(bf16[96,256]{1,0:T(8,128)(2,1)S(1)} %slice.25), channel_id=1, source_target_pairs={{0,16},{4,20},{8,24},{12,28},{16,0},{20,4},{24,8},{28,12},{1,17},{... | collective-permute-start | bytes 147464 | tf_op jit(solution)/shard_map/ppermute | solution.py:227
  (31 other events, 137.4 us)

commit v3 on v2

v3 whole, which is shorter than its diff:
```python
import functools

import jax
import jax.numpy as jnp
from jax import lax
from jax.experimental import pallas as pl
from jax.experimental.pallas import tpu as pltpu
from jax.sharding import PartitionSpec as P

QH = 64
KVH = 8
HD = 128
SLOT_DEV = 96
GROUP = QH // KVH
GW = GROUP * HD
SCALE = HD ** (-0.5)
LOG2E = 1.4426950408889634
DEAD = 1024.0
HIDDEN = 2.0**96


def nt(a, b):
    return lax.dot_general(a, b, (((1,), (1,)), ((), ())), preferred_element_type=jnp.float32)


def nn(a, b):
    return lax.dot_general(a, b, (((1,), (0,)), ((), ())), preferred_element_type=jnp.float32)


def tn(a, b):
    return lax.dot_general(a, b, (((0,), (0,)), ((), ())), preferred_element_type=jnp.float32)


def slot_picks(seg_row, tokens):
    return lax.broadcasted_iota(jnp.int32, (SLOT_DEV, tokens), 0) == seg_row


def lanes(start, size):
    return pl.ds(pl.multiple_of(start, HD), size)


def run_copies(copies):
    for copy in copies:
        copy.start()
    return copies


def wait_copies(copies):
    for copy in copies:
        copy.wait()


def pack_kernel(jobs, place_ref, *refs):
    outs = [out for _, dests in jobs for out in dests]
    sources, out_refs, sems = refs[:2], refs[-len(outs) - 1 : -1], refs[-1]
    me = place_ref[1]
    copies = []
    done = 0
    for width, dests in jobs:
        for out, pieces in zip(out_refs[done:], dests):
            for at, (m, scale, offset) in enumerate(pieces):
                start = lax.bitwise_xor(me, m) * scale + offset
                for part, source in enumerate(sources):
                    rows = source.shape[0]
                    copies.append(
                        pltpu.make_async_copy(
                            source.at[:, lanes(start, width)],
                            out.at[at * rows : (at + 1) * rows, part * width : (part + 1) * width],
                            sems.at[len(copies)],
                        )
                    )
        done += len(dests)
    wait_copies(run_copies(copies))


def gate_kernel(*refs):
    pass


def join_kernel(core_ref, across_ref, *refs):
    out, sems = refs[-2:]
    rows = core_ref.shape[0]
    wait_copies(
        run_copies(
            [
                pltpu.make_async_copy(core_ref, out.at[0:rows, :], sems.at[0]),
                pltpu.make_async_copy(
                    across_ref.at[rows : 2 * rows, :], out.at[rows : 2 * rows, :], sems.at[1]
                ),
            ]
        )
    )


def merge_kernel(place_ref, seg_ref, own_ref, across_ref, core_ref, out, whole):
    kv_heads, tokens = seg_ref.shape
    rows = own_ref.shape[0]
    me = place_ref[1]
    for m, (piece, half) in enumerate(((own_ref, 0), (core_ref, 0), (across_ref, 0), (core_ref, 1))):
        start = pl.multiple_of(lax.bitwise_xor(me, m) * rows, 16)
        whole[pl.ds(start, rows), :] = piece[half * rows : (half + 1) * rows, :]
    for g in range(kv_heads):
        picks = slot_picks(seg_ref[g : g + 1, :], tokens).astype(jnp.float32)
        counts = jnp.sum(picks, axis=1, keepdims=True)
        low_picks = picks.astype(jnp.bfloat16)
        sizes = jnp.maximum(counts, 1.0)
        for part in range(2):
            at = slice((part * kv_heads + g) * HD, (part * kv_heads + g + 1) * HD)
            rows_out = nn(low_picks, whole[:, at]) / sizes
            if part == 0:
                rows_out = jnp.where(counts == 0.0, DEAD, rows_out)
            out[:, at] = rows_out.astype(jnp.bfloat16)


def attend_kernel(
    g, order, qo_at, place_ref, segcol_ref, q_ref, o_ref, kvo_ref, kva_ref, kvc_ref, *refs
):
    shards = len(order)
    heads = 4
    kv_pieces = ((kvo_ref, 0), (kvc_ref, 0), (kva_ref, 0), (kvc_ref, 1))
    qo_pieces = [(refs[shards + i], half) for i, half in qo_at]
    blocks, refs = refs[:shards], refs[-12:]
    dq_ref, own_ref, near_ref, far_ref = refs[:4]
    kx, vx, kt, qo_all, kv_own, qo_sems, kv_sems, block_sems = refs[4:]
    rows = q_ref.shape[0]
    kv_heads = kvo_ref.shape[1] // (2 * HD)
    slots = shards * SLOT_DEV
    shard = place_ref[0]
    me = place_ref[1]
    key_at = slice(g * HD, (g + 1) * HD)
    value_at = slice((kv_heads + g) * HD, (kv_heads + g + 1) * HD)

    block_copies = []
    for r, block in enumerate(blocks):
        at = pl.ds(r * SLOT_DEV, SLOT_DEV)
        block_copies.append(
            pltpu.make_async_copy(block.at[:, key_at], kx.at[at, 0:HD], block_sems.at[2 * r])
        )
        block_copies.append(
            pltpu.make_async_copy(block.at[:, value_at], vx.at[at, :], block_sems.at[2 * r + 1])
        )
    kv_copies = []
    for m, (piece, half) in enumerate(kv_pieces):
        for part, at in enumerate((key_at, value_at)):
            kv_copies.append(
                pltpu.make_async_copy(
                    piece.at[half * rows : (half + 1) * rows, at],
                    kv_own.at[m, part],
                    kv_sems.at[2 * m + part],
                )
            )
    start = (me * kv_heads + g) * GW
    qo_copies = [
        pltpu.make_async_copy(
            source.at[:, lanes(start, GW)],
            qo_all.at[0, :, part * GW : (part + 1) * GW],
            qo_sems.at[part],
        )
        for part, source in enumerate((q_ref, o_ref))
    ]
    for m, (piece, half) in enumerate(qo_pieces):
        qo_copies.append(
            pltpu.make_async_copy(
                piece.at[half * rows : (half + 1) * rows, :], qo_all.at[m + 1], qo_sems.at[m + 2]
            )
        )
    run_copies(block_copies)
    run_copies(kv_copies)
    run_copies(qo_copies)
    wait_copies(block_copies)

    lane = lax.broadcasted_iota(jnp.int32, (SLOT_DEV, HD), 1)
    row = lax.broadcasted_iota(jnp.int32, (SLOT_DEV, HD), 0)
    for r, m in enumerate(order):
        at = pl.ds(r * SLOT_DEV, SLOT_DEV)
        key = kx[at, 0:HD].astype(jnp.float32)
        if m == 0:
            extra = jnp.where(lane == row, 1.0, 0.0)
        else:
            hide = (key[:, 0:1] > 100.0) | (lax.bitwise_xor(shard, m) > shard)
            extra = jnp.where(hide & (lane >= SLOT_DEV), -HIDDEN, 0.0)
        kx[at, 0:HD] = jnp.where(key > 100.0, 0.0, key).astype(jnp.bfloat16)
        kx[at, HD : 2 * HD] = extra.astype(jnp.bfloat16)
    kx[slots : slots + rows, HD : 2 * HD] = jnp.zeros((rows, HD), jnp.bfloat16)
    kt[...] = kx[0:slots, 0:HD].astype(jnp.float32).T.astype(jnp.bfloat16)

    width = GROUP * rows
    qlane = lax.broadcasted_iota(jnp.int32, (rows, HD), 1)
    eye_row = lax.broadcasted_iota(jnp.int32, (rows, width), 0)
    eye_lane = lax.broadcasted_iota(jnp.int32, (rows, width), 1)
    eye = eye_row == lax.rem(eye_lane, rows)
    factor = SCALE * LOG2E
    wait_copies(kv_copies)
    wait_copies(qo_copies)

    dk = None
    dv = None
    for m in range(heads):
        at = pl.ds(pl.multiple_of(lax.bitwise_xor(me, m) * rows, 16), rows)
        own_key = kv_own[m, 0]
        kx[slots : slots + rows, 0:HD] = own_key
        vx[slots : slots + rows, :] = kv_own[m, 1]
        late = (qlane >= segcol_ref[at, g : g + 1]) & (qlane < SLOT_DEV)
        qe = jnp.where(late, -HIDDEN, jnp.where(qlane == SLOT_DEV, 1.0, 0.0)).astype(jnp.bfloat16)
        q2 = jnp.concatenate([qo_all[m, :, h * HD : (h + 1) * HD] for h in range(GROUP)], axis=0)
        o2 = jnp.concatenate(
            [qo_all[m, :, GW + h * HD : GW + (h + 1) * HD] for h in range(GROUP)], axis=0
        )
        qx = jnp.concatenate([q2, jnp.concatenate([qe] * GROUP, axis=0)], axis=1)
        scores = nt(kx[...], qx)
        own_score = jnp.sum(jnp.where(eye, scores[slots:], 0.0), axis=0, keepdims=True)
        scores = scores[:slots]
        top = jnp.maximum(jnp.max(scores, axis=0, keepdims=True), own_score)
        weights = jnp.exp2((scores - top) * factor)
        own_weight = jnp.exp2((own_score - top) * factor)
        inverse = 1.0 / (jnp.sum(weights, axis=0, keepdims=True) + own_weight)
        probs = weights * inverse
        own_prob = own_weight * inverse
        grad_probs = nt(vx[...], o2)
        own_grad_prob = jnp.sum(jnp.where(eye, grad_probs[slots:], 0.0), axis=0, keepdims=True)
        grad_probs = grad_probs[:slots]
        delta = jnp.sum(probs * grad_probs, axis=0, keepdims=True) + own_prob * own_grad_prob
        low_grads = (probs * (grad_probs - delta)).astype(jnp.bfloat16)
        low_probs = probs.astype(jnp.bfloat16)
        own_grad_score = own_prob * (own_grad_prob - delta)
        own_low_probs = jnp.where(eye, own_prob, 0.0).astype(jnp.bfloat16)
        own_low_grads = jnp.where(eye, own_grad_score, 0.0).astype(jnp.bfloat16)
        dv_part = nn(low_probs, o2)
        dk_part = nn(low_grads, q2)
        dv = dv_part if dv is None else dv + dv_part
        dk = dk_part if dk is None else dk + dk_part
        own_ref[at, 0:HD] = SCALE * nn(own_low_grads, q2)
        own_ref[at, HD : 2 * HD] = nn(own_low_probs, o2)
        dq = nn(kt[...], low_grads) + tn(own_key, own_low_grads)
        dq = (SCALE * dq).T.astype(jnp.bfloat16)
        for h in range(GROUP):
            dq_ref[at, h * HD : (h + 1) * HD] = dq[h * rows : (h + 1) * rows]
    dk = dk * SCALE
    half = slots // 2
    for term, part in ((near_ref, slice(0, half)), (far_ref, slice(half, slots))):
        term[:, 0:HD] = dk[part].astype(term.dtype)
        term[:, HD : 2 * HD] = dv[part].astype(term.dtype)


def add_kernel(near_ref, far_ref, after_ref, own_ref, *part_refs):
    total = near_ref[...] + far_ref[...].astype(jnp.float32)
    own_ref[...] = total[:SLOT_DEV]
    for k, part in enumerate(part_refs):
        part[...] = total[(k + 1) * SLOT_DEV : (k + 2) * SLOT_DEV].astype(part.dtype)


def spread_kernel(parts_per_head, seg_ref, *refs):
    kv_heads, tokens = seg_ref.shape
    gk_ref, gv_ref = refs[-2:]
    for g in range(kv_heads):
        parts = refs[g * parts_per_head : (g + 1) * parts_per_head]
        total = parts[0][...].astype(jnp.float32)
        for part in parts[1:-1]:
            total = total + part[...].astype(jnp.float32)
        picks = slot_picks(seg_ref[g : g + 1, :], tokens).astype(jnp.float32)
        counts = jnp.sum(picks, axis=1, keepdims=True)
        total = total / jnp.maximum(counts, 1.0)
        high = total.astype(jnp.bfloat16)
        low = (total - high.astype(jnp.float32)).astype(jnp.bfloat16)
        picks = picks.astype(jnp.bfloat16)
        spread = tn(picks, high) + tn(picks, low) + parts[-1][...]
        gk_ref[:, g * HD : (g + 1) * HD] = spread[:, 0:HD].astype(jnp.bfloat16)
        gv_ref[:, g * HD : (g + 1) * HD] = spread[:, HD : 2 * HD].astype(jnp.bfloat16)


def in_vmem(count):
    return [pl.BlockSpec(memory_space=pltpu.VMEM)] * count


def in_smem():
    return [pl.BlockSpec(memory_space=pltpu.SMEM)]


def anywhere(count):
    return [pl.BlockSpec(memory_space=pl.ANY)] * count


def in_hbm(count):
    return [pl.BlockSpec(memory_space=pltpu.HBM)] * count


def params(mib):
    return pltpu.CompilerParams(vmem_limit_bytes=mib * 2**20)


def shape(*dims, dtype=jnp.bfloat16):
    return jax.ShapeDtypeStruct(dims, dtype)


def swap(x, axis, size, m):
    return lax.ppermute(x, axis, [(i, i ^ m) for i in range(size)])


def gate(values, after):
    return pl.pallas_call(
        gate_kernel,
        out_shape=[shape(*v.shape, dtype=v.dtype) for v in values],
        in_specs=anywhere(len(values) + len(after)),
        out_specs=anywhere(len(values)),
        input_output_aliases={i: i for i in range(len(values))},
        compiler_params=params(1),
        name="gate",
    )(*values, *after)


def exchange(across, core, heads, after=lambda: ()):
    from_across = swap(across, "head", heads, 2)
    after = after()
    both = pl.pallas_call(
        join_kernel,
        out_shape=shape(*across.shape),
        in_specs=anywhere(2 + len(after)),
        out_specs=in_vmem(1)[0],
        scratch_shapes=[pltpu.SemaphoreType.DMA((2,))],
        compiler_params=params(2),
        name="join",
    )(core, from_across, *after)
    return from_across, swap(both, "head", heads, 1), both


def local(queries, keys, values, segment_ids, grad_out):
    rows = queries.shape[0]
    heads = lax.axis_size("head")
    tokens = rows * heads
    kv_heads = KVH // heads
    shards = lax.axis_size("ctx")
    place = jnp.stack([lax.axis_index("ctx"), lax.axis_index("head")]).astype(jnp.int32)
    order = list(range(0, shards, 2)) + list(range(1, shards, 2))
    half = SLOT_DEV * shards // 2
    slots = SLOT_DEV * shards
    kv_width = kv_heads * HD

    def kv_at(m):
        return (m, kv_width, 0)

    def qo_at(m, g):
        return (m, kv_heads * GW, g * GW)

    def pack(jobs, sources, after, mib, name):
        outs = [pieces for _, dests in jobs for pieces in dests]
        return pl.pallas_call(
            functools.partial(pack_kernel, jobs),
            out_shape=[
                shape(len(pieces) * rows, 2 * width) for width, dests in jobs for pieces in dests
            ],
            in_specs=in_smem() + anywhere(2 + len(after)),
            out_specs=anywhere(len(outs)),
            scratch_shapes=[
                pltpu.SemaphoreType.DMA((2 * sum(len(p) for _, dests in jobs for p in dests),))
            ],
            compiler_params=params(mib),
            name=name,
        )(place, *sources, *after)

    kv_across, kv_core, kv_own = pack(
        [(kv_width, [[kv_at(2), kv_at(3)], [kv_at(1)], [kv_at(0)]])], (keys, values), (), 56, "pack_kv"
    )
    from_across, from_core, both = exchange(kv_across, kv_core, heads)
    kv = (kv_own, from_across, from_core)

    jobs = [(GW, [[qo_at(2, 0), qo_at(3, 0)], [qo_at(1, 0)]])]
    for g in range(1, kv_heads):
        jobs.append((GW, [[qo_at(m, g)] for m in range(1, heads)]))
    packed = pack(jobs, (queries, grad_out), (both,), 4, "pack_qo")

    merged = pl.pallas_call(
        merge_kernel,
        out_shape=shape(SLOT_DEV, 2 * kv_width),
        in_specs=in_smem() + in_vmem(4),
        out_specs=in_vmem(1)[0],
        scratch_shapes=[pltpu.VMEM((tokens, 2 * kv_width), jnp.bfloat16)],
        compiler_params=params(4),
        name="merge",
    )(place, segment_ids, *kv)

    held = {0: merged}
    for m in range(2, shards, 2):
        held[m] = swap(merged, "ctx", shards, m)
    for m in range(0, shards, 2):
        held[m + 1] = swap(held[m], "ctx", shards, 1)

    late = [held[m] for m in range(1, shards - 1)]
    qo = [exchange(*packed[:2], heads, lambda: late)[:2]]
    qo_places = [((1, 0), (0, 0), (1, 1))]
    for g in range(1, kv_heads):
        pieces = packed[2 + (g - 1) * (heads - 1) : 2 + g * (heads - 1)]
        pieces = gate(pieces, late)
        qo.append([swap(piece, "head", heads, m + 1) for m, piece in enumerate(pieces)])
        qo_places.append(((0, 0), (1, 0), (2, 0)))

    seg_col = segment_ids.T
    dq = []
    own = []
    near = []
    far = []
    for g in range(kv_heads):
        outs = pl.pallas_call(
            functools.partial(attend_kernel, g, order, qo_places[g]),
            out_shape=[
                shape(tokens, GW),
                shape(tokens, 2 * HD, dtype=jnp.float32),
                shape(half, 2 * HD, dtype=jnp.float32),
                shape(half, 2 * HD),
            ],
            in_specs=in_smem() + in_vmem(1) + in_hbm(2) + anywhere(3 + shards + len(qo[g]) + (g > 0)),
            out_specs=in_vmem(4),
            scratch_shapes=[
                pltpu.VMEM((slots + rows, 2 * HD), jnp.bfloat16),
                pltpu.VMEM((slots + rows, HD), jnp.bfloat16),
                pltpu.VMEM((HD, slots), jnp.bfloat16),
                pltpu.VMEM((heads, rows, 2 * GW), jnp.bfloat16),
                pltpu.VMEM((heads, 2, rows, HD), jnp.bfloat16),
                pltpu.SemaphoreType.DMA((heads + 1,)),
                pltpu.SemaphoreType.DMA((2 * heads,)),
                pltpu.SemaphoreType.DMA((2 * shards,)),
            ],
            compiler_params=params(24),
            cost_estimate=pl.CostEstimate(
                flops=10 * tokens * GROUP * (slots + rows) * HD,
                bytes_accessed=4 * 2**20,
                transcendentals=tokens * GROUP * slots,
            ),
            name="attend",
        )(place, seg_col, queries, grad_out, *kv, *[held[m] for m in order], *qo[g], *own[-1:])
        dq.append(outs[0])
        own.append(outs[1])
        near.append(outs[2])
        far.append(swap(outs[3], "ctx", shards, 1))

    spread_args = []
    for g in range(kv_heads):
        parts = pl.pallas_call(
            add_kernel,
            out_shape=[shape(SLOT_DEV, 2 * HD, dtype=jnp.float32)]
            + [shape(SLOT_DEV, 2 * HD)] * (shards // 2 - 1),
            in_specs=in_vmem(2) + anywhere(1),
            out_specs=in_vmem(shards // 2),
            compiler_params=params(8),
            name="add",
        )(near[g], far[g], own[-1])
        spread_args.append(parts[0])
        for k in range(1, shards // 2):
            spread_args.append(swap(parts[k], "ctx", shards, 2 * k))
        spread_args.append(own[g])

    grad_keys, grad_values = pl.pallas_call(
        functools.partial(spread_kernel, shards // 2 + 1),
        out_shape=[shape(tokens, kv_width)] * 2,
        in_specs=in_vmem(1 + len(spread_args)),
        out_specs=in_vmem(2),
        compiler_params=params(12),
        name="spread",
    )(segment_ids, *spread_args)
    return jnp.concatenate(dq, axis=1), grad_keys, grad_values


def solution(mesh):
    return jax.shard_map(
        local,
        mesh=mesh,
        in_specs=(
            P(("ctx", "head"), None),
            P(("ctx", "head"), None),
            P(("ctx", "head"), None),
            P("head", "ctx"),
            P(("ctx", "head"), None),
        ),
        out_specs=(P("ctx", "head"), P("ctx", "head"), P("ctx", "head")),
        check_vma=False,
    )
```

time: 86.4 us -> 83.6 us (0.968)
  local copies, waits for them, and re-layouts: 17.4 us -> 6.46 us
  Pallas kernels: 17.6 us -> 27.4 us
  starting transfers between devices: 34.1 us -> 28 us
  waiting for transfers between devices: 14.6 us -> 18.8 us
    unnamed x65 -> x31, local copies, waits for them, and re-layouts: 17.4 us -> 6.46 us
    pallas_call x6 -> x11, Pallas kernels: 17.6 us -> 27.4 us  [the longest x2 15.6 us: local(): pl.pallas_call(functools.partial(attend_kernel, g, order, qo_places[g]),...]
    ppermute x31 -> x22, starting transfers between devices: 34.1 us -> 28 us  [swap(): return lax.ppermute(x, axis, [(i, i ^ m) for i in range(size)])]
    ppermute x31 -> x22, waiting for transfers between devices: 14.6 us -> 18.8 us  [swap(): return lax.ppermute(x, axis, [(i, i ^ m) for i in range(size)])]
  transfers between devices with their start and end apart: 31 -> 22, of which waited for: 9 -> 10; matrix products, arithmetic and copies ran while one was open for 1% -> 1% of each run, Pallas kernels for 18% -> 20%
where the time goes in v3:
time: 83.6 us; the launch traced here: 83.1 us
  starting transfers between devices  28 us (33%)
  Pallas kernels  27.4 us (33%)
  waiting for transfers between devices  18.8 us (22%)
  local copies, waits for them, and re-layouts  6.46 us (8%)
  other arithmetic  1.61 us (2%)
    ppermute x22, starting transfers between devices, swap(): return lax.ppermute(x, axis, [(i, i ^ m) for i in range(size)])  28 us
    ppermute x22, waiting for transfers between devices, swap(): return lax.ppermute(x, axis, [(i, i ^ m) for i in range(size)])  18.8 us
    pallas_call x2, Pallas kernels, local(): pl.pallas_call(functools.partial(attend_kernel, g, order, qo_places[g]),...  15.6 us
    pallas_call x2, Pallas kernels, pack(): pl.pallas_call(functools.partial(pack_kernel, jobs), out_shape=[shape(len...  9.34 us
    unnamed x31, local copies, waits for them, and re-layouts  6.46 us
  transfers between devices with their start and end apart: 22, of which 10 were waited for; matrix products, arithmetic and copies ran while one was open for 1% of the time, Pallas kernels for 20%

profile of v3, /device:TPU:0, one launch (start us, length us, event | category | flops | bytes accessed | tf_op | source)
XLA Modules:
  0.0 83.1 jit_solution(15770877201085984733)
XLA Ops:
  1.3 7.8 %pack_kv.1 = (bf16[96,512]{1,0:T(8,128)(2,1)}, bf16[48,512]{1,0:T(8,128)(2,1)}, bf16[48,512]{1,0:T(8,128)(2,1)}) custom-call(s32[2]{0:T(128)} %pad_add_fusion.place_ref, bf16[48,1024]{1,0:T(8,128)(2,1)} %refs_0_.2, bf16[48,1024]{1,0:T(8,128)(2,1)} %refs_1_.2), custom_call_target="tpu_custom_call" | custom-call | tf_op jit(solution)/shard_map/pack_kv/pallas_call | solution.py:346
  9.1 3.0 %collective-permute-start = (bf16[96,512]{1,0:T(8,128)(2,1)}, bf16[96,512]{1,0:T(8,128)(2,1)S(1)}, u32[]{:S(2)}, u32[]{:S(2)}) collective-permute-start(bf16[96,512]{1,0:T(8,128)(2,1)} %get-tuple-element.33), channel_id=1, source_target_pairs={{0,2},{1,3},{2,0},{3,1},{4,6},{5,7},{6,4},{7,5},{8,10},{9,11},{10,... | collective-permute-start | bytes 294920 | tf_op jit(solution)/shard_map/ppermute | solution.py:296
  12.1 3.0 %collective-permute-done.across_ref.kva_ref = bf16[96,512]{1,0:T(8,128)(2,1)S(1)} collective-permute-done((bf16[96,512]{1,0:T(8,128)(2,1)}, bf16[96,512]{1,0:T(8,128)(2,1)S(1)}, u32[]{:S(2)}, u32[]{:S(2)}) %collective-permute-start) | collective-permute-done | bytes 98336 | tf_op jit(solution)/shard_map/ppermute | solution.py:296
  16.0 1.1 %copy-done = bf16[48,8192]{1,0:T(8,128)(2,1)S(1)} copy-done((bf16[48,8192]{1,0:T(8,128)(2,1)S(1)}, bf16[48,8192]{1,0:T(8,128)(2,1)}, u32[]{:S(2)}) %copy-start) | copy-done | bytes 786456
  17.2 1.1 %copy-done.2 = bf16[48,8192]{1,0:T(8,128)(2,1)S(1)} copy-done((bf16[48,8192]{1,0:T(8,128)(2,1)S(1)}, bf16[48,8192]{1,0:T(8,128)(2,1)}, u32[]{:S(2)}) %copy-start.2) | copy-done | bytes 786456
  19.0 1.5 %pack_qo.1 = (bf16[96,2048]{1,0:T(8,128)(2,1)S(1)}, bf16[48,2048]{1,0:T(8,128)(2,1)S(1)}, bf16[48,2048]{1,0:T(8,128)(2,1)S(1)}, bf16[48,2048]{1,0:T(8,128)(2,1)S(1)}, bf16[48,2048]{1,0:T(8,128)(2,1)}) custom-call(s32[2]{0:T(128)S(1)} %copy-done.13, bf16[48,8192]{1,0:T(8,128)(2,1)S(1)} %copy-done, bf16[48,8192]{1,0:T(8,128)(2,1)S(1)} %copy-done.2, ...), custom_call_target="tpu_custom_call" | custom-call | tf_op jit(solution)/shard_map/pack_qo/pallas_call | solution.py:346
  20.5 1.9 %collective-permute-start.9 = (bf16[96,2048]{1,0:T(8,128)(2,1)S(1)}, bf16[96,2048]{1,0:T(8,128)(2,1)S(1)}, u32[]{:S(2)}, u32[]{:S(2)}) collective-permute-start(bf16[96,2048]{1,0:T(8,128)(2,1)S(1)} %get-tuple-element.35), channel_id=1, source_target_pairs={{0,2},{1,3},{2,0},{3,1},{4,6},{5,7},{6,4},{7,5},{8,10},{9,11},{10,... | collective-permute-start | bytes 1179656 | tf_op jit(solution)/shard_map/ppermute | solution.py:296
  22.4 1.3 %collective-permute-done.1.core_ref.kvc_ref = bf16[96,512]{1,0:T(8,128)(2,1)S(1)} collective-permute-done((bf16[96,512]{1,0:T(8,128)(2,1)S(1)}, bf16[96,512]{1,0:T(8,128)(2,1)S(1)}, u32[]{:S(2)}, u32[]{:S(2)}) %collective-permute-start.1) | collective-permute-done | bytes 98336 | tf_op jit(solution)/shard_map/ppermute | solution.py:296
  24.5 2.7 %collective-permute-start.3 = (bf16[96,512]{1,0:T(8,128)(2,1)S(1)}, bf16[96,512]{1,0:T(8,128)(2,1)S(1)}, u32[]{:S(2)}, u32[]{:S(2)}) collective-permute-start(bf16[96,512]{1,0:T(8,128)(2,1)S(1)} %merge.1.refs_0_), channel_id=1, source_target_pairs={{0,16},{4,20},{8,24},{12,28},{16,0},{20,4},{24,8},{28,12},{1,17},{... | collective-permute-start | bytes 294920 | tf_op jit(solution)/shard_map/ppermute | solution.py:296
  27.2 1.6 %collective-permute-start.2 = (bf16[96,512]{1,0:T(8,128)(2,1)S(1)}, bf16[96,512]{1,0:T(8,128)(2,1)S(1)}, u32[]{:S(2)}, u32[]{:S(2)}) collective-permute-start(bf16[96,512]{1,0:T(8,128)(2,1)S(1)} %merge.1.refs_0_), channel_id=1, source_target_pairs={{0,8},{4,12},{8,0},{12,4},{16,24},{20,28},{24,16},{28,20},{1,9},{5... | collective-permute-start | bytes 294920 | tf_op jit(solution)/shard_map/ppermute | solution.py:296
  28.7 1.5 %collective-permute-start.5 = (bf16[96,512]{1,0:T(8,128)(2,1)S(1)}, bf16[96,512]{1,0:T(8,128)(2,1)S(1)}, u32[]{:S(2)}, u32[]{:S(2)}) collective-permute-start(bf16[96,512]{1,0:T(8,128)(2,1)S(1)} %merge.1.refs_0_), channel_id=1, source_target_pairs={{0,4},{4,0},{8,12},{12,8},{16,20},{20,16},{24,28},{28,24},{1,5},{5... | collective-permute-start | bytes 294920 | tf_op jit(solution)/shard_map/ppermute | solution.py:296
  30.5 2.2 %collective-permute-done.3.refs_3_.refs_2_.refs_6_ = bf16[96,512]{1,0:T(8,128)(2,1)S(1)} collective-permute-done((bf16[96,512]{1,0:T(8,128)(2,1)S(1)}, bf16[96,512]{1,0:T(8,128)(2,1)S(1)}, u32[]{:S(2)}, u32[]{:S(2)}) %collective-permute-start.3) | collective-permute-done | bytes 98336 | tf_op jit(solution)/shard_map/ppermute | solution.py:296
  32.7 2.3 %collective-permute-start.7 = (bf16[96,512]{1,0:T(8,128)(2,1)S(1)}, bf16[96,512]{1,0:T(8,128)(2,1)S(1)}, u32[]{:S(2)}, u32[]{:S(2)}) collective-permute-start(bf16[96,512]{1,0:T(8,128)(2,1)S(1)} %collective-permute-done.3.refs_3_.refs_2_.refs_6_), channel_id=1, source_target_pairs={{0,4},{4,0},{8,12},{12,8},{16,20},{20,16},{24,28},{28,24},{1,5},{5... | collective-permute-start | bytes 294920 | tf_op jit(solution)/shard_map/ppermute | solution.py:296
  35.0 1.8 %collective-permute-done.4.refs_5_.refs_3_.refs_8_ = bf16[96,512]{1,0:T(8,128)(2,1)S(1)} collective-permute-done((bf16[96,512]{1,0:T(8,128)(2,1)S(1)}, bf16[96,512]{1,0:T(8,128)(2,1)S(1)}, u32[]{:S(2)}, u32[]{:S(2)}) %collective-permute-start.4) | collective-permute-done | bytes 98336 | tf_op jit(solution)/shard_map/ppermute | solution.py:296
  37.5 2.0 %collective-permute-done.6.refs_2_.refs_5_ = bf16[96,512]{1,0:T(8,128)(2,1)S(1)} collective-permute-done((bf16[96,512]{1,0:T(8,128)(2,1)S(1)}, bf16[96,512]{1,0:T(8,128)(2,1)S(1)}, u32[]{:S(2)}, u32[]{:S(2)}) %collective-permute-start.6) | collective-permute-done | bytes 98336 | tf_op jit(solution)/shard_map/ppermute | solution.py:296
  40.2 1.1 %collective-permute-start.8 = (bf16[96,512]{1,0:T(8,128)(2,1)S(1)}, bf16[96,512]{1,0:T(8,128)(2,1)}, u32[]{:S(2)}, u32[]{:S(2)}) collective-permute-start(bf16[96,512]{1,0:T(8,128)(2,1)S(1)} %collective-permute-done.4.refs_5_.refs_3_.refs_8_), channel_id=1, source_target_pairs={{0,4},{4,0},{8,12},{12,8},{16,20},{20,16},{24,28},{28,24},{1,5},{5... | collective-permute-start | bytes 294920 | tf_op jit(solution)/shard_map/ppermute | solution.py:296
  42.0 1.2 %collective-permute-start.13 = (bf16[48,2048]{1,0:T(8,128)(2,1)}, bf16[48,2048]{1,0:T(8,128)(2,1)}, u32[]{:S(2)}, u32[]{:S(2)}) collective-permute-start(bf16[48,2048]{1,0:T(8,128)(2,1)} %get-tuple-element.43), channel_id=1, source_target_pairs={{0,3},{1,2},{2,1},{3,0},{4,7},{5,6},{6,5},{7,4},{8,11},{9,10},{10,... | collective-permute-start | bytes 589832 | tf_op jit(solution)/shard_map/ppermute | solution.py:296
  43.3 2.2 %collective-permute-done.8.refs_7_ = bf16[96,512]{1,0:T(8,128)(2,1)} collective-permute-done((bf16[96,512]{1,0:T(8,128)(2,1)S(1)}, bf16[96,512]{1,0:T(8,128)(2,1)}, u32[]{:S(2)}, u32[]{:S(2)}) %collective-permute-start.8) | collective-permute-done | bytes 98336 | tf_op jit(solution)/shard_map/ppermute | solution.py:296
  45.6 0.9 %copy-done.5 = bf16[96,512]{1,0:T(8,128)(2,1)S(1)} copy-done((bf16[96,512]{1,0:T(8,128)(2,1)S(1)}, bf16[96,512]{1,0:T(8,128)(2,1)}, u32[]{:S(2)}) %copy-start.5) | copy-done | bytes 98328
  46.5 0.9 %copy-done.8 = bf16[96,512]{1,0:T(8,128)(2,1)S(1)} copy-done((bf16[96,512]{1,0:T(8,128)(2,1)S(1)}, bf16[96,512]{1,0:T(8,128)(2,1)}, u32[]{:S(2)}) %copy-start.8) | copy-done | bytes 98328
  48.2 7.7 %attend.2 = (bf16[192,1024]{1,0:T(8,128)(2,1)S(1)}, f32[192,256]{1,0:T(8,128)S(1)}, f32[384,256]{1,0:T(8,128)S(1)}, bf16[384,256]{1,0:T(8,128)(2,1)S(1)}) custom-call(s32[2]{0:T(128)S(1)} %copy-done.14, s32[192,2]{1,0:T(8,128)S(1)} %bitcast.3, bf16[48,8192]{1,0:T(8,128)(2,1)S(1)} %copy-done.1, bf16[48,8192]{1,0:T(8,128)(2,1)S(1)} %copy-done.3, ...), custom_call_target="tpu_custom_call" | custom-call | flops 1604321280 | bytes 4194304 | tf_op jit(solution)/shard_map/attend/pallas_call | solution.py:402
  55.9 1.1 %collective-permute-start.14 = (bf16[384,256]{1,0:T(8,128)(2,1)S(1)}, bf16[384,256]{1,0:T(8,128)(2,1)S(1)}, u32[]{:S(2)}, u32[]{:S(2)}) collective-permute-start(bf16[384,256]{1,0:T(8,128)(2,1)S(1)} %get-tuple-element.47), channel_id=1, source_target_pairs={{0,4},{4,0},{8,12},{12,8},{16,20},{20,16},{24,28},{28,24},{1,5},{5... | collective-permute-start | bytes 589832 | tf_op jit(solution)/shard_map/ppermute | solution.py:296
  57.0 7.8 %attend.3 = (bf16[192,1024]{1,0:T(8,128)(2,1)S(1)}, f32[192,256]{1,0:T(8,128)S(1)}, f32[384,256]{1,0:T(8,128)S(1)}, bf16[384,256]{1,0:T(8,128)(2,1)S(1)}) custom-call(s32[2]{0:T(128)S(1)} %copy-done.14, s32[192,2]{1,0:T(8,128)S(1)} %bitcast.4, bf16[48,8192]{1,0:T(8,128)(2,1)S(1)} %copy-done.1, bf16[48,8192]{1,0:T(8,128)(2,1)S(1)} %copy-done.3, ...), custom_call_target="tpu_custom_call" | custom-call | flops 1604321280 | bytes 4194304 | tf_op jit(solution)/shard_map/attend/pallas_call | solution.py:402
  64.9 1.1 %collective-permute-start.18 = (bf16[384,256]{1,0:T(8,128)(2,1)S(1)}, bf16[384,256]{1,0:T(8,128)(2,1)S(1)}, u32[]{:S(2)}, u32[]{:S(2)}) collective-permute-start(bf16[384,256]{1,0:T(8,128)(2,1)S(1)} %get-tuple-element.54), channel_id=1, source_target_pairs={{0,4},{4,0},{8,12},{12,8},{16,20},{20,16},{24,28},{28,24},{1,5},{5... | collective-permute-start | bytes 589832 | tf_op jit(solution)/shard_map/ppermute | solution.py:296
  66.0 0.9 %collective-permute-start.15 = (bf16[96,256]{1,0:T(8,128)(2,1)S(1)}, bf16[96,256]{1,0:T(8,128)(2,1)S(1)}, u32[]{:S(2)}, u32[]{:S(2)}) collective-permute-start(bf16[96,256]{1,0:T(8,128)(2,1)S(1)} %get-tuple-element.50), channel_id=1, source_target_pairs={{0,8},{4,12},{8,0},{12,4},{16,24},{20,28},{24,16},{28,20},{1,9},{5... | collective-permute-start | bytes 147464 | tf_op jit(solution)/shard_map/ppermute | solution.py:296
  66.8 3.7 %collective-permute-start.16 = (bf16[96,256]{1,0:T(8,128)(2,1)S(1)}, bf16[96,256]{1,0:T(8,128)(2,1)S(1)}, u32[]{:S(2)}, u32[]{:S(2)}) collective-permute-start(bf16[96,256]{1,0:T(8,128)(2,1)S(1)} %get-tuple-element.51), channel_id=1, source_target_pairs={{0,16},{4,20},{8,24},{12,28},{16,0},{20,4},{24,8},{28,12},{1,17},{... | collective-permute-start | bytes 147464 | tf_op jit(solution)/shard_map/ppermute | solution.py:296
  71.2 1.1 %collective-permute-start.19 = (bf16[96,256]{1,0:T(8,128)(2,1)S(1)}, bf16[96,256]{1,0:T(8,128)(2,1)S(1)}, u32[]{:S(2)}, u32[]{:S(2)}) collective-permute-start(bf16[96,256]{1,0:T(8,128)(2,1)S(1)} %get-tuple-element.56), channel_id=1, source_target_pairs={{0,8},{4,12},{8,0},{12,4},{16,24},{20,28},{24,16},{28,20},{1,9},{5... | collective-permute-start | bytes 147464 | tf_op jit(solution)/shard_map/ppermute | solution.py:296
  72.3 3.9 %collective-permute-start.20 = (bf16[96,256]{1,0:T(8,128)(2,1)S(1)}, bf16[96,256]{1,0:T(8,128)(2,1)S(1)}, u32[]{:S(2)}, u32[]{:S(2)}) collective-permute-start(bf16[96,256]{1,0:T(8,128)(2,1)S(1)} %get-tuple-element.57), channel_id=1, source_target_pairs={{0,16},{4,20},{8,24},{12,28},{16,0},{20,4},{24,8},{28,12},{1,17},{... | collective-permute-start | bytes 147464 | tf_op jit(solution)/shard_map/ppermute | solution.py:296
  76.2 0.9 %pad_maximum_fusion = bf16[192,2048]{1,0:T(8,128)(2,1)} fusion(bf16[192,1024]{1,0:T(8,128)(2,1)S(1)} %get-tuple-element.45, bf16[192,1024]{1,0:T(8,128)(2,1)S(1)} %get-tuple-element.37), kind=kLoop, calls=%fused_computation | loop fusion | flops 1572864 | bytes 1572864 | tf_op jit(solution)/shard_map/concatenate | solution.py:459
  77.1 2.1 %collective-permute-done.20.refs_7_ = bf16[96,256]{1,0:T(8,128)(2,1)S(1)} collective-permute-done((bf16[96,256]{1,0:T(8,128)(2,1)S(1)}, bf16[96,256]{1,0:T(8,128)(2,1)S(1)}, u32[]{:S(2)}, u32[]{:S(2)}) %collective-permute-start.20) | collective-permute-done | bytes 49184 | tf_op jit(solution)/shard_map/ppermute | solution.py:296
  79.3 2.8 %collective-permute-done.21.refs_8_ = bf16[96,256]{1,0:T(8,128)(2,1)S(1)} collective-permute-done((bf16[96,256]{1,0:T(8,128)(2,1)S(1)}, bf16[96,256]{1,0:T(8,128)(2,1)S(1)}, u32[]{:S(2)}, u32[]{:S(2)}) %collective-permute-start.21) | collective-permute-done | bytes 49184 | tf_op jit(solution)/shard_map/ppermute | solution.py:296
  82.1 1.0 %spread.1 = (bf16[192,256]{1,0:T(8,128)(2,1)}, bf16[192,256]{1,0:T(8,128)(2,1)}) custom-call(s32[2,192]{1,0:T(2,128)S(1)} %copy-done.12, f32[96,256]{1,0:T(8,128)S(1)} %get-tuple-element.49.refs_0_, bf16[96,256]{1,0:T(8,128)(2,1)S(1)} %collective-permute-done.15.refs_1_, bf16[96,256]{1,0:T(8,128)(2,1)S(1)} %collective-permute-done.16.refs_2_, ...), custom_call_target="tpu_custom_call" | custom-call | tf_op jit(solution)/shard_map/spread/pallas_call | solution.py:451
  (56 shorter events, 7.0 us)
Async XLA Ops:
  9.1 6.0 %collective-permute-start = (bf16[96,512]{1,0:T(8,128)(2,1)}, bf16[96,512]{1,0:T(8,128)(2,1)S(1)}, u32[]{:S(2)}, u32[]{:S(2)}) collective-permute-start(bf16[96,512]{1,0:T(8,128)(2,1)} %get-tuple-element.33), channel_id=1, source_target_pairs={{0,2},{1,3},{2,0},{3,1},{4,6},{5,7},{6,4},{7,5},{8,10},{9,11},{10,... | collective-permute-start | bytes 294920 | tf_op jit(solution)/shard_map/ppermute | solution.py:296
  16.0 1.1 %copy-start = (bf16[48,8192]{1,0:T(8,128)(2,1)S(1)}, bf16[48,8192]{1,0:T(8,128)(2,1)}, u32[]{:S(2)}) copy-start(bf16[48,8192]{1,0:T(8,128)(2,1)} %q_ref.3) | copy-start | bytes 2359300
  17.2 1.1 %copy-start.2 = (bf16[48,8192]{1,0:T(8,128)(2,1)S(1)}, bf16[48,8192]{1,0:T(8,128)(2,1)}, u32[]{:S(2)}) copy-start(bf16[48,8192]{1,0:T(8,128)(2,1)} %o_ref.3) | copy-start | bytes 2359300
  19.0 4.8 %copy-start.9 = (bf16[48,512]{1,0:T(8,128)(2,1)S(1)}, bf16[48,512]{1,0:T(8,128)(2,1)}, u32[]{:S(2)}) copy-start(bf16[48,512]{1,0:T(8,128)(2,1)} %get-tuple-element.32.own_ref.kvo_ref) | copy-start | bytes 147460
  19.0 4.8 %copy-start.12 = (s32[2,192]{1,0:T(2,128)S(1)}, s32[2,192]{1,0:T(2,128)}, u32[]{:S(2)}) copy-start(s32[2,192]{1,0:T(2,128)} %seg_ref.3) | copy-start | bytes 4612
  20.5 19.0 %collective-permute-start.9 = (bf16[96,2048]{1,0:T(8,128)(2,1)S(1)}, bf16[96,2048]{1,0:T(8,128)(2,1)S(1)}, u32[]{:S(2)}, u32[]{:S(2)}) collective-permute-start(bf16[96,2048]{1,0:T(8,128)(2,1)S(1)} %get-tuple-element.35), channel_id=1, source_target_pairs={{0,2},{1,3},{2,0},{3,1},{4,6},{5,7},{6,4},{7,5},{8,10},{9,11},{10,... | collective-permute-start | bytes 1179656 | tf_op jit(solution)/shard_map/ppermute | solution.py:296
  22.4 1.3 %collective-permute-start.1 = (bf16[96,512]{1,0:T(8,128)(2,1)S(1)}, bf16[96,512]{1,0:T(8,128)(2,1)S(1)}, u32[]{:S(2)}, u32[]{:S(2)}) collective-permute-start(bf16[96,512]{1,0:T(8,128)(2,1)S(1)} %join.2.refs_2_), channel_id=1, source_target_pairs={{0,1},{1,0},{2,3},{3,2},{4,5},{5,4},{6,7},{7,6},{8,9},{9,8},{10,11... | collective-permute-start | bytes 294920 | tf_op jit(solution)/shard_map/ppermute | solution.py:296
  23.7 15.8 %copy-start.4 = (bf16[96,512]{1,0:T(8,128)(2,1)}, bf16[96,512]{1,0:T(8,128)(2,1)S(1)}, u32[]{:S(2)}) copy-start(bf16[96,512]{1,0:T(8,128)(2,1)S(1)} %collective-permute-done.1.core_ref.kvc_ref) | copy-start | bytes 294916
  24.5 15.6 %copy-start.7 = (bf16[96,512]{1,0:T(8,128)(2,1)}, bf16[96,512]{1,0:T(8,128)(2,1)S(1)}, u32[]{:S(2)}) copy-start(bf16[96,512]{1,0:T(8,128)(2,1)S(1)} %merge.1.refs_0_) | copy-start | bytes 294916
  24.5 8.2 %collective-permute-start.3 = (bf16[96,512]{1,0:T(8,128)(2,1)S(1)}, bf16[96,512]{1,0:T(8,128)(2,1)S(1)}, u32[]{:S(2)}, u32[]{:S(2)}) collective-permute-start(bf16[96,512]{1,0:T(8,128)(2,1)S(1)} %merge.1.refs_0_), channel_id=1, source_target_pairs={{0,16},{4,20},{8,24},{12,28},{16,0},{20,4},{24,8},{28,12},{1,17},{... | collective-permute-start | bytes 294920 | tf_op jit(solution)/shard_map/ppermute | solution.py:296
  27.2 7.8 %collective-permute-start.2 = (bf16[96,512]{1,0:T(8,128)(2,1)S(1)}, bf16[96,512]{1,0:T(8,128)(2,1)S(1)}, u32[]{:S(2)}, u32[]{:S(2)}) collective-permute-start(bf16[96,512]{1,0:T(8,128)(2,1)S(1)} %merge.1.refs_0_), channel_id=1, source_target_pairs={{0,8},{4,12},{8,0},{12,4},{16,24},{20,28},{24,16},{28,20},{1,9},{5... | collective-permute-start | bytes 294920 | tf_op jit(solution)/shard_map/ppermute | solution.py:296
  28.7 6.2 %collective-permute-start.5 = (bf16[96,512]{1,0:T(8,128)(2,1)S(1)}, bf16[96,512]{1,0:T(8,128)(2,1)S(1)}, u32[]{:S(2)}, u32[]{:S(2)}) collective-permute-start(bf16[96,512]{1,0:T(8,128)(2,1)S(1)} %merge.1.refs_0_), channel_id=1, source_target_pairs={{0,4},{4,0},{8,12},{12,8},{16,20},{20,16},{24,28},{28,24},{1,5},{5... | collective-permute-start | bytes 294920 | tf_op jit(solution)/shard_map/ppermute | solution.py:296
  30.3 6.5 %collective-permute-start.4 = (bf16[96,512]{1,0:T(8,128)(2,1)S(1)}, bf16[96,512]{1,0:T(8,128)(2,1)S(1)}, u32[]{:S(2)}, u32[]{:S(2)}) collective-permute-start(bf16[96,512]{1,0:T(8,128)(2,1)S(1)} %merge.1.refs_0_), channel_id=1, source_target_pairs={{0,24},{4,28},{8,16},{12,20},{16,8},{20,12},{24,0},{28,4},{1,25},{... | collective-permute-start | bytes 294920 | tf_op jit(solution)/shard_map/ppermute | solution.py:296
  32.7 4.8 %collective-permute-start.7 = (bf16[96,512]{1,0:T(8,128)(2,1)S(1)}, bf16[96,512]{1,0:T(8,128)(2,1)S(1)}, u32[]{:S(2)}, u32[]{:S(2)}) collective-permute-start(bf16[96,512]{1,0:T(8,128)(2,1)S(1)} %collective-permute-done.3.refs_3_.refs_2_.refs_6_), channel_id=1, source_target_pairs={{0,4},{4,0},{8,12},{12,8},{16,20},{20,16},{24,28},{28,24},{1,5},{5... | collective-permute-start | bytes 294920 | tf_op jit(solution)/shard_map/ppermute | solution.py:296
  34.9 4.6 %collective-permute-start.6 = (bf16[96,512]{1,0:T(8,128)(2,1)S(1)}, bf16[96,512]{1,0:T(8,128)(2,1)S(1)}, u32[]{:S(2)}, u32[]{:S(2)}) collective-permute-start(bf16[96,512]{1,0:T(8,128)(2,1)S(1)} %collective-permute-done.2.refs_1_.refs_4_), channel_id=1, source_target_pairs={{0,4},{4,0},{8,12},{12,8},{16,20},{20,16},{24,28},{28,24},{1,5},{5... | collective-permute-start | bytes 294920 | tf_op jit(solution)/shard_map/ppermute | solution.py:296
  39.6 6.0 %copy-start.3 = (bf16[48,8192]{1,0:T(8,128)(2,1)S(1)}, bf16[48,8192]{1,0:T(8,128)(2,1)}, u32[]{:S(2)}) copy-start(bf16[48,8192]{1,0:T(8,128)(2,1)} %o_ref.3) | copy-start | bytes 2359300
  40.1 5.4 %copy-start.1 = (bf16[48,8192]{1,0:T(8,128)(2,1)S(1)}, bf16[48,8192]{1,0:T(8,128)(2,1)}, u32[]{:S(2)}) copy-start(bf16[48,8192]{1,0:T(8,128)(2,1)} %q_ref.3) | copy-start | bytes 2359300
  40.1 5.4 %copy-start.14 = (s32[2]{0:T(128)S(1)}, s32[2]{0:T(128)}, u32[]{:S(2)}) copy-start(s32[2]{0:T(128)} %pad_add_fusion.place_ref) | copy-start | bytes 28
  40.1 5.4 %collective-permute-start.10 = (bf16[96,2048]{1,0:T(8,128)(2,1)S(1)}, bf16[96,2048]{1,0:T(8,128)(2,1)}, u32[]{:S(2)}, u32[]{:S(2)}) collective-permute-start(bf16[96,2048]{1,0:T(8,128)(2,1)S(1)} %join.3), channel_id=1, source_target_pairs={{0,1},{1,0},{2,3},{3,2},{4,5},{5,4},{6,7},{7,6},{8,9},{9,8},{10,11... | collective-permute-start | bytes 1179656 | tf_op jit(solution)/shard_map/ppermute | solution.py:296
  40.2 5.3 %collective-permute-start.8 = (bf16[96,512]{1,0:T(8,128)(2,1)S(1)}, bf16[96,512]{1,0:T(8,128)(2,1)}, u32[]{:S(2)}, u32[]{:S(2)}) collective-permute-start(bf16[96,512]{1,0:T(8,128)(2,1)S(1)} %collective-permute-done.4.refs_5_.refs_3_.refs_8_), channel_id=1, source_target_pairs={{0,4},{4,0},{8,12},{12,8},{16,20},{20,16},{24,28},{28,24},{1,5},{5... | collective-permute-start | bytes 294920 | tf_op jit(solution)/shard_map/ppermute | solution.py:296
  41.3 15.7 %collective-permute-start.11 = (bf16[48,2048]{1,0:T(8,128)(2,1)S(1)}, bf16[48,2048]{1,0:T(8,128)(2,1)}, u32[]{:S(2)}, u32[]{:S(2)}) collective-permute-start(bf16[48,2048]{1,0:T(8,128)(2,1)S(1)} %get-tuple-element.41), channel_id=1, source_target_pairs={{0,1},{1,0},{2,3},{3,2},{4,5},{5,4},{6,7},{7,6},{8,9},{9,8},{10,11... | collective-permute-start | bytes 589832 | tf_op jit(solution)/shard_map/ppermute | solution.py:296
  41.5 15.5 %collective-permute-start.12 = (bf16[48,2048]{1,0:T(8,128)(2,1)S(1)}, bf16[48,2048]{1,0:T(8,128)(2,1)}, u32[]{:S(2)}, u32[]{:S(2)}) collective-permute-start(bf16[48,2048]{1,0:T(8,128)(2,1)S(1)} %get-tuple-element.42), channel_id=1, source_target_pairs={{0,2},{1,3},{2,0},{3,1},{4,6},{5,7},{6,4},{7,5},{8,10},{9,11},{10,... | collective-permute-start | bytes 589832 | tf_op jit(solution)/shard_map/ppermute | solution.py:296
  42.0 15.0 %collective-permute-start.13 = (bf16[48,2048]{1,0:T(8,128)(2,1)}, bf16[48,2048]{1,0:T(8,128)(2,1)}, u32[]{:S(2)}, u32[]{:S(2)}) collective-permute-start(bf16[48,2048]{1,0:T(8,128)(2,1)} %get-tuple-element.43), channel_id=1, source_target_pairs={{0,3},{1,2},{2,1},{3,0},{4,7},{5,6},{6,5},{7,4},{8,11},{9,10},{10,... | collective-permute-start | bytes 589832 | tf_op jit(solution)/shard_map/ppermute | solution.py:296
  48.1 8.9 %copy-start.6 = (bf16[96,512]{1,0:T(8,128)(2,1)S(1)}, bf16[96,512]{1,0:T(8,128)(2,1)}, u32[]{:S(2)}) copy-start(bf16[96,512]{1,0:T(8,128)(2,1)} %copy-done.4) | copy-start | bytes 294916
  55.9 10.0 %collective-permute-start.14 = (bf16[384,256]{1,0:T(8,128)(2,1)S(1)}, bf16[384,256]{1,0:T(8,128)(2,1)S(1)}, u32[]{:S(2)}, u32[]{:S(2)}) collective-permute-start(bf16[384,256]{1,0:T(8,128)(2,1)S(1)} %get-tuple-element.47), channel_id=1, source_target_pairs={{0,4},{4,0},{8,12},{12,8},{16,20},{20,16},{24,28},{28,24},{1,5},{5... | collective-permute-start | bytes 589832 | tf_op jit(solution)/shard_map/ppermute | solution.py:296
  64.9 6.3 %collective-permute-start.18 = (bf16[384,256]{1,0:T(8,128)(2,1)S(1)}, bf16[384,256]{1,0:T(8,128)(2,1)S(1)}, u32[]{:S(2)}, u32[]{:S(2)}) collective-permute-start(bf16[384,256]{1,0:T(8,128)(2,1)S(1)} %get-tuple-element.54), channel_id=1, source_target_pairs={{0,4},{4,0},{8,12},{12,8},{16,20},{20,16},{24,28},{28,24},{1,5},{5... | collective-permute-start | bytes 589832 | tf_op jit(solution)/shard_map/ppermute | solution.py:296
  66.0 10.2 %collective-permute-start.15 = (bf16[96,256]{1,0:T(8,128)(2,1)S(1)}, bf16[96,256]{1,0:T(8,128)(2,1)S(1)}, u32[]{:S(2)}, u32[]{:S(2)}) collective-permute-start(bf16[96,256]{1,0:T(8,128)(2,1)S(1)} %get-tuple-element.50), channel_id=1, source_target_pairs={{0,8},{4,12},{8,0},{12,4},{16,24},{20,28},{24,16},{28,20},{1,9},{5... | collective-permute-start | bytes 147464 | tf_op jit(solution)/shard_map/ppermute | solution.py:296
  66.8 10.3 %collective-permute-start.16 = (bf16[96,256]{1,0:T(8,128)(2,1)S(1)}, bf16[96,256]{1,0:T(8,128)(2,1)S(1)}, u32[]{:S(2)}, u32[]{:S(2)}) collective-permute-start(bf16[96,256]{1,0:T(8,128)(2,1)S(1)} %get-tuple-element.51), channel_id=1, source_target_pairs={{0,16},{4,20},{8,24},{12,28},{16,0},{20,4},{24,8},{28,12},{1,17},{... | collective-permute-start | bytes 147464 | tf_op jit(solution)/shard_map/ppermute | solution.py:296
  70.5 6.6 %collective-permute-start.17 = (bf16[96,256]{1,0:T(8,128)(2,1)S(1)}, bf16[96,256]{1,0:T(8,128)(2,1)S(1)}, u32[]{:S(2)}, u32[]{:S(2)}) collective-permute-start(bf16[96,256]{1,0:T(8,128)(2,1)S(1)} %get-tuple-element.52), channel_id=1, source_target_pairs={{0,24},{4,28},{8,16},{12,20},{16,8},{20,12},{24,0},{28,4},{1,25},{... | collective-permute-start | bytes 147464 | tf_op jit(solution)/shard_map/ppermute | solution.py:296
  71.2 6.0 %collective-permute-start.19 = (bf16[96,256]{1,0:T(8,128)(2,1)S(1)}, bf16[96,256]{1,0:T(8,128)(2,1)S(1)}, u32[]{:S(2)}, u32[]{:S(2)}) collective-permute-start(bf16[96,256]{1,0:T(8,128)(2,1)S(1)} %get-tuple-element.56), channel_id=1, source_target_pairs={{0,8},{4,12},{8,0},{12,4},{16,24},{20,28},{24,16},{28,20},{1,9},{5... | collective-permute-start | bytes 147464 | tf_op jit(solution)/shard_map/ppermute | solution.py:296
  72.3 7.0 %collective-permute-start.20 = (bf16[96,256]{1,0:T(8,128)(2,1)S(1)}, bf16[96,256]{1,0:T(8,128)(2,1)S(1)}, u32[]{:S(2)}, u32[]{:S(2)}) collective-permute-start(bf16[96,256]{1,0:T(8,128)(2,1)S(1)} %get-tuple-element.57), channel_id=1, source_target_pairs={{0,16},{4,20},{8,24},{12,28},{16,0},{20,4},{24,8},{28,12},{1,17},{... | collective-permute-start | bytes 147464 | tf_op jit(solution)/shard_map/ppermute | solution.py:296
  76.2 5.9 %collective-permute-start.21 = (bf16[96,256]{1,0:T(8,128)(2,1)S(1)}, bf16[96,256]{1,0:T(8,128)(2,1)S(1)}, u32[]{:S(2)}, u32[]{:S(2)}) collective-permute-start(bf16[96,256]{1,0:T(8,128)(2,1)S(1)} %get-tuple-element.58), channel_id=1, source_target_pairs={{0,24},{4,28},{8,16},{12,20},{16,8},{20,12},{24,0},{28,4},{1,25},{... | collective-permute-start | bytes 147464 | tf_op jit(solution)/shard_map/ppermute | solution.py:296
  (5 other events, 4.1 us)

commit v4 on v3

--- a/solution.py
+++ b/solution.py
@@ -35,6 +35,10 @@
     return lax.broadcasted_iota(jnp.int32, (SLOT_DEV, tokens), 0) == seg_row
 
 
+def place():
+    return lax.axis_index("ctx"), lax.axis_index("head")
+
+
 def lanes(start, size):
     return pl.ds(pl.multiple_of(start, HD), size)
 
@@ -50,10 +54,10 @@
         copy.wait()
 
 
-def pack_kernel(jobs, place_ref, *refs):
+def pack_kernel(jobs, *refs):
     outs = [out for _, dests in jobs for out in dests]
     sources, out_refs, sems = refs[:2], refs[-len(outs) - 1 : -1], refs[-1]
-    me = place_ref[1]
+    me = place()[1]
     copies = []
     done = 0
     for width, dests in jobs:
@@ -92,13 +96,23 @@
     )
 
 
-def merge_kernel(place_ref, seg_ref, own_ref, across_ref, core_ref, out, whole):
+def pack_kv_kernel(kv_heads, key_ref, value_ref, *outs):
+    me = place()[1]
+    width = kv_heads * HD
+    for m, out in enumerate(outs):
+        start = lax.bitwise_xor(me, m) * width
+        out[:, 0:width] = key_ref[:, lanes(start, width)]
+        out[:, width : 2 * width] = value_ref[:, lanes(start, width)]
+
+
+def merge_kernel(heads, seg_ref, *refs):
+    pieces, (out, hide_ref, whole) = refs[:heads], refs[-3:]
     kv_heads, tokens = seg_ref.shape
-    rows = own_ref.shape[0]
-    me = place_ref[1]
-    for m, (piece, half) in enumerate(((own_ref, 0), (core_ref, 0), (across_ref, 0), (core_ref, 1))):
+    rows = tokens // heads
+    me = place()[1]
+    for m, piece in enumerate(pieces):
         start = pl.multiple_of(lax.bitwise_xor(me, m) * rows, 16)
-        whole[pl.ds(start, rows), :] = piece[half * rows : (half + 1) * rows, :]
+        whole[pl.ds(start, rows), :] = piece[...]
     for g in range(kv_heads):
         picks = slot_picks(seg_ref[g : g + 1, :], tokens).astype(jnp.float32)
         counts = jnp.sum(picks, axis=1, keepdims=True)
@@ -110,70 +124,42 @@
             if part == 0:
                 rows_out = jnp.where(counts == 0.0, DEAD, rows_out)
             out[:, at] = rows_out.astype(jnp.bfloat16)
-
-
-def attend_kernel(
-    g, order, qo_at, place_ref, segcol_ref, q_ref, o_ref, kvo_ref, kva_ref, kvc_ref, *refs
-):
+        padded = -(-tokens // HD) * HD
+        place_in = lax.broadcasted_iota(jnp.int32, (HD, padded), 0)
+        seg = jnp.concatenate([seg_ref[g : g + 1, :]] * 2, axis=1)[:, :padded]
+        late = (place_in >= seg) & (place_in < SLOT_DEV)
+        hide = jnp.where(late, -HIDDEN, jnp.where(place_in == SLOT_DEV, 1.0, 0.0))
+        hide_ref[g] = hide.T[:tokens].astype(jnp.bfloat16)
+
+
+def attend_kernel(g, order, qo_at, q_ref, o_ref, hide_ref, *refs):
     shards = len(order)
     heads = 4
-    kv_pieces = ((kvo_ref, 0), (kvc_ref, 0), (kva_ref, 0), (kvc_ref, 1))
-    qo_pieces = [(refs[shards + i], half) for i, half in qo_at]
-    blocks, refs = refs[:shards], refs[-12:]
-    dq_ref, own_ref, near_ref, far_ref = refs[:4]
-    kx, vx, kt, qo_all, kv_own, qo_sems, kv_sems, block_sems = refs[4:]
+    kv_pieces, blocks, refs = refs[:heads], refs[heads : heads + shards], refs[heads + shards :]
+    qo_pieces = [(refs[i], half) for i, half in qo_at]
+    dq_ref, own_ref, near_ref, far_ref, kx, vx, kt, mine, sems = refs[-9:]
     rows = q_ref.shape[0]
-    kv_heads = kvo_ref.shape[1] // (2 * HD)
+    kv_heads = hide_ref.shape[0]
     slots = shards * SLOT_DEV
-    shard = place_ref[0]
-    me = place_ref[1]
+    shard, me = place()
     key_at = slice(g * HD, (g + 1) * HD)
     value_at = slice((kv_heads + g) * HD, (kv_heads + g + 1) * HD)
-
-    block_copies = []
-    for r, block in enumerate(blocks):
-        at = pl.ds(r * SLOT_DEV, SLOT_DEV)
-        block_copies.append(
-            pltpu.make_async_copy(block.at[:, key_at], kx.at[at, 0:HD], block_sems.at[2 * r])
-        )
-        block_copies.append(
-            pltpu.make_async_copy(block.at[:, value_at], vx.at[at, :], block_sems.at[2 * r + 1])
-        )
-    kv_copies = []
-    for m, (piece, half) in enumerate(kv_pieces):
-        for part, at in enumerate((key_at, value_at)):
-            kv_copies.append(
-                pltpu.make_async_copy(
-                    piece.at[half * rows : (half + 1) * rows, at],
-                    kv_own.at[m, part],
-                    kv_sems.at[2 * m + part],
-                )
+    start = (me * kv_heads + g) * GW
+    copies = run_copies(
+        [
+            pltpu.make_async_copy(
+                source.at[:, lanes(start, GW)], mine.at[:, part * GW : (part + 1) * GW], sems.at[part]
             )
-    start = (me * kv_heads + g) * GW
-    qo_copies = [
-        pltpu.make_async_copy(
-            source.at[:, lanes(start, GW)],
-            qo_all.at[0, :, part * GW : (part + 1) * GW],
-            qo_sems.at[part],
-        )
-        for part, source in enumerate((q_ref, o_ref))
-    ]
-    for m, (piece, half) in enumerate(qo_pieces):
-        qo_copies.append(
-            pltpu.make_async_copy(
-                piece.at[half * rows : (half + 1) * rows, :], qo_all.at[m + 1], qo_sems.at[m + 2]
-            )
-        )
-    run_copies(block_copies)
-    run_copies(kv_copies)
-    run_copies(qo_copies)
-    wait_copies(block_copies)
+            for part, source in enumerate((q_ref, o_ref))
+        ]
+    )
 
     lane = lax.broadcasted_iota(jnp.int32, (SLOT_DEV, HD), 1)
     row = lax.broadcasted_iota(jnp.int32, (SLOT_DEV, HD), 0)
-    for r, m in enumerate(order):
+    for r, (m, block) in enumerate(zip(order, blocks)):
         at = pl.ds(r * SLOT_DEV, SLOT_DEV)
-        key = kx[at, 0:HD].astype(jnp.float32)
+        key = block[:, key_at].astype(jnp.float32)
+        vx[at, :] = block[:, value_at]
         if m == 0:
             extra = jnp.where(lane == row, 1.0, 0.0)
         else:
@@ -185,28 +171,25 @@
     kt[...] = kx[0:slots, 0:HD].astype(jnp.float32).T.astype(jnp.bfloat16)
 
     width = GROUP * rows
-    qlane = lax.broadcasted_iota(jnp.int32, (rows, HD), 1)
     eye_row = lax.broadcasted_iota(jnp.int32, (rows, width), 0)
     eye_lane = lax.broadcasted_iota(jnp.int32, (rows, width), 1)
     eye = eye_row == lax.rem(eye_lane, rows)
     factor = SCALE * LOG2E
-    wait_copies(kv_copies)
-    wait_copies(qo_copies)
+    wait_copies(copies)
 
     dk = None
     dv = None
-    for m in range(heads):
+    for m, (qo, half) in enumerate([(mine, 0)] + qo_pieces):
+        span = slice(half * rows, (half + 1) * rows)
         at = pl.ds(pl.multiple_of(lax.bitwise_xor(me, m) * rows, 16), rows)
-        own_key = kv_own[m, 0]
+        own_key = kv_pieces[m][:, key_at]
         kx[slots : slots + rows, 0:HD] = own_key
-        vx[slots : slots + rows, :] = kv_own[m, 1]
-        late = (qlane >= segcol_ref[at, g : g + 1]) & (qlane < SLOT_DEV)
-        qe = jnp.where(late, -HIDDEN, jnp.where(qlane == SLOT_DEV, 1.0, 0.0)).astype(jnp.bfloat16)
-        q2 = jnp.concatenate([qo_all[m, :, h * HD : (h + 1) * HD] for h in range(GROUP)], axis=0)
+        vx[slots : slots + rows, :] = kv_pieces[m][:, value_at]
+        q2 = jnp.concatenate([qo[span, h * HD : (h + 1) * HD] for h in range(GROUP)], axis=0)
         o2 = jnp.concatenate(
-            [qo_all[m, :, GW + h * HD : GW + (h + 1) * HD] for h in range(GROUP)], axis=0
+            [qo[span, GW + h * HD : GW + (h + 1) * HD] for h in range(GROUP)], axis=0
         )
-        qx = jnp.concatenate([q2, jnp.concatenate([qe] * GROUP, axis=0)], axis=1)
+        qx = jnp.concatenate([q2, jnp.concatenate([hide_ref[g, at, :]] * GROUP, axis=0)], axis=1)
         scores = nt(kx[...], qx)
         own_score = jnp.sum(jnp.where(eye, scores[slots:], 0.0), axis=0, keepdims=True)
         scores = scores[:slots]
@@ -272,16 +255,8 @@
     return [pl.BlockSpec(memory_space=pltpu.VMEM)] * count
 
 
-def in_smem():
-    return [pl.BlockSpec(memory_space=pltpu.SMEM)]
-
-
 def anywhere(count):
     return [pl.BlockSpec(memory_space=pl.ANY)] * count
-
-
-def in_hbm(count):
-    return [pl.BlockSpec(memory_space=pltpu.HBM)] * count
 
 
 def params(mib):
@@ -320,7 +295,7 @@
         compiler_params=params(2),
         name="join",
     )(core, from_across, *after)
-    return from_across, swap(both, "head", heads, 1), both
+    return from_across, swap(both, "head", heads, 1)
 
 
 def local(queries, keys, values, segment_ids, grad_out):
@@ -329,7 +304,6 @@
     tokens = rows * heads
     kv_heads = KVH // heads
     shards = lax.axis_size("ctx")
-    place = jnp.stack([lax.axis_index("ctx"), lax.axis_index("head")]).astype(jnp.int32)
     order = list(range(0, shards, 2)) + list(range(1, shards, 2))
     half = SLOT_DEV * shards // 2
     slots = SLOT_DEV * shards
@@ -348,35 +322,39 @@
             out_shape=[
                 shape(len(pieces) * rows, 2 * width) for width, dests in jobs for pieces in dests
             ],
-            in_specs=in_smem() + anywhere(2 + len(after)),
+            in_specs=anywhere(2 + len(after)),
             out_specs=anywhere(len(outs)),
             scratch_shapes=[
                 pltpu.SemaphoreType.DMA((2 * sum(len(p) for _, dests in jobs for p in dests),))
             ],
             compiler_params=params(mib),
             name=name,
-        )(place, *sources, *after)
-
-    kv_across, kv_core, kv_own = pack(
-        [(kv_width, [[kv_at(2), kv_at(3)], [kv_at(1)], [kv_at(0)]])], (keys, values), (), 56, "pack_kv"
-    )
-    from_across, from_core, both = exchange(kv_across, kv_core, heads)
-    kv = (kv_own, from_across, from_core)
+        )(*sources, *after)
+
+    kv_out = pl.pallas_call(
+        functools.partial(pack_kv_kernel, kv_heads),
+        out_shape=[shape(rows, 2 * kv_width)] * heads,
+        in_specs=in_vmem(2),
+        out_specs=in_vmem(heads),
+        compiler_params=params(2),
+        name="pack_kv",
+    )(keys, values)
+    kv = [kv_out[0]] + [swap(kv_out[m], "head", heads, m) for m in range(1, heads)]
 
     jobs = [(GW, [[qo_at(2, 0), qo_at(3, 0)], [qo_at(1, 0)]])]
     for g in range(1, kv_heads):
         jobs.append((GW, [[qo_at(m, g)] for m in range(1, heads)]))
-    packed = pack(jobs, (queries, grad_out), (both,), 4, "pack_qo")
-
-    merged = pl.pallas_call(
-        merge_kernel,
-        out_shape=shape(SLOT_DEV, 2 * kv_width),
-        in_specs=in_smem() + in_vmem(4),
-        out_specs=in_vmem(1)[0],
+    packed = pack(jobs, (queries, grad_out), kv_out[:1], 4, "pack_qo")
+
+    merged, hide = pl.pallas_call(
+        functools.partial(merge_kernel, heads),
+        out_shape=[shape(SLOT_DEV, 2 * kv_width), shape(kv_heads, tokens, HD)],
+        in_specs=in_vmem(1 + heads) + anywhere(1),
+        out_specs=in_vmem(2),
         scratch_shapes=[pltpu.VMEM((tokens, 2 * kv_width), jnp.bfloat16)],
         compiler_params=params(4),
         name="merge",
-    )(place, segment_ids, *kv)
+    )(segment_ids, *kv, packed[1])
 
     held = {0: merged}
     for m in range(2, shards, 2):
@@ -385,7 +363,9 @@
         held[m + 1] = swap(held[m], "ctx", shards, 1)
 
     late = [held[m] for m in range(1, shards - 1)]
-    qo = [exchange(*packed[:2], heads, lambda: late)[:2]]
+    soon = [held[m] for m in range(1, shards) if m % 2 == 0 or m in (1, shards // 2 + 1)]
+    qo_across = gate(packed[:1], kv[1:])[0]
+    qo = [exchange(qo_across, packed[1], heads, lambda: soon)]
     qo_places = [((1, 0), (0, 0), (1, 1))]
     for g in range(1, kv_heads):
         pieces = packed[2 + (g - 1) * (heads - 1) : 2 + g * (heads - 1)]
@@ -393,7 +373,6 @@
         qo.append([swap(piece, "head", heads, m + 1) for m, piece in enumerate(pieces)])
         qo_places.append(((0, 0), (1, 0), (2, 0)))
 
-    seg_col = segment_ids.T
     dq = []
     own = []
     near = []
@@ -407,17 +386,14 @@
                 shape(half, 2 * HD, dtype=jnp.float32),
                 shape(half, 2 * HD),
             ],
-            in_specs=in_smem() + in_vmem(1) + in_hbm(2) + anywhere(3 + shards + len(qo[g]) + (g > 0)),
+            in_specs=anywhere(2) + in_vmem(1 + heads + shards + len(qo[g])) + anywhere(g > 0),
             out_specs=in_vmem(4),
             scratch_shapes=[
                 pltpu.VMEM((slots + rows, 2 * HD), jnp.bfloat16),
                 pltpu.VMEM((slots + rows, HD), jnp.bfloat16),
                 pltpu.VMEM((HD, slots), jnp.bfloat16),
-                pltpu.VMEM((heads, rows, 2 * GW), jnp.bfloat16),
-                pltpu.VMEM((heads, 2, rows, HD), jnp.bfloat16),
-                pltpu.SemaphoreType.DMA((heads + 1,)),
-                pltpu.SemaphoreType.DMA((2 * heads,)),
-                pltpu.SemaphoreType.DMA((2 * shards,)),
+                pltpu.VMEM((rows, 2 * GW), jnp.bfloat16),
+                pltpu.SemaphoreType.DMA((2,)),
             ],
             compiler_params=params(24),
             cost_estimate=pl.CostEstimate(
@@ -426,7 +402,7 @@
                 transcendentals=tokens * GROUP * slots,
             ),
             name="attend",
-        )(place, seg_col, queries, grad_out, *kv, *[held[m] for m in order], *qo[g], *own[-1:])
+        )(queries, grad_out, hide, *kv, *[held[m] for m in order], *qo[g], *own[-1:])
         dq.append(outs[0])
         own.append(outs[1])
         near.append(outs[2])

time: 83.6 us -> 67.2 us (0.80)
  Pallas kernels: 27.4 us -> 14.1 us
  local copies, waits for them, and re-layouts: 6.46 us -> 4.06 us
  starting transfers between devices: 28 us -> 30 us
  waiting for transfers between devices: 18.8 us -> 17.1 us
    pallas_call x2 -> x1, Pallas kernels: 9.34 us -> 0.38 us  [pack(): pl.pallas_call(functools.partial(pack_kernel, jobs), out_shape=[shape(len...]
    pallas_call x2, Pallas kernels: 15.6 us -> 11.8 us  [local(): pl.pallas_call(functools.partial(attend_kernel, g, order, qo_places[g]),...]
    unnamed x31 -> x14, local copies, waits for them, and re-layouts: 6.46 us -> 4.06 us
    ppermute x22 -> x23, starting transfers between devices: 28 us -> 30 us  [swap(): return lax.ppermute(x, axis, [(i, i ^ m) for i in range(size)])]
    ppermute x22 -> x23, waiting for transfers between devices: 18.8 us -> 17.1 us  [swap(): return lax.ppermute(x, axis, [(i, i ^ m) for i in range(size)])]
  transfers between devices with their start and end apart: 22 -> 23, of which waited for: 10 -> 8; matrix products, arithmetic and copies ran while one was open for 1% -> 1% of each run, Pallas kernels for 20% -> 19%
where the time goes in v4:
time: 67.2 us; the launch traced here: 67 us
  starting transfers between devices  30 us (45%)
  waiting for transfers between devices  17.1 us (25%)
  Pallas kernels  14.1 us (21%)
  local copies, waits for them, and re-layouts  4.06 us (6%)
  other arithmetic  0.94 us (1%)
  between operations  0.77 us (1%)
    ppermute x23, starting transfers between devices, swap(): return lax.ppermute(x, axis, [(i, i ^ m) for i in range(size)])  30 us
    ppermute x23, waiting for transfers between devices, swap(): return lax.ppermute(x, axis, [(i, i ^ m) for i in range(size)])  17.1 us
    pallas_call x2, Pallas kernels, local(): pl.pallas_call(functools.partial(attend_kernel, g, order, qo_places[g]),...  11.8 us
    unnamed x14, local copies, waits for them, and re-layouts  4.06 us
  transfers between devices with their start and end apart: 23, of which 8 were waited for; matrix products, arithmetic and copies ran while one was open for 1% of the time, Pallas kernels for 19%

profile of v4, /device:TPU:0, one launch (start us, length us, event | category | flops | bytes accessed | tf_op | source)
XLA Modules:
  0.0 67.0 jit_solution(15777795648020348326)
XLA Ops:
  0.6 0.9 %copy-done.4 = bf16[48,1024]{1,0:T(8,128)(2,1)S(1)} copy-done((bf16[48,1024]{1,0:T(8,128)(2,1)S(1)}, bf16[48,1024]{1,0:T(8,128)(2,1)}, u32[]{:S(2)}) %copy-start.4) | copy-done | bytes 98328
  1.5 0.9 %copy-done.5 = bf16[48,1024]{1,0:T(8,128)(2,1)S(1)} copy-done((bf16[48,1024]{1,0:T(8,128)(2,1)S(1)}, bf16[48,1024]{1,0:T(8,128)(2,1)}, u32[]{:S(2)}) %copy-start.5) | copy-done | bytes 98328
  2.4 0.5 collective-permute-start
  3.0 2.6 %collective-permute-start.1 = (bf16[48,512]{1,0:T(8,128)(2,1)S(1)}, bf16[48,512]{1,0:T(8,128)(2,1)S(1)}, u32[]{:S(2)}, u32[]{:S(2)}) collective-permute-start(bf16[48,512]{1,0:T(8,128)(2,1)S(1)} %get-tuple-element.37), channel_id=1, source_target_pairs={{0,2},{1,3},{2,0},{3,1},{4,6},{5,7},{6,4},{7,5},{8,10},{9,11},{10,... | collective-permute-start | bytes 147464 | tf_op jit(solution)/shard_map/ppermute | solution.py:271
  5.6 1.1 %copy-done = bf16[48,8192]{1,0:T(8,128)(2,1)S(1)} copy-done((bf16[48,8192]{1,0:T(8,128)(2,1)S(1)}, bf16[48,8192]{1,0:T(8,128)(2,1)}, u32[]{:S(2)}) %copy-start) | copy-done | bytes 786456
  6.7 1.1 %copy-done.2 = bf16[48,8192]{1,0:T(8,128)(2,1)S(1)} copy-done((bf16[48,8192]{1,0:T(8,128)(2,1)S(1)}, bf16[48,8192]{1,0:T(8,128)(2,1)}, u32[]{:S(2)}) %copy-start.2) | copy-done | bytes 786456
  8.3 0.9 %collective-permute-done.2.refs_3_ = bf16[48,512]{1,0:T(8,128)(2,1)S(1)} collective-permute-done((bf16[48,512]{1,0:T(8,128)(2,1)S(1)}, bf16[48,512]{1,0:T(8,128)(2,1)S(1)}, u32[]{:S(2)}, u32[]{:S(2)}) %collective-permute-start.2) | collective-permute-done | bytes 49184 | tf_op jit(solution)/shard_map/ppermute | solution.py:271
  9.2 1.0 %collective-permute-start.10 = (bf16[96,2048]{1,0:T(8,128)(2,1)S(1)}, bf16[96,2048]{1,0:T(8,128)(2,1)S(1)}, u32[]{:S(2)}, u32[]{:S(2)}) collective-permute-start(bf16[96,2048]{1,0:T(8,128)(2,1)S(1)} %gate.2), channel_id=1, source_target_pairs={{0,2},{1,3},{2,0},{3,1},{4,6},{5,7},{6,4},{7,5},{8,10},{9,11},{10,... | collective-permute-start | bytes 1179656 | tf_op jit(solution)/shard_map/ppermute | solution.py:271
  10.5 2.6 %collective-permute-start.4 = (bf16[96,512]{1,0:T(8,128)(2,1)S(1)}, bf16[96,512]{1,0:T(8,128)(2,1)S(1)}, u32[]{:S(2)}, u32[]{:S(2)}) collective-permute-start(bf16[96,512]{1,0:T(8,128)(2,1)S(1)} %get-tuple-element.41.refs_4_), channel_id=1, source_target_pairs={{0,16},{4,20},{8,24},{12,28},{16,0},{20,4},{24,8},{28,12},{1,17},{... | collective-permute-start | bytes 294920 | tf_op jit(solution)/shard_map/ppermute | solution.py:271
  13.1 1.5 %collective-permute-start.6 = (bf16[96,512]{1,0:T(8,128)(2,1)S(1)}, bf16[96,512]{1,0:T(8,128)(2,1)S(1)}, u32[]{:S(2)}, u32[]{:S(2)}) collective-permute-start(bf16[96,512]{1,0:T(8,128)(2,1)S(1)} %get-tuple-element.41.refs_4_), channel_id=1, source_target_pairs={{0,4},{4,0},{8,12},{12,8},{16,20},{20,16},{24,28},{28,24},{1,5},{5... | collective-permute-start | bytes 294920 | tf_op jit(solution)/shard_map/ppermute | solution.py:271
  14.6 1.3 %collective-permute-start.5 = (bf16[96,512]{1,0:T(8,128)(2,1)S(1)}, bf16[96,512]{1,0:T(8,128)(2,1)S(1)}, u32[]{:S(2)}, u32[]{:S(2)}) collective-permute-start(bf16[96,512]{1,0:T(8,128)(2,1)S(1)} %get-tuple-element.41.refs_4_), channel_id=1, source_target_pairs={{0,24},{4,28},{8,16},{12,20},{16,8},{20,12},{24,0},{28,4},{1,25},{... | collective-permute-start | bytes 294920 | tf_op jit(solution)/shard_map/ppermute | solution.py:271
  16.2 3.5 %collective-permute-done.4.refs_2_.refs_6_ = bf16[96,512]{1,0:T(8,128)(2,1)S(1)} collective-permute-done((bf16[96,512]{1,0:T(8,128)(2,1)S(1)}, bf16[96,512]{1,0:T(8,128)(2,1)S(1)}, u32[]{:S(2)}, u32[]{:S(2)}) %collective-permute-start.4) | collective-permute-done | bytes 98336 | tf_op jit(solution)/shard_map/ppermute | solution.py:271
  19.8 3.1 %collective-permute-start.8 = (bf16[96,512]{1,0:T(8,128)(2,1)S(1)}, bf16[96,512]{1,0:T(8,128)(2,1)S(1)}, u32[]{:S(2)}, u32[]{:S(2)}) collective-permute-start(bf16[96,512]{1,0:T(8,128)(2,1)S(1)} %collective-permute-done.4.refs_2_.refs_6_), channel_id=1, source_target_pairs={{0,4},{4,0},{8,12},{12,8},{16,20},{20,16},{24,28},{28,24},{1,5},{5... | collective-permute-start | bytes 294920 | tf_op jit(solution)/shard_map/ppermute | solution.py:271
  22.8 2.6 %collective-permute-done.8.refs_3_.refs_10_.refs_7_ = bf16[96,512]{1,0:T(8,128)(2,1)S(1)} collective-permute-done((bf16[96,512]{1,0:T(8,128)(2,1)S(1)}, bf16[96,512]{1,0:T(8,128)(2,1)S(1)}, u32[]{:S(2)}, u32[]{:S(2)}) %collective-permute-start.8) | collective-permute-done | bytes 98336 | tf_op jit(solution)/shard_map/ppermute | solution.py:271
  26.0 2.1 %collective-permute-start.7 = (bf16[96,512]{1,0:T(8,128)(2,1)S(1)}, bf16[96,512]{1,0:T(8,128)(2,1)S(1)}, u32[]{:S(2)}, u32[]{:S(2)}) collective-permute-start(bf16[96,512]{1,0:T(8,128)(2,1)S(1)} %collective-permute-done.3.refs_1_.refs_5_.refs_4_), channel_id=1, source_target_pairs={{0,4},{4,0},{8,12},{12,8},{16,20},{20,16},{24,28},{28,24},{1,5},{5... | collective-permute-start | bytes 294920 | tf_op jit(solution)/shard_map/ppermute | solution.py:271
  28.2 3.6 %collective-permute-done.7.refs_9_.refs_5_ = bf16[96,512]{1,0:T(8,128)(2,1)S(1)} collective-permute-done((bf16[96,512]{1,0:T(8,128)(2,1)S(1)}, bf16[96,512]{1,0:T(8,128)(2,1)S(1)}, u32[]{:S(2)}, u32[]{:S(2)}) %collective-permute-start.7) | collective-permute-done | bytes 98336 | tf_op jit(solution)/shard_map/ppermute | solution.py:271
  31.8 1.0 %collective-permute-start.13 = (bf16[48,2048]{1,0:T(8,128)(2,1)S(1)}, bf16[48,2048]{1,0:T(8,128)(2,1)S(1)}, u32[]{:S(2)}, u32[]{:S(2)}) collective-permute-start(bf16[48,2048]{1,0:T(8,128)(2,1)S(1)} %get-tuple-element.48), channel_id=1, source_target_pairs={{0,2},{1,3},{2,0},{3,1},{4,6},{5,7},{6,4},{7,5},{8,10},{9,11},{10,... | collective-permute-start | bytes 589832 | tf_op jit(solution)/shard_map/ppermute | solution.py:271
  32.8 0.9 %collective-permute-start.14 = (bf16[48,2048]{1,0:T(8,128)(2,1)S(1)}, bf16[48,2048]{1,0:T(8,128)(2,1)S(1)}, u32[]{:S(2)}, u32[]{:S(2)}) collective-permute-start(bf16[48,2048]{1,0:T(8,128)(2,1)S(1)} %get-tuple-element.49), channel_id=1, source_target_pairs={{0,3},{1,2},{2,1},{3,0},{4,7},{5,6},{6,5},{7,4},{8,11},{9,10},{10,... | collective-permute-start | bytes 589832 | tf_op jit(solution)/shard_map/ppermute | solution.py:271
  33.7 5.8 %attend.2 = (bf16[192,1024]{1,0:T(8,128)(2,1)S(1)}, f32[192,256]{1,0:T(8,128)S(1)}, f32[384,256]{1,0:T(8,128)S(1)}, bf16[384,256]{1,0:T(8,128)(2,1)S(1)}) custom-call(bf16[48,8192]{1,0:T(8,128)(2,1)S(1)} %copy-done.1, bf16[48,8192]{1,0:T(8,128)(2,1)S(1)} %copy-done.3, bf16[2,192,128]{2,1,0:T(8,128)(2,1)S(1)} %get-tuple-element.40.hide_ref, ...), custom_call_target="tpu_custom_call" | custom-call | flops 1604321280 | bytes 4194304 | tf_op jit(solution)/shard_map/attend/pallas_call | solution.py:381
  39.5 2.0 %collective-permute-start.15 = (bf16[384,256]{1,0:T(8,128)(2,1)S(1)}, bf16[384,256]{1,0:T(8,128)(2,1)S(1)}, u32[]{:S(2)}, u32[]{:S(2)}) collective-permute-start(bf16[384,256]{1,0:T(8,128)(2,1)S(1)} %get-tuple-element.53), channel_id=1, source_target_pairs={{0,4},{4,0},{8,12},{12,8},{16,20},{20,16},{24,28},{28,24},{1,5},{5... | collective-permute-start | bytes 589832 | tf_op jit(solution)/shard_map/ppermute | solution.py:271
  41.5 1.4 %collective-permute-done.14.refs_14_ = bf16[48,2048]{1,0:T(8,128)(2,1)S(1)} collective-permute-done((bf16[48,2048]{1,0:T(8,128)(2,1)S(1)}, bf16[48,2048]{1,0:T(8,128)(2,1)S(1)}, u32[]{:S(2)}, u32[]{:S(2)}) %collective-permute-start.14) | collective-permute-done | bytes 196640 | tf_op jit(solution)/shard_map/ppermute | solution.py:271
  42.9 6.0 %attend.3 = (bf16[192,1024]{1,0:T(8,128)(2,1)S(1)}, f32[192,256]{1,0:T(8,128)S(1)}, f32[384,256]{1,0:T(8,128)S(1)}, bf16[384,256]{1,0:T(8,128)(2,1)S(1)}) custom-call(bf16[48,8192]{1,0:T(8,128)(2,1)S(1)} %copy-done.1, bf16[48,8192]{1,0:T(8,128)(2,1)S(1)} %copy-done.3, bf16[2,192,128]{2,1,0:T(8,128)(2,1)S(1)} %get-tuple-element.40.hide_ref, ...), custom_call_target="tpu_custom_call" | custom-call | flops 1604321280 | bytes 4194304 | tf_op jit(solution)/shard_map/attend/pallas_call | solution.py:381
  48.9 2.0 %collective-permute-start.19 = (bf16[384,256]{1,0:T(8,128)(2,1)S(1)}, bf16[384,256]{1,0:T(8,128)(2,1)S(1)}, u32[]{:S(2)}, u32[]{:S(2)}) collective-permute-start(bf16[384,256]{1,0:T(8,128)(2,1)S(1)} %get-tuple-element.60), channel_id=1, source_target_pairs={{0,4},{4,0},{8,12},{12,8},{16,20},{20,16},{24,28},{28,24},{1,5},{5... | collective-permute-start | bytes 589832 | tf_op jit(solution)/shard_map/ppermute | solution.py:271
  51.1 3.2 %collective-permute-start.17 = (bf16[96,256]{1,0:T(8,128)(2,1)S(1)}, bf16[96,256]{1,0:T(8,128)(2,1)S(1)}, u32[]{:S(2)}, u32[]{:S(2)}) collective-permute-start(bf16[96,256]{1,0:T(8,128)(2,1)S(1)} %get-tuple-element.57), channel_id=1, source_target_pairs={{0,16},{4,20},{8,24},{12,28},{16,0},{20,4},{24,8},{28,12},{1,17},{... | collective-permute-start | bytes 147464 | tf_op jit(solution)/shard_map/ppermute | solution.py:271
  54.3 1.2 %collective-permute-start.18 = (bf16[96,256]{1,0:T(8,128)(2,1)S(1)}, bf16[96,256]{1,0:T(8,128)(2,1)S(1)}, u32[]{:S(2)}, u32[]{:S(2)}) collective-permute-start(bf16[96,256]{1,0:T(8,128)(2,1)S(1)} %get-tuple-element.58), channel_id=1, source_target_pairs={{0,24},{4,28},{8,16},{12,20},{16,8},{20,12},{24,0},{28,4},{1,25},{... | collective-permute-start | bytes 147464 | tf_op jit(solution)/shard_map/ppermute | solution.py:271
  55.4 1.1 %collective-permute-done.19.far_ref = bf16[384,256]{1,0:T(8,128)(2,1)S(1)} collective-permute-done((bf16[384,256]{1,0:T(8,128)(2,1)S(1)}, bf16[384,256]{1,0:T(8,128)(2,1)S(1)}, u32[]{:S(2)}, u32[]{:S(2)}) %collective-permute-start.19) | collective-permute-done | bytes 196640 | tf_op jit(solution)/shard_map/ppermute | solution.py:271
  56.7 3.4 %collective-permute-start.21 = (bf16[96,256]{1,0:T(8,128)(2,1)S(1)}, bf16[96,256]{1,0:T(8,128)(2,1)S(1)}, u32[]{:S(2)}, u32[]{:S(2)}) collective-permute-start(bf16[96,256]{1,0:T(8,128)(2,1)S(1)} %get-tuple-element.63), channel_id=1, source_target_pairs={{0,16},{4,20},{8,24},{12,28},{16,0},{20,4},{24,8},{28,12},{1,17},{... | collective-permute-start | bytes 147464 | tf_op jit(solution)/shard_map/ppermute | solution.py:271
  60.1 0.9 %collective-permute-start.22 = (bf16[96,256]{1,0:T(8,128)(2,1)S(1)}, bf16[96,256]{1,0:T(8,128)(2,1)S(1)}, u32[]{:S(2)}, u32[]{:S(2)}) collective-permute-start(bf16[96,256]{1,0:T(8,128)(2,1)S(1)} %get-tuple-element.64), channel_id=1, source_target_pairs={{0,24},{4,28},{8,16},{12,20},{16,8},{20,12},{24,0},{28,4},{1,25},{... | collective-permute-start | bytes 147464 | tf_op jit(solution)/shard_map/ppermute | solution.py:271
  61.0 0.9 %pad_maximum_fusion = bf16[192,2048]{1,0:T(8,128)(2,1)} fusion(bf16[192,1024]{1,0:T(8,128)(2,1)S(1)} %get-tuple-element.51, bf16[192,1024]{1,0:T(8,128)(2,1)S(1)} %get-tuple-element.43), kind=kLoop, calls=%fused_computation | loop fusion | flops 1572864 | bytes 1572864 | tf_op jit(solution)/shard_map/concatenate | solution.py:435
  62.0 1.5 %collective-permute-done.21.refs_7_ = bf16[96,256]{1,0:T(8,128)(2,1)S(1)} collective-permute-done((bf16[96,256]{1,0:T(8,128)(2,1)S(1)}, bf16[96,256]{1,0:T(8,128)(2,1)S(1)}, u32[]{:S(2)}, u32[]{:S(2)}) %collective-permute-start.21) | collective-permute-done | bytes 49184 | tf_op jit(solution)/shard_map/ppermute | solution.py:271
  63.5 2.5 %collective-permute-done.22.refs_8_ = bf16[96,256]{1,0:T(8,128)(2,1)S(1)} collective-permute-done((bf16[96,256]{1,0:T(8,128)(2,1)S(1)}, bf16[96,256]{1,0:T(8,128)(2,1)S(1)}, u32[]{:S(2)}, u32[]{:S(2)}) %collective-permute-start.22) | collective-permute-done | bytes 49184 | tf_op jit(solution)/shard_map/ppermute | solution.py:271
  66.0 1.0 %spread.1 = (bf16[192,256]{1,0:T(8,128)(2,1)}, bf16[192,256]{1,0:T(8,128)(2,1)}) custom-call(s32[2,192]{1,0:T(2,128)S(1)} %copy-done.6, f32[96,256]{1,0:T(8,128)S(1)} %get-tuple-element.55.refs_0_, bf16[96,256]{1,0:T(8,128)(2,1)S(1)} %collective-permute-done.16.refs_1_, bf16[96,256]{1,0:T(8,128)(2,1)S(1)} %collective-permute-done.17.refs_2_, ...), custom_call_target="tpu_custom_call" | custom-call | tf_op jit(solution)/shard_map/spread/pallas_call | solution.py:427
  (40 shorter events, 2.0 us)
Async XLA Ops:
  0.6 0.9 %copy-start.4 = (bf16[48,1024]{1,0:T(8,128)(2,1)S(1)}, bf16[48,1024]{1,0:T(8,128)(2,1)}, u32[]{:S(2)}) copy-start(bf16[48,1024]{1,0:T(8,128)(2,1)} %key_ref.1) | copy-start | bytes 294916
  1.5 0.9 %copy-start.5 = (bf16[48,1024]{1,0:T(8,128)(2,1)S(1)}, bf16[48,1024]{1,0:T(8,128)(2,1)}, u32[]{:S(2)}) copy-start(bf16[48,1024]{1,0:T(8,128)(2,1)} %value_ref.1) | copy-start | bytes 294916
  2.4 5.8 %collective-permute-start = (bf16[48,512]{1,0:T(8,128)(2,1)S(1)}, bf16[48,512]{1,0:T(8,128)(2,1)S(1)}, u32[]{:S(2)}, u32[]{:S(2)}) collective-permute-start(bf16[48,512]{1,0:T(8,128)(2,1)S(1)} %get-tuple-element.36), channel_id=1, source_target_pairs={{0,1},{1,0},{2,3},{3,2},{4,5},{5,4},{6,7},{7,6},{8,9},{9,8},{10,11... | collective-permute-start | bytes 147464 | tf_op jit(solution)/shard_map/ppermute | solution.py:271
  3.0 5.3 %collective-permute-start.1 = (bf16[48,512]{1,0:T(8,128)(2,1)S(1)}, bf16[48,512]{1,0:T(8,128)(2,1)S(1)}, u32[]{:S(2)}, u32[]{:S(2)}) collective-permute-start(bf16[48,512]{1,0:T(8,128)(2,1)S(1)} %get-tuple-element.37), channel_id=1, source_target_pairs={{0,2},{1,3},{2,0},{3,1},{4,6},{5,7},{6,4},{7,5},{8,10},{9,11},{10,... | collective-permute-start | bytes 147464 | tf_op jit(solution)/shard_map/ppermute | solution.py:271
  5.5 3.7 %collective-permute-start.2 = (bf16[48,512]{1,0:T(8,128)(2,1)S(1)}, bf16[48,512]{1,0:T(8,128)(2,1)S(1)}, u32[]{:S(2)}, u32[]{:S(2)}) collective-permute-start(bf16[48,512]{1,0:T(8,128)(2,1)S(1)} %get-tuple-element.38), channel_id=1, source_target_pairs={{0,3},{1,2},{2,1},{3,0},{4,7},{5,6},{6,5},{7,4},{8,11},{9,10},{10,... | collective-permute-start | bytes 147464 | tf_op jit(solution)/shard_map/ppermute | solution.py:271
  5.6 1.1 %copy-start = (bf16[48,8192]{1,0:T(8,128)(2,1)S(1)}, bf16[48,8192]{1,0:T(8,128)(2,1)}, u32[]{:S(2)}) copy-start(bf16[48,8192]{1,0:T(8,128)(2,1)} %q_ref.3) | copy-start | bytes 2359300
  6.7 1.1 %copy-start.2 = (bf16[48,8192]{1,0:T(8,128)(2,1)S(1)}, bf16[48,8192]{1,0:T(8,128)(2,1)}, u32[]{:S(2)}) copy-start(bf16[48,8192]{1,0:T(8,128)(2,1)} %o_ref.3) | copy-start | bytes 2359300
  8.3 2.0 %copy-start.6 = (s32[2,192]{1,0:T(2,128)S(1)}, s32[2,192]{1,0:T(2,128)}, u32[]{:S(2)}) copy-start(s32[2,192]{1,0:T(2,128)} %seg_ref.3) | copy-start | bytes 4612
  9.2 16.2 %collective-permute-start.10 = (bf16[96,2048]{1,0:T(8,128)(2,1)S(1)}, bf16[96,2048]{1,0:T(8,128)(2,1)S(1)}, u32[]{:S(2)}, u32[]{:S(2)}) collective-permute-start(bf16[96,2048]{1,0:T(8,128)(2,1)S(1)} %gate.2), channel_id=1, source_target_pairs={{0,2},{1,3},{2,0},{3,1},{4,6},{5,7},{6,4},{7,5},{8,10},{9,11},{10,... | collective-permute-start | bytes 1179656 | tf_op jit(solution)/shard_map/ppermute | solution.py:271
  10.5 9.3 %collective-permute-start.4 = (bf16[96,512]{1,0:T(8,128)(2,1)S(1)}, bf16[96,512]{1,0:T(8,128)(2,1)S(1)}, u32[]{:S(2)}, u32[]{:S(2)}) collective-permute-start(bf16[96,512]{1,0:T(8,128)(2,1)S(1)} %get-tuple-element.41.refs_4_), channel_id=1, source_target_pairs={{0,16},{4,20},{8,24},{12,28},{16,0},{20,4},{24,8},{28,12},{1,17},{... | collective-permute-start | bytes 294920 | tf_op jit(solution)/shard_map/ppermute | solution.py:271
  13.1 9.7 %collective-permute-start.6 = (bf16[96,512]{1,0:T(8,128)(2,1)S(1)}, bf16[96,512]{1,0:T(8,128)(2,1)S(1)}, u32[]{:S(2)}, u32[]{:S(2)}) collective-permute-start(bf16[96,512]{1,0:T(8,128)(2,1)S(1)} %get-tuple-element.41.refs_4_), channel_id=1, source_target_pairs={{0,4},{4,0},{8,12},{12,8},{16,20},{20,16},{24,28},{28,24},{1,5},{5... | collective-permute-start | bytes 294920 | tf_op jit(solution)/shard_map/ppermute | solution.py:271
  14.6 8.2 %collective-permute-start.5 = (bf16[96,512]{1,0:T(8,128)(2,1)S(1)}, bf16[96,512]{1,0:T(8,128)(2,1)S(1)}, u32[]{:S(2)}, u32[]{:S(2)}) collective-permute-start(bf16[96,512]{1,0:T(8,128)(2,1)S(1)} %get-tuple-element.41.refs_4_), channel_id=1, source_target_pairs={{0,24},{4,28},{8,16},{12,20},{16,8},{20,12},{24,0},{28,4},{1,25},{... | collective-permute-start | bytes 294920 | tf_op jit(solution)/shard_map/ppermute | solution.py:271
  16.0 6.8 %collective-permute-start.3 = (bf16[96,512]{1,0:T(8,128)(2,1)S(1)}, bf16[96,512]{1,0:T(8,128)(2,1)S(1)}, u32[]{:S(2)}, u32[]{:S(2)}) collective-permute-start(bf16[96,512]{1,0:T(8,128)(2,1)S(1)} %get-tuple-element.41.refs_4_), channel_id=1, source_target_pairs={{0,8},{4,12},{8,0},{12,4},{16,24},{20,28},{24,16},{28,20},{1,9},{5... | collective-permute-start | bytes 294920 | tf_op jit(solution)/shard_map/ppermute | solution.py:271
  19.8 5.7 %collective-permute-start.8 = (bf16[96,512]{1,0:T(8,128)(2,1)S(1)}, bf16[96,512]{1,0:T(8,128)(2,1)S(1)}, u32[]{:S(2)}, u32[]{:S(2)}) collective-permute-start(bf16[96,512]{1,0:T(8,128)(2,1)S(1)} %collective-permute-done.4.refs_2_.refs_6_), channel_id=1, source_target_pairs={{0,4},{4,0},{8,12},{12,8},{16,20},{20,16},{24,28},{28,24},{1,5},{5... | collective-permute-start | bytes 294920 | tf_op jit(solution)/shard_map/ppermute | solution.py:271
  25.4 8.2 %copy-start.3 = (bf16[48,8192]{1,0:T(8,128)(2,1)S(1)}, bf16[48,8192]{1,0:T(8,128)(2,1)}, u32[]{:S(2)}) copy-start(bf16[48,8192]{1,0:T(8,128)(2,1)} %o_ref.3) | copy-start | bytes 2359300
  26.0 7.7 %copy-start.1 = (bf16[48,8192]{1,0:T(8,128)(2,1)S(1)}, bf16[48,8192]{1,0:T(8,128)(2,1)}, u32[]{:S(2)}) copy-start(bf16[48,8192]{1,0:T(8,128)(2,1)} %q_ref.3) | copy-start | bytes 2359300
  26.0 7.7 %collective-permute-start.11 = (bf16[96,2048]{1,0:T(8,128)(2,1)S(1)}, bf16[96,2048]{1,0:T(8,128)(2,1)S(1)}, u32[]{:S(2)}, u32[]{:S(2)}) collective-permute-start(bf16[96,2048]{1,0:T(8,128)(2,1)S(1)} %join.1), channel_id=1, source_target_pairs={{0,1},{1,0},{2,3},{3,2},{4,5},{5,4},{6,7},{7,6},{8,9},{9,8},{10,11... | collective-permute-start | bytes 1179656 | tf_op jit(solution)/shard_map/ppermute | solution.py:271
  26.0 5.7 %collective-permute-start.7 = (bf16[96,512]{1,0:T(8,128)(2,1)S(1)}, bf16[96,512]{1,0:T(8,128)(2,1)S(1)}, u32[]{:S(2)}, u32[]{:S(2)}) collective-permute-start(bf16[96,512]{1,0:T(8,128)(2,1)S(1)} %collective-permute-done.3.refs_1_.refs_5_.refs_4_), channel_id=1, source_target_pairs={{0,4},{4,0},{8,12},{12,8},{16,20},{20,16},{24,28},{28,24},{1,5},{5... | collective-permute-start | bytes 294920 | tf_op jit(solution)/shard_map/ppermute | solution.py:271
  28.1 5.5 %collective-permute-start.9 = (bf16[96,512]{1,0:T(8,128)(2,1)S(1)}, bf16[96,512]{1,0:T(8,128)(2,1)S(1)}, u32[]{:S(2)}, u32[]{:S(2)}) collective-permute-start(bf16[96,512]{1,0:T(8,128)(2,1)S(1)} %collective-permute-done.5.refs_4_.refs_7_.refs_8_), channel_id=1, source_target_pairs={{0,4},{4,0},{8,12},{12,8},{16,20},{20,16},{24,28},{28,24},{1,5},{5... | collective-permute-start | bytes 294920 | tf_op jit(solution)/shard_map/ppermute | solution.py:271
  31.8 9.7 %collective-permute-start.12 = (bf16[48,2048]{1,0:T(8,128)(2,1)S(1)}, bf16[48,2048]{1,0:T(8,128)(2,1)S(1)}, u32[]{:S(2)}, u32[]{:S(2)}) collective-permute-start(bf16[48,2048]{1,0:T(8,128)(2,1)S(1)} %get-tuple-element.47), channel_id=1, source_target_pairs={{0,1},{1,0},{2,3},{3,2},{4,5},{5,4},{6,7},{7,6},{8,9},{9,8},{10,11... | collective-permute-start | bytes 589832 | tf_op jit(solution)/shard_map/ppermute | solution.py:271
  31.8 9.7 %collective-permute-start.13 = (bf16[48,2048]{1,0:T(8,128)(2,1)S(1)}, bf16[48,2048]{1,0:T(8,128)(2,1)S(1)}, u32[]{:S(2)}, u32[]{:S(2)}) collective-permute-start(bf16[48,2048]{1,0:T(8,128)(2,1)S(1)} %get-tuple-element.48), channel_id=1, source_target_pairs={{0,2},{1,3},{2,0},{3,1},{4,6},{5,7},{6,4},{7,5},{8,10},{9,11},{10,... | collective-permute-start | bytes 589832 | tf_op jit(solution)/shard_map/ppermute | solution.py:271
  32.8 10.1 %collective-permute-start.14 = (bf16[48,2048]{1,0:T(8,128)(2,1)S(1)}, bf16[48,2048]{1,0:T(8,128)(2,1)S(1)}, u32[]{:S(2)}, u32[]{:S(2)}) collective-permute-start(bf16[48,2048]{1,0:T(8,128)(2,1)S(1)} %get-tuple-element.49), channel_id=1, source_target_pairs={{0,3},{1,2},{2,1},{3,0},{4,7},{5,6},{6,5},{7,4},{8,11},{9,10},{10,... | collective-permute-start | bytes 589832 | tf_op jit(solution)/shard_map/ppermute | solution.py:271
  39.5 11.4 %collective-permute-start.15 = (bf16[384,256]{1,0:T(8,128)(2,1)S(1)}, bf16[384,256]{1,0:T(8,128)(2,1)S(1)}, u32[]{:S(2)}, u32[]{:S(2)}) collective-permute-start(bf16[384,256]{1,0:T(8,128)(2,1)S(1)} %get-tuple-element.53), channel_id=1, source_target_pairs={{0,4},{4,0},{8,12},{12,8},{16,20},{20,16},{24,28},{28,24},{1,5},{5... | collective-permute-start | bytes 589832 | tf_op jit(solution)/shard_map/ppermute | solution.py:271
  48.9 7.6 %collective-permute-start.19 = (bf16[384,256]{1,0:T(8,128)(2,1)S(1)}, bf16[384,256]{1,0:T(8,128)(2,1)S(1)}, u32[]{:S(2)}, u32[]{:S(2)}) collective-permute-start(bf16[384,256]{1,0:T(8,128)(2,1)S(1)} %get-tuple-element.60), channel_id=1, source_target_pairs={{0,4},{4,0},{8,12},{12,8},{16,20},{20,16},{24,28},{28,24},{1,5},{5... | collective-permute-start | bytes 589832 | tf_op jit(solution)/shard_map/ppermute | solution.py:271
  51.0 9.1 %collective-permute-start.16 = (bf16[96,256]{1,0:T(8,128)(2,1)S(1)}, bf16[96,256]{1,0:T(8,128)(2,1)S(1)}, u32[]{:S(2)}, u32[]{:S(2)}) collective-permute-start(bf16[96,256]{1,0:T(8,128)(2,1)S(1)} %get-tuple-element.56), channel_id=1, source_target_pairs={{0,8},{4,12},{8,0},{12,4},{16,24},{20,28},{24,16},{28,20},{1,9},{5... | collective-permute-start | bytes 147464 | tf_op jit(solution)/shard_map/ppermute | solution.py:271
  51.1 10.9 %collective-permute-start.17 = (bf16[96,256]{1,0:T(8,128)(2,1)S(1)}, bf16[96,256]{1,0:T(8,128)(2,1)S(1)}, u32[]{:S(2)}, u32[]{:S(2)}) collective-permute-start(bf16[96,256]{1,0:T(8,128)(2,1)S(1)} %get-tuple-element.57), channel_id=1, source_target_pairs={{0,16},{4,20},{8,24},{12,28},{16,0},{20,4},{24,8},{28,12},{1,17},{... | collective-permute-start | bytes 147464 | tf_op jit(solution)/shard_map/ppermute | solution.py:271
  54.3 7.7 %collective-permute-start.18 = (bf16[96,256]{1,0:T(8,128)(2,1)S(1)}, bf16[96,256]{1,0:T(8,128)(2,1)S(1)}, u32[]{:S(2)}, u32[]{:S(2)}) collective-permute-start(bf16[96,256]{1,0:T(8,128)(2,1)S(1)} %get-tuple-element.58), channel_id=1, source_target_pairs={{0,24},{4,28},{8,16},{12,20},{16,8},{20,12},{24,0},{28,4},{1,25},{... | collective-permute-start | bytes 147464 | tf_op jit(solution)/shard_map/ppermute | solution.py:271
  56.5 5.4 %collective-permute-start.20 = (bf16[96,256]{1,0:T(8,128)(2,1)S(1)}, bf16[96,256]{1,0:T(8,128)(2,1)S(1)}, u32[]{:S(2)}, u32[]{:S(2)}) collective-permute-start(bf16[96,256]{1,0:T(8,128)(2,1)S(1)} %get-tuple-element.62), channel_id=1, source_target_pairs={{0,8},{4,12},{8,0},{12,4},{16,24},{20,28},{24,16},{28,20},{1,9},{5... | collective-permute-start | bytes 147464 | tf_op jit(solution)/shard_map/ppermute | solution.py:271
  56.7 6.8 %collective-permute-start.21 = (bf16[96,256]{1,0:T(8,128)(2,1)S(1)}, bf16[96,256]{1,0:T(8,128)(2,1)S(1)}, u32[]{:S(2)}, u32[]{:S(2)}) collective-permute-start(bf16[96,256]{1,0:T(8,128)(2,1)S(1)} %get-tuple-element.63), channel_id=1, source_target_pairs={{0,16},{4,20},{8,24},{12,28},{16,0},{20,4},{24,8},{28,12},{1,17},{... | collective-permute-start | bytes 147464 | tf_op jit(solution)/shard_map/ppermute | solution.py:271
  60.1 5.9 %collective-permute-start.22 = (bf16[96,256]{1,0:T(8,128)(2,1)S(1)}, bf16[96,256]{1,0:T(8,128)(2,1)S(1)}, u32[]{:S(2)}, u32[]{:S(2)}) collective-permute-start(bf16[96,256]{1,0:T(8,128)(2,1)S(1)} %get-tuple-element.64), channel_id=1, source_target_pairs={{0,24},{4,28},{8,16},{12,20},{16,8},{20,12},{24,0},{28,4},{1,25},{... | collective-permute-start | bytes 147464 | tf_op jit(solution)/shard_map/ppermute | solution.py:271

commit v5 on v4

--- a/solution.py
+++ b/solution.py
@@ -81,15 +81,15 @@
     pass
 
 
-def join_kernel(core_ref, across_ref, *refs):
+def join_kernel(own_ref, core_ref, *refs):
     out, sems = refs[-2:]
-    rows = core_ref.shape[0]
+    rows = own_ref.shape[0]
     wait_copies(
         run_copies(
             [
-                pltpu.make_async_copy(core_ref, out.at[0:rows, :], sems.at[0]),
+                pltpu.make_async_copy(own_ref, out.at[0:rows, :], sems.at[0]),
                 pltpu.make_async_copy(
-                    across_ref.at[rows : 2 * rows, :], out.at[rows : 2 * rows, :], sems.at[1]
+                    core_ref.at[rows : 2 * rows, :], out.at[rows : 2 * rows, :], sems.at[1]
                 ),
             ]
         )
@@ -132,11 +132,11 @@
         hide_ref[g] = hide.T[:tokens].astype(jnp.bfloat16)
 
 
-def attend_kernel(g, order, qo_at, q_ref, o_ref, hide_ref, *refs):
+def attend_kernel(g, order, q_ref, o_ref, hide_ref, *refs):
     shards = len(order)
     heads = 4
     kv_pieces, blocks, refs = refs[:heads], refs[heads : heads + shards], refs[heads + shards :]
-    qo_pieces = [(refs[i], half) for i, half in qo_at]
+    qo_pieces = [(refs[0], 0), (refs[1], 0), (refs[1], 1)]
     dq_ref, own_ref, near_ref, far_ref, kx, vx, kt, mine, sems = refs[-9:]
     rows = q_ref.shape[0]
     kv_heads = hide_ref.shape[0]
@@ -225,11 +225,11 @@
         term[:, HD : 2 * HD] = dv[part].astype(term.dtype)
 
 
-def add_kernel(near_ref, far_ref, after_ref, own_ref, *part_refs):
+def add_kernel(near_ref, far_ref, after_ref, keep_ref, send_ref):
     total = near_ref[...] + far_ref[...].astype(jnp.float32)
-    own_ref[...] = total[:SLOT_DEV]
-    for k, part in enumerate(part_refs):
-        part[...] = total[(k + 1) * SLOT_DEV : (k + 2) * SLOT_DEV].astype(part.dtype)
+    half = keep_ref.shape[0]
+    keep_ref[...] = total[:half]
+    send_ref[...] = total[half:].astype(send_ref.dtype)
 
 
 def spread_kernel(parts_per_head, seg_ref, *refs):
@@ -271,31 +271,36 @@
     return lax.ppermute(x, axis, [(i, i ^ m) for i in range(size)])
 
 
-def gate(values, after):
+def gate(value, after):
     return pl.pallas_call(
         gate_kernel,
-        out_shape=[shape(*v.shape, dtype=v.dtype) for v in values],
-        in_specs=anywhere(len(values) + len(after)),
-        out_specs=anywhere(len(values)),
-        input_output_aliases={i: i for i in range(len(values))},
+        out_shape=shape(*value.shape, dtype=value.dtype),
+        in_specs=anywhere(1 + len(after)),
+        out_specs=anywhere(1)[0],
+        input_output_aliases={0: 0},
         compiler_params=params(1),
         name="gate",
-    )(*values, *after)
-
-
-def exchange(across, core, heads, after=lambda: ()):
-    from_across = swap(across, "head", heads, 2)
-    after = after()
+    )(value, *after)
+
+
+def across(own, from_core, heads, after):
     both = pl.pallas_call(
         join_kernel,
-        out_shape=shape(*across.shape),
+        out_shape=shape(*from_core.shape),
         in_specs=anywhere(2 + len(after)),
         out_specs=in_vmem(1)[0],
         scratch_shapes=[pltpu.SemaphoreType.DMA((2,))],
         compiler_params=params(2),
         name="join",
-    )(core, from_across, *after)
-    return from_across, swap(both, "head", heads, 1)
+    )(own, from_core, *after)
+    return swap(both, "head", heads, 2)
+
+
+def bit_reversed(count):
+    if count == 1:
+        return [0]
+    half = [2 * i for i in bit_reversed(count // 2)]
+    return half + [i + 1 for i in half]
 
 
 def local(queries, keys, values, segment_ids, grad_out):
@@ -304,7 +309,7 @@
     tokens = rows * heads
     kv_heads = KVH // heads
     shards = lax.axis_size("ctx")
-    order = list(range(0, shards, 2)) + list(range(1, shards, 2))
+    order = bit_reversed(shards)
     half = SLOT_DEV * shards // 2
     slots = SLOT_DEV * shards
     kv_width = kv_heads * HD
@@ -341,10 +346,9 @@
     )(keys, values)
     kv = [kv_out[0]] + [swap(kv_out[m], "head", heads, m) for m in range(1, heads)]
 
-    jobs = [(GW, [[qo_at(2, 0), qo_at(3, 0)], [qo_at(1, 0)]])]
-    for g in range(1, kv_heads):
-        jobs.append((GW, [[qo_at(m, g)] for m in range(1, heads)]))
+    jobs = [(GW, [[qo_at(1, g), qo_at(3, g)], [qo_at(2, g)]]) for g in range(kv_heads)]
     packed = pack(jobs, (queries, grad_out), kv_out[:1], 4, "pack_qo")
+    from_core = [swap(gate(packed[2 * g], kv[1:]), "head", heads, 1) for g in range(kv_heads)]
 
     merged, hide = pl.pallas_call(
         functools.partial(merge_kernel, heads),
@@ -357,21 +361,14 @@
     )(segment_ids, *kv, packed[1])
 
     held = {0: merged}
-    for m in range(2, shards, 2):
-        held[m] = swap(merged, "ctx", shards, m)
-    for m in range(0, shards, 2):
-        held[m + 1] = swap(held[m], "ctx", shards, 1)
-
-    late = [held[m] for m in range(1, shards - 1)]
-    soon = [held[m] for m in range(1, shards) if m % 2 == 0 or m in (1, shards // 2 + 1)]
-    qo_across = gate(packed[:1], kv[1:])[0]
-    qo = [exchange(qo_across, packed[1], heads, lambda: soon)]
-    qo_places = [((1, 0), (0, 0), (1, 1))]
+    for m in range(1, shards):
+        low = m & -m
+        held[m] = swap(held[m - low], "ctx", shards, low)
+
+    qo = [(from_core[0], across(packed[1], from_core[0], heads, [merged] + from_core[1:]))]
+    late = [held[m] for m in range(1, shards - 1)] + [qo[0][1]]
     for g in range(1, kv_heads):
-        pieces = packed[2 + (g - 1) * (heads - 1) : 2 + g * (heads - 1)]
-        pieces = gate(pieces, late)
-        qo.append([swap(piece, "head", heads, m + 1) for m, piece in enumerate(pieces)])
-        qo_places.append(((0, 0), (1, 0), (2, 0)))
+        qo.append((from_core[g], across(packed[2 * g + 1], from_core[g], heads, late)))
 
     dq = []
     own = []
@@ -379,7 +376,7 @@
     far = []
     for g in range(kv_heads):
         outs = pl.pallas_call(
-            functools.partial(attend_kernel, g, order, qo_places[g]),
+            functools.partial(attend_kernel, g, order),
             out_shape=[
                 shape(tokens, GW),
                 shape(tokens, 2 * HD, dtype=jnp.float32),
@@ -410,22 +407,23 @@
 
     spread_args = []
     for g in range(kv_heads):
-        parts = pl.pallas_call(
-            add_kernel,
-            out_shape=[shape(SLOT_DEV, 2 * HD, dtype=jnp.float32)]
-            + [shape(SLOT_DEV, 2 * HD)] * (shards // 2 - 1),
-            in_specs=in_vmem(2) + anywhere(1),
-            out_specs=in_vmem(shards // 2),
-            compiler_params=params(8),
-            name="add",
-        )(near[g], far[g], own[-1])
-        spread_args.append(parts[0])
-        for k in range(1, shards // 2):
-            spread_args.append(swap(parts[k], "ctx", shards, 2 * k))
-        spread_args.append(own[g])
+        keep, received, step = near[g], far[g], 2
+        while step < shards:
+            count = keep.shape[0] // 2
+            keep, send = pl.pallas_call(
+                add_kernel,
+                out_shape=[shape(count, 2 * HD, dtype=jnp.float32), shape(count, 2 * HD)],
+                in_specs=in_vmem(2) + anywhere(1),
+                out_specs=in_vmem(2),
+                compiler_params=params(8),
+                name="add",
+            )(keep, received, own[-1])
+            received = swap(send, "ctx", shards, step)
+            step *= 2
+        spread_args += [keep, received, own[g]]
 
     grad_keys, grad_values = pl.pallas_call(
-        functools.partial(spread_kernel, shards // 2 + 1),
+        functools.partial(spread_kernel, 3),
         out_shape=[shape(tokens, kv_width)] * 2,
         in_specs=in_vmem(1 + len(spread_args)),
         out_specs=in_vmem(2),

time: 67.2 us -> 64 us (0.952)
  starting transfers between devices: 30 us -> 20.8 us
  waiting for transfers between devices: 17.1 us -> 22.3 us
    ppermute x23 -> x20, starting transfers between devices: 30 us -> 20.8 us  [swap(): return lax.ppermute(x, axis, [(i, i ^ m) for i in range(size)])]
    ppermute x23 -> x20, waiting for transfers between devices: 17.1 us -> 22.3 us  [swap(): return lax.ppermute(x, axis, [(i, i ^ m) for i in range(size)])]
    pallas_call x8 -> x11, Pallas kernels: 13.4 us -> 13.9 us  [the longest x2 11.8 us: local(): pl.pallas_call(functools.partial(attend_kernel, g, order), out_shape=[sha...]
  transfers between devices with their start and end apart: 23 -> 20, of which waited for: 8 -> 12; matrix products, arithmetic and copies ran while one was open for 1% -> 1% of each run, Pallas kernels for 19% -> 20%
where the time goes in v5:
time: 64 us; the launch traced here: 63.7 us
  waiting for transfers between devices  22.3 us (35%)
  starting transfers between devices  20.8 us (32%)
  Pallas kernels  14.6 us (23%)
  local copies, waits for them, and re-layouts  4.22 us (7%)
  other arithmetic  0.94 us (1%)
  between operations  0.74 us (1%)
    ppermute x20, waiting for transfers between devices, swap(): return lax.ppermute(x, axis, [(i, i ^ m) for i in range(size)])  22.3 us
    ppermute x20, starting transfers between devices, swap(): return lax.ppermute(x, axis, [(i, i ^ m) for i in range(size)])  20.8 us
    pallas_call x2, Pallas kernels, local(): pl.pallas_call(functools.partial(attend_kernel, g, order), out_shape=[sha...  11.8 us
    unnamed x14, local copies, waits for them, and re-layouts  4.22 us
  transfers between devices with their start and end apart: 20, of which 12 were waited for; matrix products, arithmetic and copies ran while one was open for 1% of the time, Pallas kernels for 20%

profile of v5, /device:TPU:0, one launch (start us, length us, event | category | flops | bytes accessed | tf_op | source)
XLA Modules:
  0.0 63.7 jit_solution(3079626225968068617)
XLA Ops:
  0.6 0.9 %copy-done.4 = bf16[48,1024]{1,0:T(8,128)(2,1)S(1)} copy-done((bf16[48,1024]{1,0:T(8,128)(2,1)S(1)}, bf16[48,1024]{1,0:T(8,128)(2,1)}, u32[]{:S(2)}) %copy-start.4) | copy-done | bytes 98328
  1.5 0.9 %copy-done.5 = bf16[48,1024]{1,0:T(8,128)(2,1)S(1)} copy-done((bf16[48,1024]{1,0:T(8,128)(2,1)S(1)}, bf16[48,1024]{1,0:T(8,128)(2,1)}, u32[]{:S(2)}) %copy-start.5) | copy-done | bytes 98328
  3.0 2.6 %collective-permute-start.1 = (bf16[48,512]{1,0:T(8,128)(2,1)S(1)}, bf16[48,512]{1,0:T(8,128)(2,1)S(1)}, u32[]{:S(2)}, u32[]{:S(2)}) collective-permute-start(bf16[48,512]{1,0:T(8,128)(2,1)S(1)} %get-tuple-element.33), channel_id=1, source_target_pairs={{0,2},{1,3},{2,0},{3,1},{4,6},{5,7},{6,4},{7,5},{8,10},{9,11},{10,... | collective-permute-start | bytes 147464 | tf_op jit(solution)/shard_map/ppermute | solution.py:271
  5.6 1.1 %copy-done = bf16[48,8192]{1,0:T(8,128)(2,1)S(1)} copy-done((bf16[48,8192]{1,0:T(8,128)(2,1)S(1)}, bf16[48,8192]{1,0:T(8,128)(2,1)}, u32[]{:S(2)}) %copy-start) | copy-done | bytes 786456
  6.7 1.1 %copy-done.2 = bf16[48,8192]{1,0:T(8,128)(2,1)S(1)} copy-done((bf16[48,8192]{1,0:T(8,128)(2,1)S(1)}, bf16[48,8192]{1,0:T(8,128)(2,1)}, u32[]{:S(2)}) %copy-start.2) | copy-done | bytes 786456
  8.3 1.0 %collective-permute-done.2.refs_3_ = bf16[48,512]{1,0:T(8,128)(2,1)S(1)} collective-permute-done((bf16[48,512]{1,0:T(8,128)(2,1)S(1)}, bf16[48,512]{1,0:T(8,128)(2,1)S(1)}, u32[]{:S(2)}, u32[]{:S(2)}) %collective-permute-start.2) | collective-permute-done | bytes 49184 | tf_op jit(solution)/shard_map/ppermute | solution.py:271
  10.2 0.8 %collective-permute-done.11.refs_1_.core_ref.refs_12_ = bf16[96,2048]{1,0:T(8,128)(2,1)S(1)} collective-permute-done((bf16[96,2048]{1,0:T(8,128)(2,1)S(1)}, bf16[96,2048]{1,0:T(8,128)(2,1)S(1)}, u32[]{:S(2)}, u32[]{:S(2)}) %collective-permute-start.11) | collective-permute-done | bytes 393248 | tf_op jit(solution)/shard_map/ppermute | solution.py:271
  11.0 0.6 collective-permute-done.10.core_ref.refs_12_
  12.0 1.1 %collective-permute-start.12 = (bf16[96,2048]{1,0:T(8,128)(2,1)S(1)}, bf16[96,2048]{1,0:T(8,128)(2,1)S(1)}, u32[]{:S(2)}, u32[]{:S(2)}) collective-permute-start(bf16[96,2048]{1,0:T(8,128)(2,1)S(1)} %join.2), channel_id=1, source_target_pairs={{0,2},{1,3},{2,0},{3,1},{4,6},{5,7},{6,4},{7,5},{8,10},{9,11},{10,... | collective-permute-start | bytes 1179656 | tf_op jit(solution)/shard_map/ppermute | solution.py:271
  13.1 1.6 %collective-permute-start.4 = (bf16[96,512]{1,0:T(8,128)(2,1)S(1)}, bf16[96,512]{1,0:T(8,128)(2,1)S(1)}, u32[]{:S(2)}, u32[]{:S(2)}) collective-permute-start(bf16[96,512]{1,0:T(8,128)(2,1)S(1)} %get-tuple-element.37.refs_0_.refs_4_), channel_id=1, source_target_pairs={{0,8},{4,12},{8,0},{12,4},{16,24},{20,28},{24,16},{28,20},{1,9},{5... | collective-permute-start | bytes 294920 | tf_op jit(solution)/shard_map/ppermute | solution.py:271
  14.7 2.6 %collective-permute-start.3 = (bf16[96,512]{1,0:T(8,128)(2,1)S(1)}, bf16[96,512]{1,0:T(8,128)(2,1)S(1)}, u32[]{:S(2)}, u32[]{:S(2)}) collective-permute-start(bf16[96,512]{1,0:T(8,128)(2,1)S(1)} %get-tuple-element.37.refs_0_.refs_4_), channel_id=1, source_target_pairs={{0,16},{4,20},{8,24},{12,28},{16,0},{20,4},{24,8},{28,12},{1,17},{... | collective-permute-start | bytes 294920 | tf_op jit(solution)/shard_map/ppermute | solution.py:271
  17.2 1.5 %collective-permute-start.6 = (bf16[96,512]{1,0:T(8,128)(2,1)S(1)}, bf16[96,512]{1,0:T(8,128)(2,1)S(1)}, u32[]{:S(2)}, u32[]{:S(2)}) collective-permute-start(bf16[96,512]{1,0:T(8,128)(2,1)S(1)} %get-tuple-element.37.refs_0_.refs_4_), channel_id=1, source_target_pairs={{0,4},{4,0},{8,12},{12,8},{16,20},{20,16},{24,28},{28,24},{1,5},{5... | collective-permute-start | bytes 294920 | tf_op jit(solution)/shard_map/ppermute | solution.py:271
  18.8 0.5 collective-permute-start.8
  19.3 2.8 %collective-permute-done.3.refs_5_.refs_3_ = bf16[96,512]{1,0:T(8,128)(2,1)S(1)} collective-permute-done((bf16[96,512]{1,0:T(8,128)(2,1)S(1)}, bf16[96,512]{1,0:T(8,128)(2,1)S(1)}, u32[]{:S(2)}, u32[]{:S(2)}) %collective-permute-start.3) | collective-permute-done | bytes 98336 | tf_op jit(solution)/shard_map/ppermute | solution.py:271
  22.1 1.5 %collective-permute-start.7 = (bf16[96,512]{1,0:T(8,128)(2,1)S(1)}, bf16[96,512]{1,0:T(8,128)(2,1)S(1)}, u32[]{:S(2)}, u32[]{:S(2)}) collective-permute-start(bf16[96,512]{1,0:T(8,128)(2,1)S(1)} %collective-permute-done.3.refs_5_.refs_3_), channel_id=1, source_target_pairs={{0,4},{4,0},{8,12},{12,8},{16,20},{20,16},{24,28},{28,24},{1,5},{5... | collective-permute-start | bytes 294920 | tf_op jit(solution)/shard_map/ppermute | solution.py:271
  24.1 0.6 collective-permute-done.8.refs_10_.refs_2_
  24.7 2.0 %collective-permute-done.7.refs_9_.refs_4_ = bf16[96,512]{1,0:T(8,128)(2,1)S(1)} collective-permute-done((bf16[96,512]{1,0:T(8,128)(2,1)S(1)}, bf16[96,512]{1,0:T(8,128)(2,1)S(1)}, u32[]{:S(2)}, u32[]{:S(2)}) %collective-permute-start.7) | collective-permute-done | bytes 98336 | tf_op jit(solution)/shard_map/ppermute | solution.py:271
  26.8 1.5 %collective-permute-done.5.refs_7_.refs_5_ = bf16[96,512]{1,0:T(8,128)(2,1)S(1)} collective-permute-done((bf16[96,512]{1,0:T(8,128)(2,1)S(1)}, bf16[96,512]{1,0:T(8,128)(2,1)S(1)}, u32[]{:S(2)}, u32[]{:S(2)}) %collective-permute-start.5) | collective-permute-done | bytes 98336 | tf_op jit(solution)/shard_map/ppermute | solution.py:271
  28.3 0.5 join.3
  28.8 1.0 %collective-permute-start.13 = (bf16[96,2048]{1,0:T(8,128)(2,1)S(1)}, bf16[96,2048]{1,0:T(8,128)(2,1)S(1)}, u32[]{:S(2)}, u32[]{:S(2)}) collective-permute-start(bf16[96,2048]{1,0:T(8,128)(2,1)S(1)} %join.3), channel_id=1, source_target_pairs={{0,2},{1,3},{2,0},{3,1},{4,6},{5,7},{6,4},{7,5},{8,10},{9,11},{10,... | collective-permute-start | bytes 1179656 | tf_op jit(solution)/shard_map/ppermute | solution.py:271
  30.3 4.1 %collective-permute-done.9.refs_11_ = bf16[96,512]{1,0:T(8,128)(2,1)S(1)} collective-permute-done((bf16[96,512]{1,0:T(8,128)(2,1)S(1)}, bf16[96,512]{1,0:T(8,128)(2,1)S(1)}, u32[]{:S(2)}, u32[]{:S(2)}) %collective-permute-start.9) | collective-permute-done | bytes 98336 | tf_op jit(solution)/shard_map/ppermute | solution.py:271
  34.4 5.8 %attend.2 = (bf16[192,1024]{1,0:T(8,128)(2,1)S(1)}, f32[192,256]{1,0:T(8,128)S(1)}, f32[384,256]{1,0:T(8,128)S(1)}, bf16[384,256]{1,0:T(8,128)(2,1)S(1)}) custom-call(bf16[48,8192]{1,0:T(8,128)(2,1)S(1)} %copy-done.1, bf16[48,8192]{1,0:T(8,128)(2,1)S(1)} %copy-done.3, bf16[2,192,128]{2,1,0:T(8,128)(2,1)S(1)} %get-tuple-element.36.hide_ref, ...), custom_call_target="tpu_custom_call" | custom-call | flops 1604321280 | bytes 4194304 | tf_op jit(solution)/shard_map/attend/pallas_call | solution.py:378
  40.2 0.6 collective-permute-start.14
  40.8 6.0 %attend.3 = (bf16[192,1024]{1,0:T(8,128)(2,1)S(1)}, f32[192,256]{1,0:T(8,128)S(1)}, f32[384,256]{1,0:T(8,128)S(1)}, bf16[384,256]{1,0:T(8,128)(2,1)S(1)}) custom-call(bf16[48,8192]{1,0:T(8,128)(2,1)S(1)} %copy-done.1, bf16[48,8192]{1,0:T(8,128)(2,1)S(1)} %copy-done.3, bf16[2,192,128]{2,1,0:T(8,128)(2,1)S(1)} %get-tuple-element.36.hide_ref, ...), custom_call_target="tpu_custom_call" | custom-call | flops 1604321280 | bytes 4194304 | tf_op jit(solution)/shard_map/attend/pallas_call | solution.py:378
  46.8 1.6 %collective-permute-start.17 = (bf16[384,256]{1,0:T(8,128)(2,1)S(1)}, bf16[384,256]{1,0:T(8,128)(2,1)S(1)}, u32[]{:S(2)}, u32[]{:S(2)}) collective-permute-start(bf16[384,256]{1,0:T(8,128)(2,1)S(1)} %get-tuple-element.52), channel_id=1, source_target_pairs={{0,4},{4,0},{8,12},{12,8},{16,20},{20,16},{24,28},{28,24},{1,5},{5... | collective-permute-start | bytes 589832 | tf_op jit(solution)/shard_map/ppermute | solution.py:271
  48.8 3.7 %collective-permute-done.17.far_ref = bf16[384,256]{1,0:T(8,128)(2,1)S(1)} collective-permute-done((bf16[384,256]{1,0:T(8,128)(2,1)S(1)}, bf16[384,256]{1,0:T(8,128)(2,1)S(1)}, u32[]{:S(2)}, u32[]{:S(2)}) %collective-permute-start.17) | collective-permute-done | bytes 196640 | tf_op jit(solution)/shard_map/ppermute | solution.py:271
  53.3 2.5 %collective-permute-start.16 = (bf16[96,256]{1,0:T(8,128)(2,1)S(1)}, bf16[96,256]{1,0:T(8,128)(2,1)S(1)}, u32[]{:S(2)}, u32[]{:S(2)}) collective-permute-start(bf16[96,256]{1,0:T(8,128)(2,1)S(1)} %get-tuple-element.50), channel_id=1, source_target_pairs={{0,16},{4,20},{8,24},{12,28},{16,0},{20,4},{24,8},{28,12},{1,17},{... | collective-permute-start | bytes 147464 | tf_op jit(solution)/shard_map/ppermute | solution.py:271
  55.7 1.5 %collective-permute-done.18.far_ref = bf16[192,256]{1,0:T(8,128)(2,1)S(1)} collective-permute-done((bf16[192,256]{1,0:T(8,128)(2,1)S(1)}, bf16[192,256]{1,0:T(8,128)(2,1)S(1)}, u32[]{:S(2)}, u32[]{:S(2)}) %collective-permute-start.18) | collective-permute-done | bytes 98336 | tf_op jit(solution)/shard_map/ppermute | solution.py:271
  57.3 1.0 %collective-permute-start.19 = (bf16[96,256]{1,0:T(8,128)(2,1)S(1)}, bf16[96,256]{1,0:T(8,128)(2,1)S(1)}, u32[]{:S(2)}, u32[]{:S(2)}) collective-permute-start(bf16[96,256]{1,0:T(8,128)(2,1)S(1)} %get-tuple-element.56), channel_id=1, source_target_pairs={{0,16},{4,20},{8,24},{12,28},{16,0},{20,4},{24,8},{28,12},{1,17},{... | collective-permute-start | bytes 147464 | tf_op jit(solution)/shard_map/ppermute | solution.py:271
  58.3 0.9 %pad_maximum_fusion = bf16[192,2048]{1,0:T(8,128)(2,1)} fusion(bf16[192,1024]{1,0:T(8,128)(2,1)S(1)} %get-tuple-element.43, bf16[192,1024]{1,0:T(8,128)(2,1)S(1)} %get-tuple-element.40), kind=kLoop, calls=%fused_computation | loop fusion | flops 1572864 | bytes 1572864 | tf_op jit(solution)/shard_map/concatenate | solution.py:433
  59.3 3.4 %collective-permute-done.19.refs_4_ = bf16[96,256]{1,0:T(8,128)(2,1)S(1)} collective-permute-done((bf16[96,256]{1,0:T(8,128)(2,1)S(1)}, bf16[96,256]{1,0:T(8,128)(2,1)S(1)}, u32[]{:S(2)}, u32[]{:S(2)}) %collective-permute-start.19) | collective-permute-done | bytes 49184 | tf_op jit(solution)/shard_map/ppermute | solution.py:271
  62.6 1.0 %spread.1 = (bf16[192,256]{1,0:T(8,128)(2,1)}, bf16[192,256]{1,0:T(8,128)(2,1)}) custom-call(s32[2,192]{1,0:T(2,128)S(1)} %copy-done.6, f32[96,256]{1,0:T(8,128)S(1)} %get-tuple-element.49.refs_0_, bf16[96,256]{1,0:T(8,128)(2,1)S(1)} %collective-permute-done.16.refs_1_, f32[192,256]{1,0:T(8,128)S(1)} %get-tuple-element.42.refs_14_.refs_2_, ...), custom_call_target="tpu_custom_call" | custom-call | tf_op jit(solution)/shard_map/spread/pallas_call | solution.py:425
  (37 shorter events, 4.6 us)
Async XLA Ops:
  0.6 0.9 %copy-start.4 = (bf16[48,1024]{1,0:T(8,128)(2,1)S(1)}, bf16[48,1024]{1,0:T(8,128)(2,1)}, u32[]{:S(2)}) copy-start(bf16[48,1024]{1,0:T(8,128)(2,1)} %key_ref.1) | copy-start | bytes 294916
  1.5 0.9 %copy-start.5 = (bf16[48,1024]{1,0:T(8,128)(2,1)S(1)}, bf16[48,1024]{1,0:T(8,128)(2,1)}, u32[]{:S(2)}) copy-start(bf16[48,1024]{1,0:T(8,128)(2,1)} %value_ref.1) | copy-start | bytes 294916
  2.4 5.8 %collective-permute-start = (bf16[48,512]{1,0:T(8,128)(2,1)S(1)}, bf16[48,512]{1,0:T(8,128)(2,1)S(1)}, u32[]{:S(2)}, u32[]{:S(2)}) collective-permute-start(bf16[48,512]{1,0:T(8,128)(2,1)S(1)} %get-tuple-element.32), channel_id=1, source_target_pairs={{0,1},{1,0},{2,3},{3,2},{4,5},{5,4},{6,7},{7,6},{8,9},{9,8},{10,11... | collective-permute-start | bytes 147464 | tf_op jit(solution)/shard_map/ppermute | solution.py:271
  3.0 5.3 %collective-permute-start.1 = (bf16[48,512]{1,0:T(8,128)(2,1)S(1)}, bf16[48,512]{1,0:T(8,128)(2,1)S(1)}, u32[]{:S(2)}, u32[]{:S(2)}) collective-permute-start(bf16[48,512]{1,0:T(8,128)(2,1)S(1)} %get-tuple-element.33), channel_id=1, source_target_pairs={{0,2},{1,3},{2,0},{3,1},{4,6},{5,7},{6,4},{7,5},{8,10},{9,11},{10,... | collective-permute-start | bytes 147464 | tf_op jit(solution)/shard_map/ppermute | solution.py:271
  5.5 3.7 %collective-permute-start.2 = (bf16[48,512]{1,0:T(8,128)(2,1)S(1)}, bf16[48,512]{1,0:T(8,128)(2,1)S(1)}, u32[]{:S(2)}, u32[]{:S(2)}) collective-permute-start(bf16[48,512]{1,0:T(8,128)(2,1)S(1)} %get-tuple-element.34), channel_id=1, source_target_pairs={{0,3},{1,2},{2,1},{3,0},{4,7},{5,6},{6,5},{7,4},{8,11},{9,10},{10,... | collective-permute-start | bytes 147464 | tf_op jit(solution)/shard_map/ppermute | solution.py:271
  5.6 1.1 %copy-start = (bf16[48,8192]{1,0:T(8,128)(2,1)S(1)}, bf16[48,8192]{1,0:T(8,128)(2,1)}, u32[]{:S(2)}) copy-start(bf16[48,8192]{1,0:T(8,128)(2,1)} %q_ref.3) | copy-start | bytes 2359300
  6.7 1.1 %copy-start.2 = (bf16[48,8192]{1,0:T(8,128)(2,1)S(1)}, bf16[48,8192]{1,0:T(8,128)(2,1)}, u32[]{:S(2)}) copy-start(bf16[48,8192]{1,0:T(8,128)(2,1)} %o_ref.3) | copy-start | bytes 2359300
  9.2 0.7 %copy-start.6 = (s32[2,192]{1,0:T(2,128)S(1)}, s32[2,192]{1,0:T(2,128)}, u32[]{:S(2)}) copy-start(s32[2,192]{1,0:T(2,128)} %seg_ref.3) | copy-start | bytes 4612
  9.2 1.7 %collective-permute-start.11 = (bf16[96,2048]{1,0:T(8,128)(2,1)S(1)}, bf16[96,2048]{1,0:T(8,128)(2,1)S(1)}, u32[]{:S(2)}, u32[]{:S(2)}) collective-permute-start(bf16[96,2048]{1,0:T(8,128)(2,1)S(1)} %gate.3), channel_id=1, source_target_pairs={{0,1},{1,0},{2,3},{3,2},{4,5},{5,4},{6,7},{7,6},{8,9},{9,8},{10,11... | collective-permute-start | bytes 1179656 | tf_op jit(solution)/shard_map/ppermute | solution.py:271
  9.4 2.1 %collective-permute-start.10 = (bf16[96,2048]{1,0:T(8,128)(2,1)S(1)}, bf16[96,2048]{1,0:T(8,128)(2,1)S(1)}, u32[]{:S(2)}, u32[]{:S(2)}) collective-permute-start(bf16[96,2048]{1,0:T(8,128)(2,1)S(1)} %gate.2), channel_id=1, source_target_pairs={{0,1},{1,0},{2,3},{3,2},{4,5},{5,4},{6,7},{7,6},{8,9},{9,8},{10,11... | collective-permute-start | bytes 1179656 | tf_op jit(solution)/shard_map/ppermute | solution.py:271
  12.0 16.3 %collective-permute-start.12 = (bf16[96,2048]{1,0:T(8,128)(2,1)S(1)}, bf16[96,2048]{1,0:T(8,128)(2,1)S(1)}, u32[]{:S(2)}, u32[]{:S(2)}) collective-permute-start(bf16[96,2048]{1,0:T(8,128)(2,1)S(1)} %join.2), channel_id=1, source_target_pairs={{0,2},{1,3},{2,0},{3,1},{4,6},{5,7},{6,4},{7,5},{8,10},{9,11},{10,... | collective-permute-start | bytes 1179656 | tf_op jit(solution)/shard_map/ppermute | solution.py:271
  13.1 5.7 %collective-permute-start.4 = (bf16[96,512]{1,0:T(8,128)(2,1)S(1)}, bf16[96,512]{1,0:T(8,128)(2,1)S(1)}, u32[]{:S(2)}, u32[]{:S(2)}) collective-permute-start(bf16[96,512]{1,0:T(8,128)(2,1)S(1)} %get-tuple-element.37.refs_0_.refs_4_), channel_id=1, source_target_pairs={{0,8},{4,12},{8,0},{12,4},{16,24},{20,28},{24,16},{28,20},{1,9},{5... | collective-permute-start | bytes 294920 | tf_op jit(solution)/shard_map/ppermute | solution.py:271
  14.7 7.5 %collective-permute-start.3 = (bf16[96,512]{1,0:T(8,128)(2,1)S(1)}, bf16[96,512]{1,0:T(8,128)(2,1)S(1)}, u32[]{:S(2)}, u32[]{:S(2)}) collective-permute-start(bf16[96,512]{1,0:T(8,128)(2,1)S(1)} %get-tuple-element.37.refs_0_.refs_4_), channel_id=1, source_target_pairs={{0,16},{4,20},{8,24},{12,28},{16,0},{20,4},{24,8},{28,12},{1,17},{... | collective-permute-start | bytes 294920 | tf_op jit(solution)/shard_map/ppermute | solution.py:271
  17.2 6.9 %collective-permute-start.6 = (bf16[96,512]{1,0:T(8,128)(2,1)S(1)}, bf16[96,512]{1,0:T(8,128)(2,1)S(1)}, u32[]{:S(2)}, u32[]{:S(2)}) collective-permute-start(bf16[96,512]{1,0:T(8,128)(2,1)S(1)} %get-tuple-element.37.refs_0_.refs_4_), channel_id=1, source_target_pairs={{0,4},{4,0},{8,12},{12,8},{16,20},{20,16},{24,28},{28,24},{1,5},{5... | collective-permute-start | bytes 294920 | tf_op jit(solution)/shard_map/ppermute | solution.py:271
  18.8 6.0 %collective-permute-start.8 = (bf16[96,512]{1,0:T(8,128)(2,1)S(1)}, bf16[96,512]{1,0:T(8,128)(2,1)S(1)}, u32[]{:S(2)}, u32[]{:S(2)}) collective-permute-start(bf16[96,512]{1,0:T(8,128)(2,1)S(1)} %collective-permute-done.4.refs_6_.refs_1_), channel_id=1, source_target_pairs={{0,4},{4,0},{8,12},{12,8},{16,20},{20,16},{24,28},{28,24},{1,5},{5... | collective-permute-start | bytes 294920 | tf_op jit(solution)/shard_map/ppermute | solution.py:271
  22.1 4.6 %collective-permute-start.7 = (bf16[96,512]{1,0:T(8,128)(2,1)S(1)}, bf16[96,512]{1,0:T(8,128)(2,1)S(1)}, u32[]{:S(2)}, u32[]{:S(2)}) collective-permute-start(bf16[96,512]{1,0:T(8,128)(2,1)S(1)} %collective-permute-done.3.refs_5_.refs_3_), channel_id=1, source_target_pairs={{0,4},{4,0},{8,12},{12,8},{16,20},{20,16},{24,28},{28,24},{1,5},{5... | collective-permute-start | bytes 294920 | tf_op jit(solution)/shard_map/ppermute | solution.py:271
  23.7 4.6 %collective-permute-start.5 = (bf16[96,512]{1,0:T(8,128)(2,1)S(1)}, bf16[96,512]{1,0:T(8,128)(2,1)S(1)}, u32[]{:S(2)}, u32[]{:S(2)}) collective-permute-start(bf16[96,512]{1,0:T(8,128)(2,1)S(1)} %collective-permute-done.3.refs_5_.refs_3_), channel_id=1, source_target_pairs={{0,8},{4,12},{8,0},{12,4},{16,24},{20,28},{24,16},{28,20},{1,9},{5... | collective-permute-start | bytes 294920 | tf_op jit(solution)/shard_map/ppermute | solution.py:271
  28.3 6.1 %copy-start.1 = (bf16[48,8192]{1,0:T(8,128)(2,1)S(1)}, bf16[48,8192]{1,0:T(8,128)(2,1)}, u32[]{:S(2)}) copy-start(bf16[48,8192]{1,0:T(8,128)(2,1)} %q_ref.3) | copy-start | bytes 2359300
  28.3 6.1 %copy-start.3 = (bf16[48,8192]{1,0:T(8,128)(2,1)S(1)}, bf16[48,8192]{1,0:T(8,128)(2,1)}, u32[]{:S(2)}) copy-start(bf16[48,8192]{1,0:T(8,128)(2,1)} %o_ref.3) | copy-start | bytes 2359300
  28.8 12.0 %collective-permute-start.13 = (bf16[96,2048]{1,0:T(8,128)(2,1)S(1)}, bf16[96,2048]{1,0:T(8,128)(2,1)S(1)}, u32[]{:S(2)}, u32[]{:S(2)}) collective-permute-start(bf16[96,2048]{1,0:T(8,128)(2,1)S(1)} %join.3), channel_id=1, source_target_pairs={{0,2},{1,3},{2,0},{3,1},{4,6},{5,7},{6,4},{7,5},{8,10},{9,11},{10,... | collective-permute-start | bytes 1179656 | tf_op jit(solution)/shard_map/ppermute | solution.py:271
  29.8 4.6 %collective-permute-start.9 = (bf16[96,512]{1,0:T(8,128)(2,1)S(1)}, bf16[96,512]{1,0:T(8,128)(2,1)S(1)}, u32[]{:S(2)}, u32[]{:S(2)}) collective-permute-start(bf16[96,512]{1,0:T(8,128)(2,1)S(1)} %collective-permute-done.5.refs_7_.refs_5_), channel_id=1, source_target_pairs={{0,4},{4,0},{8,12},{12,8},{16,20},{20,16},{24,28},{28,24},{1,5},{5... | collective-permute-start | bytes 294920 | tf_op jit(solution)/shard_map/ppermute | solution.py:271
  40.2 8.2 %collective-permute-start.14 = (bf16[384,256]{1,0:T(8,128)(2,1)S(1)}, bf16[384,256]{1,0:T(8,128)(2,1)S(1)}, u32[]{:S(2)}, u32[]{:S(2)}) collective-permute-start(bf16[384,256]{1,0:T(8,128)(2,1)S(1)} %get-tuple-element.45), channel_id=1, source_target_pairs={{0,4},{4,0},{8,12},{12,8},{16,20},{20,16},{24,28},{28,24},{1,5},{5... | collective-permute-start | bytes 589832 | tf_op jit(solution)/shard_map/ppermute | solution.py:271
  46.8 5.7 %collective-permute-start.17 = (bf16[384,256]{1,0:T(8,128)(2,1)S(1)}, bf16[384,256]{1,0:T(8,128)(2,1)S(1)}, u32[]{:S(2)}, u32[]{:S(2)}) collective-permute-start(bf16[384,256]{1,0:T(8,128)(2,1)S(1)} %get-tuple-element.52), channel_id=1, source_target_pairs={{0,4},{4,0},{8,12},{12,8},{16,20},{20,16},{24,28},{28,24},{1,5},{5... | collective-permute-start | bytes 589832 | tf_op jit(solution)/shard_map/ppermute | solution.py:271
  48.4 4.8 %collective-permute-start.15 = (bf16[192,256]{1,0:T(8,128)(2,1)S(1)}, bf16[192,256]{1,0:T(8,128)(2,1)S(1)}, u32[]{:S(2)}, u32[]{:S(2)}) collective-permute-start(bf16[192,256]{1,0:T(8,128)(2,1)S(1)} %get-tuple-element.48), channel_id=1, source_target_pairs={{0,8},{4,12},{8,0},{12,4},{16,24},{20,28},{24,16},{28,20},{1,9},{5... | collective-permute-start | bytes 294920 | tf_op jit(solution)/shard_map/ppermute | solution.py:271
  52.6 4.7 %collective-permute-start.18 = (bf16[192,256]{1,0:T(8,128)(2,1)S(1)}, bf16[192,256]{1,0:T(8,128)(2,1)S(1)}, u32[]{:S(2)}, u32[]{:S(2)}) collective-permute-start(bf16[192,256]{1,0:T(8,128)(2,1)S(1)} %get-tuple-element.54), channel_id=1, source_target_pairs={{0,8},{4,12},{8,0},{12,4},{16,24},{20,28},{24,16},{28,20},{1,9},{5... | collective-permute-start | bytes 294920 | tf_op jit(solution)/shard_map/ppermute | solution.py:271
  53.3 6.0 %collective-permute-start.16 = (bf16[96,256]{1,0:T(8,128)(2,1)S(1)}, bf16[96,256]{1,0:T(8,128)(2,1)S(1)}, u32[]{:S(2)}, u32[]{:S(2)}) collective-permute-start(bf16[96,256]{1,0:T(8,128)(2,1)S(1)} %get-tuple-element.50), channel_id=1, source_target_pairs={{0,16},{4,20},{8,24},{12,28},{16,0},{20,4},{24,8},{28,12},{1,17},{... | collective-permute-start | bytes 147464 | tf_op jit(solution)/shard_map/ppermute | solution.py:271
  57.3 5.4 %collective-permute-start.19 = (bf16[96,256]{1,0:T(8,128)(2,1)S(1)}, bf16[96,256]{1,0:T(8,128)(2,1)S(1)}, u32[]{:S(2)}, u32[]{:S(2)}) collective-permute-start(bf16[96,256]{1,0:T(8,128)(2,1)S(1)} %get-tuple-element.56), channel_id=1, source_target_pairs={{0,16},{4,20},{8,24},{12,28},{16,0},{20,4},{24,8},{28,12},{1,17},{... | collective-permute-start | bytes 147464 | tf_op jit(solution)/shard_map/ppermute | solution.py:271

commit v6 on v5

--- a/solution.py
+++ b/solution.py
@@ -137,7 +137,10 @@
     heads = 4
     kv_pieces, blocks, refs = refs[:heads], refs[heads : heads + shards], refs[heads + shards :]
     qo_pieces = [(refs[0], 0), (refs[1], 0), (refs[1], 1)]
-    dq_ref, own_ref, near_ref, far_ref, kx, vx, kt, mine, sems = refs[-9:]
+    (
+        p_ref, ds_ref, own_p_ref, own_ds_ref, qs_ref, os_ref, kt_ref, far_ref,
+        kx, vx, mine, sems,
+    ) = refs[-12:]
     rows = q_ref.shape[0]
     kv_heads = hide_ref.shape[0]
     slots = shards * SLOT_DEV
@@ -168,27 +171,28 @@
         kx[at, 0:HD] = jnp.where(key > 100.0, 0.0, key).astype(jnp.bfloat16)
         kx[at, HD : 2 * HD] = extra.astype(jnp.bfloat16)
     kx[slots : slots + rows, HD : 2 * HD] = jnp.zeros((rows, HD), jnp.bfloat16)
-    kt[...] = kx[0:slots, 0:HD].astype(jnp.float32).T.astype(jnp.bfloat16)
 
     width = GROUP * rows
     eye_row = lax.broadcasted_iota(jnp.int32, (rows, width), 0)
     eye_lane = lax.broadcasted_iota(jnp.int32, (rows, width), 1)
     eye = eye_row == lax.rem(eye_lane, rows)
     factor = SCALE * LOG2E
-    wait_copies(copies)
-
-    dk = None
-    dv = None
-    for m, (qo, half) in enumerate([(mine, 0)] + qo_pieces):
+
+    for m in list(range(1, heads)) + [0]:
+        if m == 0:
+            wait_copies(copies)
+        qo, half = qo_pieces[m - 1] if m else (mine, 0)
         span = slice(half * rows, (half + 1) * rows)
         at = pl.ds(pl.multiple_of(lax.bitwise_xor(me, m) * rows, 16), rows)
-        own_key = kv_pieces[m][:, key_at]
-        kx[slots : slots + rows, 0:HD] = own_key
+        chunk = slice(m * width, (m + 1) * width)
+        kx[slots : slots + rows, 0:HD] = kv_pieces[m][:, key_at]
         vx[slots : slots + rows, :] = kv_pieces[m][:, value_at]
         q2 = jnp.concatenate([qo[span, h * HD : (h + 1) * HD] for h in range(GROUP)], axis=0)
         o2 = jnp.concatenate(
             [qo[span, GW + h * HD : GW + (h + 1) * HD] for h in range(GROUP)], axis=0
         )
+        qs_ref[chunk, :] = q2
+        os_ref[chunk, :] = o2
         qx = jnp.concatenate([q2, jnp.concatenate([hide_ref[g, at, :]] * GROUP, axis=0)], axis=1)
         scores = nt(kx[...], qx)
         own_score = jnp.sum(jnp.where(eye, scores[slots:], 0.0), axis=0, keepdims=True)
@@ -203,29 +207,40 @@
         own_grad_prob = jnp.sum(jnp.where(eye, grad_probs[slots:], 0.0), axis=0, keepdims=True)
         grad_probs = grad_probs[:slots]
         delta = jnp.sum(probs * grad_probs, axis=0, keepdims=True) + own_prob * own_grad_prob
-        low_grads = (probs * (grad_probs - delta)).astype(jnp.bfloat16)
-        low_probs = probs.astype(jnp.bfloat16)
+        ds_ref[:, chunk] = (probs * (grad_probs - delta)).astype(jnp.bfloat16)
+        p_ref[:, chunk] = probs.astype(jnp.bfloat16)
         own_grad_score = own_prob * (own_grad_prob - delta)
-        own_low_probs = jnp.where(eye, own_prob, 0.0).astype(jnp.bfloat16)
-        own_low_grads = jnp.where(eye, own_grad_score, 0.0).astype(jnp.bfloat16)
-        dv_part = nn(low_probs, o2)
-        dk_part = nn(low_grads, q2)
-        dv = dv_part if dv is None else dv + dv_part
-        dk = dk_part if dk is None else dk + dk_part
-        own_ref[at, 0:HD] = SCALE * nn(own_low_grads, q2)
-        own_ref[at, HD : 2 * HD] = nn(own_low_probs, o2)
-        dq = nn(kt[...], low_grads) + tn(own_key, own_low_grads)
+        own_p_ref[:, chunk] = jnp.where(eye, own_prob, 0.0).astype(jnp.bfloat16)
+        own_ds_ref[:, chunk] = jnp.where(eye, own_grad_score, 0.0).astype(jnp.bfloat16)
+    far = slice(slots // 2, slots)
+    far_ref[:, 0:HD] = (SCALE * nn(ds_ref[far, :], qs_ref[...])).astype(far_ref.dtype)
+    far_ref[:, HD : 2 * HD] = nn(p_ref[far, :], os_ref[...]).astype(far_ref.dtype)
+    kt_ref[...] = kx[0:slots, 0:HD].astype(jnp.float32).T.astype(jnp.bfloat16)
+
+
+def finish_kernel(
+    g, heads, p_ref, ds_ref, own_p_ref, own_ds_ref, qs_ref, os_ref, kt_ref, after_ref, *refs
+):
+    kv_pieces, (near_ref, own_ref, dq_ref) = refs[:heads], refs[heads:]
+    rows = own_p_ref.shape[0]
+    near = slice(0, near_ref.shape[0])
+    near_ref[:, 0:HD] = SCALE * nn(ds_ref[near, :], qs_ref[...])
+    near_ref[:, HD : 2 * HD] = nn(p_ref[near, :], os_ref[...])
+    me = place()[1]
+    width = GROUP * rows
+    for m in range(heads):
+        at = pl.ds(pl.multiple_of(lax.bitwise_xor(me, m) * rows, 16), rows)
+        chunk = slice(m * width, (m + 1) * width)
+        own_ref[at, 0:HD] = SCALE * nn(own_ds_ref[:, chunk], qs_ref[chunk, :])
+        own_ref[at, HD : 2 * HD] = nn(own_p_ref[:, chunk], os_ref[chunk, :])
+        own_key = kv_pieces[m][:, g * HD : (g + 1) * HD]
+        dq = nn(kt_ref[...], ds_ref[:, chunk]) + tn(own_key, own_ds_ref[:, chunk])
         dq = (SCALE * dq).T.astype(jnp.bfloat16)
         for h in range(GROUP):
             dq_ref[at, h * HD : (h + 1) * HD] = dq[h * rows : (h + 1) * rows]
-    dk = dk * SCALE
-    half = slots // 2
-    for term, part in ((near_ref, slice(0, half)), (far_ref, slice(half, slots))):
-        term[:, 0:HD] = dk[part].astype(term.dtype)
-        term[:, HD : 2 * HD] = dv[part].astype(term.dtype)
-
-
-def add_kernel(near_ref, far_ref, after_ref, keep_ref, send_ref):
+
+
+def add_kernel(near_ref, far_ref, keep_ref, send_ref):
     total = near_ref[...] + far_ref[...].astype(jnp.float32)
     half = keep_ref.shape[0]
     keep_ref[...] = total[:half]
@@ -283,7 +298,7 @@
     )(value, *after)
 
 
-def across(own, from_core, heads, after):
+def across(own, from_core, heads, after, late=()):
     both = pl.pallas_call(
         join_kernel,
         out_shape=shape(*from_core.shape),
@@ -293,7 +308,7 @@
         compiler_params=params(2),
         name="join",
     )(own, from_core, *after)
-    return swap(both, "head", heads, 2)
+    return swap(gate(both, late) if late else both, "head", heads, 2)
 
 
 def bit_reversed(count):
@@ -365,45 +380,77 @@
         low = m & -m
         held[m] = swap(held[m - low], "ctx", shards, low)
 
-    qo = [(from_core[0], across(packed[1], from_core[0], heads, [merged] + from_core[1:]))]
+    early = [merged] + from_core
+    qo = [(from_core[0], across(packed[1], from_core[0], heads, early))]
     late = [held[m] for m in range(1, shards - 1)] + [qo[0][1]]
     for g in range(1, kv_heads):
-        qo.append((from_core[g], across(packed[2 * g + 1], from_core[g], heads, late)))
-
-    dq = []
-    own = []
-    near = []
-    far = []
+        qo.append((from_core[g], across(packed[2 * g + 1], from_core[g], heads, early, late)))
+
+    all_rows = tokens * GROUP
+    saved = []
     for g in range(kv_heads):
         outs = pl.pallas_call(
             functools.partial(attend_kernel, g, order),
             out_shape=[
-                shape(tokens, GW),
-                shape(tokens, 2 * HD, dtype=jnp.float32),
-                shape(half, 2 * HD, dtype=jnp.float32),
+                shape(slots, all_rows),
+                shape(slots, all_rows),
+                shape(rows, all_rows),
+                shape(rows, all_rows),
+                shape(all_rows, HD),
+                shape(all_rows, HD),
+                shape(HD, slots),
                 shape(half, 2 * HD),
             ],
             in_specs=anywhere(2) + in_vmem(1 + heads + shards + len(qo[g])) + anywhere(g > 0),
-            out_specs=in_vmem(4),
+            out_specs=in_vmem(8),
             scratch_shapes=[
                 pltpu.VMEM((slots + rows, 2 * HD), jnp.bfloat16),
                 pltpu.VMEM((slots + rows, HD), jnp.bfloat16),
-                pltpu.VMEM((HD, slots), jnp.bfloat16),
                 pltpu.VMEM((rows, 2 * GW), jnp.bfloat16),
                 pltpu.SemaphoreType.DMA((2,)),
             ],
             compiler_params=params(24),
             cost_estimate=pl.CostEstimate(
-                flops=10 * tokens * GROUP * (slots + rows) * HD,
-                bytes_accessed=4 * 2**20,
-                transcendentals=tokens * GROUP * slots,
+                flops=6 * all_rows * (slots + rows) * HD,
+                bytes_accessed=8 * 2**20,
+                transcendentals=all_rows * slots,
             ),
             name="attend",
-        )(queries, grad_out, hide, *kv, *[held[m] for m in order], *qo[g], *own[-1:])
-        dq.append(outs[0])
+        )(
+            queries,
+            grad_out,
+            hide,
+            *kv,
+            *[held[m] for m in order],
+            *qo[g],
+            *([saved[-1][2]] if g else []),
+        )
+        saved.append(outs)
+    far = [swap(outs[7], "ctx", shards, 1) for outs in saved]
+    near = []
+    own = []
+    dq = []
+    for g in range(kv_heads):
+        outs = pl.pallas_call(
+            functools.partial(finish_kernel, g, heads),
+            out_shape=[
+                shape(half, 2 * HD, dtype=jnp.float32),
+                shape(tokens, 2 * HD, dtype=jnp.float32),
+                shape(tokens, GW),
+            ],
+            in_specs=in_vmem(7) + anywhere(1) + in_vmem(heads),
+            out_specs=in_vmem(3),
+            compiler_params=params(16),
+            cost_estimate=pl.CostEstimate(
+                flops=4 * all_rows * (slots + rows) * HD,
+                bytes_accessed=8 * 2**20,
+                transcendentals=0,
+            ),
+            name="finish",
+        )(*saved[g][:7], saved[-1][2], *kv)
+        near.append(outs[0])
         own.append(outs[1])
-        near.append(outs[2])
-        far.append(swap(outs[3], "ctx", shards, 1))
+        dq.append(outs[2])
 
     spread_args = []
     for g in range(kv_heads):
@@ -413,11 +460,11 @@
             keep, send = pl.pallas_call(
                 add_kernel,
                 out_shape=[shape(count, 2 * HD, dtype=jnp.float32), shape(count, 2 * HD)],
-                in_specs=in_vmem(2) + anywhere(1),
+                in_specs=in_vmem(2),
                 out_specs=in_vmem(2),
                 compiler_params=params(8),
                 name="add",
-            )(keep, received, own[-1])
+            )(keep, received)
             received = swap(send, "ctx", shards, step)
             step *= 2
         spread_args += [keep, received, own[g]]

time: 64 us -> 61.7 us (0.964)
  waiting for transfers between devices: 22.3 us -> 19.6 us
  Pallas kernels: 14.6 us -> 15.3 us
    pallas_call x0 -> x2, Pallas kernels: none -> 2.98 us  [local(): pl.pallas_call(functools.partial(finish_kernel, g, heads), out_shape=[sha...]
    ppermute x20, waiting for transfers between devices: 22.3 us -> 19.6 us  [swap(): return lax.ppermute(x, axis, [(i, i ^ m) for i in range(size)])]
    pallas_call x2, Pallas kernels: 11.8 us -> 9.53 us  [local(): pl.pallas_call(functools.partial(attend_kernel, g, order), out_shape=[sha...]
  transfers between devices with their start and end apart: 20 -> 20, of which waited for: 12 -> 12; matrix products, arithmetic and copies ran while one was open for 1% -> 2% of each run, Pallas kernels for 20% -> 22%
where the time goes in v6:
time: 61.7 us; the launch traced here: 61.4 us
  starting transfers between devices  20.7 us (34%)
  waiting for transfers between devices  19.6 us (32%)
  Pallas kernels  15.3 us (25%)
  local copies, waits for them, and re-layouts  4.05 us (7%)
  other arithmetic  0.94 us (2%)
  between operations  0.78 us (1%)
    ppermute x20, starting transfers between devices, swap(): return lax.ppermute(x, axis, [(i, i ^ m) for i in range(size)])  20.7 us
    ppermute x20, waiting for transfers between devices, swap(): return lax.ppermute(x, axis, [(i, i ^ m) for i in range(size)])  19.6 us
    pallas_call x2, Pallas kernels, local(): pl.pallas_call(functools.partial(attend_kernel, g, order), out_shape=[sha...  9.53 us
    unnamed x14, local copies, waits for them, and re-layouts  4.05 us
    pallas_call x2, Pallas kernels, local(): pl.pallas_call(functools.partial(finish_kernel, g, heads), out_shape=[sha...  2.98 us
  transfers between devices with their start and end apart: 20, of which 12 were waited for; matrix products, arithmetic and copies ran while one was open for 2% of the time, Pallas kernels for 22%

profile of v6, /device:TPU:0, one launch (start us, length us, event | category | flops | bytes accessed | tf_op | source)
XLA Modules:
  0.0 61.4 jit_solution(16747365010020655611)
XLA Ops:
  0.6 0.9 %copy-done.4 = bf16[48,1024]{1,0:T(8,128)(2,1)S(1)} copy-done((bf16[48,1024]{1,0:T(8,128)(2,1)S(1)}, bf16[48,1024]{1,0:T(8,128)(2,1)}, u32[]{:S(2)}) %copy-start.4) | copy-done | bytes 98328
  1.5 0.9 %copy-done.5 = bf16[48,1024]{1,0:T(8,128)(2,1)S(1)} copy-done((bf16[48,1024]{1,0:T(8,128)(2,1)S(1)}, bf16[48,1024]{1,0:T(8,128)(2,1)}, u32[]{:S(2)}) %copy-start.5) | copy-done | bytes 98328
  3.0 2.6 %collective-permute-start.1 = (bf16[48,512]{1,0:T(8,128)(2,1)S(1)}, bf16[48,512]{1,0:T(8,128)(2,1)S(1)}, u32[]{:S(2)}, u32[]{:S(2)}) collective-permute-start(bf16[48,512]{1,0:T(8,128)(2,1)S(1)} %get-tuple-element.47), channel_id=1, source_target_pairs={{0,2},{1,3},{2,0},{3,1},{4,6},{5,7},{6,4},{7,5},{8,10},{9,11},{10,... | collective-permute-start | bytes 147464 | tf_op jit(solution)/shard_map/ppermute | solution.py:286
  5.6 1.1 %copy-done = bf16[48,8192]{1,0:T(8,128)(2,1)S(1)} copy-done((bf16[48,8192]{1,0:T(8,128)(2,1)S(1)}, bf16[48,8192]{1,0:T(8,128)(2,1)}, u32[]{:S(2)}) %copy-start) | copy-done | bytes 786456
  6.7 1.1 %copy-done.2 = bf16[48,8192]{1,0:T(8,128)(2,1)S(1)} copy-done((bf16[48,8192]{1,0:T(8,128)(2,1)S(1)}, bf16[48,8192]{1,0:T(8,128)(2,1)}, u32[]{:S(2)}) %copy-start.2) | copy-done | bytes 786456
  8.3 1.0 %collective-permute-done.2.refs_3_ = bf16[48,512]{1,0:T(8,128)(2,1)S(1)} collective-permute-done((bf16[48,512]{1,0:T(8,128)(2,1)S(1)}, bf16[48,512]{1,0:T(8,128)(2,1)S(1)}, u32[]{:S(2)}, u32[]{:S(2)}) %collective-permute-start.2) | collective-permute-done | bytes 49184 | tf_op jit(solution)/shard_map/ppermute | solution.py:286
  10.0 1.0 %collective-permute-done.11.refs_2_.core_ref.refs_12_ = bf16[96,2048]{1,0:T(8,128)(2,1)S(1)} collective-permute-done((bf16[96,2048]{1,0:T(8,128)(2,1)S(1)}, bf16[96,2048]{1,0:T(8,128)(2,1)S(1)}, u32[]{:S(2)}, u32[]{:S(2)}) %collective-permute-start.11) | collective-permute-done | bytes 393248 | tf_op jit(solution)/shard_map/ppermute | solution.py:286
  11.0 0.6 collective-permute-done.10.core_ref.refs_1_.refs_12_
  12.0 1.1 %collective-permute-start.12 = (bf16[96,2048]{1,0:T(8,128)(2,1)S(1)}, bf16[96,2048]{1,0:T(8,128)(2,1)S(1)}, u32[]{:S(2)}, u32[]{:S(2)}) collective-permute-start(bf16[96,2048]{1,0:T(8,128)(2,1)S(1)} %join.2), channel_id=1, source_target_pairs={{0,2},{1,3},{2,0},{3,1},{4,6},{5,7},{6,4},{7,5},{8,10},{9,11},{10,... | collective-permute-start | bytes 1179656 | tf_op jit(solution)/shard_map/ppermute | solution.py:286
  13.1 1.6 %collective-permute-start.4 = (bf16[96,512]{1,0:T(8,128)(2,1)S(1)}, bf16[96,512]{1,0:T(8,128)(2,1)S(1)}, u32[]{:S(2)}, u32[]{:S(2)}) collective-permute-start(bf16[96,512]{1,0:T(8,128)(2,1)S(1)} %get-tuple-element.51.refs_0_.refs_4_), channel_id=1, source_target_pairs={{0,8},{4,12},{8,0},{12,4},{16,24},{20,28},{24,16},{28,20},{1,9},{5... | collective-permute-start | bytes 294920 | tf_op jit(solution)/shard_map/ppermute | solution.py:286
  14.7 2.6 %collective-permute-start.3 = (bf16[96,512]{1,0:T(8,128)(2,1)S(1)}, bf16[96,512]{1,0:T(8,128)(2,1)S(1)}, u32[]{:S(2)}, u32[]{:S(2)}) collective-permute-start(bf16[96,512]{1,0:T(8,128)(2,1)S(1)} %get-tuple-element.51.refs_0_.refs_4_), channel_id=1, source_target_pairs={{0,16},{4,20},{8,24},{12,28},{16,0},{20,4},{24,8},{28,12},{1,17},{... | collective-permute-start | bytes 294920 | tf_op jit(solution)/shard_map/ppermute | solution.py:286
  17.3 1.5 %collective-permute-start.6 = (bf16[96,512]{1,0:T(8,128)(2,1)S(1)}, bf16[96,512]{1,0:T(8,128)(2,1)S(1)}, u32[]{:S(2)}, u32[]{:S(2)}) collective-permute-start(bf16[96,512]{1,0:T(8,128)(2,1)S(1)} %get-tuple-element.51.refs_0_.refs_4_), channel_id=1, source_target_pairs={{0,4},{4,0},{8,12},{12,8},{16,20},{20,16},{24,28},{28,24},{1,5},{5... | collective-permute-start | bytes 294920 | tf_op jit(solution)/shard_map/ppermute | solution.py:286
  19.3 2.8 %collective-permute-done.3.refs_5_.refs_4_ = bf16[96,512]{1,0:T(8,128)(2,1)S(1)} collective-permute-done((bf16[96,512]{1,0:T(8,128)(2,1)S(1)}, bf16[96,512]{1,0:T(8,128)(2,1)S(1)}, u32[]{:S(2)}, u32[]{:S(2)}) %collective-permute-start.3) | collective-permute-done | bytes 98336 | tf_op jit(solution)/shard_map/ppermute | solution.py:286
  22.2 1.5 %collective-permute-start.7 = (bf16[96,512]{1,0:T(8,128)(2,1)S(1)}, bf16[96,512]{1,0:T(8,128)(2,1)S(1)}, u32[]{:S(2)}, u32[]{:S(2)}) collective-permute-start(bf16[96,512]{1,0:T(8,128)(2,1)S(1)} %collective-permute-done.3.refs_5_.refs_4_), channel_id=1, source_target_pairs={{0,4},{4,0},{8,12},{12,8},{16,20},{20,16},{24,28},{28,24},{1,5},{5... | collective-permute-start | bytes 294920 | tf_op jit(solution)/shard_map/ppermute | solution.py:286
  24.8 2.0 %collective-permute-done.7.refs_9_.refs_5_ = bf16[96,512]{1,0:T(8,128)(2,1)S(1)} collective-permute-done((bf16[96,512]{1,0:T(8,128)(2,1)S(1)}, bf16[96,512]{1,0:T(8,128)(2,1)S(1)}, u32[]{:S(2)}, u32[]{:S(2)}) %collective-permute-start.7) | collective-permute-done | bytes 98336 | tf_op jit(solution)/shard_map/ppermute | solution.py:286
  26.8 1.5 %collective-permute-done.5.refs_7_.refs_6_ = bf16[96,512]{1,0:T(8,128)(2,1)S(1)} collective-permute-done((bf16[96,512]{1,0:T(8,128)(2,1)S(1)}, bf16[96,512]{1,0:T(8,128)(2,1)S(1)}, u32[]{:S(2)}, u32[]{:S(2)}) %collective-permute-start.5) | collective-permute-done | bytes 98336 | tf_op jit(solution)/shard_map/ppermute | solution.py:286
  28.3 0.9 %collective-permute-start.13 = (bf16[96,2048]{1,0:T(8,128)(2,1)S(1)}, bf16[96,2048]{1,0:T(8,128)(2,1)S(1)}, u32[]{:S(2)}, u32[]{:S(2)}) collective-permute-start(bf16[96,2048]{1,0:T(8,128)(2,1)S(1)} %gate.5), channel_id=1, source_target_pairs={{0,2},{1,3},{2,0},{3,1},{4,6},{5,7},{6,4},{7,5},{8,10},{9,11},{10,... | collective-permute-start | bytes 1179656 | tf_op jit(solution)/shard_map/ppermute | solution.py:286
  29.7 4.1 %collective-permute-done.9.refs_11_ = bf16[96,512]{1,0:T(8,128)(2,1)S(1)} collective-permute-done((bf16[96,512]{1,0:T(8,128)(2,1)S(1)}, bf16[96,512]{1,0:T(8,128)(2,1)S(1)}, u32[]{:S(2)}, u32[]{:S(2)}) %collective-permute-start.9) | collective-permute-done | bytes 98336 | tf_op jit(solution)/shard_map/ppermute | solution.py:286
  33.8 4.7 %attend.2 = (bf16[768,1536]{1,0:T(8,128)(2,1)S(1)}, bf16[768,1536]{1,0:T(8,128)(2,1)S(1)}, bf16[48,1536]{1,0:T(8,128)(2,1)S(1)}, bf16[48,1536]{1,0:T(8,128)(2,1)...) custom-call(bf16[48,8192]{1,0:T(8,128)(2,1)S(1)} %copy-done.1, ...), custom_call_target="tpu_custom_call" | custom-call | flops 962592768 | bytes 8388608 | tf_op jit(solution)/shard_map/attend/pallas_call | solution.py:392
  39.1 4.9 %attend.3 = (bf16[768,1536]{1,0:T(8,128)(2,1)S(1)}, bf16[768,1536]{1,0:T(8,128)(2,1)S(1)}, bf16[48,1536]{1,0:T(8,128)(2,1)S(1)}, bf16[48,1536]{1,0:T(8,128)(2,1)...) custom-call(bf16[48,8192]{1,0:T(8,128)(2,1)S(1)} %copy-done.1, ...), custom_call_target="tpu_custom_call" | custom-call | flops 962592768 | bytes 8388608 | tf_op jit(solution)/shard_map/attend/pallas_call | solution.py:392
  43.9 1.6 %collective-permute-start.17 = (bf16[384,256]{1,0:T(8,128)(2,1)S(1)}, bf16[384,256]{1,0:T(8,128)(2,1)S(1)}, u32[]{:S(2)}, u32[]{:S(2)}) collective-permute-start(bf16[384,256]{1,0:T(8,128)(2,1)S(1)} %get-tuple-element.79), channel_id=1, source_target_pairs={{0,4},{4,0},{8,12},{12,8},{16,20},{20,16},{24,28},{28,24},{1,5},{5... | collective-permute-start | bytes 589832 | tf_op jit(solution)/shard_map/ppermute | solution.py:286
  45.5 1.5 %finish.2 = (f32[384,256]{1,0:T(8,128)S(1)}, f32[192,256]{1,0:T(8,128)S(1)}, bf16[192,1024]{1,0:T(8,128)(2,1)S(1)}) custom-call(bf16[768,1536]{1,0:T(8,128)(2,1)S(1)} %get-tuple-element.54.p_ref, bf16[768,1536]{1,0:T(8,128)(2,1)S(1)} %get-tuple-element.55.ds_ref, bf16[48,1536]{1,0:T(8,128)(2,1)S(1)} %get-tuple-element.56.refs_14_.own_p_ref, ...), custom_call_target="tpu_custom_call" | custom-call | flops 641728512 | bytes 8388608 | tf_op jit(solution)/shard_map/finish/pallas_call | solution.py:434
  47.5 1.5 %finish.3 = (f32[384,256]{1,0:T(8,128)S(1)}, f32[192,256]{1,0:T(8,128)S(1)}, bf16[192,1024]{1,0:T(8,128)(2,1)S(1)}) custom-call(bf16[768,1536]{1,0:T(8,128)(2,1)S(1)} %get-tuple-element.64.p_ref, bf16[768,1536]{1,0:T(8,128)(2,1)S(1)} %get-tuple-element.65.ds_ref, bf16[48,1536]{1,0:T(8,128)(2,1)S(1)} %get-tuple-element.62.after_ref.own_p_ref, ...), custom_call_target="tpu_custom_call" | custom-call | flops 641728512 | bytes 8388608 | tf_op jit(solution)/shard_map/finish/pallas_call | solution.py:434
  49.0 0.7 %collective-permute-done.17.far_ref = bf16[384,256]{1,0:T(8,128)(2,1)S(1)} collective-permute-done((bf16[384,256]{1,0:T(8,128)(2,1)S(1)}, bf16[384,256]{1,0:T(8,128)(2,1)S(1)}, u32[]{:S(2)}, u32[]{:S(2)}) %collective-permute-start.17) | collective-permute-done | bytes 196640 | tf_op jit(solution)/shard_map/ppermute | solution.py:286
  49.7 1.1 %collective-permute-start.18 = (bf16[192,256]{1,0:T(8,128)(2,1)S(1)}, bf16[192,256]{1,0:T(8,128)(2,1)S(1)}, u32[]{:S(2)}, u32[]{:S(2)}) collective-permute-start(bf16[192,256]{1,0:T(8,128)(2,1)S(1)} %get-tuple-element.81), channel_id=1, source_target_pairs={{0,8},{4,12},{8,0},{12,4},{16,24},{20,28},{24,16},{28,20},{1,9},{5... | collective-permute-start | bytes 294920 | tf_op jit(solution)/shard_map/ppermute | solution.py:286
  50.8 1.0 %collective-permute-done.15.far_ref = bf16[192,256]{1,0:T(8,128)(2,1)S(1)} collective-permute-done((bf16[192,256]{1,0:T(8,128)(2,1)S(1)}, bf16[192,256]{1,0:T(8,128)(2,1)S(1)}, u32[]{:S(2)}, u32[]{:S(2)}) %collective-permute-start.15) | collective-permute-done | bytes 98336 | tf_op jit(solution)/shard_map/ppermute | solution.py:286
  51.8 1.1 %collective-permute-start.16 = (bf16[96,256]{1,0:T(8,128)(2,1)S(1)}, bf16[96,256]{1,0:T(8,128)(2,1)S(1)}, u32[]{:S(2)}, u32[]{:S(2)}) collective-permute-start(bf16[96,256]{1,0:T(8,128)(2,1)S(1)} %get-tuple-element.76), channel_id=1, source_target_pairs={{0,16},{4,20},{8,24},{12,28},{16,0},{20,4},{24,8},{28,12},{1,17},{... | collective-permute-start | bytes 147464 | tf_op jit(solution)/shard_map/ppermute | solution.py:286
  52.9 1.9 %collective-permute-done.18.far_ref = bf16[192,256]{1,0:T(8,128)(2,1)S(1)} collective-permute-done((bf16[192,256]{1,0:T(8,128)(2,1)S(1)}, bf16[192,256]{1,0:T(8,128)(2,1)S(1)}, u32[]{:S(2)}, u32[]{:S(2)}) %collective-permute-start.18) | collective-permute-done | bytes 98336 | tf_op jit(solution)/shard_map/ppermute | solution.py:286
  54.8 1.7 %collective-permute-start.19 = (bf16[96,256]{1,0:T(8,128)(2,1)S(1)}, bf16[96,256]{1,0:T(8,128)(2,1)S(1)}, u32[]{:S(2)}, u32[]{:S(2)}) collective-permute-start(bf16[96,256]{1,0:T(8,128)(2,1)S(1)} %get-tuple-element.83), channel_id=1, source_target_pairs={{0,16},{4,20},{8,24},{12,28},{16,0},{20,4},{24,8},{28,12},{1,17},{... | collective-permute-start | bytes 147464 | tf_op jit(solution)/shard_map/ppermute | solution.py:286
  56.5 0.9 %pad_maximum_fusion = bf16[192,2048]{1,0:T(8,128)(2,1)} fusion(bf16[192,1024]{1,0:T(8,128)(2,1)S(1)} %get-tuple-element.70, bf16[192,1024]{1,0:T(8,128)(2,1)S(1)} %get-tuple-element.63), kind=kLoop, calls=%fused_computation | loop fusion | flops 1572864 | bytes 1572864 | tf_op jit(solution)/shard_map/concatenate | solution.py:480
  57.4 3.0 %collective-permute-done.19.refs_4_ = bf16[96,256]{1,0:T(8,128)(2,1)S(1)} collective-permute-done((bf16[96,256]{1,0:T(8,128)(2,1)S(1)}, bf16[96,256]{1,0:T(8,128)(2,1)S(1)}, u32[]{:S(2)}, u32[]{:S(2)}) %collective-permute-start.19) | collective-permute-done | bytes 49184 | tf_op jit(solution)/shard_map/ppermute | solution.py:286
  60.4 1.0 %spread.1 = (bf16[192,256]{1,0:T(8,128)(2,1)}, bf16[192,256]{1,0:T(8,128)(2,1)}) custom-call(s32[2,192]{1,0:T(2,128)S(1)} %copy-done.6, f32[96,256]{1,0:T(8,128)S(1)} %get-tuple-element.75.refs_0_, bf16[96,256]{1,0:T(8,128)(2,1)S(1)} %collective-permute-done.16.refs_1_, f32[192,256]{1,0:T(8,128)S(1)} %get-tuple-element.77.refs_2_, ...), custom_call_target="tpu_custom_call" | custom-call | tf_op jit(solution)/shard_map/spread/pallas_call | solution.py:472
  (40 shorter events, 5.5 us)
Async XLA Ops:
  0.6 0.9 %copy-start.4 = (bf16[48,1024]{1,0:T(8,128)(2,1)S(1)}, bf16[48,1024]{1,0:T(8,128)(2,1)}, u32[]{:S(2)}) copy-start(bf16[48,1024]{1,0:T(8,128)(2,1)} %key_ref.1) | copy-start | bytes 294916
  1.5 0.9 %copy-start.5 = (bf16[48,1024]{1,0:T(8,128)(2,1)S(1)}, bf16[48,1024]{1,0:T(8,128)(2,1)}, u32[]{:S(2)}) copy-start(bf16[48,1024]{1,0:T(8,128)(2,1)} %value_ref.1) | copy-start | bytes 294916
  2.4 7.3 %copy-start.6 = (s32[2,192]{1,0:T(2,128)S(1)}, s32[2,192]{1,0:T(2,128)}, u32[]{:S(2)}) copy-start(s32[2,192]{1,0:T(2,128)} %seg_ref.3) | copy-start | bytes 4612
  2.4 5.8 %collective-permute-start = (bf16[48,512]{1,0:T(8,128)(2,1)S(1)}, bf16[48,512]{1,0:T(8,128)(2,1)S(1)}, u32[]{:S(2)}, u32[]{:S(2)}) collective-permute-start(bf16[48,512]{1,0:T(8,128)(2,1)S(1)} %get-tuple-element.46), channel_id=1, source_target_pairs={{0,1},{1,0},{2,3},{3,2},{4,5},{5,4},{6,7},{7,6},{8,9},{9,8},{10,11... | collective-permute-start | bytes 147464 | tf_op jit(solution)/shard_map/ppermute | solution.py:286
  3.0 5.3 %collective-permute-start.1 = (bf16[48,512]{1,0:T(8,128)(2,1)S(1)}, bf16[48,512]{1,0:T(8,128)(2,1)S(1)}, u32[]{:S(2)}, u32[]{:S(2)}) collective-permute-start(bf16[48,512]{1,0:T(8,128)(2,1)S(1)} %get-tuple-element.47), channel_id=1, source_target_pairs={{0,2},{1,3},{2,0},{3,1},{4,6},{5,7},{6,4},{7,5},{8,10},{9,11},{10,... | collective-permute-start | bytes 147464 | tf_op jit(solution)/shard_map/ppermute | solution.py:286
  5.5 3.7 %collective-permute-start.2 = (bf16[48,512]{1,0:T(8,128)(2,1)S(1)}, bf16[48,512]{1,0:T(8,128)(2,1)S(1)}, u32[]{:S(2)}, u32[]{:S(2)}) collective-permute-start(bf16[48,512]{1,0:T(8,128)(2,1)S(1)} %get-tuple-element.48), channel_id=1, source_target_pairs={{0,3},{1,2},{2,1},{3,0},{4,7},{5,6},{6,5},{7,4},{8,11},{9,10},{10,... | collective-permute-start | bytes 147464 | tf_op jit(solution)/shard_map/ppermute | solution.py:286
  5.6 1.1 %copy-start = (bf16[48,8192]{1,0:T(8,128)(2,1)S(1)}, bf16[48,8192]{1,0:T(8,128)(2,1)}, u32[]{:S(2)}) copy-start(bf16[48,8192]{1,0:T(8,128)(2,1)} %q_ref.3) | copy-start | bytes 2359300
  6.7 1.1 %copy-start.2 = (bf16[48,8192]{1,0:T(8,128)(2,1)S(1)}, bf16[48,8192]{1,0:T(8,128)(2,1)}, u32[]{:S(2)}) copy-start(bf16[48,8192]{1,0:T(8,128)(2,1)} %o_ref.3) | copy-start | bytes 2359300
  9.2 1.7 %collective-permute-start.11 = (bf16[96,2048]{1,0:T(8,128)(2,1)S(1)}, bf16[96,2048]{1,0:T(8,128)(2,1)S(1)}, u32[]{:S(2)}, u32[]{:S(2)}) collective-permute-start(bf16[96,2048]{1,0:T(8,128)(2,1)S(1)} %gate.4), channel_id=1, source_target_pairs={{0,1},{1,0},{2,3},{3,2},{4,5},{5,4},{6,7},{7,6},{8,9},{9,8},{10,11... | collective-permute-start | bytes 1179656 | tf_op jit(solution)/shard_map/ppermute | solution.py:286
  9.4 2.1 %collective-permute-start.10 = (bf16[96,2048]{1,0:T(8,128)(2,1)S(1)}, bf16[96,2048]{1,0:T(8,128)(2,1)S(1)}, u32[]{:S(2)}, u32[]{:S(2)}) collective-permute-start(bf16[96,2048]{1,0:T(8,128)(2,1)S(1)} %gate.3), channel_id=1, source_target_pairs={{0,1},{1,0},{2,3},{3,2},{4,5},{5,4},{6,7},{7,6},{8,9},{9,8},{10,11... | collective-permute-start | bytes 1179656 | tf_op jit(solution)/shard_map/ppermute | solution.py:286
  11.5 22.3 %copy-start.1 = (bf16[48,8192]{1,0:T(8,128)(2,1)S(1)}, bf16[48,8192]{1,0:T(8,128)(2,1)}, u32[]{:S(2)}) copy-start(bf16[48,8192]{1,0:T(8,128)(2,1)} %q_ref.3) | copy-start | bytes 2359300
  11.5 22.3 %copy-start.3 = (bf16[48,8192]{1,0:T(8,128)(2,1)S(1)}, bf16[48,8192]{1,0:T(8,128)(2,1)}, u32[]{:S(2)}) copy-start(bf16[48,8192]{1,0:T(8,128)(2,1)} %o_ref.3) | copy-start | bytes 2359300
  12.0 16.3 %collective-permute-start.12 = (bf16[96,2048]{1,0:T(8,128)(2,1)S(1)}, bf16[96,2048]{1,0:T(8,128)(2,1)S(1)}, u32[]{:S(2)}, u32[]{:S(2)}) collective-permute-start(bf16[96,2048]{1,0:T(8,128)(2,1)S(1)} %join.2), channel_id=1, source_target_pairs={{0,2},{1,3},{2,0},{3,1},{4,6},{5,7},{6,4},{7,5},{8,10},{9,11},{10,... | collective-permute-start | bytes 1179656 | tf_op jit(solution)/shard_map/ppermute | solution.py:286
  13.1 5.7 %collective-permute-start.4 = (bf16[96,512]{1,0:T(8,128)(2,1)S(1)}, bf16[96,512]{1,0:T(8,128)(2,1)S(1)}, u32[]{:S(2)}, u32[]{:S(2)}) collective-permute-start(bf16[96,512]{1,0:T(8,128)(2,1)S(1)} %get-tuple-element.51.refs_0_.refs_4_), channel_id=1, source_target_pairs={{0,8},{4,12},{8,0},{12,4},{16,24},{20,28},{24,16},{28,20},{1,9},{5... | collective-permute-start | bytes 294920 | tf_op jit(solution)/shard_map/ppermute | solution.py:286
  14.7 7.5 %collective-permute-start.3 = (bf16[96,512]{1,0:T(8,128)(2,1)S(1)}, bf16[96,512]{1,0:T(8,128)(2,1)S(1)}, u32[]{:S(2)}, u32[]{:S(2)}) collective-permute-start(bf16[96,512]{1,0:T(8,128)(2,1)S(1)} %get-tuple-element.51.refs_0_.refs_4_), channel_id=1, source_target_pairs={{0,16},{4,20},{8,24},{12,28},{16,0},{20,4},{24,8},{28,12},{1,17},{... | collective-permute-start | bytes 294920 | tf_op jit(solution)/shard_map/ppermute | solution.py:286
  17.3 7.4 %collective-permute-start.6 = (bf16[96,512]{1,0:T(8,128)(2,1)S(1)}, bf16[96,512]{1,0:T(8,128)(2,1)S(1)}, u32[]{:S(2)}, u32[]{:S(2)}) collective-permute-start(bf16[96,512]{1,0:T(8,128)(2,1)S(1)} %get-tuple-element.51.refs_0_.refs_4_), channel_id=1, source_target_pairs={{0,4},{4,0},{8,12},{12,8},{16,20},{20,16},{24,28},{28,24},{1,5},{5... | collective-permute-start | bytes 294920 | tf_op jit(solution)/shard_map/ppermute | solution.py:286
  18.8 6.0 %collective-permute-start.8 = (bf16[96,512]{1,0:T(8,128)(2,1)S(1)}, bf16[96,512]{1,0:T(8,128)(2,1)S(1)}, u32[]{:S(2)}, u32[]{:S(2)}) collective-permute-start(bf16[96,512]{1,0:T(8,128)(2,1)S(1)} %collective-permute-done.4.refs_6_.refs_2_), channel_id=1, source_target_pairs={{0,4},{4,0},{8,12},{12,8},{16,20},{20,16},{24,28},{28,24},{1,5},{5... | collective-permute-start | bytes 294920 | tf_op jit(solution)/shard_map/ppermute | solution.py:286
  22.2 4.6 %collective-permute-start.7 = (bf16[96,512]{1,0:T(8,128)(2,1)S(1)}, bf16[96,512]{1,0:T(8,128)(2,1)S(1)}, u32[]{:S(2)}, u32[]{:S(2)}) collective-permute-start(bf16[96,512]{1,0:T(8,128)(2,1)S(1)} %collective-permute-done.3.refs_5_.refs_4_), channel_id=1, source_target_pairs={{0,4},{4,0},{8,12},{12,8},{16,20},{20,16},{24,28},{28,24},{1,5},{5... | collective-permute-start | bytes 294920 | tf_op jit(solution)/shard_map/ppermute | solution.py:286
  23.7 4.6 %collective-permute-start.5 = (bf16[96,512]{1,0:T(8,128)(2,1)S(1)}, bf16[96,512]{1,0:T(8,128)(2,1)S(1)}, u32[]{:S(2)}, u32[]{:S(2)}) collective-permute-start(bf16[96,512]{1,0:T(8,128)(2,1)S(1)} %collective-permute-done.3.refs_5_.refs_4_), channel_id=1, source_target_pairs={{0,8},{4,12},{8,0},{12,4},{16,24},{20,28},{24,16},{28,20},{1,9},{5... | collective-permute-start | bytes 294920 | tf_op jit(solution)/shard_map/ppermute | solution.py:286
  28.3 10.8 %collective-permute-start.13 = (bf16[96,2048]{1,0:T(8,128)(2,1)S(1)}, bf16[96,2048]{1,0:T(8,128)(2,1)S(1)}, u32[]{:S(2)}, u32[]{:S(2)}) collective-permute-start(bf16[96,2048]{1,0:T(8,128)(2,1)S(1)} %gate.5), channel_id=1, source_target_pairs={{0,2},{1,3},{2,0},{3,1},{4,6},{5,7},{6,4},{7,5},{8,10},{9,11},{10,... | collective-permute-start | bytes 1179656 | tf_op jit(solution)/shard_map/ppermute | solution.py:286
  29.2 4.6 %collective-permute-start.9 = (bf16[96,512]{1,0:T(8,128)(2,1)S(1)}, bf16[96,512]{1,0:T(8,128)(2,1)S(1)}, u32[]{:S(2)}, u32[]{:S(2)}) collective-permute-start(bf16[96,512]{1,0:T(8,128)(2,1)S(1)} %collective-permute-done.5.refs_7_.refs_6_), channel_id=1, source_target_pairs={{0,4},{4,0},{8,12},{12,8},{16,20},{20,16},{24,28},{28,24},{1,5},{5... | collective-permute-start | bytes 294920 | tf_op jit(solution)/shard_map/ppermute | solution.py:286
  38.5 8.5 %collective-permute-start.14 = (bf16[384,256]{1,0:T(8,128)(2,1)S(1)}, bf16[384,256]{1,0:T(8,128)(2,1)S(1)}, u32[]{:S(2)}, u32[]{:S(2)}) collective-permute-start(bf16[384,256]{1,0:T(8,128)(2,1)S(1)} %get-tuple-element.72), channel_id=1, source_target_pairs={{0,4},{4,0},{8,12},{12,8},{16,20},{20,16},{24,28},{28,24},{1,5},{5... | collective-permute-start | bytes 589832 | tf_op jit(solution)/shard_map/ppermute | solution.py:286
  43.9 5.7 %collective-permute-start.17 = (bf16[384,256]{1,0:T(8,128)(2,1)S(1)}, bf16[384,256]{1,0:T(8,128)(2,1)S(1)}, u32[]{:S(2)}, u32[]{:S(2)}) collective-permute-start(bf16[384,256]{1,0:T(8,128)(2,1)S(1)} %get-tuple-element.79), channel_id=1, source_target_pairs={{0,4},{4,0},{8,12},{12,8},{16,20},{20,16},{24,28},{28,24},{1,5},{5... | collective-permute-start | bytes 589832 | tf_op jit(solution)/shard_map/ppermute | solution.py:286
  47.1 4.7 %collective-permute-start.15 = (bf16[192,256]{1,0:T(8,128)(2,1)S(1)}, bf16[192,256]{1,0:T(8,128)(2,1)S(1)}, u32[]{:S(2)}, u32[]{:S(2)}) collective-permute-start(bf16[192,256]{1,0:T(8,128)(2,1)S(1)} %get-tuple-element.74), channel_id=1, source_target_pairs={{0,8},{4,12},{8,0},{12,4},{16,24},{20,28},{24,16},{28,20},{1,9},{5... | collective-permute-start | bytes 294920 | tf_op jit(solution)/shard_map/ppermute | solution.py:286
  49.7 5.1 %collective-permute-start.18 = (bf16[192,256]{1,0:T(8,128)(2,1)S(1)}, bf16[192,256]{1,0:T(8,128)(2,1)S(1)}, u32[]{:S(2)}, u32[]{:S(2)}) collective-permute-start(bf16[192,256]{1,0:T(8,128)(2,1)S(1)} %get-tuple-element.81), channel_id=1, source_target_pairs={{0,8},{4,12},{8,0},{12,4},{16,24},{20,28},{24,16},{28,20},{1,9},{5... | collective-permute-start | bytes 294920 | tf_op jit(solution)/shard_map/ppermute | solution.py:286
  51.8 5.6 %collective-permute-start.16 = (bf16[96,256]{1,0:T(8,128)(2,1)S(1)}, bf16[96,256]{1,0:T(8,128)(2,1)S(1)}, u32[]{:S(2)}, u32[]{:S(2)}) collective-permute-start(bf16[96,256]{1,0:T(8,128)(2,1)S(1)} %get-tuple-element.76), channel_id=1, source_target_pairs={{0,16},{4,20},{8,24},{12,28},{16,0},{20,4},{24,8},{28,12},{1,17},{... | collective-permute-start | bytes 147464 | tf_op jit(solution)/shard_map/ppermute | solution.py:286
  54.8 5.6 %collective-permute-start.19 = (bf16[96,256]{1,0:T(8,128)(2,1)S(1)}, bf16[96,256]{1,0:T(8,128)(2,1)S(1)}, u32[]{:S(2)}, u32[]{:S(2)}) collective-permute-start(bf16[96,256]{1,0:T(8,128)(2,1)S(1)} %get-tuple-element.83), channel_id=1, source_target_pairs={{0,16},{4,20},{8,24},{12,28},{16,0},{20,4},{24,8},{28,12},{1,17},{... | collective-permute-start | bytes 147464 | tf_op jit(solution)/shard_map/ppermute | solution.py:286

commit v7 on v6

--- a/solution.py
+++ b/solution.py
@@ -81,16 +81,14 @@
     pass
 
 
-def join_kernel(own_ref, core_ref, *refs):
+def join_kernel(first_ref, second_ref, *refs):
     out, sems = refs[-2:]
-    rows = own_ref.shape[0]
+    rows = first_ref.shape[0]
     wait_copies(
         run_copies(
             [
-                pltpu.make_async_copy(own_ref, out.at[0:rows, :], sems.at[0]),
-                pltpu.make_async_copy(
-                    core_ref.at[rows : 2 * rows, :], out.at[rows : 2 * rows, :], sems.at[1]
-                ),
+                pltpu.make_async_copy(first_ref, out.at[0:rows, :], sems.at[0]),
+                pltpu.make_async_copy(second_ref, out.at[rows : 2 * rows, :], sems.at[1]),
             ]
         )
     )
@@ -136,7 +134,7 @@
     shards = len(order)
     heads = 4
     kv_pieces, blocks, refs = refs[:heads], refs[heads : heads + shards], refs[heads + shards :]
-    qo_pieces = [(refs[0], 0), (refs[1], 0), (refs[1], 1)]
+    qo_pieces = ((refs[0], g), (refs[1], 0), (refs[1], 1))
     (
         p_ref, ds_ref, own_p_ref, own_ds_ref, qs_ref, os_ref, kt_ref, far_ref,
         kx, vx, mine, sems,
@@ -181,8 +179,8 @@
     for m in list(range(1, heads)) + [0]:
         if m == 0:
             wait_copies(copies)
-        qo, half = qo_pieces[m - 1] if m else (mine, 0)
-        span = slice(half * rows, (half + 1) * rows)
+        qo, part = qo_pieces[m - 1] if m else (mine, 0)
+        span = slice(part * rows, (part + 1) * rows)
         at = pl.ds(pl.multiple_of(lax.bitwise_xor(me, m) * rows, 16), rows)
         chunk = slice(m * width, (m + 1) * width)
         kx[slots : slots + rows, 0:HD] = kv_pieces[m][:, key_at]
@@ -218,10 +216,7 @@
     kt_ref[...] = kx[0:slots, 0:HD].astype(jnp.float32).T.astype(jnp.bfloat16)
 
 
-def finish_kernel(
-    g, heads, p_ref, ds_ref, own_p_ref, own_ds_ref, qs_ref, os_ref, kt_ref, after_ref, *refs
-):
-    kv_pieces, (near_ref, own_ref, dq_ref) = refs[:heads], refs[heads:]
+def terms_kernel(heads, p_ref, ds_ref, own_p_ref, own_ds_ref, qs_ref, os_ref, after_ref, near_ref, own_ref):
     rows = own_p_ref.shape[0]
     near = slice(0, near_ref.shape[0])
     near_ref[:, 0:HD] = SCALE * nn(ds_ref[near, :], qs_ref[...])
@@ -233,11 +228,24 @@
         chunk = slice(m * width, (m + 1) * width)
         own_ref[at, 0:HD] = SCALE * nn(own_ds_ref[:, chunk], qs_ref[chunk, :])
         own_ref[at, HD : 2 * HD] = nn(own_p_ref[:, chunk], os_ref[chunk, :])
-        own_key = kv_pieces[m][:, g * HD : (g + 1) * HD]
-        dq = nn(kt_ref[...], ds_ref[:, chunk]) + tn(own_key, own_ds_ref[:, chunk])
-        dq = (SCALE * dq).T.astype(jnp.bfloat16)
-        for h in range(GROUP):
-            dq_ref[at, h * HD : (h + 1) * HD] = dq[h * rows : (h + 1) * rows]
+
+
+def queries_kernel(heads, *refs):
+    kv_pieces, refs, dq_ref = refs[:heads], refs[heads:-1], refs[-1]
+    me = place()[1]
+    for g in range(len(refs) // 3):
+        ds_ref, own_ds_ref, kt_ref = refs[3 * g : 3 * g + 3]
+        rows = own_ds_ref.shape[0]
+        width = GROUP * rows
+        for m in range(heads):
+            at = pl.ds(pl.multiple_of(lax.bitwise_xor(me, m) * rows, 16), rows)
+            chunk = slice(m * width, (m + 1) * width)
+            own_key = kv_pieces[m][:, g * HD : (g + 1) * HD]
+            dq = nn(kt_ref[...], ds_ref[:, chunk]) + tn(own_key, own_ds_ref[:, chunk])
+            dq = (SCALE * dq).T.astype(jnp.bfloat16)
+            for h in range(GROUP):
+                column = (g * GROUP + h) * HD
+                dq_ref[at, column : column + HD] = dq[h * rows : (h + 1) * rows]
 
 
 def add_kernel(near_ref, far_ref, keep_ref, send_ref):
@@ -298,17 +306,17 @@
     )(value, *after)
 
 
-def across(own, from_core, heads, after, late=()):
-    both = pl.pallas_call(
+def join(first, second, after):
+    rows, columns = first.shape
+    return pl.pallas_call(
         join_kernel,
-        out_shape=shape(*from_core.shape),
+        out_shape=shape(2 * rows, columns),
         in_specs=anywhere(2 + len(after)),
         out_specs=in_vmem(1)[0],
         scratch_shapes=[pltpu.SemaphoreType.DMA((2,))],
         compiler_params=params(2),
         name="join",
-    )(own, from_core, *after)
-    return swap(gate(both, late) if late else both, "head", heads, 2)
+    )(first, second, *after)
 
 
 def bit_reversed(count):
@@ -361,30 +369,33 @@
     )(keys, values)
     kv = [kv_out[0]] + [swap(kv_out[m], "head", heads, m) for m in range(1, heads)]
 
-    jobs = [(GW, [[qo_at(1, g), qo_at(3, g)], [qo_at(2, g)]]) for g in range(kv_heads)]
-    packed = pack(jobs, (queries, grad_out), kv_out[:1], 4, "pack_qo")
-    from_core = [swap(gate(packed[2 * g], kv[1:]), "head", heads, 1) for g in range(kv_heads)]
+    dests = [[qo_at(1, g) for g in range(kv_heads)]]
+    for g in range(kv_heads):
+        dests += [[qo_at(2, g)], [qo_at(3, g)]]
+    packed = pack([(GW, dests)], (queries, grad_out), kv_out[:1], 4, "pack_qo")
+    handed = swap(gate(packed[2], kv[1:]), "head", heads, 1)
 
     merged, hide = pl.pallas_call(
         functools.partial(merge_kernel, heads),
         out_shape=[shape(SLOT_DEV, 2 * kv_width), shape(kv_heads, tokens, HD)],
-        in_specs=in_vmem(1 + heads) + anywhere(1),
+        in_specs=in_vmem(1 + heads),
         out_specs=in_vmem(2),
         scratch_shapes=[pltpu.VMEM((tokens, 2 * kv_width), jnp.bfloat16)],
         compiler_params=params(4),
         name="merge",
-    )(segment_ids, *kv, packed[1])
+    )(segment_ids, *kv)
 
     held = {0: merged}
     for m in range(1, shards):
         low = m & -m
         held[m] = swap(held[m - low], "ctx", shards, low)
-
-    early = [merged] + from_core
-    qo = [(from_core[0], across(packed[1], from_core[0], heads, early))]
-    late = [held[m] for m in range(1, shards - 1)] + [qo[0][1]]
+    from_core = swap(gate(packed[0], [held[shards // 2]]), "head", heads, 1)
+    from_across = [swap(join(packed[1], handed, [merged]), "head", heads, 2)]
     for g in range(1, kv_heads):
-        qo.append((from_core[g], across(packed[2 * g + 1], from_core[g], heads, early, late)))
+        handed = swap(gate(packed[2 * g + 2], [merged]), "head", heads, 1)
+        both = join(packed[2 * g + 1], handed, ())
+        late = [held[m] for m in range(1, shards - 1)] + from_across[-1:]
+        from_across.append(swap(gate(both, late), "head", heads, 2))
 
     all_rows = tokens * GROUP
     saved = []
@@ -401,7 +412,7 @@
                 shape(HD, slots),
                 shape(half, 2 * HD),
             ],
-            in_specs=anywhere(2) + in_vmem(1 + heads + shards + len(qo[g])) + anywhere(g > 0),
+            in_specs=anywhere(2) + in_vmem(3 + heads + shards) + anywhere(g > 0),
             out_specs=in_vmem(8),
             scratch_shapes=[
                 pltpu.VMEM((slots + rows, 2 * HD), jnp.bfloat16),
@@ -422,35 +433,42 @@
             hide,
             *kv,
             *[held[m] for m in order],
-            *qo[g],
+            from_core,
+            from_across[g],
             *([saved[-1][2]] if g else []),
         )
         saved.append(outs)
     far = [swap(outs[7], "ctx", shards, 1) for outs in saved]
     near = []
     own = []
-    dq = []
     for g in range(kv_heads):
         outs = pl.pallas_call(
-            functools.partial(finish_kernel, g, heads),
+            functools.partial(terms_kernel, heads),
             out_shape=[
                 shape(half, 2 * HD, dtype=jnp.float32),
                 shape(tokens, 2 * HD, dtype=jnp.float32),
-                shape(tokens, GW),
             ],
-            in_specs=in_vmem(7) + anywhere(1) + in_vmem(heads),
-            out_specs=in_vmem(3),
+            in_specs=in_vmem(6) + anywhere(1),
+            out_specs=in_vmem(2),
             compiler_params=params(16),
             cost_estimate=pl.CostEstimate(
-                flops=4 * all_rows * (slots + rows) * HD,
-                bytes_accessed=8 * 2**20,
-                transcendentals=0,
+                flops=2 * all_rows * slots * HD, bytes_accessed=2**20, transcendentals=0
             ),
-            name="finish",
-        )(*saved[g][:7], saved[-1][2], *kv)
+            name="terms",
+        )(*saved[g][:6], saved[-1][2])
         near.append(outs[0])
         own.append(outs[1])
-        dq.append(outs[2])
+    dq = pl.pallas_call(
+        functools.partial(queries_kernel, heads),
+        out_shape=shape(tokens, kv_heads * GW),
+        in_specs=in_vmem(heads + 3 * kv_heads),
+        out_specs=in_vmem(1)[0],
+        compiler_params=params(16),
+        cost_estimate=pl.CostEstimate(
+            flops=2 * kv_heads * all_rows * slots * HD, bytes_accessed=2**20, transcendentals=0
+        ),
+        name="queries",
+    )(*kv, *[x for outs in saved for x in (outs[1], outs[3], outs[6])])
 
     spread_args = []
     for g in range(kv_heads):
@@ -477,7 +495,7 @@
         compiler_params=params(12),
         name="spread",
     )(segment_ids, *spread_args)
-    return jnp.concatenate(dq, axis=1), grad_keys, grad_values
+    return dq, grad_keys, grad_values
 
 
 def solution(mesh):

time: 61.7 us -> 61.5 us (level)
  Pallas kernels: 15.3 us -> 16.4 us
  other arithmetic: 0.94 us -> 0 us
  starting transfers between devices: 20.7 us -> 19.9 us
    pallas_call x4 -> x5, Pallas kernels: 3.99 us -> 5.03 us  [the longest x1 2.19 us: local(): pl.pallas_call(functools.partial(queries_kernel, heads), out_shape=shape(...]
    concatenate x1 -> x0, other arithmetic: 0.94 us -> none  [local(): return (jnp.concatenate(dq, axis=1), grad_keys, grad_values)]
    ppermute x20 -> x21, starting transfers between devices: 20.7 us -> 19.9 us  [swap(): return lax.ppermute(x, axis, [(i, i ^ m) for i in range(size)])]
    ppermute x20 -> x21, waiting for transfers between devices: 19.6 us -> 20.2 us  [swap(): return lax.ppermute(x, axis, [(i, i ^ m) for i in range(size)])]
  transfers between devices with their start and end apart: 20 -> 21, of which waited for: 12 -> 10; matrix products, arithmetic and copies ran while one was open for 2% -> 0% of each run, Pallas kernels for 22% -> 24%
where the time goes in v7:
time: 61.5 us; the launch traced here: 61.2 us
  waiting for transfers between devices  20.2 us (33%)
  starting transfers between devices  19.9 us (32%)
  Pallas kernels  16.4 us (27%)
  local copies, waits for them, and re-layouts  4.05 us (7%)
  between operations  0.78 us (1%)
    ppermute x21, waiting for transfers between devices, swap(): return lax.ppermute(x, axis, [(i, i ^ m) for i in range(size)])  20.2 us
    ppermute x21, starting transfers between devices, swap(): return lax.ppermute(x, axis, [(i, i ^ m) for i in range(size)])  19.9 us
    pallas_call x2, Pallas kernels, local(): pl.pallas_call(functools.partial(attend_kernel, g, order), out_shape=[sha...  9.54 us
    unnamed x14, local copies, waits for them, and re-layouts  4.05 us
    pallas_call x1, Pallas kernels, local(): pl.pallas_call(functools.partial(queries_kernel, heads), out_shape=shape(...  2.19 us
    pallas_call x2, Pallas kernels, local(): pl.pallas_call(functools.partial(terms_kernel, heads), out_shape=[shape(h...  1.8 us
  transfers between devices with their start and end apart: 21, of which 10 were waited for; matrix products, arithmetic and copies ran while one was open for 0% of the time, Pallas kernels for 24%

profile of v7, /device:TPU:0, one launch (start us, length us, event | category | flops | bytes accessed | tf_op | source)
XLA Modules:
  0.0 61.2 jit_solution(16669972496780586676)
XLA Ops:
  0.6 0.9 %copy-done.4 = bf16[48,1024]{1,0:T(8,128)(2,1)S(1)} copy-done((bf16[48,1024]{1,0:T(8,128)(2,1)S(1)}, bf16[48,1024]{1,0:T(8,128)(2,1)}, u32[]{:S(2)}) %copy-start.4) | copy-done | bytes 98328
  1.5 0.9 %copy-done.5 = bf16[48,1024]{1,0:T(8,128)(2,1)S(1)} copy-done((bf16[48,1024]{1,0:T(8,128)(2,1)S(1)}, bf16[48,1024]{1,0:T(8,128)(2,1)}, u32[]{:S(2)}) %copy-start.5) | copy-done | bytes 98328
  3.0 2.6 %collective-permute-start.1 = (bf16[48,512]{1,0:T(8,128)(2,1)S(1)}, bf16[48,512]{1,0:T(8,128)(2,1)S(1)}, u32[]{:S(2)}, u32[]{:S(2)}) collective-permute-start(bf16[48,512]{1,0:T(8,128)(2,1)S(1)} %get-tuple-element.46), channel_id=1, source_target_pairs={{0,2},{1,3},{2,0},{3,1},{4,6},{5,7},{6,4},{7,5},{8,10},{9,11},{10,... | collective-permute-start | bytes 147464 | tf_op jit(solution)/shard_map/ppermute | solution.py:294
  5.6 1.1 %copy-done = bf16[48,8192]{1,0:T(8,128)(2,1)S(1)} copy-done((bf16[48,8192]{1,0:T(8,128)(2,1)S(1)}, bf16[48,8192]{1,0:T(8,128)(2,1)}, u32[]{:S(2)}) %copy-start) | copy-done | bytes 786456
  6.7 1.1 %copy-done.2 = bf16[48,8192]{1,0:T(8,128)(2,1)S(1)} copy-done((bf16[48,8192]{1,0:T(8,128)(2,1)S(1)}, bf16[48,8192]{1,0:T(8,128)(2,1)}, u32[]{:S(2)}) %copy-start.2) | copy-done | bytes 786456
  8.3 1.0 %collective-permute-done.2.refs_3_ = bf16[48,512]{1,0:T(8,128)(2,1)S(1)} collective-permute-done((bf16[48,512]{1,0:T(8,128)(2,1)S(1)}, bf16[48,512]{1,0:T(8,128)(2,1)S(1)}, u32[]{:S(2)}, u32[]{:S(2)}) %collective-permute-start.2) | collective-permute-done | bytes 49184 | tf_op jit(solution)/shard_map/ppermute | solution.py:294
  9.7 1.0 %collective-permute-done.11.second_ref = bf16[48,2048]{1,0:T(8,128)(2,1)S(1)} collective-permute-done((bf16[48,2048]{1,0:T(8,128)(2,1)S(1)}, bf16[48,2048]{1,0:T(8,128)(2,1)S(1)}, u32[]{:S(2)}, u32[]{:S(2)}) %collective-permute-start.11) | collective-permute-done | bytes 196640 | tf_op jit(solution)/shard_map/ppermute | solution.py:294
  11.2 1.1 %collective-permute-start.12 = (bf16[96,2048]{1,0:T(8,128)(2,1)S(1)}, bf16[96,2048]{1,0:T(8,128)(2,1)S(1)}, u32[]{:S(2)}, u32[]{:S(2)}) collective-permute-start(bf16[96,2048]{1,0:T(8,128)(2,1)S(1)} %join.2), channel_id=1, source_target_pairs={{0,2},{1,3},{2,0},{3,1},{4,6},{5,7},{6,4},{7,5},{8,10},{9,11},{10,... | collective-permute-start | bytes 1179656 | tf_op jit(solution)/shard_map/ppermute | solution.py:294
  12.3 1.6 %collective-permute-start.4 = (bf16[96,512]{1,0:T(8,128)(2,1)S(1)}, bf16[96,512]{1,0:T(8,128)(2,1)S(1)}, u32[]{:S(2)}, u32[]{:S(2)}) collective-permute-start(bf16[96,512]{1,0:T(8,128)(2,1)S(1)} %get-tuple-element.49.refs_0_.refs_4_.refs_1_), channel_id=1, source_target_pairs={{0,8},{4,12},{8,0},{12,4},{16,24},{20,28},{24,16},{28,20},{1,9},{5... | collective-permute-start | bytes 294920 | tf_op jit(solution)/shard_map/ppermute | solution.py:294
  13.8 2.6 %collective-permute-start.3 = (bf16[96,512]{1,0:T(8,128)(2,1)S(1)}, bf16[96,512]{1,0:T(8,128)(2,1)S(1)}, u32[]{:S(2)}, u32[]{:S(2)}) collective-permute-start(bf16[96,512]{1,0:T(8,128)(2,1)S(1)} %get-tuple-element.49.refs_0_.refs_4_.refs_1_), channel_id=1, source_target_pairs={{0,16},{4,20},{8,24},{12,28},{16,0},{20,4},{24,8},{28,12},{1,17},{... | collective-permute-start | bytes 294920 | tf_op jit(solution)/shard_map/ppermute | solution.py:294
  16.4 1.5 %collective-permute-start.6 = (bf16[96,512]{1,0:T(8,128)(2,1)S(1)}, bf16[96,512]{1,0:T(8,128)(2,1)S(1)}, u32[]{:S(2)}, u32[]{:S(2)}) collective-permute-start(bf16[96,512]{1,0:T(8,128)(2,1)S(1)} %get-tuple-element.49.refs_0_.refs_4_.refs_1_), channel_id=1, source_target_pairs={{0,4},{4,0},{8,12},{12,8},{16,20},{20,16},{24,28},{28,24},{1,5},{5... | collective-permute-start | bytes 294920 | tf_op jit(solution)/shard_map/ppermute | solution.py:294
  18.0 1.0 %collective-permute-start.8 = (bf16[96,512]{1,0:T(8,128)(2,1)S(1)}, bf16[96,512]{1,0:T(8,128)(2,1)S(1)}, u32[]{:S(2)}, u32[]{:S(2)}) collective-permute-start(bf16[96,512]{1,0:T(8,128)(2,1)S(1)} %collective-permute-done.4.refs_6_.refs_2_), channel_id=1, source_target_pairs={{0,4},{4,0},{8,12},{12,8},{16,20},{20,16},{24,28},{28,24},{1,5},{5... | collective-permute-start | bytes 294920 | tf_op jit(solution)/shard_map/ppermute | solution.py:294
  19.0 2.8 %collective-permute-done.3.refs_1_.refs_5_.refs_4_ = bf16[96,512]{1,0:T(8,128)(2,1)S(1)} collective-permute-done((bf16[96,512]{1,0:T(8,128)(2,1)S(1)}, bf16[96,512]{1,0:T(8,128)(2,1)S(1)}, u32[]{:S(2)}, u32[]{:S(2)}) %collective-permute-start.3) | collective-permute-done | bytes 98336 | tf_op jit(solution)/shard_map/ppermute | solution.py:294
  21.8 1.5 %collective-permute-start.7 = (bf16[96,512]{1,0:T(8,128)(2,1)S(1)}, bf16[96,512]{1,0:T(8,128)(2,1)S(1)}, u32[]{:S(2)}, u32[]{:S(2)}) collective-permute-start(bf16[96,512]{1,0:T(8,128)(2,1)S(1)} %collective-permute-done.3.refs_1_.refs_5_.refs_4_), channel_id=1, source_target_pairs={{0,4},{4,0},{8,12},{12,8},{16,20},{20,16},{24,28},{28,24},{1,5},{5... | collective-permute-start | bytes 294920 | tf_op jit(solution)/shard_map/ppermute | solution.py:294
  24.3 2.1 %collective-permute-done.7.refs_9_.refs_5_ = bf16[96,512]{1,0:T(8,128)(2,1)S(1)} collective-permute-done((bf16[96,512]{1,0:T(8,128)(2,1)S(1)}, bf16[96,512]{1,0:T(8,128)(2,1)S(1)}, u32[]{:S(2)}, u32[]{:S(2)}) %collective-permute-start.7) | collective-permute-done | bytes 98336 | tf_op jit(solution)/shard_map/ppermute | solution.py:294
  26.4 1.5 %collective-permute-done.5.refs_7_.refs_6_ = bf16[96,512]{1,0:T(8,128)(2,1)S(1)} collective-permute-done((bf16[96,512]{1,0:T(8,128)(2,1)S(1)}, bf16[96,512]{1,0:T(8,128)(2,1)S(1)}, u32[]{:S(2)}, u32[]{:S(2)}) %collective-permute-start.5) | collective-permute-done | bytes 98336 | tf_op jit(solution)/shard_map/ppermute | solution.py:294
  27.9 1.0 %collective-permute-start.14 = (bf16[96,2048]{1,0:T(8,128)(2,1)S(1)}, bf16[96,2048]{1,0:T(8,128)(2,1)S(1)}, u32[]{:S(2)}, u32[]{:S(2)}) collective-permute-start(bf16[96,2048]{1,0:T(8,128)(2,1)S(1)} %gate.7), channel_id=1, source_target_pairs={{0,2},{1,3},{2,0},{3,1},{4,6},{5,7},{6,4},{7,5},{8,10},{9,11},{10,... | collective-permute-start | bytes 1179656 | tf_op jit(solution)/shard_map/ppermute | solution.py:294
  29.5 4.1 %collective-permute-done.9.refs_11_ = bf16[96,512]{1,0:T(8,128)(2,1)S(1)} collective-permute-done((bf16[96,512]{1,0:T(8,128)(2,1)S(1)}, bf16[96,512]{1,0:T(8,128)(2,1)S(1)}, u32[]{:S(2)}, u32[]{:S(2)}) %collective-permute-start.9) | collective-permute-done | bytes 98336 | tf_op jit(solution)/shard_map/ppermute | solution.py:294
  33.6 4.7 %attend.2 = (bf16[768,1536]{1,0:T(8,128)(2,1)S(1)}, bf16[768,1536]{1,0:T(8,128)(2,1)S(1)}, bf16[48,1536]{1,0:T(8,128)(2,1)S(1)}, bf16[48,1536]{1,0:T(8,128)(2,1)...) custom-call(bf16[48,8192]{1,0:T(8,128)(2,1)S(1)} %copy-done.1, ...), custom_call_target="tpu_custom_call" | custom-call | flops 962592768 | bytes 8388608 | tf_op jit(solution)/shard_map/attend/pallas_call | solution.py:403
  38.3 0.6 collective-permute-start.15
  38.9 4.8 %attend.3 = (bf16[768,1536]{1,0:T(8,128)(2,1)S(1)}, bf16[768,1536]{1,0:T(8,128)(2,1)S(1)}, bf16[48,1536]{1,0:T(8,128)(2,1)S(1)}, bf16[48,1536]{1,0:T(8,128)(2,1)...) custom-call(bf16[48,8192]{1,0:T(8,128)(2,1)S(1)} %copy-done.1, ...), custom_call_target="tpu_custom_call" | custom-call | flops 962592768 | bytes 8388608 | tf_op jit(solution)/shard_map/attend/pallas_call | solution.py:403
  43.7 1.6 %collective-permute-start.18 = (bf16[384,256]{1,0:T(8,128)(2,1)S(1)}, bf16[384,256]{1,0:T(8,128)(2,1)S(1)}, u32[]{:S(2)}, u32[]{:S(2)}) collective-permute-start(bf16[384,256]{1,0:T(8,128)(2,1)S(1)} %get-tuple-element.77), channel_id=1, source_target_pairs={{0,4},{4,0},{8,12},{12,8},{16,20},{20,16},{24,28},{28,24},{1,5},{5... | collective-permute-start | bytes 589832 | tf_op jit(solution)/shard_map/ppermute | solution.py:294
  45.3 0.9 %terms.2 = (f32[384,256]{1,0:T(8,128)S(1)}, f32[192,256]{1,0:T(8,128)S(1)}) custom-call(bf16[768,1536]{1,0:T(8,128)(2,1)S(1)} %get-tuple-element.62.p_ref, bf16[768,1536]{1,0:T(8,128)(2,1)S(1)} %get-tuple-element.53.refs_4_.ds_ref, bf16[48,1536]{1,0:T(8,128)(2,1)S(1)} %get-tuple-element.58.refs_14_.own_p_ref, ...), custom_call_target="tpu_custom_call" | custom-call | flops 301989888 | bytes 1048576 | tf_op jit(solution)/shard_map/terms/pallas_call | solution.py:445
  46.8 0.9 %terms.3 = (f32[384,256]{1,0:T(8,128)S(1)}, f32[192,256]{1,0:T(8,128)S(1)}) custom-call(bf16[768,1536]{1,0:T(8,128)(2,1)S(1)} %get-tuple-element.73.p_ref, bf16[768,1536]{1,0:T(8,128)(2,1)S(1)} %get-tuple-element.59.refs_7_.ds_ref, bf16[48,1536]{1,0:T(8,128)(2,1)S(1)} %get-tuple-element.65.after_ref.own_p_ref, ...), custom_call_target="tpu_custom_call" | custom-call | flops 301989888 | bytes 1048576 | tf_op jit(solution)/shard_map/terms/pallas_call | solution.py:445
  47.7 1.7 %collective-permute-done.18.far_ref = bf16[384,256]{1,0:T(8,128)(2,1)S(1)} collective-permute-done((bf16[384,256]{1,0:T(8,128)(2,1)S(1)}, bf16[384,256]{1,0:T(8,128)(2,1)S(1)}, u32[]{:S(2)}, u32[]{:S(2)}) %collective-permute-start.18) | collective-permute-done | bytes 196640 | tf_op jit(solution)/shard_map/ppermute | solution.py:294
  50.0 1.4 %collective-permute-done.16.far_ref = bf16[192,256]{1,0:T(8,128)(2,1)S(1)} collective-permute-done((bf16[192,256]{1,0:T(8,128)(2,1)S(1)}, bf16[192,256]{1,0:T(8,128)(2,1)S(1)}, u32[]{:S(2)}, u32[]{:S(2)}) %collective-permute-start.16) | collective-permute-done | bytes 98336 | tf_op jit(solution)/shard_map/ppermute | solution.py:294
  51.5 1.3 %collective-permute-start.17 = (bf16[96,256]{1,0:T(8,128)(2,1)S(1)}, bf16[96,256]{1,0:T(8,128)(2,1)S(1)}, u32[]{:S(2)}, u32[]{:S(2)}) collective-permute-start(bf16[96,256]{1,0:T(8,128)(2,1)S(1)} %get-tuple-element.71), channel_id=1, source_target_pairs={{0,16},{4,20},{8,24},{12,28},{16,0},{20,4},{24,8},{28,12},{1,17},{... | collective-permute-start | bytes 147464 | tf_op jit(solution)/shard_map/ppermute | solution.py:294
  52.7 2.0 %collective-permute-done.19.far_ref = bf16[192,256]{1,0:T(8,128)(2,1)S(1)} collective-permute-done((bf16[192,256]{1,0:T(8,128)(2,1)S(1)}, bf16[192,256]{1,0:T(8,128)(2,1)S(1)}, u32[]{:S(2)}, u32[]{:S(2)}) %collective-permute-start.19) | collective-permute-done | bytes 98336 | tf_op jit(solution)/shard_map/ppermute | solution.py:294
  54.7 0.7 %collective-permute-start.20 = (bf16[96,256]{1,0:T(8,128)(2,1)S(1)}, bf16[96,256]{1,0:T(8,128)(2,1)S(1)}, u32[]{:S(2)}, u32[]{:S(2)}) collective-permute-start(bf16[96,256]{1,0:T(8,128)(2,1)S(1)} %get-tuple-element.81), channel_id=1, source_target_pairs={{0,16},{4,20},{8,24},{12,28},{16,0},{20,4},{24,8},{28,12},{1,17},{... | collective-permute-start | bytes 147464 | tf_op jit(solution)/shard_map/ppermute | solution.py:294
  55.4 2.2 %queries.1 = bf16[192,2048]{1,0:T(8,128)(2,1)} custom-call(bf16[48,512]{1,0:T(8,128)(2,1)S(1)} %get-tuple-element.44.refs_0_.refs_2_, bf16[48,512]{1,0:T(8,128)(2,1)S(1)} %collective-permute-done.refs_1_, bf16[48,512]{1,0:T(8,128)(2,1)S(1)} %collective-permute-done.1.refs_2_, bf16[48,512]{1,0:T(8,128)(2,1)S(1)} %collective-permute-done.2.refs_3_, ...), custom_call_target="tpu_custom_call" | custom-call | flops 603979776 | bytes 1048576 | tf_op jit(solution)/shard_map/queries/pallas_call | solution.py:461
  57.6 2.6 %collective-permute-done.20.refs_4_ = bf16[96,256]{1,0:T(8,128)(2,1)S(1)} collective-permute-done((bf16[96,256]{1,0:T(8,128)(2,1)S(1)}, bf16[96,256]{1,0:T(8,128)(2,1)S(1)}, u32[]{:S(2)}, u32[]{:S(2)}) %collective-permute-start.20) | collective-permute-done | bytes 49184 | tf_op jit(solution)/shard_map/ppermute | solution.py:294
  60.2 1.0 %spread.1 = (bf16[192,256]{1,0:T(8,128)(2,1)}, bf16[192,256]{1,0:T(8,128)(2,1)}) custom-call(s32[2,192]{1,0:T(2,128)S(1)} %copy-done.6, f32[96,256]{1,0:T(8,128)S(1)} %get-tuple-element.70.refs_0_, bf16[96,256]{1,0:T(8,128)(2,1)S(1)} %collective-permute-done.17.refs_1_, f32[192,256]{1,0:T(8,128)S(1)} %get-tuple-element.72.refs_2_, ...), custom_call_target="tpu_custom_call" | custom-call | tf_op jit(solution)/shard_map/spread/pallas_call | solution.py:490
  (43 shorter events, 4.7 us)
Async XLA Ops:
  0.6 0.9 %copy-start.4 = (bf16[48,1024]{1,0:T(8,128)(2,1)S(1)}, bf16[48,1024]{1,0:T(8,128)(2,1)}, u32[]{:S(2)}) copy-start(bf16[48,1024]{1,0:T(8,128)(2,1)} %key_ref.1) | copy-start | bytes 294916
  1.5 0.9 %copy-start.5 = (bf16[48,1024]{1,0:T(8,128)(2,1)S(1)}, bf16[48,1024]{1,0:T(8,128)(2,1)}, u32[]{:S(2)}) copy-start(bf16[48,1024]{1,0:T(8,128)(2,1)} %value_ref.1) | copy-start | bytes 294916
  2.4 7.0 %copy-start.6 = (s32[2,192]{1,0:T(2,128)S(1)}, s32[2,192]{1,0:T(2,128)}, u32[]{:S(2)}) copy-start(s32[2,192]{1,0:T(2,128)} %seg_ref.3) | copy-start | bytes 4612
  2.4 5.8 %collective-permute-start = (bf16[48,512]{1,0:T(8,128)(2,1)S(1)}, bf16[48,512]{1,0:T(8,128)(2,1)S(1)}, u32[]{:S(2)}, u32[]{:S(2)}) collective-permute-start(bf16[48,512]{1,0:T(8,128)(2,1)S(1)} %get-tuple-element.45), channel_id=1, source_target_pairs={{0,1},{1,0},{2,3},{3,2},{4,5},{5,4},{6,7},{7,6},{8,9},{9,8},{10,11... | collective-permute-start | bytes 147464 | tf_op jit(solution)/shard_map/ppermute | solution.py:294
  3.0 5.3 %collective-permute-start.1 = (bf16[48,512]{1,0:T(8,128)(2,1)S(1)}, bf16[48,512]{1,0:T(8,128)(2,1)S(1)}, u32[]{:S(2)}, u32[]{:S(2)}) collective-permute-start(bf16[48,512]{1,0:T(8,128)(2,1)S(1)} %get-tuple-element.46), channel_id=1, source_target_pairs={{0,2},{1,3},{2,0},{3,1},{4,6},{5,7},{6,4},{7,5},{8,10},{9,11},{10,... | collective-permute-start | bytes 147464 | tf_op jit(solution)/shard_map/ppermute | solution.py:294
  5.5 3.7 %collective-permute-start.2 = (bf16[48,512]{1,0:T(8,128)(2,1)S(1)}, bf16[48,512]{1,0:T(8,128)(2,1)S(1)}, u32[]{:S(2)}, u32[]{:S(2)}) collective-permute-start(bf16[48,512]{1,0:T(8,128)(2,1)S(1)} %get-tuple-element.47), channel_id=1, source_target_pairs={{0,3},{1,2},{2,1},{3,0},{4,7},{5,6},{6,5},{7,4},{8,11},{9,10},{10,... | collective-permute-start | bytes 147464 | tf_op jit(solution)/shard_map/ppermute | solution.py:294
  5.6 1.1 %copy-start = (bf16[48,8192]{1,0:T(8,128)(2,1)S(1)}, bf16[48,8192]{1,0:T(8,128)(2,1)}, u32[]{:S(2)}) copy-start(bf16[48,8192]{1,0:T(8,128)(2,1)} %q_ref.3) | copy-start | bytes 2359300
  6.7 1.1 %copy-start.2 = (bf16[48,8192]{1,0:T(8,128)(2,1)S(1)}, bf16[48,8192]{1,0:T(8,128)(2,1)}, u32[]{:S(2)}) copy-start(bf16[48,8192]{1,0:T(8,128)(2,1)} %o_ref.3) | copy-start | bytes 2359300
  9.2 1.4 %collective-permute-start.11 = (bf16[48,2048]{1,0:T(8,128)(2,1)S(1)}, bf16[48,2048]{1,0:T(8,128)(2,1)S(1)}, u32[]{:S(2)}, u32[]{:S(2)}) collective-permute-start(bf16[48,2048]{1,0:T(8,128)(2,1)S(1)} %gate.5), channel_id=1, source_target_pairs={{0,1},{1,0},{2,3},{3,2},{4,5},{5,4},{6,7},{7,6},{8,9},{9,8},{10,11... | collective-permute-start | bytes 589832 | tf_op jit(solution)/shard_map/ppermute | solution.py:294
  10.7 22.9 %copy-start.1 = (bf16[48,8192]{1,0:T(8,128)(2,1)S(1)}, bf16[48,8192]{1,0:T(8,128)(2,1)}, u32[]{:S(2)}) copy-start(bf16[48,8192]{1,0:T(8,128)(2,1)} %q_ref.3) | copy-start | bytes 2359300
  10.7 22.9 %copy-start.3 = (bf16[48,8192]{1,0:T(8,128)(2,1)S(1)}, bf16[48,8192]{1,0:T(8,128)(2,1)}, u32[]{:S(2)}) copy-start(bf16[48,8192]{1,0:T(8,128)(2,1)} %o_ref.3) | copy-start | bytes 2359300
  11.2 16.7 %collective-permute-start.12 = (bf16[96,2048]{1,0:T(8,128)(2,1)S(1)}, bf16[96,2048]{1,0:T(8,128)(2,1)S(1)}, u32[]{:S(2)}, u32[]{:S(2)}) collective-permute-start(bf16[96,2048]{1,0:T(8,128)(2,1)S(1)} %join.2), channel_id=1, source_target_pairs={{0,2},{1,3},{2,0},{3,1},{4,6},{5,7},{6,4},{7,5},{8,10},{9,11},{10,... | collective-permute-start | bytes 1179656 | tf_op jit(solution)/shard_map/ppermute | solution.py:294
  12.3 11.5 %collective-permute-start.13 = (bf16[48,2048]{1,0:T(8,128)(2,1)S(1)}, bf16[48,2048]{1,0:T(8,128)(2,1)S(1)}, u32[]{:S(2)}, u32[]{:S(2)}) collective-permute-start(bf16[48,2048]{1,0:T(8,128)(2,1)S(1)} %gate.6), channel_id=1, source_target_pairs={{0,1},{1,0},{2,3},{3,2},{4,5},{5,4},{6,7},{7,6},{8,9},{9,8},{10,11... | collective-permute-start | bytes 589832 | tf_op jit(solution)/shard_map/ppermute | solution.py:294
  12.3 5.7 %collective-permute-start.4 = (bf16[96,512]{1,0:T(8,128)(2,1)S(1)}, bf16[96,512]{1,0:T(8,128)(2,1)S(1)}, u32[]{:S(2)}, u32[]{:S(2)}) collective-permute-start(bf16[96,512]{1,0:T(8,128)(2,1)S(1)} %get-tuple-element.49.refs_0_.refs_4_.refs_1_), channel_id=1, source_target_pairs={{0,8},{4,12},{8,0},{12,4},{16,24},{20,28},{24,16},{28,20},{1,9},{5... | collective-permute-start | bytes 294920 | tf_op jit(solution)/shard_map/ppermute | solution.py:294
  13.8 7.9 %collective-permute-start.3 = (bf16[96,512]{1,0:T(8,128)(2,1)S(1)}, bf16[96,512]{1,0:T(8,128)(2,1)S(1)}, u32[]{:S(2)}, u32[]{:S(2)}) collective-permute-start(bf16[96,512]{1,0:T(8,128)(2,1)S(1)} %get-tuple-element.49.refs_0_.refs_4_.refs_1_), channel_id=1, source_target_pairs={{0,16},{4,20},{8,24},{12,28},{16,0},{20,4},{24,8},{28,12},{1,17},{... | collective-permute-start | bytes 294920 | tf_op jit(solution)/shard_map/ppermute | solution.py:294
  16.4 6.9 %collective-permute-start.6 = (bf16[96,512]{1,0:T(8,128)(2,1)S(1)}, bf16[96,512]{1,0:T(8,128)(2,1)S(1)}, u32[]{:S(2)}, u32[]{:S(2)}) collective-permute-start(bf16[96,512]{1,0:T(8,128)(2,1)S(1)} %get-tuple-element.49.refs_0_.refs_4_.refs_1_), channel_id=1, source_target_pairs={{0,4},{4,0},{8,12},{12,8},{16,20},{20,16},{24,28},{28,24},{1,5},{5... | collective-permute-start | bytes 294920 | tf_op jit(solution)/shard_map/ppermute | solution.py:294
  18.0 6.4 %collective-permute-start.8 = (bf16[96,512]{1,0:T(8,128)(2,1)S(1)}, bf16[96,512]{1,0:T(8,128)(2,1)S(1)}, u32[]{:S(2)}, u32[]{:S(2)}) collective-permute-start(bf16[96,512]{1,0:T(8,128)(2,1)S(1)} %collective-permute-done.4.refs_6_.refs_2_), channel_id=1, source_target_pairs={{0,4},{4,0},{8,12},{12,8},{16,20},{20,16},{24,28},{28,24},{1,5},{5... | collective-permute-start | bytes 294920 | tf_op jit(solution)/shard_map/ppermute | solution.py:294
  21.8 4.6 %collective-permute-start.7 = (bf16[96,512]{1,0:T(8,128)(2,1)S(1)}, bf16[96,512]{1,0:T(8,128)(2,1)S(1)}, u32[]{:S(2)}, u32[]{:S(2)}) collective-permute-start(bf16[96,512]{1,0:T(8,128)(2,1)S(1)} %collective-permute-done.3.refs_1_.refs_5_.refs_4_), channel_id=1, source_target_pairs={{0,4},{4,0},{8,12},{12,8},{16,20},{20,16},{24,28},{28,24},{1,5},{5... | collective-permute-start | bytes 294920 | tf_op jit(solution)/shard_map/ppermute | solution.py:294
  23.3 4.6 %collective-permute-start.5 = (bf16[96,512]{1,0:T(8,128)(2,1)S(1)}, bf16[96,512]{1,0:T(8,128)(2,1)S(1)}, u32[]{:S(2)}, u32[]{:S(2)}) collective-permute-start(bf16[96,512]{1,0:T(8,128)(2,1)S(1)} %collective-permute-done.3.refs_1_.refs_5_.refs_4_), channel_id=1, source_target_pairs={{0,8},{4,12},{8,0},{12,4},{16,24},{20,28},{24,16},{28,20},{1,9},{5... | collective-permute-start | bytes 294920 | tf_op jit(solution)/shard_map/ppermute | solution.py:294
  23.8 9.8 %collective-permute-start.10 = (bf16[96,2048]{1,0:T(8,128)(2,1)S(1)}, bf16[96,2048]{1,0:T(8,128)(2,1)S(1)}, u32[]{:S(2)}, u32[]{:S(2)}) collective-permute-start(bf16[96,2048]{1,0:T(8,128)(2,1)S(1)} %gate.4), channel_id=1, source_target_pairs={{0,1},{1,0},{2,3},{3,2},{4,5},{5,4},{6,7},{7,6},{8,9},{9,8},{10,11... | collective-permute-start | bytes 1179656 | tf_op jit(solution)/shard_map/ppermute | solution.py:294
  27.9 10.9 %collective-permute-start.14 = (bf16[96,2048]{1,0:T(8,128)(2,1)S(1)}, bf16[96,2048]{1,0:T(8,128)(2,1)S(1)}, u32[]{:S(2)}, u32[]{:S(2)}) collective-permute-start(bf16[96,2048]{1,0:T(8,128)(2,1)S(1)} %gate.7), channel_id=1, source_target_pairs={{0,2},{1,3},{2,0},{3,1},{4,6},{5,7},{6,4},{7,5},{8,10},{9,11},{10,... | collective-permute-start | bytes 1179656 | tf_op jit(solution)/shard_map/ppermute | solution.py:294
  29.0 4.6 %collective-permute-start.9 = (bf16[96,512]{1,0:T(8,128)(2,1)S(1)}, bf16[96,512]{1,0:T(8,128)(2,1)S(1)}, u32[]{:S(2)}, u32[]{:S(2)}) collective-permute-start(bf16[96,512]{1,0:T(8,128)(2,1)S(1)} %collective-permute-done.5.refs_7_.refs_6_), channel_id=1, source_target_pairs={{0,4},{4,0},{8,12},{12,8},{16,20},{20,16},{24,28},{28,24},{1,5},{5... | collective-permute-start | bytes 294920 | tf_op jit(solution)/shard_map/ppermute | solution.py:294
  38.3 7.9 %collective-permute-start.15 = (bf16[384,256]{1,0:T(8,128)(2,1)S(1)}, bf16[384,256]{1,0:T(8,128)(2,1)S(1)}, u32[]{:S(2)}, u32[]{:S(2)}) collective-permute-start(bf16[384,256]{1,0:T(8,128)(2,1)S(1)} %get-tuple-element.67), channel_id=1, source_target_pairs={{0,4},{4,0},{8,12},{12,8},{16,20},{20,16},{24,28},{28,24},{1,5},{5... | collective-permute-start | bytes 589832 | tf_op jit(solution)/shard_map/ppermute | solution.py:294
  43.7 5.7 %collective-permute-start.18 = (bf16[384,256]{1,0:T(8,128)(2,1)S(1)}, bf16[384,256]{1,0:T(8,128)(2,1)S(1)}, u32[]{:S(2)}, u32[]{:S(2)}) collective-permute-start(bf16[384,256]{1,0:T(8,128)(2,1)S(1)} %get-tuple-element.77), channel_id=1, source_target_pairs={{0,4},{4,0},{8,12},{12,8},{16,20},{20,16},{24,28},{28,24},{1,5},{5... | collective-permute-start | bytes 589832 | tf_op jit(solution)/shard_map/ppermute | solution.py:294
  46.3 5.2 %collective-permute-start.16 = (bf16[192,256]{1,0:T(8,128)(2,1)S(1)}, bf16[192,256]{1,0:T(8,128)(2,1)S(1)}, u32[]{:S(2)}, u32[]{:S(2)}) collective-permute-start(bf16[192,256]{1,0:T(8,128)(2,1)S(1)} %get-tuple-element.69), channel_id=1, source_target_pairs={{0,8},{4,12},{8,0},{12,4},{16,24},{20,28},{24,16},{28,20},{1,9},{5... | collective-permute-start | bytes 294920 | tf_op jit(solution)/shard_map/ppermute | solution.py:294
  49.5 5.2 %collective-permute-start.19 = (bf16[192,256]{1,0:T(8,128)(2,1)S(1)}, bf16[192,256]{1,0:T(8,128)(2,1)S(1)}, u32[]{:S(2)}, u32[]{:S(2)}) collective-permute-start(bf16[192,256]{1,0:T(8,128)(2,1)S(1)} %get-tuple-element.79), channel_id=1, source_target_pairs={{0,8},{4,12},{8,0},{12,4},{16,24},{20,28},{24,16},{28,20},{1,9},{5... | collective-permute-start | bytes 294920 | tf_op jit(solution)/shard_map/ppermute | solution.py:294
  51.5 6.2 %collective-permute-start.17 = (bf16[96,256]{1,0:T(8,128)(2,1)S(1)}, bf16[96,256]{1,0:T(8,128)(2,1)S(1)}, u32[]{:S(2)}, u32[]{:S(2)}) collective-permute-start(bf16[96,256]{1,0:T(8,128)(2,1)S(1)} %get-tuple-element.71), channel_id=1, source_target_pairs={{0,16},{4,20},{8,24},{12,28},{16,0},{20,4},{24,8},{28,12},{1,17},{... | collective-permute-start | bytes 147464 | tf_op jit(solution)/shard_map/ppermute | solution.py:294
  54.7 5.5 %collective-permute-start.20 = (bf16[96,256]{1,0:T(8,128)(2,1)S(1)}, bf16[96,256]{1,0:T(8,128)(2,1)S(1)}, u32[]{:S(2)}, u32[]{:S(2)}) collective-permute-start(bf16[96,256]{1,0:T(8,128)(2,1)S(1)} %get-tuple-element.81), channel_id=1, source_target_pairs={{0,16},{4,20},{8,24},{12,28},{16,0},{20,4},{24,8},{28,12},{1,17},{... | collective-permute-start | bytes 147464 | tf_op jit(solution)/shard_map/ppermute | solution.py:294

commit v8 on v7

--- a/solution.py
+++ b/solution.py
@@ -81,14 +81,15 @@
     pass
 
 
-def join_kernel(first_ref, second_ref, *refs):
+def join_kernel(part, own_ref, handed_ref, *refs):
     out, sems = refs[-2:]
-    rows = first_ref.shape[0]
+    rows = own_ref.shape[0]
+    handed = handed_ref.at[part * rows : (part + 1) * rows, :]
     wait_copies(
         run_copies(
             [
-                pltpu.make_async_copy(first_ref, out.at[0:rows, :], sems.at[0]),
-                pltpu.make_async_copy(second_ref, out.at[rows : 2 * rows, :], sems.at[1]),
+                pltpu.make_async_copy(own_ref, out.at[0:rows, :], sems.at[0]),
+                pltpu.make_async_copy(handed, out.at[rows : 2 * rows, :], sems.at[1]),
             ]
         )
     )
@@ -306,17 +307,17 @@
     )(value, *after)
 
 
-def join(first, second, after):
-    rows, columns = first.shape
+def join(own, handed, part, after):
+    rows, columns = own.shape
     return pl.pallas_call(
-        join_kernel,
+        functools.partial(join_kernel, part),
         out_shape=shape(2 * rows, columns),
         in_specs=anywhere(2 + len(after)),
         out_specs=in_vmem(1)[0],
         scratch_shapes=[pltpu.SemaphoreType.DMA((2,))],
         compiler_params=params(2),
         name="join",
-    )(first, second, *after)
+    )(own, handed, *after)
 
 
 def bit_reversed(count):
@@ -369,11 +370,11 @@
     )(keys, values)
     kv = [kv_out[0]] + [swap(kv_out[m], "head", heads, m) for m in range(1, heads)]
 
-    dests = [[qo_at(1, g) for g in range(kv_heads)]]
-    for g in range(kv_heads):
-        dests += [[qo_at(2, g)], [qo_at(3, g)]]
+    groups = range(kv_heads)
+    dests = [[qo_at(1, g) for g in groups], [qo_at(3, g) for g in groups]]
+    dests += [[qo_at(2, g)] for g in groups]
     packed = pack([(GW, dests)], (queries, grad_out), kv_out[:1], 4, "pack_qo")
-    handed = swap(gate(packed[2], kv[1:]), "head", heads, 1)
+    handed = swap(gate(packed[1], kv[1:]), "head", heads, 1)
 
     merged, hide = pl.pallas_call(
         functools.partial(merge_kernel, heads),
@@ -386,15 +387,15 @@
     )(segment_ids, *kv)
 
     held = {0: merged}
-    for m in range(1, shards):
-        low = m & -m
-        held[m] = swap(held[m - low], "ctx", shards, low)
+    for m in range(2, shards, 2):
+        held[m] = swap(merged, "ctx", shards, m)
+    for m in range(0, shards, 2):
+        held[m + 1] = swap(held[m], "ctx", shards, 1)
     from_core = swap(gate(packed[0], [held[shards // 2]]), "head", heads, 1)
-    from_across = [swap(join(packed[1], handed, [merged]), "head", heads, 2)]
+    from_across = [swap(join(packed[2], handed, 0, [merged]), "head", heads, 2)]
     for g in range(1, kv_heads):
-        handed = swap(gate(packed[2 * g + 2], [merged]), "head", heads, 1)
-        both = join(packed[2 * g + 1], handed, ())
-        late = [held[m] for m in range(1, shards - 1)] + from_across[-1:]
+        both = join(packed[2 + g], handed, g, ())
+        late = [held[m] for m in range(1, shards) if m % 2 == 0 or m < 4] + from_across[-1:]
         from_across.append(swap(gate(both, late), "head", heads, 2))
 
     all_rows = tokens * GROUP

time: 61.5 us -> 61.9 us (level)
  starting transfers between devices: 19.9 us -> 20.9 us
  waiting for transfers between devices: 20.2 us -> 19.5 us
    ppermute x21 -> x20, starting transfers between devices: 19.9 us -> 20.9 us  [swap(): return lax.ppermute(x, axis, [(i, i ^ m) for i in range(size)])]
    ppermute x21 -> x20, waiting for transfers between devices: 20.2 us -> 19.5 us  [swap(): return lax.ppermute(x, axis, [(i, i ^ m) for i in range(size)])]
  transfers between devices with their start and end apart: 21 -> 20, of which waited for: 10 -> 9; matrix products, arithmetic and copies ran while one was open for 0% -> 0% of each run, Pallas kernels for 24% -> 24%
where the time goes in v8:
time: 61.9 us; the launch traced here: 61.7 us
  starting transfers between devices  20.9 us (34%)
  waiting for transfers between devices  19.5 us (32%)
  Pallas kernels  16.4 us (26%)
  local copies, waits for them, and re-layouts  4.06 us (7%)
  between operations  0.81 us (1%)
    ppermute x20, starting transfers between devices, swap(): return lax.ppermute(x, axis, [(i, i ^ m) for i in range(size)])  20.9 us
    ppermute x20, waiting for transfers between devices, swap(): return lax.ppermute(x, axis, [(i, i ^ m) for i in range(size)])  19.5 us
    pallas_call x2, Pallas kernels, local(): pl.pallas_call(functools.partial(attend_kernel, g, order), out_shape=[sha...  9.55 us
    unnamed x14, local copies, waits for them, and re-layouts  4.06 us
    pallas_call x1, Pallas kernels, local(): pl.pallas_call(functools.partial(queries_kernel, heads), out_shape=shape(...  2.19 us
    pallas_call x2, Pallas kernels, local(): pl.pallas_call(functools.partial(terms_kernel, heads), out_shape=[shape(h...  1.8 us
  transfers between devices with their start and end apart: 20, of which 9 were waited for; matrix products, arithmetic and copies ran while one was open for 0% of the time, Pallas kernels for 24%

profile of v8, /device:TPU:0, one launch (start us, length us, event | category | flops | bytes accessed | tf_op | source)
XLA Modules:
  0.0 61.7 jit_solution(1337006932435052317)
XLA Ops:
  0.6 0.9 %copy-done.4 = bf16[48,1024]{1,0:T(8,128)(2,1)S(1)} copy-done((bf16[48,1024]{1,0:T(8,128)(2,1)S(1)}, bf16[48,1024]{1,0:T(8,128)(2,1)}, u32[]{:S(2)}) %copy-start.4) | copy-done | bytes 98328
  1.5 0.9 %copy-done.5 = bf16[48,1024]{1,0:T(8,128)(2,1)S(1)} copy-done((bf16[48,1024]{1,0:T(8,128)(2,1)S(1)}, bf16[48,1024]{1,0:T(8,128)(2,1)}, u32[]{:S(2)}) %copy-start.5) | copy-done | bytes 98328
  2.4 0.5 collective-permute-start
  3.0 2.6 %collective-permute-start.1 = (bf16[48,512]{1,0:T(8,128)(2,1)S(1)}, bf16[48,512]{1,0:T(8,128)(2,1)S(1)}, u32[]{:S(2)}, u32[]{:S(2)}) collective-permute-start(bf16[48,512]{1,0:T(8,128)(2,1)S(1)} %get-tuple-element.45), channel_id=1, source_target_pairs={{0,2},{1,3},{2,0},{3,1},{4,6},{5,7},{6,4},{7,5},{8,10},{9,11},{10,... | collective-permute-start | bytes 147464 | tf_op jit(solution)/shard_map/ppermute | solution.py:295
  5.6 1.1 %copy-done = bf16[48,8192]{1,0:T(8,128)(2,1)S(1)} copy-done((bf16[48,8192]{1,0:T(8,128)(2,1)S(1)}, bf16[48,8192]{1,0:T(8,128)(2,1)}, u32[]{:S(2)}) %copy-start) | copy-done | bytes 786456
  6.7 1.1 %copy-done.2 = bf16[48,8192]{1,0:T(8,128)(2,1)S(1)} copy-done((bf16[48,8192]{1,0:T(8,128)(2,1)S(1)}, bf16[48,8192]{1,0:T(8,128)(2,1)}, u32[]{:S(2)}) %copy-start.2) | copy-done | bytes 786456
  8.3 1.0 %collective-permute-done.2.refs_3_ = bf16[48,512]{1,0:T(8,128)(2,1)S(1)} collective-permute-done((bf16[48,512]{1,0:T(8,128)(2,1)S(1)}, bf16[48,512]{1,0:T(8,128)(2,1)S(1)}, u32[]{:S(2)}, u32[]{:S(2)}) %collective-permute-start.2) | collective-permute-done | bytes 49184 | tf_op jit(solution)/shard_map/ppermute | solution.py:295
  9.7 1.3 %collective-permute-done.11.handed_ref = bf16[96,2048]{1,0:T(8,128)(2,1)S(1)} collective-permute-done((bf16[96,2048]{1,0:T(8,128)(2,1)S(1)}, bf16[96,2048]{1,0:T(8,128)(2,1)S(1)}, u32[]{:S(2)}, u32[]{:S(2)}) %collective-permute-start.11) | collective-permute-done | bytes 393248 | tf_op jit(solution)/shard_map/ppermute | solution.py:295
  11.5 1.1 %collective-permute-start.12 = (bf16[96,2048]{1,0:T(8,128)(2,1)S(1)}, bf16[96,2048]{1,0:T(8,128)(2,1)S(1)}, u32[]{:S(2)}, u32[]{:S(2)}) collective-permute-start(bf16[96,2048]{1,0:T(8,128)(2,1)S(1)} %join.2), channel_id=1, source_target_pairs={{0,2},{1,3},{2,0},{3,1},{4,6},{5,7},{6,4},{7,5},{8,10},{9,11},{10,... | collective-permute-start | bytes 1179656 | tf_op jit(solution)/shard_map/ppermute | solution.py:295
  12.5 1.6 %collective-permute-start.4 = (bf16[96,512]{1,0:T(8,128)(2,1)S(1)}, bf16[96,512]{1,0:T(8,128)(2,1)S(1)}, u32[]{:S(2)}, u32[]{:S(2)}) collective-permute-start(bf16[96,512]{1,0:T(8,128)(2,1)S(1)} %get-tuple-element.48.refs_0_.refs_4_), channel_id=1, source_target_pairs={{0,8},{4,12},{8,0},{12,4},{16,24},{20,28},{24,16},{28,20},{1,9},{5... | collective-permute-start | bytes 294920 | tf_op jit(solution)/shard_map/ppermute | solution.py:295
  14.1 2.6 %collective-permute-start.3 = (bf16[96,512]{1,0:T(8,128)(2,1)S(1)}, bf16[96,512]{1,0:T(8,128)(2,1)S(1)}, u32[]{:S(2)}, u32[]{:S(2)}) collective-permute-start(bf16[96,512]{1,0:T(8,128)(2,1)S(1)} %get-tuple-element.48.refs_0_.refs_4_), channel_id=1, source_target_pairs={{0,16},{4,20},{8,24},{12,28},{16,0},{20,4},{24,8},{28,12},{1,17},{... | collective-permute-start | bytes 294920 | tf_op jit(solution)/shard_map/ppermute | solution.py:295
  16.7 1.5 %collective-permute-start.6 = (bf16[96,512]{1,0:T(8,128)(2,1)S(1)}, bf16[96,512]{1,0:T(8,128)(2,1)S(1)}, u32[]{:S(2)}, u32[]{:S(2)}) collective-permute-start(bf16[96,512]{1,0:T(8,128)(2,1)S(1)} %get-tuple-element.48.refs_0_.refs_4_), channel_id=1, source_target_pairs={{0,4},{4,0},{8,12},{12,8},{16,20},{20,16},{24,28},{28,24},{1,5},{5... | collective-permute-start | bytes 294920 | tf_op jit(solution)/shard_map/ppermute | solution.py:295
  18.9 4.1 %collective-permute-done.3.refs_1_.refs_5_.refs_4_ = bf16[96,512]{1,0:T(8,128)(2,1)S(1)} collective-permute-done((bf16[96,512]{1,0:T(8,128)(2,1)S(1)}, bf16[96,512]{1,0:T(8,128)(2,1)S(1)}, u32[]{:S(2)}, u32[]{:S(2)}) %collective-permute-start.3) | collective-permute-done | bytes 98336 | tf_op jit(solution)/shard_map/ppermute | solution.py:295
  23.0 0.5 join.3.refs_0_
  23.5 1.2 %collective-permute-done.5.refs_7_.refs_5_ = bf16[96,512]{1,0:T(8,128)(2,1)S(1)} collective-permute-done((bf16[96,512]{1,0:T(8,128)(2,1)S(1)}, bf16[96,512]{1,0:T(8,128)(2,1)S(1)}, u32[]{:S(2)}, u32[]{:S(2)}) %collective-permute-start.5) | collective-permute-done | bytes 98336 | tf_op jit(solution)/shard_map/ppermute | solution.py:295
  24.7 1.1 %collective-permute-start.13 = (bf16[96,2048]{1,0:T(8,128)(2,1)S(1)}, bf16[96,2048]{1,0:T(8,128)(2,1)S(1)}, u32[]{:S(2)}, u32[]{:S(2)}) collective-permute-start(bf16[96,2048]{1,0:T(8,128)(2,1)S(1)} %gate.5), channel_id=1, source_target_pairs={{0,2},{1,3},{2,0},{3,1},{4,6},{5,7},{6,4},{7,5},{8,10},{9,11},{10,... | collective-permute-start | bytes 1179656 | tf_op jit(solution)/shard_map/ppermute | solution.py:295
  25.8 1.9 %collective-permute-start.9 = (bf16[96,512]{1,0:T(8,128)(2,1)S(1)}, bf16[96,512]{1,0:T(8,128)(2,1)S(1)}, u32[]{:S(2)}, u32[]{:S(2)}) collective-permute-start(bf16[96,512]{1,0:T(8,128)(2,1)S(1)} %collective-permute-done.5.refs_7_.refs_5_), channel_id=1, source_target_pairs={{0,4},{4,0},{8,12},{12,8},{16,20},{20,16},{24,28},{28,24},{1,5},{5... | collective-permute-start | bytes 294920 | tf_op jit(solution)/shard_map/ppermute | solution.py:295
  27.9 3.6 %collective-permute-done.9.refs_11_ = bf16[96,512]{1,0:T(8,128)(2,1)S(1)} collective-permute-done((bf16[96,512]{1,0:T(8,128)(2,1)S(1)}, bf16[96,512]{1,0:T(8,128)(2,1)S(1)}, u32[]{:S(2)}, u32[]{:S(2)}) %collective-permute-start.9) | collective-permute-done | bytes 98336 | tf_op jit(solution)/shard_map/ppermute | solution.py:295
  31.4 1.6 %collective-permute-done.7.refs_9_ = bf16[96,512]{1,0:T(8,128)(2,1)S(1)} collective-permute-done((bf16[96,512]{1,0:T(8,128)(2,1)S(1)}, bf16[96,512]{1,0:T(8,128)(2,1)S(1)}, u32[]{:S(2)}, u32[]{:S(2)}) %collective-permute-start.7) | collective-permute-done | bytes 98336 | tf_op jit(solution)/shard_map/ppermute | solution.py:295
  33.0 4.7 %attend.2 = (bf16[768,1536]{1,0:T(8,128)(2,1)S(1)}, bf16[768,1536]{1,0:T(8,128)(2,1)S(1)}, bf16[48,1536]{1,0:T(8,128)(2,1)S(1)}, bf16[48,1536]{1,0:T(8,128)(2,1)...) custom-call(bf16[48,8192]{1,0:T(8,128)(2,1)S(1)} %copy-done.1, ...), custom_call_target="tpu_custom_call" | custom-call | flops 962592768 | bytes 8388608 | tf_op jit(solution)/shard_map/attend/pallas_call | solution.py:404
  37.7 1.8 %collective-permute-start.14 = (bf16[384,256]{1,0:T(8,128)(2,1)S(1)}, bf16[384,256]{1,0:T(8,128)(2,1)S(1)}, u32[]{:S(2)}, u32[]{:S(2)}) collective-permute-start(bf16[384,256]{1,0:T(8,128)(2,1)S(1)} %get-tuple-element.65), channel_id=1, source_target_pairs={{0,4},{4,0},{8,12},{12,8},{16,20},{20,16},{24,28},{28,24},{1,5},{5... | collective-permute-start | bytes 589832 | tf_op jit(solution)/shard_map/ppermute | solution.py:295
  39.5 4.9 %attend.3 = (bf16[768,1536]{1,0:T(8,128)(2,1)S(1)}, bf16[768,1536]{1,0:T(8,128)(2,1)S(1)}, bf16[48,1536]{1,0:T(8,128)(2,1)S(1)}, bf16[48,1536]{1,0:T(8,128)(2,1)...) custom-call(bf16[48,8192]{1,0:T(8,128)(2,1)S(1)} %copy-done.1, ...), custom_call_target="tpu_custom_call" | custom-call | flops 962592768 | bytes 8388608 | tf_op jit(solution)/shard_map/attend/pallas_call | solution.py:404
  44.7 0.9 %terms.2 = (f32[384,256]{1,0:T(8,128)S(1)}, f32[192,256]{1,0:T(8,128)S(1)}) custom-call(bf16[768,1536]{1,0:T(8,128)(2,1)S(1)} %get-tuple-element.60.p_ref, bf16[768,1536]{1,0:T(8,128)(2,1)S(1)} %get-tuple-element.52.refs_4_.ds_ref, bf16[48,1536]{1,0:T(8,128)(2,1)S(1)} %get-tuple-element.56.refs_14_.own_p_ref, ...), custom_call_target="tpu_custom_call" | custom-call | flops 301989888 | bytes 1048576 | tf_op jit(solution)/shard_map/terms/pallas_call | solution.py:446
  45.7 0.6 collective-permute-start.15
  46.3 0.9 %terms.3 = (f32[384,256]{1,0:T(8,128)S(1)}, f32[192,256]{1,0:T(8,128)S(1)}) custom-call(bf16[768,1536]{1,0:T(8,128)(2,1)S(1)} %get-tuple-element.71.p_ref, bf16[768,1536]{1,0:T(8,128)(2,1)S(1)} %get-tuple-element.57.refs_7_.ds_ref, bf16[48,1536]{1,0:T(8,128)(2,1)S(1)} %get-tuple-element.63.after_ref.own_p_ref, ...), custom_call_target="tpu_custom_call" | custom-call | flops 301989888 | bytes 1048576 | tf_op jit(solution)/shard_map/terms/pallas_call | solution.py:446
  47.2 3.2 %collective-permute-done.17.far_ref = bf16[384,256]{1,0:T(8,128)(2,1)S(1)} collective-permute-done((bf16[384,256]{1,0:T(8,128)(2,1)S(1)}, bf16[384,256]{1,0:T(8,128)(2,1)S(1)}, u32[]{:S(2)}, u32[]{:S(2)}) %collective-permute-start.17) | collective-permute-done | bytes 196640 | tf_op jit(solution)/shard_map/ppermute | solution.py:295
  50.5 3.1 %collective-permute-start.16 = (bf16[96,256]{1,0:T(8,128)(2,1)S(1)}, bf16[96,256]{1,0:T(8,128)(2,1)S(1)}, u32[]{:S(2)}, u32[]{:S(2)}) collective-permute-start(bf16[96,256]{1,0:T(8,128)(2,1)S(1)} %get-tuple-element.69), channel_id=1, source_target_pairs={{0,16},{4,20},{8,24},{12,28},{16,0},{20,4},{24,8},{28,12},{1,17},{... | collective-permute-start | bytes 147464 | tf_op jit(solution)/shard_map/ppermute | solution.py:295
  53.6 1.5 %collective-permute-done.18.far_ref = bf16[192,256]{1,0:T(8,128)(2,1)S(1)} collective-permute-done((bf16[192,256]{1,0:T(8,128)(2,1)S(1)}, bf16[192,256]{1,0:T(8,128)(2,1)S(1)}, u32[]{:S(2)}, u32[]{:S(2)}) %collective-permute-start.18) | collective-permute-done | bytes 98336 | tf_op jit(solution)/shard_map/ppermute | solution.py:295
  55.1 1.1 %collective-permute-start.19 = (bf16[96,256]{1,0:T(8,128)(2,1)S(1)}, bf16[96,256]{1,0:T(8,128)(2,1)S(1)}, u32[]{:S(2)}, u32[]{:S(2)}) collective-permute-start(bf16[96,256]{1,0:T(8,128)(2,1)S(1)} %get-tuple-element.79), channel_id=1, source_target_pairs={{0,16},{4,20},{8,24},{12,28},{16,0},{20,4},{24,8},{28,12},{1,17},{... | collective-permute-start | bytes 147464 | tf_op jit(solution)/shard_map/ppermute | solution.py:295
  56.2 2.2 %queries.1 = bf16[192,2048]{1,0:T(8,128)(2,1)} custom-call(bf16[48,512]{1,0:T(8,128)(2,1)S(1)} %get-tuple-element.43.refs_0_.refs_2_, bf16[48,512]{1,0:T(8,128)(2,1)S(1)} %collective-permute-done.refs_1_, bf16[48,512]{1,0:T(8,128)(2,1)S(1)} %collective-permute-done.1.refs_2_, bf16[48,512]{1,0:T(8,128)(2,1)S(1)} %collective-permute-done.2.refs_3_, ...), custom_call_target="tpu_custom_call" | custom-call | flops 603979776 | bytes 1048576 | tf_op jit(solution)/shard_map/queries/pallas_call | solution.py:462
  58.4 2.2 %collective-permute-done.19.refs_4_ = bf16[96,256]{1,0:T(8,128)(2,1)S(1)} collective-permute-done((bf16[96,256]{1,0:T(8,128)(2,1)S(1)}, bf16[96,256]{1,0:T(8,128)(2,1)S(1)}, u32[]{:S(2)}, u32[]{:S(2)}) %collective-permute-start.19) | collective-permute-done | bytes 49184 | tf_op jit(solution)/shard_map/ppermute | solution.py:295
  60.7 1.0 %spread.1 = (bf16[192,256]{1,0:T(8,128)(2,1)}, bf16[192,256]{1,0:T(8,128)(2,1)}) custom-call(s32[2,192]{1,0:T(2,128)S(1)} %copy-done.6, f32[96,256]{1,0:T(8,128)S(1)} %get-tuple-element.68.refs_0_, bf16[96,256]{1,0:T(8,128)(2,1)S(1)} %collective-permute-done.16.refs_1_, f32[192,256]{1,0:T(8,128)S(1)} %get-tuple-element.70.refs_2_, ...), custom_call_target="tpu_custom_call" | custom-call | tf_op jit(solution)/shard_map/spread/pallas_call | solution.py:491
  (40 shorter events, 2.8 us)
Async XLA Ops:
  0.6 0.9 %copy-start.4 = (bf16[48,1024]{1,0:T(8,128)(2,1)S(1)}, bf16[48,1024]{1,0:T(8,128)(2,1)}, u32[]{:S(2)}) copy-start(bf16[48,1024]{1,0:T(8,128)(2,1)} %key_ref.1) | copy-start | bytes 294916
  1.5 0.9 %copy-start.5 = (bf16[48,1024]{1,0:T(8,128)(2,1)S(1)}, bf16[48,1024]{1,0:T(8,128)(2,1)}, u32[]{:S(2)}) copy-start(bf16[48,1024]{1,0:T(8,128)(2,1)} %value_ref.1) | copy-start | bytes 294916
  2.4 7.0 %copy-start.6 = (s32[2,192]{1,0:T(2,128)S(1)}, s32[2,192]{1,0:T(2,128)}, u32[]{:S(2)}) copy-start(s32[2,192]{1,0:T(2,128)} %seg_ref.3) | copy-start | bytes 4612
  2.4 5.8 %collective-permute-start = (bf16[48,512]{1,0:T(8,128)(2,1)S(1)}, bf16[48,512]{1,0:T(8,128)(2,1)S(1)}, u32[]{:S(2)}, u32[]{:S(2)}) collective-permute-start(bf16[48,512]{1,0:T(8,128)(2,1)S(1)} %get-tuple-element.44), channel_id=1, source_target_pairs={{0,1},{1,0},{2,3},{3,2},{4,5},{5,4},{6,7},{7,6},{8,9},{9,8},{10,11... | collective-permute-start | bytes 147464 | tf_op jit(solution)/shard_map/ppermute | solution.py:295
  3.0 5.3 %collective-permute-start.1 = (bf16[48,512]{1,0:T(8,128)(2,1)S(1)}, bf16[48,512]{1,0:T(8,128)(2,1)S(1)}, u32[]{:S(2)}, u32[]{:S(2)}) collective-permute-start(bf16[48,512]{1,0:T(8,128)(2,1)S(1)} %get-tuple-element.45), channel_id=1, source_target_pairs={{0,2},{1,3},{2,0},{3,1},{4,6},{5,7},{6,4},{7,5},{8,10},{9,11},{10,... | collective-permute-start | bytes 147464 | tf_op jit(solution)/shard_map/ppermute | solution.py:295
  5.5 3.7 %collective-permute-start.2 = (bf16[48,512]{1,0:T(8,128)(2,1)S(1)}, bf16[48,512]{1,0:T(8,128)(2,1)S(1)}, u32[]{:S(2)}, u32[]{:S(2)}) collective-permute-start(bf16[48,512]{1,0:T(8,128)(2,1)S(1)} %get-tuple-element.46), channel_id=1, source_target_pairs={{0,3},{1,2},{2,1},{3,0},{4,7},{5,6},{6,5},{7,4},{8,11},{9,10},{10,... | collective-permute-start | bytes 147464 | tf_op jit(solution)/shard_map/ppermute | solution.py:295
  5.6 1.1 %copy-start = (bf16[48,8192]{1,0:T(8,128)(2,1)S(1)}, bf16[48,8192]{1,0:T(8,128)(2,1)}, u32[]{:S(2)}) copy-start(bf16[48,8192]{1,0:T(8,128)(2,1)} %q_ref.3) | copy-start | bytes 2359300
  6.7 1.1 %copy-start.2 = (bf16[48,8192]{1,0:T(8,128)(2,1)S(1)}, bf16[48,8192]{1,0:T(8,128)(2,1)}, u32[]{:S(2)}) copy-start(bf16[48,8192]{1,0:T(8,128)(2,1)} %o_ref.3) | copy-start | bytes 2359300
  9.2 1.7 %collective-permute-start.11 = (bf16[96,2048]{1,0:T(8,128)(2,1)S(1)}, bf16[96,2048]{1,0:T(8,128)(2,1)S(1)}, u32[]{:S(2)}, u32[]{:S(2)}) collective-permute-start(bf16[96,2048]{1,0:T(8,128)(2,1)S(1)} %gate.4), channel_id=1, source_target_pairs={{0,1},{1,0},{2,3},{3,2},{4,5},{5,4},{6,7},{7,6},{8,9},{9,8},{10,11... | collective-permute-start | bytes 1179656 | tf_op jit(solution)/shard_map/ppermute | solution.py:295
  9.7 23.4 %copy-start.1 = (bf16[48,8192]{1,0:T(8,128)(2,1)S(1)}, bf16[48,8192]{1,0:T(8,128)(2,1)}, u32[]{:S(2)}) copy-start(bf16[48,8192]{1,0:T(8,128)(2,1)} %q_ref.3) | copy-start | bytes 2359300
  9.7 23.3 %copy-start.3 = (bf16[48,8192]{1,0:T(8,128)(2,1)S(1)}, bf16[48,8192]{1,0:T(8,128)(2,1)}, u32[]{:S(2)}) copy-start(bf16[48,8192]{1,0:T(8,128)(2,1)} %o_ref.3) | copy-start | bytes 2359300
  11.5 13.3 %collective-permute-start.12 = (bf16[96,2048]{1,0:T(8,128)(2,1)S(1)}, bf16[96,2048]{1,0:T(8,128)(2,1)S(1)}, u32[]{:S(2)}, u32[]{:S(2)}) collective-permute-start(bf16[96,2048]{1,0:T(8,128)(2,1)S(1)} %join.2), channel_id=1, source_target_pairs={{0,2},{1,3},{2,0},{3,1},{4,6},{5,7},{6,4},{7,5},{8,10},{9,11},{10,... | collective-permute-start | bytes 1179656 | tf_op jit(solution)/shard_map/ppermute | solution.py:295
  12.5 5.9 %collective-permute-start.4 = (bf16[96,512]{1,0:T(8,128)(2,1)S(1)}, bf16[96,512]{1,0:T(8,128)(2,1)S(1)}, u32[]{:S(2)}, u32[]{:S(2)}) collective-permute-start(bf16[96,512]{1,0:T(8,128)(2,1)S(1)} %get-tuple-element.48.refs_0_.refs_4_), channel_id=1, source_target_pairs={{0,8},{4,12},{8,0},{12,4},{16,24},{20,28},{24,16},{28,20},{1,9},{5... | collective-permute-start | bytes 294920 | tf_op jit(solution)/shard_map/ppermute | solution.py:295
  14.1 8.9 %collective-permute-start.3 = (bf16[96,512]{1,0:T(8,128)(2,1)S(1)}, bf16[96,512]{1,0:T(8,128)(2,1)S(1)}, u32[]{:S(2)}, u32[]{:S(2)}) collective-permute-start(bf16[96,512]{1,0:T(8,128)(2,1)S(1)} %get-tuple-element.48.refs_0_.refs_4_), channel_id=1, source_target_pairs={{0,16},{4,20},{8,24},{12,28},{16,0},{20,4},{24,8},{28,12},{1,17},{... | collective-permute-start | bytes 294920 | tf_op jit(solution)/shard_map/ppermute | solution.py:295
  16.7 6.8 %collective-permute-start.6 = (bf16[96,512]{1,0:T(8,128)(2,1)S(1)}, bf16[96,512]{1,0:T(8,128)(2,1)S(1)}, u32[]{:S(2)}, u32[]{:S(2)}) collective-permute-start(bf16[96,512]{1,0:T(8,128)(2,1)S(1)} %get-tuple-element.48.refs_0_.refs_4_), channel_id=1, source_target_pairs={{0,4},{4,0},{8,12},{12,8},{16,20},{20,16},{24,28},{28,24},{1,5},{5... | collective-permute-start | bytes 294920 | tf_op jit(solution)/shard_map/ppermute | solution.py:295
  18.2 6.5 %collective-permute-start.5 = (bf16[96,512]{1,0:T(8,128)(2,1)S(1)}, bf16[96,512]{1,0:T(8,128)(2,1)S(1)}, u32[]{:S(2)}, u32[]{:S(2)}) collective-permute-start(bf16[96,512]{1,0:T(8,128)(2,1)S(1)} %get-tuple-element.48.refs_0_.refs_4_), channel_id=1, source_target_pairs={{0,24},{4,28},{8,16},{12,20},{16,8},{20,12},{24,0},{28,4},{1,25},{... | collective-permute-start | bytes 294920 | tf_op jit(solution)/shard_map/ppermute | solution.py:295
  18.4 6.3 %collective-permute-start.8 = (bf16[96,512]{1,0:T(8,128)(2,1)S(1)}, bf16[96,512]{1,0:T(8,128)(2,1)S(1)}, u32[]{:S(2)}, u32[]{:S(2)}) collective-permute-start(bf16[96,512]{1,0:T(8,128)(2,1)S(1)} %collective-permute-done.4.refs_6_.refs_2_), channel_id=1, source_target_pairs={{0,4},{4,0},{8,12},{12,8},{16,20},{20,16},{24,28},{28,24},{1,5},{5... | collective-permute-start | bytes 294920 | tf_op jit(solution)/shard_map/ppermute | solution.py:295
  23.0 10.0 %collective-permute-start.10 = (bf16[96,2048]{1,0:T(8,128)(2,1)S(1)}, bf16[96,2048]{1,0:T(8,128)(2,1)S(1)}, u32[]{:S(2)}, u32[]{:S(2)}) collective-permute-start(bf16[96,2048]{1,0:T(8,128)(2,1)S(1)} %gate.3), channel_id=1, source_target_pairs={{0,1},{1,0},{2,3},{3,2},{4,5},{5,4},{6,7},{7,6},{8,9},{9,8},{10,11... | collective-permute-start | bytes 1179656 | tf_op jit(solution)/shard_map/ppermute | solution.py:295
  24.7 14.8 %collective-permute-start.13 = (bf16[96,2048]{1,0:T(8,128)(2,1)S(1)}, bf16[96,2048]{1,0:T(8,128)(2,1)S(1)}, u32[]{:S(2)}, u32[]{:S(2)}) collective-permute-start(bf16[96,2048]{1,0:T(8,128)(2,1)S(1)} %gate.5), channel_id=1, source_target_pairs={{0,2},{1,3},{2,0},{3,1},{4,6},{5,7},{6,4},{7,5},{8,10},{9,11},{10,... | collective-permute-start | bytes 1179656 | tf_op jit(solution)/shard_map/ppermute | solution.py:295
  25.8 5.6 %collective-permute-start.9 = (bf16[96,512]{1,0:T(8,128)(2,1)S(1)}, bf16[96,512]{1,0:T(8,128)(2,1)S(1)}, u32[]{:S(2)}, u32[]{:S(2)}) collective-permute-start(bf16[96,512]{1,0:T(8,128)(2,1)S(1)} %collective-permute-done.5.refs_7_.refs_5_), channel_id=1, source_target_pairs={{0,4},{4,0},{8,12},{12,8},{16,20},{20,16},{24,28},{28,24},{1,5},{5... | collective-permute-start | bytes 294920 | tf_op jit(solution)/shard_map/ppermute | solution.py:295
  27.7 5.3 %collective-permute-start.7 = (bf16[96,512]{1,0:T(8,128)(2,1)S(1)}, bf16[96,512]{1,0:T(8,128)(2,1)S(1)}, u32[]{:S(2)}, u32[]{:S(2)}) collective-permute-start(bf16[96,512]{1,0:T(8,128)(2,1)S(1)} %collective-permute-done.3.refs_1_.refs_5_.refs_4_), channel_id=1, source_target_pairs={{0,4},{4,0},{8,12},{12,8},{16,20},{20,16},{24,28},{28,24},{1,5},{5... | collective-permute-start | bytes 294920 | tf_op jit(solution)/shard_map/ppermute | solution.py:295
  37.7 7.9 %collective-permute-start.14 = (bf16[384,256]{1,0:T(8,128)(2,1)S(1)}, bf16[384,256]{1,0:T(8,128)(2,1)S(1)}, u32[]{:S(2)}, u32[]{:S(2)}) collective-permute-start(bf16[384,256]{1,0:T(8,128)(2,1)S(1)} %get-tuple-element.65), channel_id=1, source_target_pairs={{0,4},{4,0},{8,12},{12,8},{16,20},{20,16},{24,28},{28,24},{1,5},{5... | collective-permute-start | bytes 589832 | tf_op jit(solution)/shard_map/ppermute | solution.py:295
  44.4 6.0 %collective-permute-start.17 = (bf16[384,256]{1,0:T(8,128)(2,1)S(1)}, bf16[384,256]{1,0:T(8,128)(2,1)S(1)}, u32[]{:S(2)}, u32[]{:S(2)}) collective-permute-start(bf16[384,256]{1,0:T(8,128)(2,1)S(1)} %get-tuple-element.75), channel_id=1, source_target_pairs={{0,4},{4,0},{8,12},{12,8},{16,20},{20,16},{24,28},{28,24},{1,5},{5... | collective-permute-start | bytes 589832 | tf_op jit(solution)/shard_map/ppermute | solution.py:295
  45.7 4.8 %collective-permute-start.15 = (bf16[192,256]{1,0:T(8,128)(2,1)S(1)}, bf16[192,256]{1,0:T(8,128)(2,1)S(1)}, u32[]{:S(2)}, u32[]{:S(2)}) collective-permute-start(bf16[192,256]{1,0:T(8,128)(2,1)S(1)} %get-tuple-element.67), channel_id=1, source_target_pairs={{0,8},{4,12},{8,0},{12,4},{16,24},{20,28},{24,16},{28,20},{1,9},{5... | collective-permute-start | bytes 294920 | tf_op jit(solution)/shard_map/ppermute | solution.py:295
  50.4 4.7 %collective-permute-start.18 = (bf16[192,256]{1,0:T(8,128)(2,1)S(1)}, bf16[192,256]{1,0:T(8,128)(2,1)S(1)}, u32[]{:S(2)}, u32[]{:S(2)}) collective-permute-start(bf16[192,256]{1,0:T(8,128)(2,1)S(1)} %get-tuple-element.77), channel_id=1, source_target_pairs={{0,8},{4,12},{8,0},{12,4},{16,24},{20,28},{24,16},{28,20},{1,9},{5... | collective-permute-start | bytes 294920 | tf_op jit(solution)/shard_map/ppermute | solution.py:295
  50.5 7.9 %collective-permute-start.16 = (bf16[96,256]{1,0:T(8,128)(2,1)S(1)}, bf16[96,256]{1,0:T(8,128)(2,1)S(1)}, u32[]{:S(2)}, u32[]{:S(2)}) collective-permute-start(bf16[96,256]{1,0:T(8,128)(2,1)S(1)} %get-tuple-element.69), channel_id=1, source_target_pairs={{0,16},{4,20},{8,24},{12,28},{16,0},{20,4},{24,8},{28,12},{1,17},{... | collective-permute-start | bytes 147464 | tf_op jit(solution)/shard_map/ppermute | solution.py:295
  55.1 5.5 %collective-permute-start.19 = (bf16[96,256]{1,0:T(8,128)(2,1)S(1)}, bf16[96,256]{1,0:T(8,128)(2,1)S(1)}, u32[]{:S(2)}, u32[]{:S(2)}) collective-permute-start(bf16[96,256]{1,0:T(8,128)(2,1)S(1)} %get-tuple-element.79), channel_id=1, source_target_pairs={{0,16},{4,20},{8,24},{12,28},{16,0},{20,4},{24,8},{28,12},{1,17},{... | collective-permute-start | bytes 147464 | tf_op jit(solution)/shard_map/ppermute | solution.py:295

commit v9 on v7

--- a/solution.py
+++ b/solution.py
@@ -79,19 +79,6 @@
 
 def gate_kernel(*refs):
     pass
-
-
-def join_kernel(first_ref, second_ref, *refs):
-    out, sems = refs[-2:]
-    rows = first_ref.shape[0]
-    wait_copies(
-        run_copies(
-            [
-                pltpu.make_async_copy(first_ref, out.at[0:rows, :], sems.at[0]),
-                pltpu.make_async_copy(second_ref, out.at[rows : 2 * rows, :], sems.at[1]),
-            ]
-        )
-    )
 
 
 def pack_kv_kernel(kv_heads, key_ref, value_ref, *outs):
@@ -134,7 +121,7 @@
     shards = len(order)
     heads = 4
     kv_pieces, blocks, refs = refs[:heads], refs[heads : heads + shards], refs[heads + shards :]
-    qo_pieces = ((refs[0], g), (refs[1], 0), (refs[1], 1))
+    qo_pieces = refs[: heads - 1]
     (
         p_ref, ds_ref, own_p_ref, own_ds_ref, qs_ref, os_ref, kt_ref, far_ref,
         kx, vx, mine, sems,
@@ -179,7 +166,7 @@
     for m in list(range(1, heads)) + [0]:
         if m == 0:
             wait_copies(copies)
-        qo, part = qo_pieces[m - 1] if m else (mine, 0)
+        qo, part = (qo_pieces[m - 1], g) if m else (mine, 0)
         span = slice(part * rows, (part + 1) * rows)
         at = pl.ds(pl.multiple_of(lax.bitwise_xor(me, m) * rows, 16), rows)
         chunk = slice(m * width, (m + 1) * width)
@@ -294,7 +281,7 @@
     return lax.ppermute(x, axis, [(i, i ^ m) for i in range(size)])
 
 
-def gate(value, after):
+def gate(value, after, mib=0):
     return pl.pallas_call(
         gate_kernel,
         out_shape=shape(*value.shape, dtype=value.dtype),
@@ -302,21 +289,9 @@
         out_specs=anywhere(1)[0],
         input_output_aliases={0: 0},
         compiler_params=params(1),
+        cost_estimate=pl.CostEstimate(flops=0, bytes_accessed=mib * 2**20, transcendentals=0),
         name="gate",
     )(value, *after)
-
-
-def join(first, second, after):
-    rows, columns = first.shape
-    return pl.pallas_call(
-        join_kernel,
-        out_shape=shape(2 * rows, columns),
-        in_specs=anywhere(2 + len(after)),
-        out_specs=in_vmem(1)[0],
-        scratch_shapes=[pltpu.SemaphoreType.DMA((2,))],
-        compiler_params=params(2),
-        name="join",
-    )(first, second, *after)
 
 
 def bit_reversed(count):
@@ -369,11 +344,11 @@
     )(keys, values)
     kv = [kv_out[0]] + [swap(kv_out[m], "head", heads, m) for m in range(1, heads)]
 
-    dests = [[qo_at(1, g) for g in range(kv_heads)]]
-    for g in range(kv_heads):
-        dests += [[qo_at(2, g)], [qo_at(3, g)]]
-    packed = pack([(GW, dests)], (queries, grad_out), kv_out[:1], 4, "pack_qo")
+    jobs = [(GW, [[qo_at(m, g) for g in range(kv_heads)] for m in range(1, heads)])]
+    packed = pack(jobs, (queries, grad_out), kv_out[:1], 4, "pack_qo")
     handed = swap(gate(packed[2], kv[1:]), "head", heads, 1)
+    from_across = swap(gate(packed[1], kv[1:]), "head", heads, 2)
+    from_corner = swap(handed, "head", heads, 2)
 
     merged, hide = pl.pallas_call(
         functools.partial(merge_kernel, heads),
@@ -389,13 +364,10 @@
     for m in range(1, shards):
         low = m & -m
         held[m] = swap(held[m - low], "ctx", shards, low)
-    from_core = swap(gate(packed[0], [held[shards // 2]]), "head", heads, 1)
-    from_across = [swap(join(packed[1], handed, [merged]), "head", heads, 2)]
-    for g in range(1, kv_heads):
-        handed = swap(gate(packed[2 * g + 2], [merged]), "head", heads, 1)
-        both = join(packed[2 * g + 1], handed, ())
-        late = [held[m] for m in range(1, shards - 1)] + from_across[-1:]
-        from_across.append(swap(gate(both, late), "head", heads, 2))
+    late = [held[m] for m in range(1, shards - 1)] + [from_across]
+    from_core = swap(gate(packed[0], late), "head", heads, 1)
+    from_corner = gate(from_corner, (), 40)
+    qo = (from_core, from_across, from_corner)
 
     all_rows = tokens * GROUP
     saved = []
@@ -412,7 +384,7 @@
                 shape(HD, slots),
                 shape(half, 2 * HD),
             ],
-            in_specs=anywhere(2) + in_vmem(3 + heads + shards) + anywhere(g > 0),
+            in_specs=anywhere(2) + in_vmem(heads + heads + shards) + anywhere(g > 0),
             out_specs=in_vmem(8),
             scratch_shapes=[
                 pltpu.VMEM((slots + rows, 2 * HD), jnp.bfloat16),
@@ -433,8 +405,7 @@
             hide,
             *kv,
             *[held[m] for m in order],
-            from_core,
-            from_across[g],
+            *qo,
             *([saved[-1][2]] if g else []),
         )
         saved.append(outs)

time: 61.5 us -> 59.8 us (0.972)
  Pallas kernels: 16.4 us -> 15.3 us
  starting transfers between devices: 19.9 us -> 19 us
    pallas_call x2 -> x0, Pallas kernels: 1.03 us -> none  [join(): pl.pallas_call(join_kernel, out_shape=shape(2 * rows, columns), in_specs=...]
    ppermute x21 -> x20, starting transfers between devices: 19.9 us -> 19 us  [swap(): return lax.ppermute(x, axis, [(i, i ^ m) for i in range(size)])]
    ppermute x21 -> x20, waiting for transfers between devices: 20.2 us -> 20.4 us  [swap(): return lax.ppermute(x, axis, [(i, i ^ m) for i in range(size)])]
  transfers between devices with their start and end apart: 21 -> 20, of which waited for: 10 -> 10; matrix products, arithmetic and copies ran while one was open for 0% -> 0% of each run, Pallas kernels for 24% -> 16%
where the time goes in v9:
time: 59.8 us; the launch traced here: 59.6 us
  waiting for transfers between devices  20.4 us (34%)
  starting transfers between devices  19 us (32%)
  Pallas kernels  15.3 us (26%)
  local copies, waits for them, and re-layouts  4.06 us (7%)
  between operations  0.78 us (1%)
    ppermute x20, waiting for transfers between devices, swap(): return lax.ppermute(x, axis, [(i, i ^ m) for i in range(size)])  20.4 us
    ppermute x20, starting transfers between devices, swap(): return lax.ppermute(x, axis, [(i, i ^ m) for i in range(size)])  19 us
    pallas_call x2, Pallas kernels, local(): pl.pallas_call(functools.partial(attend_kernel, g, order), out_shape=[sha...  9.55 us
    unnamed x14, local copies, waits for them, and re-layouts  4.06 us
    pallas_call x1, Pallas kernels, local(): pl.pallas_call(functools.partial(queries_kernel, heads), out_shape=shape(...  2.19 us
    pallas_call x2, Pallas kernels, local(): pl.pallas_call(functools.partial(terms_kernel, heads), out_shape=[shape(h...  1.8 us
  transfers between devices with their start and end apart: 20, of which 10 were waited for; matrix products, arithmetic and copies ran while one was open for 0% of the time, Pallas kernels for 16%

profile of v9, /device:TPU:0, one launch (start us, length us, event | category | flops | bytes accessed | tf_op | source)
XLA Modules:
  0.0 59.6 jit_solution(1315287890945640771)
XLA Ops:
  0.6 0.9 %copy-done.4 = bf16[48,1024]{1,0:T(8,128)(2,1)S(1)} copy-done((bf16[48,1024]{1,0:T(8,128)(2,1)S(1)}, bf16[48,1024]{1,0:T(8,128)(2,1)}, u32[]{:S(2)}) %copy-start.4) | copy-done | bytes 98328
  1.5 0.9 %copy-done.5 = bf16[48,1024]{1,0:T(8,128)(2,1)S(1)} copy-done((bf16[48,1024]{1,0:T(8,128)(2,1)S(1)}, bf16[48,1024]{1,0:T(8,128)(2,1)}, u32[]{:S(2)}) %copy-start.5) | copy-done | bytes 98328
  2.4 0.5 collective-permute-start
  3.0 2.6 %collective-permute-start.1 = (bf16[48,512]{1,0:T(8,128)(2,1)S(1)}, bf16[48,512]{1,0:T(8,128)(2,1)S(1)}, u32[]{:S(2)}, u32[]{:S(2)}) collective-permute-start(bf16[48,512]{1,0:T(8,128)(2,1)S(1)} %get-tuple-element.44), channel_id=1, source_target_pairs={{0,2},{1,3},{2,0},{3,1},{4,6},{5,7},{6,4},{7,5},{8,10},{9,11},{10,... | collective-permute-start | bytes 147464 | tf_op jit(solution)/shard_map/ppermute | solution.py:281
  5.6 1.1 %copy-done = bf16[48,8192]{1,0:T(8,128)(2,1)S(1)} copy-done((bf16[48,8192]{1,0:T(8,128)(2,1)S(1)}, bf16[48,8192]{1,0:T(8,128)(2,1)}, u32[]{:S(2)}) %copy-start) | copy-done | bytes 786456
  6.7 1.1 %copy-done.2 = bf16[48,8192]{1,0:T(8,128)(2,1)S(1)} copy-done((bf16[48,8192]{1,0:T(8,128)(2,1)S(1)}, bf16[48,8192]{1,0:T(8,128)(2,1)}, u32[]{:S(2)}) %copy-start.2) | copy-done | bytes 786456
  8.3 0.9 %collective-permute-done.2.refs_3_ = bf16[48,512]{1,0:T(8,128)(2,1)S(1)} collective-permute-done((bf16[48,512]{1,0:T(8,128)(2,1)S(1)}, bf16[48,512]{1,0:T(8,128)(2,1)S(1)}, u32[]{:S(2)}, u32[]{:S(2)}) %collective-permute-start.2) | collective-permute-done | bytes 49184 | tf_op jit(solution)/shard_map/ppermute | solution.py:281
  9.4 1.1 %collective-permute-start.10 = (bf16[96,2048]{1,0:T(8,128)(2,1)S(1)}, bf16[96,2048]{1,0:T(8,128)(2,1)S(1)}, u32[]{:S(2)}, u32[]{:S(2)}) collective-permute-start(bf16[96,2048]{1,0:T(8,128)(2,1)S(1)} %gate.4), channel_id=1, source_target_pairs={{0,2},{1,3},{2,0},{3,1},{4,6},{5,7},{6,4},{7,5},{8,10},{9,11},{10,... | collective-permute-start | bytes 1179656 | tf_op jit(solution)/shard_map/ppermute | solution.py:281
  10.8 1.6 %collective-permute-start.4 = (bf16[96,512]{1,0:T(8,128)(2,1)S(1)}, bf16[96,512]{1,0:T(8,128)(2,1)S(1)}, u32[]{:S(2)}, u32[]{:S(2)}) collective-permute-start(bf16[96,512]{1,0:T(8,128)(2,1)S(1)} %get-tuple-element.47.refs_4_), channel_id=1, source_target_pairs={{0,8},{4,12},{8,0},{12,4},{16,24},{20,28},{24,16},{28,20},{1,9},{5... | collective-permute-start | bytes 294920 | tf_op jit(solution)/shard_map/ppermute | solution.py:281
  12.4 2.6 %collective-permute-start.3 = (bf16[96,512]{1,0:T(8,128)(2,1)S(1)}, bf16[96,512]{1,0:T(8,128)(2,1)S(1)}, u32[]{:S(2)}, u32[]{:S(2)}) collective-permute-start(bf16[96,512]{1,0:T(8,128)(2,1)S(1)} %get-tuple-element.47.refs_4_), channel_id=1, source_target_pairs={{0,16},{4,20},{8,24},{12,28},{16,0},{20,4},{24,8},{28,12},{1,17},{... | collective-permute-start | bytes 294920 | tf_op jit(solution)/shard_map/ppermute | solution.py:281
  15.0 1.5 %collective-permute-start.6 = (bf16[96,512]{1,0:T(8,128)(2,1)S(1)}, bf16[96,512]{1,0:T(8,128)(2,1)S(1)}, u32[]{:S(2)}, u32[]{:S(2)}) collective-permute-start(bf16[96,512]{1,0:T(8,128)(2,1)S(1)} %get-tuple-element.47.refs_4_), channel_id=1, source_target_pairs={{0,4},{4,0},{8,12},{12,8},{16,20},{20,16},{24,28},{28,24},{1,5},{5... | collective-permute-start | bytes 294920 | tf_op jit(solution)/shard_map/ppermute | solution.py:281
  16.5 0.5 collective-permute-start.8
  17.0 2.8 %collective-permute-done.3.refs_4_.refs_5_ = bf16[96,512]{1,0:T(8,128)(2,1)S(1)} collective-permute-done((bf16[96,512]{1,0:T(8,128)(2,1)S(1)}, bf16[96,512]{1,0:T(8,128)(2,1)S(1)}, u32[]{:S(2)}, u32[]{:S(2)}) %collective-permute-start.3) | collective-permute-done | bytes 98336 | tf_op jit(solution)/shard_map/ppermute | solution.py:281
  19.8 1.5 %collective-permute-start.7 = (bf16[96,512]{1,0:T(8,128)(2,1)S(1)}, bf16[96,512]{1,0:T(8,128)(2,1)S(1)}, u32[]{:S(2)}, u32[]{:S(2)}) collective-permute-start(bf16[96,512]{1,0:T(8,128)(2,1)S(1)} %collective-permute-done.3.refs_4_.refs_5_), channel_id=1, source_target_pairs={{0,4},{4,0},{8,12},{12,8},{16,20},{20,16},{24,28},{28,24},{1,5},{5... | collective-permute-start | bytes 294920 | tf_op jit(solution)/shard_map/ppermute | solution.py:281
  21.8 1.0 %collective-permute-start.13 = (bf16[96,2048]{1,0:T(8,128)(2,1)S(1)}, bf16[96,2048]{1,0:T(8,128)(2,1)S(1)}, u32[]{:S(2)}, u32[]{:S(2)}) collective-permute-start(bf16[96,2048]{1,0:T(8,128)(2,1)S(1)} %collective-permute-done.12), channel_id=1, source_target_pairs={{0,2},{1,3},{2,0},{3,1},{4,6},{5,7},{6,4},{7,5},{8,10},{9,11},{10,... | collective-permute-start | bytes 1179656 | tf_op jit(solution)/shard_map/ppermute | solution.py:281
  22.8 1.6 %collective-permute-done.7.refs_5_.refs_9_ = bf16[96,512]{1,0:T(8,128)(2,1)S(1)} collective-permute-done((bf16[96,512]{1,0:T(8,128)(2,1)S(1)}, bf16[96,512]{1,0:T(8,128)(2,1)S(1)}, u32[]{:S(2)}, u32[]{:S(2)}) %collective-permute-start.7) | collective-permute-done | bytes 98336 | tf_op jit(solution)/shard_map/ppermute | solution.py:281
  24.4 1.5 %collective-permute-done.5.refs_6_.refs_7_ = bf16[96,512]{1,0:T(8,128)(2,1)S(1)} collective-permute-done((bf16[96,512]{1,0:T(8,128)(2,1)S(1)}, bf16[96,512]{1,0:T(8,128)(2,1)S(1)}, u32[]{:S(2)}, u32[]{:S(2)}) %collective-permute-start.5) | collective-permute-done | bytes 98336 | tf_op jit(solution)/shard_map/ppermute | solution.py:281
  26.0 0.9 %collective-permute-start.9 = (bf16[96,512]{1,0:T(8,128)(2,1)S(1)}, bf16[96,512]{1,0:T(8,128)(2,1)S(1)}, u32[]{:S(2)}, u32[]{:S(2)}) collective-permute-start(bf16[96,512]{1,0:T(8,128)(2,1)S(1)} %collective-permute-done.5.refs_6_.refs_7_), channel_id=1, source_target_pairs={{0,4},{4,0},{8,12},{12,8},{16,20},{20,16},{24,28},{28,24},{1,5},{5... | collective-permute-start | bytes 294920 | tf_op jit(solution)/shard_map/ppermute | solution.py:281
  26.9 4.3 %collective-permute-done.13.refs_0_ = bf16[96,2048]{1,0:T(8,128)(2,1)S(1)} collective-permute-done((bf16[96,2048]{1,0:T(8,128)(2,1)S(1)}, bf16[96,2048]{1,0:T(8,128)(2,1)S(1)}, u32[]{:S(2)}, u32[]{:S(2)}) %collective-permute-start.13) | collective-permute-done | bytes 393248 | tf_op jit(solution)/shard_map/ppermute | solution.py:281
  31.3 4.7 %attend.2 = (bf16[768,1536]{1,0:T(8,128)(2,1)S(1)}, bf16[768,1536]{1,0:T(8,128)(2,1)S(1)}, bf16[48,1536]{1,0:T(8,128)(2,1)S(1)}, bf16[48,1536]{1,0:T(8,128)(2,1)...) custom-call(bf16[48,8192]{1,0:T(8,128)(2,1)S(1)} %copy-done.1, ...), custom_call_target="tpu_custom_call" | custom-call | flops 962592768 | bytes 8388608 | tf_op jit(solution)/shard_map/attend/pallas_call | solution.py:375
  36.0 0.9 %collective-permute-start.14 = (bf16[384,256]{1,0:T(8,128)(2,1)S(1)}, bf16[384,256]{1,0:T(8,128)(2,1)S(1)}, u32[]{:S(2)}, u32[]{:S(2)}) collective-permute-start(bf16[384,256]{1,0:T(8,128)(2,1)S(1)} %get-tuple-element.63), channel_id=1, source_target_pairs={{0,4},{4,0},{8,12},{12,8},{16,20},{20,16},{24,28},{28,24},{1,5},{5... | collective-permute-start | bytes 589832 | tf_op jit(solution)/shard_map/ppermute | solution.py:281
  36.9 4.8 %attend.3 = (bf16[768,1536]{1,0:T(8,128)(2,1)S(1)}, bf16[768,1536]{1,0:T(8,128)(2,1)S(1)}, bf16[48,1536]{1,0:T(8,128)(2,1)S(1)}, bf16[48,1536]{1,0:T(8,128)(2,1)...) custom-call(bf16[48,8192]{1,0:T(8,128)(2,1)S(1)} %copy-done.1, ...), custom_call_target="tpu_custom_call" | custom-call | flops 962592768 | bytes 8388608 | tf_op jit(solution)/shard_map/attend/pallas_call | solution.py:375
  41.7 1.3 %collective-permute-start.17 = (bf16[384,256]{1,0:T(8,128)(2,1)S(1)}, bf16[384,256]{1,0:T(8,128)(2,1)S(1)}, u32[]{:S(2)}, u32[]{:S(2)}) collective-permute-start(bf16[384,256]{1,0:T(8,128)(2,1)S(1)} %get-tuple-element.73), channel_id=1, source_target_pairs={{0,4},{4,0},{8,12},{12,8},{16,20},{20,16},{24,28},{28,24},{1,5},{5... | collective-permute-start | bytes 589832 | tf_op jit(solution)/shard_map/ppermute | solution.py:281
  43.0 0.9 %terms.2 = (f32[384,256]{1,0:T(8,128)S(1)}, f32[192,256]{1,0:T(8,128)S(1)}) custom-call(bf16[768,1536]{1,0:T(8,128)(2,1)S(1)} %get-tuple-element.58.p_ref, bf16[768,1536]{1,0:T(8,128)(2,1)S(1)} %get-tuple-element.51.refs_4_.ds_ref, bf16[48,1536]{1,0:T(8,128)(2,1)S(1)} %get-tuple-element.54.refs_15_.own_p_ref, ...), custom_call_target="tpu_custom_call" | custom-call | flops 301989888 | bytes 1048576 | tf_op jit(solution)/shard_map/terms/pallas_call | solution.py:416
  43.9 0.9 %terms.3 = (f32[384,256]{1,0:T(8,128)S(1)}, f32[192,256]{1,0:T(8,128)S(1)}) custom-call(bf16[768,1536]{1,0:T(8,128)(2,1)S(1)} %get-tuple-element.69.p_ref, bf16[768,1536]{1,0:T(8,128)(2,1)S(1)} %get-tuple-element.55.refs_7_.ds_ref, bf16[48,1536]{1,0:T(8,128)(2,1)S(1)} %get-tuple-element.61.after_ref.own_p_ref, ...), custom_call_target="tpu_custom_call" | custom-call | flops 301989888 | bytes 1048576 | tf_op jit(solution)/shard_map/terms/pallas_call | solution.py:416
  45.3 2.7 %collective-permute-done.17.far_ref = bf16[384,256]{1,0:T(8,128)(2,1)S(1)} collective-permute-done((bf16[384,256]{1,0:T(8,128)(2,1)S(1)}, bf16[384,256]{1,0:T(8,128)(2,1)S(1)}, u32[]{:S(2)}, u32[]{:S(2)}) %collective-permute-start.17) | collective-permute-done | bytes 196640 | tf_op jit(solution)/shard_map/ppermute | solution.py:281
  48.2 1.8 %collective-permute-done.15.far_ref = bf16[192,256]{1,0:T(8,128)(2,1)S(1)} collective-permute-done((bf16[192,256]{1,0:T(8,128)(2,1)S(1)}, bf16[192,256]{1,0:T(8,128)(2,1)S(1)}, u32[]{:S(2)}, u32[]{:S(2)}) %collective-permute-start.15) | collective-permute-done | bytes 98336 | tf_op jit(solution)/shard_map/ppermute | solution.py:281
  50.1 1.2 %collective-permute-start.16 = (bf16[96,256]{1,0:T(8,128)(2,1)S(1)}, bf16[96,256]{1,0:T(8,128)(2,1)S(1)}, u32[]{:S(2)}, u32[]{:S(2)}) collective-permute-start(bf16[96,256]{1,0:T(8,128)(2,1)S(1)} %get-tuple-element.67), channel_id=1, source_target_pairs={{0,16},{4,20},{8,24},{12,28},{16,0},{20,4},{24,8},{28,12},{1,17},{... | collective-permute-start | bytes 147464 | tf_op jit(solution)/shard_map/ppermute | solution.py:281
  51.3 1.8 %collective-permute-done.18.far_ref = bf16[192,256]{1,0:T(8,128)(2,1)S(1)} collective-permute-done((bf16[192,256]{1,0:T(8,128)(2,1)S(1)}, bf16[192,256]{1,0:T(8,128)(2,1)S(1)}, u32[]{:S(2)}, u32[]{:S(2)}) %collective-permute-start.18) | collective-permute-done | bytes 98336 | tf_op jit(solution)/shard_map/ppermute | solution.py:281
  53.5 2.2 %queries.1 = bf16[192,2048]{1,0:T(8,128)(2,1)} custom-call(bf16[48,512]{1,0:T(8,128)(2,1)S(1)} %get-tuple-element.42.refs_0_.refs_2_, bf16[48,512]{1,0:T(8,128)(2,1)S(1)} %collective-permute-done.refs_1_, bf16[48,512]{1,0:T(8,128)(2,1)S(1)} %collective-permute-done.1.refs_2_, bf16[48,512]{1,0:T(8,128)(2,1)S(1)} %collective-permute-done.2.refs_3_, ...), custom_call_target="tpu_custom_call" | custom-call | flops 603979776 | bytes 1048576 | tf_op jit(solution)/shard_map/queries/pallas_call | solution.py:432
  56.0 2.5 %collective-permute-done.19.refs_4_ = bf16[96,256]{1,0:T(8,128)(2,1)S(1)} collective-permute-done((bf16[96,256]{1,0:T(8,128)(2,1)S(1)}, bf16[96,256]{1,0:T(8,128)(2,1)S(1)}, u32[]{:S(2)}, u32[]{:S(2)}) %collective-permute-start.19) | collective-permute-done | bytes 49184 | tf_op jit(solution)/shard_map/ppermute | solution.py:281
  58.5 1.0 %spread.1 = (bf16[192,256]{1,0:T(8,128)(2,1)}, bf16[192,256]{1,0:T(8,128)(2,1)}) custom-call(s32[2,192]{1,0:T(2,128)S(1)} %copy-done.6, f32[96,256]{1,0:T(8,128)S(1)} %get-tuple-element.66.refs_0_, bf16[96,256]{1,0:T(8,128)(2,1)S(1)} %collective-permute-done.16.refs_1_, f32[192,256]{1,0:T(8,128)S(1)} %get-tuple-element.68.refs_2_, ...), custom_call_target="tpu_custom_call" | custom-call | tf_op jit(solution)/shard_map/spread/pallas_call | solution.py:461
  (39 shorter events, 2.8 us)
Async XLA Ops:
  0.6 0.9 %copy-start.4 = (bf16[48,1024]{1,0:T(8,128)(2,1)S(1)}, bf16[48,1024]{1,0:T(8,128)(2,1)}, u32[]{:S(2)}) copy-start(bf16[48,1024]{1,0:T(8,128)(2,1)} %key_ref.1) | copy-start | bytes 294916
  1.5 0.9 %copy-start.5 = (bf16[48,1024]{1,0:T(8,128)(2,1)S(1)}, bf16[48,1024]{1,0:T(8,128)(2,1)}, u32[]{:S(2)}) copy-start(bf16[48,1024]{1,0:T(8,128)(2,1)} %value_ref.1) | copy-start | bytes 294916
  2.4 8.1 %copy-start.6 = (s32[2,192]{1,0:T(2,128)S(1)}, s32[2,192]{1,0:T(2,128)}, u32[]{:S(2)}) copy-start(s32[2,192]{1,0:T(2,128)} %seg_ref.3) | copy-start | bytes 4612
  2.4 5.8 %collective-permute-start = (bf16[48,512]{1,0:T(8,128)(2,1)S(1)}, bf16[48,512]{1,0:T(8,128)(2,1)S(1)}, u32[]{:S(2)}, u32[]{:S(2)}) collective-permute-start(bf16[48,512]{1,0:T(8,128)(2,1)S(1)} %get-tuple-element.43), channel_id=1, source_target_pairs={{0,1},{1,0},{2,3},{3,2},{4,5},{5,4},{6,7},{7,6},{8,9},{9,8},{10,11... | collective-permute-start | bytes 147464 | tf_op jit(solution)/shard_map/ppermute | solution.py:281
  3.0 5.3 %collective-permute-start.1 = (bf16[48,512]{1,0:T(8,128)(2,1)S(1)}, bf16[48,512]{1,0:T(8,128)(2,1)S(1)}, u32[]{:S(2)}, u32[]{:S(2)}) collective-permute-start(bf16[48,512]{1,0:T(8,128)(2,1)S(1)} %get-tuple-element.44), channel_id=1, source_target_pairs={{0,2},{1,3},{2,0},{3,1},{4,6},{5,7},{6,4},{7,5},{8,10},{9,11},{10,... | collective-permute-start | bytes 147464 | tf_op jit(solution)/shard_map/ppermute | solution.py:281
  5.5 3.7 %collective-permute-start.2 = (bf16[48,512]{1,0:T(8,128)(2,1)S(1)}, bf16[48,512]{1,0:T(8,128)(2,1)S(1)}, u32[]{:S(2)}, u32[]{:S(2)}) collective-permute-start(bf16[48,512]{1,0:T(8,128)(2,1)S(1)} %get-tuple-element.45), channel_id=1, source_target_pairs={{0,3},{1,2},{2,1},{3,0},{4,7},{5,6},{6,5},{7,4},{8,11},{9,10},{10,... | collective-permute-start | bytes 147464 | tf_op jit(solution)/shard_map/ppermute | solution.py:281
  5.6 1.1 %copy-start = (bf16[48,8192]{1,0:T(8,128)(2,1)S(1)}, bf16[48,8192]{1,0:T(8,128)(2,1)}, u32[]{:S(2)}) copy-start(bf16[48,8192]{1,0:T(8,128)(2,1)} %q_ref.3) | copy-start | bytes 2359300
  6.7 1.1 %copy-start.2 = (bf16[48,8192]{1,0:T(8,128)(2,1)S(1)}, bf16[48,8192]{1,0:T(8,128)(2,1)}, u32[]{:S(2)}) copy-start(bf16[48,8192]{1,0:T(8,128)(2,1)} %o_ref.3) | copy-start | bytes 2359300
  8.3 23.0 %copy-start.1 = (bf16[48,8192]{1,0:T(8,128)(2,1)S(1)}, bf16[48,8192]{1,0:T(8,128)(2,1)}, u32[]{:S(2)}) copy-start(bf16[48,8192]{1,0:T(8,128)(2,1)} %q_ref.3) | copy-start | bytes 2359300
  8.3 23.0 %copy-start.3 = (bf16[48,8192]{1,0:T(8,128)(2,1)S(1)}, bf16[48,8192]{1,0:T(8,128)(2,1)}, u32[]{:S(2)}) copy-start(bf16[48,8192]{1,0:T(8,128)(2,1)} %o_ref.3) | copy-start | bytes 2359300
  9.2 12.6 %collective-permute-start.12 = (bf16[96,2048]{1,0:T(8,128)(2,1)S(1)}, bf16[96,2048]{1,0:T(8,128)(2,1)S(1)}, u32[]{:S(2)}, u32[]{:S(2)}) collective-permute-start(bf16[96,2048]{1,0:T(8,128)(2,1)S(1)} %gate.6), channel_id=1, source_target_pairs={{0,1},{1,0},{2,3},{3,2},{4,5},{5,4},{6,7},{7,6},{8,9},{9,8},{10,11... | collective-permute-start | bytes 1179656 | tf_op jit(solution)/shard_map/ppermute | solution.py:281
  9.4 16.6 %collective-permute-start.10 = (bf16[96,2048]{1,0:T(8,128)(2,1)S(1)}, bf16[96,2048]{1,0:T(8,128)(2,1)S(1)}, u32[]{:S(2)}, u32[]{:S(2)}) collective-permute-start(bf16[96,2048]{1,0:T(8,128)(2,1)S(1)} %gate.4), channel_id=1, source_target_pairs={{0,2},{1,3},{2,0},{3,1},{4,6},{5,7},{6,4},{7,5},{8,10},{9,11},{10,... | collective-permute-start | bytes 1179656 | tf_op jit(solution)/shard_map/ppermute | solution.py:281
  10.8 5.7 %collective-permute-start.4 = (bf16[96,512]{1,0:T(8,128)(2,1)S(1)}, bf16[96,512]{1,0:T(8,128)(2,1)S(1)}, u32[]{:S(2)}, u32[]{:S(2)}) collective-permute-start(bf16[96,512]{1,0:T(8,128)(2,1)S(1)} %get-tuple-element.47.refs_4_), channel_id=1, source_target_pairs={{0,8},{4,12},{8,0},{12,4},{16,24},{20,28},{24,16},{28,20},{1,9},{5... | collective-permute-start | bytes 294920 | tf_op jit(solution)/shard_map/ppermute | solution.py:281
  12.4 7.4 %collective-permute-start.3 = (bf16[96,512]{1,0:T(8,128)(2,1)S(1)}, bf16[96,512]{1,0:T(8,128)(2,1)S(1)}, u32[]{:S(2)}, u32[]{:S(2)}) collective-permute-start(bf16[96,512]{1,0:T(8,128)(2,1)S(1)} %get-tuple-element.47.refs_4_), channel_id=1, source_target_pairs={{0,16},{4,20},{8,24},{12,28},{16,0},{20,4},{24,8},{28,12},{1,17},{... | collective-permute-start | bytes 294920 | tf_op jit(solution)/shard_map/ppermute | solution.py:281
  15.0 6.4 %collective-permute-start.6 = (bf16[96,512]{1,0:T(8,128)(2,1)S(1)}, bf16[96,512]{1,0:T(8,128)(2,1)S(1)}, u32[]{:S(2)}, u32[]{:S(2)}) collective-permute-start(bf16[96,512]{1,0:T(8,128)(2,1)S(1)} %get-tuple-element.47.refs_4_), channel_id=1, source_target_pairs={{0,4},{4,0},{8,12},{12,8},{16,20},{20,16},{24,28},{28,24},{1,5},{5... | collective-permute-start | bytes 294920 | tf_op jit(solution)/shard_map/ppermute | solution.py:281
  16.5 6.3 %collective-permute-start.8 = (bf16[96,512]{1,0:T(8,128)(2,1)S(1)}, bf16[96,512]{1,0:T(8,128)(2,1)S(1)}, u32[]{:S(2)}, u32[]{:S(2)}) collective-permute-start(bf16[96,512]{1,0:T(8,128)(2,1)S(1)} %collective-permute-done.4.refs_2_.refs_6_), channel_id=1, source_target_pairs={{0,4},{4,0},{8,12},{12,8},{16,20},{20,16},{24,28},{28,24},{1,5},{5... | collective-permute-start | bytes 294920 | tf_op jit(solution)/shard_map/ppermute | solution.py:281
  19.8 4.6 %collective-permute-start.7 = (bf16[96,512]{1,0:T(8,128)(2,1)S(1)}, bf16[96,512]{1,0:T(8,128)(2,1)S(1)}, u32[]{:S(2)}, u32[]{:S(2)}) collective-permute-start(bf16[96,512]{1,0:T(8,128)(2,1)S(1)} %collective-permute-done.3.refs_4_.refs_5_), channel_id=1, source_target_pairs={{0,4},{4,0},{8,12},{12,8},{16,20},{20,16},{24,28},{28,24},{1,5},{5... | collective-permute-start | bytes 294920 | tf_op jit(solution)/shard_map/ppermute | solution.py:281
  21.4 4.6 %collective-permute-start.5 = (bf16[96,512]{1,0:T(8,128)(2,1)S(1)}, bf16[96,512]{1,0:T(8,128)(2,1)S(1)}, u32[]{:S(2)}, u32[]{:S(2)}) collective-permute-start(bf16[96,512]{1,0:T(8,128)(2,1)S(1)} %collective-permute-done.3.refs_4_.refs_5_), channel_id=1, source_target_pairs={{0,8},{4,12},{8,0},{12,4},{16,24},{20,28},{24,16},{28,20},{1,9},{5... | collective-permute-start | bytes 294920 | tf_op jit(solution)/shard_map/ppermute | solution.py:281
  21.8 9.5 %collective-permute-start.13 = (bf16[96,2048]{1,0:T(8,128)(2,1)S(1)}, bf16[96,2048]{1,0:T(8,128)(2,1)S(1)}, u32[]{:S(2)}, u32[]{:S(2)}) collective-permute-start(bf16[96,2048]{1,0:T(8,128)(2,1)S(1)} %collective-permute-done.12), channel_id=1, source_target_pairs={{0,2},{1,3},{2,0},{3,1},{4,6},{5,7},{6,4},{7,5},{8,10},{9,11},{10,... | collective-permute-start | bytes 1179656 | tf_op jit(solution)/shard_map/ppermute | solution.py:281
  26.0 5.3 %collective-permute-start.11 = (bf16[96,2048]{1,0:T(8,128)(2,1)S(1)}, bf16[96,2048]{1,0:T(8,128)(2,1)S(1)}, u32[]{:S(2)}, u32[]{:S(2)}) collective-permute-start(bf16[96,2048]{1,0:T(8,128)(2,1)S(1)} %gate.5), channel_id=1, source_target_pairs={{0,1},{1,0},{2,3},{3,2},{4,5},{5,4},{6,7},{7,6},{8,9},{9,8},{10,11... | collective-permute-start | bytes 1179656 | tf_op jit(solution)/shard_map/ppermute | solution.py:281
  26.0 5.3 %collective-permute-start.9 = (bf16[96,512]{1,0:T(8,128)(2,1)S(1)}, bf16[96,512]{1,0:T(8,128)(2,1)S(1)}, u32[]{:S(2)}, u32[]{:S(2)}) collective-permute-start(bf16[96,512]{1,0:T(8,128)(2,1)S(1)} %collective-permute-done.5.refs_6_.refs_7_), channel_id=1, source_target_pairs={{0,4},{4,0},{8,12},{12,8},{16,20},{20,16},{24,28},{28,24},{1,5},{5... | collective-permute-start | bytes 294920 | tf_op jit(solution)/shard_map/ppermute | solution.py:281
  36.0 8.8 %collective-permute-start.14 = (bf16[384,256]{1,0:T(8,128)(2,1)S(1)}, bf16[384,256]{1,0:T(8,128)(2,1)S(1)}, u32[]{:S(2)}, u32[]{:S(2)}) collective-permute-start(bf16[384,256]{1,0:T(8,128)(2,1)S(1)} %get-tuple-element.63), channel_id=1, source_target_pairs={{0,4},{4,0},{8,12},{12,8},{16,20},{20,16},{24,28},{28,24},{1,5},{5... | collective-permute-start | bytes 589832 | tf_op jit(solution)/shard_map/ppermute | solution.py:281
  41.7 6.3 %collective-permute-start.17 = (bf16[384,256]{1,0:T(8,128)(2,1)S(1)}, bf16[384,256]{1,0:T(8,128)(2,1)S(1)}, u32[]{:S(2)}, u32[]{:S(2)}) collective-permute-start(bf16[384,256]{1,0:T(8,128)(2,1)S(1)} %get-tuple-element.73), channel_id=1, source_target_pairs={{0,4},{4,0},{8,12},{12,8},{16,20},{20,16},{24,28},{28,24},{1,5},{5... | collective-permute-start | bytes 589832 | tf_op jit(solution)/shard_map/ppermute | solution.py:281
  44.9 5.2 %collective-permute-start.15 = (bf16[192,256]{1,0:T(8,128)(2,1)S(1)}, bf16[192,256]{1,0:T(8,128)(2,1)S(1)}, u32[]{:S(2)}, u32[]{:S(2)}) collective-permute-start(bf16[192,256]{1,0:T(8,128)(2,1)S(1)} %get-tuple-element.65), channel_id=1, source_target_pairs={{0,8},{4,12},{8,0},{12,4},{16,24},{20,28},{24,16},{28,20},{1,9},{5... | collective-permute-start | bytes 294920 | tf_op jit(solution)/shard_map/ppermute | solution.py:281
  48.0 5.1 %collective-permute-start.18 = (bf16[192,256]{1,0:T(8,128)(2,1)S(1)}, bf16[192,256]{1,0:T(8,128)(2,1)S(1)}, u32[]{:S(2)}, u32[]{:S(2)}) collective-permute-start(bf16[192,256]{1,0:T(8,128)(2,1)S(1)} %get-tuple-element.75), channel_id=1, source_target_pairs={{0,8},{4,12},{8,0},{12,4},{16,24},{20,28},{24,16},{28,20},{1,9},{5... | collective-permute-start | bytes 294920 | tf_op jit(solution)/shard_map/ppermute | solution.py:281
  50.1 5.9 %collective-permute-start.16 = (bf16[96,256]{1,0:T(8,128)(2,1)S(1)}, bf16[96,256]{1,0:T(8,128)(2,1)S(1)}, u32[]{:S(2)}, u32[]{:S(2)}) collective-permute-start(bf16[96,256]{1,0:T(8,128)(2,1)S(1)} %get-tuple-element.67), channel_id=1, source_target_pairs={{0,16},{4,20},{8,24},{12,28},{16,0},{20,4},{24,8},{28,12},{1,17},{... | collective-permute-start | bytes 147464 | tf_op jit(solution)/shard_map/ppermute | solution.py:281
  53.1 5.4 %collective-permute-start.19 = (bf16[96,256]{1,0:T(8,128)(2,1)S(1)}, bf16[96,256]{1,0:T(8,128)(2,1)S(1)}, u32[]{:S(2)}, u32[]{:S(2)}) collective-permute-start(bf16[96,256]{1,0:T(8,128)(2,1)S(1)} %get-tuple-element.77), channel_id=1, source_target_pairs={{0,16},{4,20},{8,24},{12,28},{16,0},{20,4},{24,8},{28,12},{1,17},{... | collective-permute-start | bytes 147464 | tf_op jit(solution)/shard_map/ppermute | solution.py:281

commit v10 on v9

--- a/solution.py
+++ b/solution.py
@@ -117,6 +117,10 @@
         hide_ref[g] = hide.T[:tokens].astype(jnp.bfloat16)
 
 
+def folded(x, reduce):
+    return reduce(x.reshape(x.shape[0] // 8, 8, x.shape[1]), axis=0)
+
+
 def attend_kernel(g, order, q_ref, o_ref, hide_ref, *refs):
     shards = len(order)
     heads = 4
@@ -124,8 +128,8 @@
     qo_pieces = refs[: heads - 1]
     (
         p_ref, ds_ref, own_p_ref, own_ds_ref, qs_ref, os_ref, kt_ref, far_ref,
-        kx, vx, mine, sems,
-    ) = refs[-12:]
+        kx, vx, mine, s_ref, g_ref, sems,
+    ) = refs[-14:]
     rows = q_ref.shape[0]
     kv_heads = hide_ref.shape[0]
     slots = shards * SLOT_DEV
@@ -179,21 +183,30 @@
         qs_ref[chunk, :] = q2
         os_ref[chunk, :] = o2
         qx = jnp.concatenate([q2, jnp.concatenate([hide_ref[g, at, :]] * GROUP, axis=0)], axis=1)
-        scores = nt(kx[...], qx)
-        own_score = jnp.sum(jnp.where(eye, scores[slots:], 0.0), axis=0, keepdims=True)
-        scores = scores[:slots]
-        top = jnp.maximum(jnp.max(scores, axis=0, keepdims=True), own_score)
-        weights = jnp.exp2((scores - top) * factor)
+        s_at, g_at = s_ref.at[m % 2], g_ref.at[m % 2]
+        s_at[...] = nt(kx[...], qx)
+        g_at[...] = nt(vx[...], o2)
+        own_score = jnp.sum(jnp.where(eye, s_at[slots:, :], 0.0), axis=0, keepdims=True)
+        own_grad_prob = jnp.sum(jnp.where(eye, g_at[slots:, :], 0.0), axis=0, keepdims=True)
+        parts = [slice(r * SLOT_DEV, (r + 1) * SLOT_DEV) for r in range(shards)]
+        top = folded(functools.reduce(jnp.maximum, [s_at[part, :] for part in parts]), jnp.max)
+        top = jnp.maximum(jnp.max(top, axis=0, keepdims=True), own_score)
+        total = 0.0
+        delta = 0.0
+        for part in parts:
+            weights = jnp.exp2((s_at[part, :] - top) * factor)
+            total = total + folded(weights, jnp.sum)
+            delta = delta + folded(weights * g_at[part, :], jnp.sum)
         own_weight = jnp.exp2((own_score - top) * factor)
-        inverse = 1.0 / (jnp.sum(weights, axis=0, keepdims=True) + own_weight)
-        probs = weights * inverse
-        own_prob = own_weight * inverse
-        grad_probs = nt(vx[...], o2)
-        own_grad_prob = jnp.sum(jnp.where(eye, grad_probs[slots:], 0.0), axis=0, keepdims=True)
-        grad_probs = grad_probs[:slots]
-        delta = jnp.sum(probs * grad_probs, axis=0, keepdims=True) + own_prob * own_grad_prob
-        ds_ref[:, chunk] = (probs * (grad_probs - delta)).astype(jnp.bfloat16)
-        p_ref[:, chunk] = probs.astype(jnp.bfloat16)
+        total = jnp.sum(total, axis=0, keepdims=True) + own_weight
+        delta = jnp.sum(delta, axis=0, keepdims=True) + own_weight * own_grad_prob
+        delta = delta / total
+        own_prob = own_weight / total
+        log_total = jnp.log2(total)
+        for part in parts:
+            probs = jnp.exp2((s_at[part, :] - top) * factor - log_total)
+            p_ref[part, chunk] = probs.astype(jnp.bfloat16)
+            ds_ref[part, chunk] = (probs * (g_at[part, :] - delta)).astype(jnp.bfloat16)
         own_grad_score = own_prob * (own_grad_prob - delta)
         own_p_ref[:, chunk] = jnp.where(eye, own_prob, 0.0).astype(jnp.bfloat16)
         own_ds_ref[:, chunk] = jnp.where(eye, own_grad_score, 0.0).astype(jnp.bfloat16)
@@ -390,6 +403,8 @@
                 pltpu.VMEM((slots + rows, 2 * HD), jnp.bfloat16),
                 pltpu.VMEM((slots + rows, HD), jnp.bfloat16),
                 pltpu.VMEM((rows, 2 * GW), jnp.bfloat16),
+                pltpu.VMEM((2, slots + rows, GROUP * rows), jnp.float32),
+                pltpu.VMEM((2, slots + rows, GROUP * rows), jnp.float32),
                 pltpu.SemaphoreType.DMA((2,)),
             ],
             compiler_params=params(24),

time: 59.8 us -> 59.4 us (level)
  no operation moved by 1% of the time
where the time goes in v10:
time: 59.4 us; the launch traced here: 59.1 us
  waiting for transfers between devices  20.4 us (34%)
  starting transfers between devices  19 us (32%)
  Pallas kernels  14.9 us (25%)
  local copies, waits for them, and re-layouts  4.06 us (7%)
  between operations  0.78 us (1%)
    ppermute x20, waiting for transfers between devices, swap(): return lax.ppermute(x, axis, [(i, i ^ m) for i in range(size)])  20.4 us
    ppermute x20, starting transfers between devices, swap(): return lax.ppermute(x, axis, [(i, i ^ m) for i in range(size)])  19 us
    pallas_call x2, Pallas kernels, local(): pl.pallas_call(functools.partial(attend_kernel, g, order), out_shape=[sha...  9.13 us
    unnamed x14, local copies, waits for them, and re-layouts  4.06 us
    pallas_call x1, Pallas kernels, local(): pl.pallas_call(functools.partial(queries_kernel, heads), out_shape=shape(...  2.2 us
    pallas_call x2, Pallas kernels, local(): pl.pallas_call(functools.partial(terms_kernel, heads), out_shape=[shape(h...  1.8 us
  transfers between devices with their start and end apart: 20, of which 10 were waited for; matrix products, arithmetic and copies ran while one was open for 0% of the time, Pallas kernels for 16%

profile of v10, /device:TPU:0, one launch (start us, length us, event | category | flops | bytes accessed | tf_op | source)
XLA Modules:
  0.0 59.1 jit_solution(15283756136317311375)
XLA Ops:
  0.6 0.9 %copy-done.4 = bf16[48,1024]{1,0:T(8,128)(2,1)S(1)} copy-done((bf16[48,1024]{1,0:T(8,128)(2,1)S(1)}, bf16[48,1024]{1,0:T(8,128)(2,1)}, u32[]{:S(2)}) %copy-start.4) | copy-done | bytes 98328
  1.5 0.9 %copy-done.5 = bf16[48,1024]{1,0:T(8,128)(2,1)S(1)} copy-done((bf16[48,1024]{1,0:T(8,128)(2,1)S(1)}, bf16[48,1024]{1,0:T(8,128)(2,1)}, u32[]{:S(2)}) %copy-start.5) | copy-done | bytes 98328
  2.4 0.5 collective-permute-start
  3.0 2.6 %collective-permute-start.1 = (bf16[48,512]{1,0:T(8,128)(2,1)S(1)}, bf16[48,512]{1,0:T(8,128)(2,1)S(1)}, u32[]{:S(2)}, u32[]{:S(2)}) collective-permute-start(bf16[48,512]{1,0:T(8,128)(2,1)S(1)} %get-tuple-element.44), channel_id=1, source_target_pairs={{0,2},{1,3},{2,0},{3,1},{4,6},{5,7},{6,4},{7,5},{8,10},{9,11},{10,... | collective-permute-start | bytes 147464 | tf_op jit(solution)/shard_map/ppermute | solution.py:294
  5.6 1.1 %copy-done = bf16[48,8192]{1,0:T(8,128)(2,1)S(1)} copy-done((bf16[48,8192]{1,0:T(8,128)(2,1)S(1)}, bf16[48,8192]{1,0:T(8,128)(2,1)}, u32[]{:S(2)}) %copy-start) | copy-done | bytes 786456
  6.7 1.1 %copy-done.2 = bf16[48,8192]{1,0:T(8,128)(2,1)S(1)} copy-done((bf16[48,8192]{1,0:T(8,128)(2,1)S(1)}, bf16[48,8192]{1,0:T(8,128)(2,1)}, u32[]{:S(2)}) %copy-start.2) | copy-done | bytes 786456
  8.3 0.9 %collective-permute-done.2.refs_3_ = bf16[48,512]{1,0:T(8,128)(2,1)S(1)} collective-permute-done((bf16[48,512]{1,0:T(8,128)(2,1)S(1)}, bf16[48,512]{1,0:T(8,128)(2,1)S(1)}, u32[]{:S(2)}, u32[]{:S(2)}) %collective-permute-start.2) | collective-permute-done | bytes 49184 | tf_op jit(solution)/shard_map/ppermute | solution.py:294
  9.4 1.1 %collective-permute-start.10 = (bf16[96,2048]{1,0:T(8,128)(2,1)S(1)}, bf16[96,2048]{1,0:T(8,128)(2,1)S(1)}, u32[]{:S(2)}, u32[]{:S(2)}) collective-permute-start(bf16[96,2048]{1,0:T(8,128)(2,1)S(1)} %gate.4), channel_id=1, source_target_pairs={{0,2},{1,3},{2,0},{3,1},{4,6},{5,7},{6,4},{7,5},{8,10},{9,11},{10,... | collective-permute-start | bytes 1179656 | tf_op jit(solution)/shard_map/ppermute | solution.py:294
  10.8 1.6 %collective-permute-start.4 = (bf16[96,512]{1,0:T(8,128)(2,1)S(1)}, bf16[96,512]{1,0:T(8,128)(2,1)S(1)}, u32[]{:S(2)}, u32[]{:S(2)}) collective-permute-start(bf16[96,512]{1,0:T(8,128)(2,1)S(1)} %get-tuple-element.47.refs_4_), channel_id=1, source_target_pairs={{0,8},{4,12},{8,0},{12,4},{16,24},{20,28},{24,16},{28,20},{1,9},{5... | collective-permute-start | bytes 294920 | tf_op jit(solution)/shard_map/ppermute | solution.py:294
  12.4 2.6 %collective-permute-start.3 = (bf16[96,512]{1,0:T(8,128)(2,1)S(1)}, bf16[96,512]{1,0:T(8,128)(2,1)S(1)}, u32[]{:S(2)}, u32[]{:S(2)}) collective-permute-start(bf16[96,512]{1,0:T(8,128)(2,1)S(1)} %get-tuple-element.47.refs_4_), channel_id=1, source_target_pairs={{0,16},{4,20},{8,24},{12,28},{16,0},{20,4},{24,8},{28,12},{1,17},{... | collective-permute-start | bytes 294920 | tf_op jit(solution)/shard_map/ppermute | solution.py:294
  15.0 1.5 %collective-permute-start.6 = (bf16[96,512]{1,0:T(8,128)(2,1)S(1)}, bf16[96,512]{1,0:T(8,128)(2,1)S(1)}, u32[]{:S(2)}, u32[]{:S(2)}) collective-permute-start(bf16[96,512]{1,0:T(8,128)(2,1)S(1)} %get-tuple-element.47.refs_4_), channel_id=1, source_target_pairs={{0,4},{4,0},{8,12},{12,8},{16,20},{20,16},{24,28},{28,24},{1,5},{5... | collective-permute-start | bytes 294920 | tf_op jit(solution)/shard_map/ppermute | solution.py:294
  16.5 0.5 collective-permute-start.8
  17.0 2.8 %collective-permute-done.3.refs_4_.refs_5_ = bf16[96,512]{1,0:T(8,128)(2,1)S(1)} collective-permute-done((bf16[96,512]{1,0:T(8,128)(2,1)S(1)}, bf16[96,512]{1,0:T(8,128)(2,1)S(1)}, u32[]{:S(2)}, u32[]{:S(2)}) %collective-permute-start.3) | collective-permute-done | bytes 98336 | tf_op jit(solution)/shard_map/ppermute | solution.py:294
  19.8 1.5 %collective-permute-start.7 = (bf16[96,512]{1,0:T(8,128)(2,1)S(1)}, bf16[96,512]{1,0:T(8,128)(2,1)S(1)}, u32[]{:S(2)}, u32[]{:S(2)}) collective-permute-start(bf16[96,512]{1,0:T(8,128)(2,1)S(1)} %collective-permute-done.3.refs_4_.refs_5_), channel_id=1, source_target_pairs={{0,4},{4,0},{8,12},{12,8},{16,20},{20,16},{24,28},{28,24},{1,5},{5... | collective-permute-start | bytes 294920 | tf_op jit(solution)/shard_map/ppermute | solution.py:294
  21.8 1.0 %collective-permute-start.13 = (bf16[96,2048]{1,0:T(8,128)(2,1)S(1)}, bf16[96,2048]{1,0:T(8,128)(2,1)S(1)}, u32[]{:S(2)}, u32[]{:S(2)}) collective-permute-start(bf16[96,2048]{1,0:T(8,128)(2,1)S(1)} %collective-permute-done.12), channel_id=1, source_target_pairs={{0,2},{1,3},{2,0},{3,1},{4,6},{5,7},{6,4},{7,5},{8,10},{9,11},{10,... | collective-permute-start | bytes 1179656 | tf_op jit(solution)/shard_map/ppermute | solution.py:294
  22.8 1.6 %collective-permute-done.7.refs_5_.refs_9_ = bf16[96,512]{1,0:T(8,128)(2,1)S(1)} collective-permute-done((bf16[96,512]{1,0:T(8,128)(2,1)S(1)}, bf16[96,512]{1,0:T(8,128)(2,1)S(1)}, u32[]{:S(2)}, u32[]{:S(2)}) %collective-permute-start.7) | collective-permute-done | bytes 98336 | tf_op jit(solution)/shard_map/ppermute | solution.py:294
  24.4 1.5 %collective-permute-done.5.refs_6_.refs_7_ = bf16[96,512]{1,0:T(8,128)(2,1)S(1)} collective-permute-done((bf16[96,512]{1,0:T(8,128)(2,1)S(1)}, bf16[96,512]{1,0:T(8,128)(2,1)S(1)}, u32[]{:S(2)}, u32[]{:S(2)}) %collective-permute-start.5) | collective-permute-done | bytes 98336 | tf_op jit(solution)/shard_map/ppermute | solution.py:294
  26.0 0.9 %collective-permute-start.9 = (bf16[96,512]{1,0:T(8,128)(2,1)S(1)}, bf16[96,512]{1,0:T(8,128)(2,1)S(1)}, u32[]{:S(2)}, u32[]{:S(2)}) collective-permute-start(bf16[96,512]{1,0:T(8,128)(2,1)S(1)} %collective-permute-done.5.refs_6_.refs_7_), channel_id=1, source_target_pairs={{0,4},{4,0},{8,12},{12,8},{16,20},{20,16},{24,28},{28,24},{1,5},{5... | collective-permute-start | bytes 294920 | tf_op jit(solution)/shard_map/ppermute | solution.py:294
  26.9 4.3 %collective-permute-done.13.refs_0_ = bf16[96,2048]{1,0:T(8,128)(2,1)S(1)} collective-permute-done((bf16[96,2048]{1,0:T(8,128)(2,1)S(1)}, bf16[96,2048]{1,0:T(8,128)(2,1)S(1)}, u32[]{:S(2)}, u32[]{:S(2)}) %collective-permute-start.13) | collective-permute-done | bytes 393248 | tf_op jit(solution)/shard_map/ppermute | solution.py:294
  31.3 4.5 %attend.2 = (bf16[768,1536]{1,0:T(8,128)(2,1)S(1)}, bf16[768,1536]{1,0:T(8,128)(2,1)S(1)}, bf16[48,1536]{1,0:T(8,128)(2,1)S(1)}, bf16[48,1536]{1,0:T(8,128)(2,1)...) custom-call(bf16[48,8192]{1,0:T(8,128)(2,1)S(1)} %copy-done.1, ...), custom_call_target="tpu_custom_call" | custom-call | flops 962592768 | bytes 8388608 | tf_op jit(solution)/shard_map/attend/pallas_call | solution.py:388
  35.8 0.9 %collective-permute-start.14 = (bf16[384,256]{1,0:T(8,128)(2,1)S(1)}, bf16[384,256]{1,0:T(8,128)(2,1)S(1)}, u32[]{:S(2)}, u32[]{:S(2)}) collective-permute-start(bf16[384,256]{1,0:T(8,128)(2,1)S(1)} %get-tuple-element.63), channel_id=1, source_target_pairs={{0,4},{4,0},{8,12},{12,8},{16,20},{20,16},{24,28},{28,24},{1,5},{5... | collective-permute-start | bytes 589832 | tf_op jit(solution)/shard_map/ppermute | solution.py:294
  36.6 4.6 %attend.3 = (bf16[768,1536]{1,0:T(8,128)(2,1)S(1)}, bf16[768,1536]{1,0:T(8,128)(2,1)S(1)}, bf16[48,1536]{1,0:T(8,128)(2,1)S(1)}, bf16[48,1536]{1,0:T(8,128)(2,1)...) custom-call(bf16[48,8192]{1,0:T(8,128)(2,1)S(1)} %copy-done.1, ...), custom_call_target="tpu_custom_call" | custom-call | flops 962592768 | bytes 8388608 | tf_op jit(solution)/shard_map/attend/pallas_call | solution.py:388
  41.3 1.3 %collective-permute-start.17 = (bf16[384,256]{1,0:T(8,128)(2,1)S(1)}, bf16[384,256]{1,0:T(8,128)(2,1)S(1)}, u32[]{:S(2)}, u32[]{:S(2)}) collective-permute-start(bf16[384,256]{1,0:T(8,128)(2,1)S(1)} %get-tuple-element.73), channel_id=1, source_target_pairs={{0,4},{4,0},{8,12},{12,8},{16,20},{20,16},{24,28},{28,24},{1,5},{5... | collective-permute-start | bytes 589832 | tf_op jit(solution)/shard_map/ppermute | solution.py:294
  42.6 0.9 %terms.2 = (f32[384,256]{1,0:T(8,128)S(1)}, f32[192,256]{1,0:T(8,128)S(1)}) custom-call(bf16[768,1536]{1,0:T(8,128)(2,1)S(1)} %get-tuple-element.58.p_ref, bf16[768,1536]{1,0:T(8,128)(2,1)S(1)} %get-tuple-element.51.refs_4_.ds_ref, bf16[48,1536]{1,0:T(8,128)(2,1)S(1)} %get-tuple-element.54.refs_15_.own_p_ref, ...), custom_call_target="tpu_custom_call" | custom-call | flops 301989888 | bytes 1048576 | tf_op jit(solution)/shard_map/terms/pallas_call | solution.py:431
  43.5 0.9 %terms.3 = (f32[384,256]{1,0:T(8,128)S(1)}, f32[192,256]{1,0:T(8,128)S(1)}) custom-call(bf16[768,1536]{1,0:T(8,128)(2,1)S(1)} %get-tuple-element.69.p_ref, bf16[768,1536]{1,0:T(8,128)(2,1)S(1)} %get-tuple-element.55.refs_7_.ds_ref, bf16[48,1536]{1,0:T(8,128)(2,1)S(1)} %get-tuple-element.61.after_ref.own_p_ref, ...), custom_call_target="tpu_custom_call" | custom-call | flops 301989888 | bytes 1048576 | tf_op jit(solution)/shard_map/terms/pallas_call | solution.py:431
  44.9 2.7 %collective-permute-done.17.far_ref = bf16[384,256]{1,0:T(8,128)(2,1)S(1)} collective-permute-done((bf16[384,256]{1,0:T(8,128)(2,1)S(1)}, bf16[384,256]{1,0:T(8,128)(2,1)S(1)}, u32[]{:S(2)}, u32[]{:S(2)}) %collective-permute-start.17) | collective-permute-done | bytes 196640 | tf_op jit(solution)/shard_map/ppermute | solution.py:294
  47.8 1.9 %collective-permute-done.15.far_ref = bf16[192,256]{1,0:T(8,128)(2,1)S(1)} collective-permute-done((bf16[192,256]{1,0:T(8,128)(2,1)S(1)}, bf16[192,256]{1,0:T(8,128)(2,1)S(1)}, u32[]{:S(2)}, u32[]{:S(2)}) %collective-permute-start.15) | collective-permute-done | bytes 98336 | tf_op jit(solution)/shard_map/ppermute | solution.py:294
  49.6 1.2 %collective-permute-start.16 = (bf16[96,256]{1,0:T(8,128)(2,1)S(1)}, bf16[96,256]{1,0:T(8,128)(2,1)S(1)}, u32[]{:S(2)}, u32[]{:S(2)}) collective-permute-start(bf16[96,256]{1,0:T(8,128)(2,1)S(1)} %get-tuple-element.67), channel_id=1, source_target_pairs={{0,16},{4,20},{8,24},{12,28},{16,0},{20,4},{24,8},{28,12},{1,17},{... | collective-permute-start | bytes 147464 | tf_op jit(solution)/shard_map/ppermute | solution.py:294
  50.8 1.8 %collective-permute-done.18.far_ref = bf16[192,256]{1,0:T(8,128)(2,1)S(1)} collective-permute-done((bf16[192,256]{1,0:T(8,128)(2,1)S(1)}, bf16[192,256]{1,0:T(8,128)(2,1)S(1)}, u32[]{:S(2)}, u32[]{:S(2)}) %collective-permute-start.18) | collective-permute-done | bytes 98336 | tf_op jit(solution)/shard_map/ppermute | solution.py:294
  53.1 2.2 %queries.1 = bf16[192,2048]{1,0:T(8,128)(2,1)} custom-call(bf16[48,512]{1,0:T(8,128)(2,1)S(1)} %get-tuple-element.42.refs_0_.refs_2_, bf16[48,512]{1,0:T(8,128)(2,1)S(1)} %collective-permute-done.refs_1_, bf16[48,512]{1,0:T(8,128)(2,1)S(1)} %collective-permute-done.1.refs_2_, bf16[48,512]{1,0:T(8,128)(2,1)S(1)} %collective-permute-done.2.refs_3_, ...), custom_call_target="tpu_custom_call" | custom-call | flops 603979776 | bytes 1048576 | tf_op jit(solution)/shard_map/queries/pallas_call | solution.py:447
  55.6 2.5 %collective-permute-done.19.refs_4_ = bf16[96,256]{1,0:T(8,128)(2,1)S(1)} collective-permute-done((bf16[96,256]{1,0:T(8,128)(2,1)S(1)}, bf16[96,256]{1,0:T(8,128)(2,1)S(1)}, u32[]{:S(2)}, u32[]{:S(2)}) %collective-permute-start.19) | collective-permute-done | bytes 49184 | tf_op jit(solution)/shard_map/ppermute | solution.py:294
  58.1 1.0 %spread.1 = (bf16[192,256]{1,0:T(8,128)(2,1)}, bf16[192,256]{1,0:T(8,128)(2,1)}) custom-call(s32[2,192]{1,0:T(2,128)S(1)} %copy-done.6, f32[96,256]{1,0:T(8,128)S(1)} %get-tuple-element.66.refs_0_, bf16[96,256]{1,0:T(8,128)(2,1)S(1)} %collective-permute-done.16.refs_1_, f32[192,256]{1,0:T(8,128)S(1)} %get-tuple-element.68.refs_2_, ...), custom_call_target="tpu_custom_call" | custom-call | tf_op jit(solution)/shard_map/spread/pallas_call | solution.py:476
  (39 shorter events, 2.8 us)
Async XLA Ops:
  0.6 0.9 %copy-start.4 = (bf16[48,1024]{1,0:T(8,128)(2,1)S(1)}, bf16[48,1024]{1,0:T(8,128)(2,1)}, u32[]{:S(2)}) copy-start(bf16[48,1024]{1,0:T(8,128)(2,1)} %key_ref.1) | copy-start | bytes 294916
  1.5 0.9 %copy-start.5 = (bf16[48,1024]{1,0:T(8,128)(2,1)S(1)}, bf16[48,1024]{1,0:T(8,128)(2,1)}, u32[]{:S(2)}) copy-start(bf16[48,1024]{1,0:T(8,128)(2,1)} %value_ref.1) | copy-start | bytes 294916
  2.4 8.1 %copy-start.6 = (s32[2,192]{1,0:T(2,128)S(1)}, s32[2,192]{1,0:T(2,128)}, u32[]{:S(2)}) copy-start(s32[2,192]{1,0:T(2,128)} %seg_ref.3) | copy-start | bytes 4612
  2.4 5.8 %collective-permute-start = (bf16[48,512]{1,0:T(8,128)(2,1)S(1)}, bf16[48,512]{1,0:T(8,128)(2,1)S(1)}, u32[]{:S(2)}, u32[]{:S(2)}) collective-permute-start(bf16[48,512]{1,0:T(8,128)(2,1)S(1)} %get-tuple-element.43), channel_id=1, source_target_pairs={{0,1},{1,0},{2,3},{3,2},{4,5},{5,4},{6,7},{7,6},{8,9},{9,8},{10,11... | collective-permute-start | bytes 147464 | tf_op jit(solution)/shard_map/ppermute | solution.py:294
  3.0 5.3 %collective-permute-start.1 = (bf16[48,512]{1,0:T(8,128)(2,1)S(1)}, bf16[48,512]{1,0:T(8,128)(2,1)S(1)}, u32[]{:S(2)}, u32[]{:S(2)}) collective-permute-start(bf16[48,512]{1,0:T(8,128)(2,1)S(1)} %get-tuple-element.44), channel_id=1, source_target_pairs={{0,2},{1,3},{2,0},{3,1},{4,6},{5,7},{6,4},{7,5},{8,10},{9,11},{10,... | collective-permute-start | bytes 147464 | tf_op jit(solution)/shard_map/ppermute | solution.py:294
  5.5 3.7 %collective-permute-start.2 = (bf16[48,512]{1,0:T(8,128)(2,1)S(1)}, bf16[48,512]{1,0:T(8,128)(2,1)S(1)}, u32[]{:S(2)}, u32[]{:S(2)}) collective-permute-start(bf16[48,512]{1,0:T(8,128)(2,1)S(1)} %get-tuple-element.45), channel_id=1, source_target_pairs={{0,3},{1,2},{2,1},{3,0},{4,7},{5,6},{6,5},{7,4},{8,11},{9,10},{10,... | collective-permute-start | bytes 147464 | tf_op jit(solution)/shard_map/ppermute | solution.py:294
  5.6 1.1 %copy-start = (bf16[48,8192]{1,0:T(8,128)(2,1)S(1)}, bf16[48,8192]{1,0:T(8,128)(2,1)}, u32[]{:S(2)}) copy-start(bf16[48,8192]{1,0:T(8,128)(2,1)} %q_ref.3) | copy-start | bytes 2359300
  6.7 1.1 %copy-start.2 = (bf16[48,8192]{1,0:T(8,128)(2,1)S(1)}, bf16[48,8192]{1,0:T(8,128)(2,1)}, u32[]{:S(2)}) copy-start(bf16[48,8192]{1,0:T(8,128)(2,1)} %o_ref.3) | copy-start | bytes 2359300
  8.3 23.0 %copy-start.1 = (bf16[48,8192]{1,0:T(8,128)(2,1)S(1)}, bf16[48,8192]{1,0:T(8,128)(2,1)}, u32[]{:S(2)}) copy-start(bf16[48,8192]{1,0:T(8,128)(2,1)} %q_ref.3) | copy-start | bytes 2359300
  8.3 23.0 %copy-start.3 = (bf16[48,8192]{1,0:T(8,128)(2,1)S(1)}, bf16[48,8192]{1,0:T(8,128)(2,1)}, u32[]{:S(2)}) copy-start(bf16[48,8192]{1,0:T(8,128)(2,1)} %o_ref.3) | copy-start | bytes 2359300
  9.2 12.6 %collective-permute-start.12 = (bf16[96,2048]{1,0:T(8,128)(2,1)S(1)}, bf16[96,2048]{1,0:T(8,128)(2,1)S(1)}, u32[]{:S(2)}, u32[]{:S(2)}) collective-permute-start(bf16[96,2048]{1,0:T(8,128)(2,1)S(1)} %gate.6), channel_id=1, source_target_pairs={{0,1},{1,0},{2,3},{3,2},{4,5},{5,4},{6,7},{7,6},{8,9},{9,8},{10,11... | collective-permute-start | bytes 1179656 | tf_op jit(solution)/shard_map/ppermute | solution.py:294
  9.4 16.6 %collective-permute-start.10 = (bf16[96,2048]{1,0:T(8,128)(2,1)S(1)}, bf16[96,2048]{1,0:T(8,128)(2,1)S(1)}, u32[]{:S(2)}, u32[]{:S(2)}) collective-permute-start(bf16[96,2048]{1,0:T(8,128)(2,1)S(1)} %gate.4), channel_id=1, source_target_pairs={{0,2},{1,3},{2,0},{3,1},{4,6},{5,7},{6,4},{7,5},{8,10},{9,11},{10,... | collective-permute-start | bytes 1179656 | tf_op jit(solution)/shard_map/ppermute | solution.py:294
  10.8 5.7 %collective-permute-start.4 = (bf16[96,512]{1,0:T(8,128)(2,1)S(1)}, bf16[96,512]{1,0:T(8,128)(2,1)S(1)}, u32[]{:S(2)}, u32[]{:S(2)}) collective-permute-start(bf16[96,512]{1,0:T(8,128)(2,1)S(1)} %get-tuple-element.47.refs_4_), channel_id=1, source_target_pairs={{0,8},{4,12},{8,0},{12,4},{16,24},{20,28},{24,16},{28,20},{1,9},{5... | collective-permute-start | bytes 294920 | tf_op jit(solution)/shard_map/ppermute | solution.py:294
  12.4 7.4 %collective-permute-start.3 = (bf16[96,512]{1,0:T(8,128)(2,1)S(1)}, bf16[96,512]{1,0:T(8,128)(2,1)S(1)}, u32[]{:S(2)}, u32[]{:S(2)}) collective-permute-start(bf16[96,512]{1,0:T(8,128)(2,1)S(1)} %get-tuple-element.47.refs_4_), channel_id=1, source_target_pairs={{0,16},{4,20},{8,24},{12,28},{16,0},{20,4},{24,8},{28,12},{1,17},{... | collective-permute-start | bytes 294920 | tf_op jit(solution)/shard_map/ppermute | solution.py:294
  15.0 6.4 %collective-permute-start.6 = (bf16[96,512]{1,0:T(8,128)(2,1)S(1)}, bf16[96,512]{1,0:T(8,128)(2,1)S(1)}, u32[]{:S(2)}, u32[]{:S(2)}) collective-permute-start(bf16[96,512]{1,0:T(8,128)(2,1)S(1)} %get-tuple-element.47.refs_4_), channel_id=1, source_target_pairs={{0,4},{4,0},{8,12},{12,8},{16,20},{20,16},{24,28},{28,24},{1,5},{5... | collective-permute-start | bytes 294920 | tf_op jit(solution)/shard_map/ppermute | solution.py:294
  16.5 6.3 %collective-permute-start.8 = (bf16[96,512]{1,0:T(8,128)(2,1)S(1)}, bf16[96,512]{1,0:T(8,128)(2,1)S(1)}, u32[]{:S(2)}, u32[]{:S(2)}) collective-permute-start(bf16[96,512]{1,0:T(8,128)(2,1)S(1)} %collective-permute-done.4.refs_2_.refs_6_), channel_id=1, source_target_pairs={{0,4},{4,0},{8,12},{12,8},{16,20},{20,16},{24,28},{28,24},{1,5},{5... | collective-permute-start | bytes 294920 | tf_op jit(solution)/shard_map/ppermute | solution.py:294
  19.8 4.6 %collective-permute-start.7 = (bf16[96,512]{1,0:T(8,128)(2,1)S(1)}, bf16[96,512]{1,0:T(8,128)(2,1)S(1)}, u32[]{:S(2)}, u32[]{:S(2)}) collective-permute-start(bf16[96,512]{1,0:T(8,128)(2,1)S(1)} %collective-permute-done.3.refs_4_.refs_5_), channel_id=1, source_target_pairs={{0,4},{4,0},{8,12},{12,8},{16,20},{20,16},{24,28},{28,24},{1,5},{5... | collective-permute-start | bytes 294920 | tf_op jit(solution)/shard_map/ppermute | solution.py:294
  21.4 4.6 %collective-permute-start.5 = (bf16[96,512]{1,0:T(8,128)(2,1)S(1)}, bf16[96,512]{1,0:T(8,128)(2,1)S(1)}, u32[]{:S(2)}, u32[]{:S(2)}) collective-permute-start(bf16[96,512]{1,0:T(8,128)(2,1)S(1)} %collective-permute-done.3.refs_4_.refs_5_), channel_id=1, source_target_pairs={{0,8},{4,12},{8,0},{12,4},{16,24},{20,28},{24,16},{28,20},{1,9},{5... | collective-permute-start | bytes 294920 | tf_op jit(solution)/shard_map/ppermute | solution.py:294
  21.8 9.5 %collective-permute-start.13 = (bf16[96,2048]{1,0:T(8,128)(2,1)S(1)}, bf16[96,2048]{1,0:T(8,128)(2,1)S(1)}, u32[]{:S(2)}, u32[]{:S(2)}) collective-permute-start(bf16[96,2048]{1,0:T(8,128)(2,1)S(1)} %collective-permute-done.12), channel_id=1, source_target_pairs={{0,2},{1,3},{2,0},{3,1},{4,6},{5,7},{6,4},{7,5},{8,10},{9,11},{10,... | collective-permute-start | bytes 1179656 | tf_op jit(solution)/shard_map/ppermute | solution.py:294
  26.0 5.3 %collective-permute-start.11 = (bf16[96,2048]{1,0:T(8,128)(2,1)S(1)}, bf16[96,2048]{1,0:T(8,128)(2,1)S(1)}, u32[]{:S(2)}, u32[]{:S(2)}) collective-permute-start(bf16[96,2048]{1,0:T(8,128)(2,1)S(1)} %gate.5), channel_id=1, source_target_pairs={{0,1},{1,0},{2,3},{3,2},{4,5},{5,4},{6,7},{7,6},{8,9},{9,8},{10,11... | collective-permute-start | bytes 1179656 | tf_op jit(solution)/shard_map/ppermute | solution.py:294
  26.0 5.3 %collective-permute-start.9 = (bf16[96,512]{1,0:T(8,128)(2,1)S(1)}, bf16[96,512]{1,0:T(8,128)(2,1)S(1)}, u32[]{:S(2)}, u32[]{:S(2)}) collective-permute-start(bf16[96,512]{1,0:T(8,128)(2,1)S(1)} %collective-permute-done.5.refs_6_.refs_7_), channel_id=1, source_target_pairs={{0,4},{4,0},{8,12},{12,8},{16,20},{20,16},{24,28},{28,24},{1,5},{5... | collective-permute-start | bytes 294920 | tf_op jit(solution)/shard_map/ppermute | solution.py:294
  35.8 8.6 %collective-permute-start.14 = (bf16[384,256]{1,0:T(8,128)(2,1)S(1)}, bf16[384,256]{1,0:T(8,128)(2,1)S(1)}, u32[]{:S(2)}, u32[]{:S(2)}) collective-permute-start(bf16[384,256]{1,0:T(8,128)(2,1)S(1)} %get-tuple-element.63), channel_id=1, source_target_pairs={{0,4},{4,0},{8,12},{12,8},{16,20},{20,16},{24,28},{28,24},{1,5},{5... | collective-permute-start | bytes 589832 | tf_op jit(solution)/shard_map/ppermute | solution.py:294
  41.3 6.3 %collective-permute-start.17 = (bf16[384,256]{1,0:T(8,128)(2,1)S(1)}, bf16[384,256]{1,0:T(8,128)(2,1)S(1)}, u32[]{:S(2)}, u32[]{:S(2)}) collective-permute-start(bf16[384,256]{1,0:T(8,128)(2,1)S(1)} %get-tuple-element.73), channel_id=1, source_target_pairs={{0,4},{4,0},{8,12},{12,8},{16,20},{20,16},{24,28},{28,24},{1,5},{5... | collective-permute-start | bytes 589832 | tf_op jit(solution)/shard_map/ppermute | solution.py:294
  44.5 5.2 %collective-permute-start.15 = (bf16[192,256]{1,0:T(8,128)(2,1)S(1)}, bf16[192,256]{1,0:T(8,128)(2,1)S(1)}, u32[]{:S(2)}, u32[]{:S(2)}) collective-permute-start(bf16[192,256]{1,0:T(8,128)(2,1)S(1)} %get-tuple-element.65), channel_id=1, source_target_pairs={{0,8},{4,12},{8,0},{12,4},{16,24},{20,28},{24,16},{28,20},{1,9},{5... | collective-permute-start | bytes 294920 | tf_op jit(solution)/shard_map/ppermute | solution.py:294
  47.6 5.1 %collective-permute-start.18 = (bf16[192,256]{1,0:T(8,128)(2,1)S(1)}, bf16[192,256]{1,0:T(8,128)(2,1)S(1)}, u32[]{:S(2)}, u32[]{:S(2)}) collective-permute-start(bf16[192,256]{1,0:T(8,128)(2,1)S(1)} %get-tuple-element.75), channel_id=1, source_target_pairs={{0,8},{4,12},{8,0},{12,4},{16,24},{20,28},{24,16},{28,20},{1,9},{5... | collective-permute-start | bytes 294920 | tf_op jit(solution)/shard_map/ppermute | solution.py:294
  49.6 5.9 %collective-permute-start.16 = (bf16[96,256]{1,0:T(8,128)(2,1)S(1)}, bf16[96,256]{1,0:T(8,128)(2,1)S(1)}, u32[]{:S(2)}, u32[]{:S(2)}) collective-permute-start(bf16[96,256]{1,0:T(8,128)(2,1)S(1)} %get-tuple-element.67), channel_id=1, source_target_pairs={{0,16},{4,20},{8,24},{12,28},{16,0},{20,4},{24,8},{28,12},{1,17},{... | collective-permute-start | bytes 147464 | tf_op jit(solution)/shard_map/ppermute | solution.py:294
  52.7 5.4 %collective-permute-start.19 = (bf16[96,256]{1,0:T(8,128)(2,1)S(1)}, bf16[96,256]{1,0:T(8,128)(2,1)S(1)}, u32[]{:S(2)}, u32[]{:S(2)}) collective-permute-start(bf16[96,256]{1,0:T(8,128)(2,1)S(1)} %get-tuple-element.77), channel_id=1, source_target_pairs={{0,16},{4,20},{8,24},{12,28},{16,0},{20,4},{24,8},{28,12},{1,17},{... | collective-permute-start | bytes 147464 | tf_op jit(solution)/shard_map/ppermute | solution.py:294

commit v11 on v10

--- a/solution.py
+++ b/solution.py
@@ -121,15 +121,13 @@
     return reduce(x.reshape(x.shape[0] // 8, 8, x.shape[1]), axis=0)
 
 
-def attend_kernel(g, order, q_ref, o_ref, hide_ref, *refs):
+def attend_kernel(g, order, far_parts, q_ref, o_ref, hide_ref, *refs):
     shards = len(order)
     heads = 4
     kv_pieces, blocks, refs = refs[:heads], refs[heads : heads + shards], refs[heads + shards :]
     qo_pieces = refs[: heads - 1]
-    (
-        p_ref, ds_ref, own_p_ref, own_ds_ref, qs_ref, os_ref, kt_ref, far_ref,
-        kx, vx, mine, s_ref, g_ref, sems,
-    ) = refs[-14:]
+    p_ref, ds_ref, own_p_ref, own_ds_ref, qs_ref, os_ref, kt_ref = refs[-13 - far_parts :][:7]
+    far_refs, (kx, vx, mine, s_ref, g_ref, sems) = refs[-6 - far_parts : -6], refs[-6:]
     rows = q_ref.shape[0]
     kv_heads = hide_ref.shape[0]
     slots = shards * SLOT_DEV
@@ -210,9 +208,12 @@
         own_grad_score = own_prob * (own_grad_prob - delta)
         own_p_ref[:, chunk] = jnp.where(eye, own_prob, 0.0).astype(jnp.bfloat16)
         own_ds_ref[:, chunk] = jnp.where(eye, own_grad_score, 0.0).astype(jnp.bfloat16)
-    far = slice(slots // 2, slots)
-    far_ref[:, 0:HD] = (SCALE * nn(ds_ref[far, :], qs_ref[...])).astype(far_ref.dtype)
-    far_ref[:, HD : 2 * HD] = nn(p_ref[far, :], os_ref[...]).astype(far_ref.dtype)
+    stop = slots
+    for far_ref in far_refs:
+        far = slice(stop - far_ref.shape[0], stop)
+        far_ref[:, 0:HD] = (SCALE * nn(ds_ref[far, :], qs_ref[...])).astype(far_ref.dtype)
+        far_ref[:, HD : 2 * HD] = nn(p_ref[far, :], os_ref[...]).astype(far_ref.dtype)
+        stop = far.start
     kt_ref[...] = kx[0:slots, 0:HD].astype(jnp.float32).T.astype(jnp.bfloat16)
 
 
@@ -248,11 +249,13 @@
                 dq_ref[at, column : column + HD] = dq[h * rows : (h + 1) * rows]
 
 
-def add_kernel(near_ref, far_ref, keep_ref, send_ref):
-    total = near_ref[...] + far_ref[...].astype(jnp.float32)
-    half = keep_ref.shape[0]
-    keep_ref[...] = total[:half]
-    send_ref[...] = total[half:].astype(send_ref.dtype)
+def add_kernel(starts, *refs):
+    out = refs[-1]
+    rows = out.shape[0]
+    total = 0.0
+    for start, ref in zip(starts, refs[:-1]):
+        total = total + ref[start : start + rows, :].astype(jnp.float32)
+    out[...] = total.astype(out.dtype)
 
 
 def spread_kernel(parts_per_head, seg_ref, *refs):
@@ -260,9 +263,9 @@
     gk_ref, gv_ref = refs[-2:]
     for g in range(kv_heads):
         parts = refs[g * parts_per_head : (g + 1) * parts_per_head]
-        total = parts[0][...].astype(jnp.float32)
-        for part in parts[1:-1]:
-            total = total + part[...].astype(jnp.float32)
+        total = 0.0
+        for part in parts[:-1]:
+            total = total + part[0:SLOT_DEV, :].astype(jnp.float32)
         picks = slot_picks(seg_ref[g : g + 1, :], tokens).astype(jnp.float32)
         counts = jnp.sum(picks, axis=1, keepdims=True)
         total = total / jnp.maximum(counts, 1.0)
@@ -385,8 +388,9 @@
     all_rows = tokens * GROUP
     saved = []
     for g in range(kv_heads):
+        far_parts = 2 if g == kv_heads - 1 else 1
         outs = pl.pallas_call(
-            functools.partial(attend_kernel, g, order),
+            functools.partial(attend_kernel, g, order, far_parts),
             out_shape=[
                 shape(slots, all_rows),
                 shape(slots, all_rows),
@@ -395,10 +399,10 @@
                 shape(all_rows, HD),
                 shape(all_rows, HD),
                 shape(HD, slots),
-                shape(half, 2 * HD),
-            ],
+            ]
+            + [shape(half // far_parts, 2 * HD)] * far_parts,
             in_specs=anywhere(2) + in_vmem(heads + heads + shards) + anywhere(g > 0),
-            out_specs=in_vmem(8),
+            out_specs=in_vmem(7 + far_parts),
             scratch_shapes=[
                 pltpu.VMEM((slots + rows, 2 * HD), jnp.bfloat16),
                 pltpu.VMEM((slots + rows, HD), jnp.bfloat16),
@@ -424,7 +428,7 @@
             *([saved[-1][2]] if g else []),
         )
         saved.append(outs)
-    far = [swap(outs[7], "ctx", shards, 1) for outs in saved]
+    far = [[swap(part, "ctx", shards, 1) for part in outs[7:]] for outs in saved]
     near = []
     own = []
     for g in range(kv_heads):
@@ -458,23 +462,28 @@
 
     spread_args = []
     for g in range(kv_heads):
-        keep, received, step = near[g], far[g], 2
+        rows_left, step = half // 2, 2
+        first, rest = far[g][0], far[g][-1]
+        terms = [(near[g], rows_left), (first, rows_left % first.shape[0])]
+        kept = [near[g], rest]
         while step < shards:
-            count = keep.shape[0] // 2
-            keep, send = pl.pallas_call(
-                add_kernel,
-                out_shape=[shape(count, 2 * HD, dtype=jnp.float32), shape(count, 2 * HD)],
-                in_specs=in_vmem(2),
-                out_specs=in_vmem(2),
+            send = pl.pallas_call(
+                functools.partial(add_kernel, [start for _, start in terms]),
+                out_shape=shape(rows_left, 2 * HD),
+                in_specs=in_vmem(len(terms)),
+                out_specs=in_vmem(1)[0],
                 compiler_params=params(8),
                 name="add",
-            )(keep, received)
-            received = swap(send, "ctx", shards, step)
+            )(*[term for term, _ in terms])
+            kept.append(swap(send, "ctx", shards, step))
+            rows_left //= 2
             step *= 2
-        spread_args += [keep, received, own[g]]
+            terms = [(term, rows_left) for term in kept]
+        spread_args += kept + [own[g]]
+    parts_per_head = len(spread_args) // kv_heads
 
     grad_keys, grad_values = pl.pallas_call(
-        functools.partial(spread_kernel, 3),
+        functools.partial(spread_kernel, parts_per_head),
         out_shape=[shape(tokens, kv_width)] * 2,
         in_specs=in_vmem(1 + len(spread_args)),
         out_specs=in_vmem(2),

time: 59.4 us -> 60.2 us (1.013)
  starting transfers between devices: 19 us -> 22.2 us
  waiting for transfers between devices: 20.4 us -> 18 us
    ppermute x20 -> x21, starting transfers between devices: 19 us -> 22.2 us  [swap(): return lax.ppermute(x, axis, [(i, i ^ m) for i in range(size)])]
    ppermute x20 -> x21, waiting for transfers between devices: 20.4 us -> 18 us  [swap(): return lax.ppermute(x, axis, [(i, i ^ m) for i in range(size)])]
  transfers between devices with their start and end apart: 20 -> 21, of which waited for: 10 -> 9; matrix products, arithmetic and copies ran while one was open for 0% -> 0% of each run, Pallas kernels for 16% -> 16%
where the time goes in v11:
time: 60.2 us; the launch traced here: 59.9 us
  starting transfers between devices  22.2 us (37%)
  waiting for transfers between devices  18 us (30%)
  Pallas kernels  14.9 us (25%)
  local copies, waits for them, and re-layouts  4.06 us (7%)
  between operations  0.77 us (1%)
    ppermute x21, starting transfers between devices, swap(): return lax.ppermute(x, axis, [(i, i ^ m) for i in range(size)])  22.2 us
    ppermute x21, waiting for transfers between devices, swap(): return lax.ppermute(x, axis, [(i, i ^ m) for i in range(size)])  18 us
    pallas_call x2, Pallas kernels, local(): pl.pallas_call(functools.partial(attend_kernel, g, order, far_parts), out...  9.13 us
    unnamed x14, local copies, waits for them, and re-layouts  4.06 us
    pallas_call x1, Pallas kernels, local(): pl.pallas_call(functools.partial(queries_kernel, heads), out_shape=shape(...  2.19 us
    pallas_call x2, Pallas kernels, local(): pl.pallas_call(functools.partial(terms_kernel, heads), out_shape=[shape(h...  1.8 us
  transfers between devices with their start and end apart: 21, of which 9 were waited for; matrix products, arithmetic and copies ran while one was open for 0% of the time, Pallas kernels for 16%

profile of v11, /device:TPU:0, one launch (start us, length us, event | category | flops | bytes accessed | tf_op | source)
XLA Modules:
  0.0 59.9 jit_solution(3339077181946719476)
XLA Ops:
  0.6 0.9 %copy-done.4 = bf16[48,1024]{1,0:T(8,128)(2,1)S(1)} copy-done((bf16[48,1024]{1,0:T(8,128)(2,1)S(1)}, bf16[48,1024]{1,0:T(8,128)(2,1)}, u32[]{:S(2)}) %copy-start.4) | copy-done | bytes 98328
  1.5 0.9 %copy-done.5 = bf16[48,1024]{1,0:T(8,128)(2,1)S(1)} copy-done((bf16[48,1024]{1,0:T(8,128)(2,1)S(1)}, bf16[48,1024]{1,0:T(8,128)(2,1)}, u32[]{:S(2)}) %copy-start.5) | copy-done | bytes 98328
  3.0 2.6 %collective-permute-start.1 = (bf16[48,512]{1,0:T(8,128)(2,1)S(1)}, bf16[48,512]{1,0:T(8,128)(2,1)S(1)}, u32[]{:S(2)}, u32[]{:S(2)}) collective-permute-start(bf16[48,512]{1,0:T(8,128)(2,1)S(1)} %get-tuple-element.37), channel_id=1, source_target_pairs={{0,2},{1,3},{2,0},{3,1},{4,6},{5,7},{6,4},{7,5},{8,10},{9,11},{10,... | collective-permute-start | bytes 147464 | tf_op jit(solution)/shard_map/ppermute | solution.py:297
  5.6 1.1 %copy-done = bf16[48,8192]{1,0:T(8,128)(2,1)S(1)} copy-done((bf16[48,8192]{1,0:T(8,128)(2,1)S(1)}, bf16[48,8192]{1,0:T(8,128)(2,1)}, u32[]{:S(2)}) %copy-start) | copy-done | bytes 786456
  6.7 1.1 %copy-done.2 = bf16[48,8192]{1,0:T(8,128)(2,1)S(1)} copy-done((bf16[48,8192]{1,0:T(8,128)(2,1)S(1)}, bf16[48,8192]{1,0:T(8,128)(2,1)}, u32[]{:S(2)}) %copy-start.2) | copy-done | bytes 786456
  8.3 0.9 %collective-permute-done.2.refs_3_ = bf16[48,512]{1,0:T(8,128)(2,1)S(1)} collective-permute-done((bf16[48,512]{1,0:T(8,128)(2,1)S(1)}, bf16[48,512]{1,0:T(8,128)(2,1)S(1)}, u32[]{:S(2)}, u32[]{:S(2)}) %collective-permute-start.2) | collective-permute-done | bytes 49184 | tf_op jit(solution)/shard_map/ppermute | solution.py:297
  9.4 1.1 %collective-permute-start.10 = (bf16[96,2048]{1,0:T(8,128)(2,1)S(1)}, bf16[96,2048]{1,0:T(8,128)(2,1)S(1)}, u32[]{:S(2)}, u32[]{:S(2)}) collective-permute-start(bf16[96,2048]{1,0:T(8,128)(2,1)S(1)} %gate.4), channel_id=1, source_target_pairs={{0,2},{1,3},{2,0},{3,1},{4,6},{5,7},{6,4},{7,5},{8,10},{9,11},{10,... | collective-permute-start | bytes 1179656 | tf_op jit(solution)/shard_map/ppermute | solution.py:297
  10.8 1.6 %collective-permute-start.4 = (bf16[96,512]{1,0:T(8,128)(2,1)S(1)}, bf16[96,512]{1,0:T(8,128)(2,1)S(1)}, u32[]{:S(2)}, u32[]{:S(2)}) collective-permute-start(bf16[96,512]{1,0:T(8,128)(2,1)S(1)} %get-tuple-element.40.refs_4_), channel_id=1, source_target_pairs={{0,8},{4,12},{8,0},{12,4},{16,24},{20,28},{24,16},{28,20},{1,9},{5... | collective-permute-start | bytes 294920 | tf_op jit(solution)/shard_map/ppermute | solution.py:297
  12.4 2.6 %collective-permute-start.3 = (bf16[96,512]{1,0:T(8,128)(2,1)S(1)}, bf16[96,512]{1,0:T(8,128)(2,1)S(1)}, u32[]{:S(2)}, u32[]{:S(2)}) collective-permute-start(bf16[96,512]{1,0:T(8,128)(2,1)S(1)} %get-tuple-element.40.refs_4_), channel_id=1, source_target_pairs={{0,16},{4,20},{8,24},{12,28},{16,0},{20,4},{24,8},{28,12},{1,17},{... | collective-permute-start | bytes 294920 | tf_op jit(solution)/shard_map/ppermute | solution.py:297
  15.0 1.5 %collective-permute-start.6 = (bf16[96,512]{1,0:T(8,128)(2,1)S(1)}, bf16[96,512]{1,0:T(8,128)(2,1)S(1)}, u32[]{:S(2)}, u32[]{:S(2)}) collective-permute-start(bf16[96,512]{1,0:T(8,128)(2,1)S(1)} %get-tuple-element.40.refs_4_), channel_id=1, source_target_pairs={{0,4},{4,0},{8,12},{12,8},{16,20},{20,16},{24,28},{28,24},{1,5},{5... | collective-permute-start | bytes 294920 | tf_op jit(solution)/shard_map/ppermute | solution.py:297
  17.0 2.8 %collective-permute-done.3.refs_4_.refs_5_ = bf16[96,512]{1,0:T(8,128)(2,1)S(1)} collective-permute-done((bf16[96,512]{1,0:T(8,128)(2,1)S(1)}, bf16[96,512]{1,0:T(8,128)(2,1)S(1)}, u32[]{:S(2)}, u32[]{:S(2)}) %collective-permute-start.3) | collective-permute-done | bytes 98336 | tf_op jit(solution)/shard_map/ppermute | solution.py:297
  19.8 1.5 %collective-permute-start.7 = (bf16[96,512]{1,0:T(8,128)(2,1)S(1)}, bf16[96,512]{1,0:T(8,128)(2,1)S(1)}, u32[]{:S(2)}, u32[]{:S(2)}) collective-permute-start(bf16[96,512]{1,0:T(8,128)(2,1)S(1)} %collective-permute-done.3.refs_4_.refs_5_), channel_id=1, source_target_pairs={{0,4},{4,0},{8,12},{12,8},{16,20},{20,16},{24,28},{28,24},{1,5},{5... | collective-permute-start | bytes 294920 | tf_op jit(solution)/shard_map/ppermute | solution.py:297
  21.8 1.0 %collective-permute-start.13 = (bf16[96,2048]{1,0:T(8,128)(2,1)S(1)}, bf16[96,2048]{1,0:T(8,128)(2,1)S(1)}, u32[]{:S(2)}, u32[]{:S(2)}) collective-permute-start(bf16[96,2048]{1,0:T(8,128)(2,1)S(1)} %collective-permute-done.12), channel_id=1, source_target_pairs={{0,2},{1,3},{2,0},{3,1},{4,6},{5,7},{6,4},{7,5},{8,10},{9,11},{10,... | collective-permute-start | bytes 1179656 | tf_op jit(solution)/shard_map/ppermute | solution.py:297
  22.8 1.6 %collective-permute-done.7.refs_5_.refs_9_ = bf16[96,512]{1,0:T(8,128)(2,1)S(1)} collective-permute-done((bf16[96,512]{1,0:T(8,128)(2,1)S(1)}, bf16[96,512]{1,0:T(8,128)(2,1)S(1)}, u32[]{:S(2)}, u32[]{:S(2)}) %collective-permute-start.7) | collective-permute-done | bytes 98336 | tf_op jit(solution)/shard_map/ppermute | solution.py:297
  24.4 1.5 %collective-permute-done.5.refs_6_.refs_7_ = bf16[96,512]{1,0:T(8,128)(2,1)S(1)} collective-permute-done((bf16[96,512]{1,0:T(8,128)(2,1)S(1)}, bf16[96,512]{1,0:T(8,128)(2,1)S(1)}, u32[]{:S(2)}, u32[]{:S(2)}) %collective-permute-start.5) | collective-permute-done | bytes 98336 | tf_op jit(solution)/shard_map/ppermute | solution.py:297
  26.0 0.9 %collective-permute-start.9 = (bf16[96,512]{1,0:T(8,128)(2,1)S(1)}, bf16[96,512]{1,0:T(8,128)(2,1)S(1)}, u32[]{:S(2)}, u32[]{:S(2)}) collective-permute-start(bf16[96,512]{1,0:T(8,128)(2,1)S(1)} %collective-permute-done.5.refs_6_.refs_7_), channel_id=1, source_target_pairs={{0,4},{4,0},{8,12},{12,8},{16,20},{20,16},{24,28},{28,24},{1,5},{5... | collective-permute-start | bytes 294920 | tf_op jit(solution)/shard_map/ppermute | solution.py:297
  26.9 4.3 %collective-permute-done.13.refs_0_ = bf16[96,2048]{1,0:T(8,128)(2,1)S(1)} collective-permute-done((bf16[96,2048]{1,0:T(8,128)(2,1)S(1)}, bf16[96,2048]{1,0:T(8,128)(2,1)S(1)}, u32[]{:S(2)}, u32[]{:S(2)}) %collective-permute-start.13) | collective-permute-done | bytes 393248 | tf_op jit(solution)/shard_map/ppermute | solution.py:297
  31.3 4.5 %attend.2 = (bf16[768,1536]{1,0:T(8,128)(2,1)S(1)}, bf16[768,1536]{1,0:T(8,128)(2,1)S(1)}, bf16[48,1536]{1,0:T(8,128)(2,1)S(1)}, bf16[48,1536]{1,0:T(8,128)(2,1)...) custom-call(bf16[48,8192]{1,0:T(8,128)(2,1)S(1)} %copy-done.1, ...), custom_call_target="tpu_custom_call" | custom-call | flops 962592768 | bytes 8388608 | tf_op jit(solution)/shard_map/attend/pallas_call | solution.py:392
  35.8 0.9 %collective-permute-start.14 = (bf16[384,256]{1,0:T(8,128)(2,1)S(1)}, bf16[384,256]{1,0:T(8,128)(2,1)S(1)}, u32[]{:S(2)}, u32[]{:S(2)}) collective-permute-start(bf16[384,256]{1,0:T(8,128)(2,1)S(1)} %get-tuple-element.56), channel_id=1, source_target_pairs={{0,4},{4,0},{8,12},{12,8},{16,20},{20,16},{24,28},{28,24},{1,5},{5... | collective-permute-start | bytes 589832 | tf_op jit(solution)/shard_map/ppermute | solution.py:297
  36.6 4.6 %attend.3 = (bf16[768,1536]{1,0:T(8,128)(2,1)S(1)}, bf16[768,1536]{1,0:T(8,128)(2,1)S(1)}, bf16[48,1536]{1,0:T(8,128)(2,1)S(1)}, bf16[48,1536]{1,0:T(8,128)(2,1)...) custom-call(bf16[48,8192]{1,0:T(8,128)(2,1)S(1)} %copy-done.1, ...), custom_call_target="tpu_custom_call" | custom-call | flops 962592768 | bytes 8388608 | tf_op jit(solution)/shard_map/attend/pallas_call | solution.py:392
  41.3 1.3 %collective-permute-start.18 = (bf16[192,256]{1,0:T(8,128)(2,1)S(1)}, bf16[192,256]{1,0:T(8,128)(2,1)S(1)}, u32[]{:S(2)}, u32[]{:S(2)}) collective-permute-start(bf16[192,256]{1,0:T(8,128)(2,1)S(1)} %get-tuple-element.63), channel_id=1, source_target_pairs={{0,4},{4,0},{8,12},{12,8},{16,20},{20,16},{24,28},{28,24},{1,5},{5... | collective-permute-start | bytes 294920 | tf_op jit(solution)/shard_map/ppermute | solution.py:297
  42.6 0.8 %collective-permute-start.17 = (bf16[192,256]{1,0:T(8,128)(2,1)S(1)}, bf16[192,256]{1,0:T(8,128)(2,1)S(1)}, u32[]{:S(2)}, u32[]{:S(2)}) collective-permute-start(bf16[192,256]{1,0:T(8,128)(2,1)S(1)} %get-tuple-element.62), channel_id=1, source_target_pairs={{0,4},{4,0},{8,12},{12,8},{16,20},{20,16},{24,28},{28,24},{1,5},{5... | collective-permute-start | bytes 294920 | tf_op jit(solution)/shard_map/ppermute | solution.py:297
  43.4 0.9 %terms.2 = (f32[384,256]{1,0:T(8,128)S(1)}, f32[192,256]{1,0:T(8,128)S(1)}) custom-call(bf16[768,1536]{1,0:T(8,128)(2,1)S(1)} %get-tuple-element.51.p_ref, bf16[768,1536]{1,0:T(8,128)(2,1)S(1)} %get-tuple-element.44.refs_4_.ds_ref, bf16[48,1536]{1,0:T(8,128)(2,1)S(1)} %get-tuple-element.47.refs_15_.own_p_ref, ...), custom_call_target="tpu_custom_call" | custom-call | flops 301989888 | bytes 1048576 | tf_op jit(solution)/shard_map/terms/pallas_call | solution.py:435
  44.3 0.9 %terms.3 = (f32[384,256]{1,0:T(8,128)S(1)}, f32[192,256]{1,0:T(8,128)S(1)}) custom-call(bf16[768,1536]{1,0:T(8,128)(2,1)S(1)} %get-tuple-element.58.p_ref, bf16[768,1536]{1,0:T(8,128)(2,1)S(1)} %get-tuple-element.48.refs_7_.ds_ref, bf16[48,1536]{1,0:T(8,128)(2,1)S(1)} %get-tuple-element.54.after_ref.own_p_ref, ...), custom_call_target="tpu_custom_call" | custom-call | flops 301989888 | bytes 1048576 | tf_op jit(solution)/shard_map/terms/pallas_call | solution.py:435
  45.2 1.3 %collective-permute-done.18.refs_1_ = bf16[192,256]{1,0:T(8,128)(2,1)S(1)} collective-permute-done((bf16[192,256]{1,0:T(8,128)(2,1)S(1)}, bf16[192,256]{1,0:T(8,128)(2,1)S(1)}, u32[]{:S(2)}, u32[]{:S(2)}) %collective-permute-start.18) | collective-permute-done | bytes 98336 | tf_op jit(solution)/shard_map/ppermute | solution.py:297
  46.8 1.9 %collective-permute-start.15 = (bf16[192,256]{1,0:T(8,128)(2,1)S(1)}, bf16[192,256]{1,0:T(8,128)(2,1)S(1)}, u32[]{:S(2)}, u32[]{:S(2)}) collective-permute-start(bf16[192,256]{1,0:T(8,128)(2,1)S(1)} %add.4), channel_id=1, source_target_pairs={{0,8},{4,12},{8,0},{12,4},{16,24},{20,28},{24,16},{28,20},{1,9},{5... | collective-permute-start | bytes 294920 | tf_op jit(solution)/shard_map/ppermute | solution.py:297
  48.7 2.5 %collective-permute-done.19.refs_2_.refs_7_ = bf16[192,256]{1,0:T(8,128)(2,1)S(1)} collective-permute-done((bf16[192,256]{1,0:T(8,128)(2,1)S(1)}, bf16[192,256]{1,0:T(8,128)(2,1)S(1)}, u32[]{:S(2)}, u32[]{:S(2)}) %collective-permute-start.19) | collective-permute-done | bytes 98336 | tf_op jit(solution)/shard_map/ppermute | solution.py:297
  51.2 1.3 %collective-permute-start.20 = (bf16[96,256]{1,0:T(8,128)(2,1)S(1)}, bf16[96,256]{1,0:T(8,128)(2,1)S(1)}, u32[]{:S(2)}, u32[]{:S(2)}) collective-permute-start(bf16[96,256]{1,0:T(8,128)(2,1)S(1)} %add.7), channel_id=1, source_target_pairs={{0,16},{4,20},{8,24},{12,28},{16,0},{20,4},{24,8},{28,12},{1,17},{... | collective-permute-start | bytes 147464 | tf_op jit(solution)/shard_map/ppermute | solution.py:297
  53.3 1.2 %collective-permute-start.16 = (bf16[96,256]{1,0:T(8,128)(2,1)S(1)}, bf16[96,256]{1,0:T(8,128)(2,1)S(1)}, u32[]{:S(2)}, u32[]{:S(2)}) collective-permute-start(bf16[96,256]{1,0:T(8,128)(2,1)S(1)} %add.5), channel_id=1, source_target_pairs={{0,16},{4,20},{8,24},{12,28},{16,0},{20,4},{24,8},{28,12},{1,17},{... | collective-permute-start | bytes 147464 | tf_op jit(solution)/shard_map/ppermute | solution.py:297
  54.5 2.2 %queries.1 = bf16[192,2048]{1,0:T(8,128)(2,1)} custom-call(bf16[48,512]{1,0:T(8,128)(2,1)S(1)} %get-tuple-element.35.refs_0_.refs_2_, bf16[48,512]{1,0:T(8,128)(2,1)S(1)} %collective-permute-done.refs_1_, bf16[48,512]{1,0:T(8,128)(2,1)S(1)} %collective-permute-done.1.refs_2_, bf16[48,512]{1,0:T(8,128)(2,1)S(1)} %collective-permute-done.2.refs_3_, ...), custom_call_target="tpu_custom_call" | custom-call | flops 603979776 | bytes 1048576 | tf_op jit(solution)/shard_map/queries/pallas_call | solution.py:451
  56.7 2.2 %collective-permute-done.16.refs_3_ = bf16[96,256]{1,0:T(8,128)(2,1)S(1)} collective-permute-done((bf16[96,256]{1,0:T(8,128)(2,1)S(1)}, bf16[96,256]{1,0:T(8,128)(2,1)S(1)}, u32[]{:S(2)}, u32[]{:S(2)}) %collective-permute-start.16) | collective-permute-done | bytes 49184 | tf_op jit(solution)/shard_map/ppermute | solution.py:297
  58.9 1.0 %spread.1 = (bf16[192,256]{1,0:T(8,128)(2,1)}, bf16[192,256]{1,0:T(8,128)(2,1)}) custom-call(s32[2,192]{1,0:T(2,128)S(1)} %copy-done.6, f32[384,256]{1,0:T(8,128)S(1)} %get-tuple-element.55.refs_0_, bf16[384,256]{1,0:T(8,128)(2,1)S(1)} %collective-permute-done.14.refs_1_, bf16[192,256]{1,0:T(8,128)(2,1)S(1)} %collective-permute-done.15.refs_2_, ...), custom_call_target="tpu_custom_call" | custom-call | tf_op jit(solution)/shard_map/spread/pallas_call | solution.py:485
  (41 shorter events, 3.6 us)
Async XLA Ops:
  0.6 0.9 %copy-start.4 = (bf16[48,1024]{1,0:T(8,128)(2,1)S(1)}, bf16[48,1024]{1,0:T(8,128)(2,1)}, u32[]{:S(2)}) copy-start(bf16[48,1024]{1,0:T(8,128)(2,1)} %key_ref.1) | copy-start | bytes 294916
  1.5 0.9 %copy-start.5 = (bf16[48,1024]{1,0:T(8,128)(2,1)S(1)}, bf16[48,1024]{1,0:T(8,128)(2,1)}, u32[]{:S(2)}) copy-start(bf16[48,1024]{1,0:T(8,128)(2,1)} %value_ref.1) | copy-start | bytes 294916
  2.4 8.1 %copy-start.6 = (s32[2,192]{1,0:T(2,128)S(1)}, s32[2,192]{1,0:T(2,128)}, u32[]{:S(2)}) copy-start(s32[2,192]{1,0:T(2,128)} %seg_ref.3) | copy-start | bytes 4612
  2.4 5.8 %collective-permute-start = (bf16[48,512]{1,0:T(8,128)(2,1)S(1)}, bf16[48,512]{1,0:T(8,128)(2,1)S(1)}, u32[]{:S(2)}, u32[]{:S(2)}) collective-permute-start(bf16[48,512]{1,0:T(8,128)(2,1)S(1)} %get-tuple-element.36), channel_id=1, source_target_pairs={{0,1},{1,0},{2,3},{3,2},{4,5},{5,4},{6,7},{7,6},{8,9},{9,8},{10,11... | collective-permute-start | bytes 147464 | tf_op jit(solution)/shard_map/ppermute | solution.py:297
  3.0 5.3 %collective-permute-start.1 = (bf16[48,512]{1,0:T(8,128)(2,1)S(1)}, bf16[48,512]{1,0:T(8,128)(2,1)S(1)}, u32[]{:S(2)}, u32[]{:S(2)}) collective-permute-start(bf16[48,512]{1,0:T(8,128)(2,1)S(1)} %get-tuple-element.37), channel_id=1, source_target_pairs={{0,2},{1,3},{2,0},{3,1},{4,6},{5,7},{6,4},{7,5},{8,10},{9,11},{10,... | collective-permute-start | bytes 147464 | tf_op jit(solution)/shard_map/ppermute | solution.py:297
  5.5 3.7 %collective-permute-start.2 = (bf16[48,512]{1,0:T(8,128)(2,1)S(1)}, bf16[48,512]{1,0:T(8,128)(2,1)S(1)}, u32[]{:S(2)}, u32[]{:S(2)}) collective-permute-start(bf16[48,512]{1,0:T(8,128)(2,1)S(1)} %get-tuple-element.38), channel_id=1, source_target_pairs={{0,3},{1,2},{2,1},{3,0},{4,7},{5,6},{6,5},{7,4},{8,11},{9,10},{10,... | collective-permute-start | bytes 147464 | tf_op jit(solution)/shard_map/ppermute | solution.py:297
  5.6 1.1 %copy-start = (bf16[48,8192]{1,0:T(8,128)(2,1)S(1)}, bf16[48,8192]{1,0:T(8,128)(2,1)}, u32[]{:S(2)}) copy-start(bf16[48,8192]{1,0:T(8,128)(2,1)} %q_ref.3) | copy-start | bytes 2359300
  6.7 1.1 %copy-start.2 = (bf16[48,8192]{1,0:T(8,128)(2,1)S(1)}, bf16[48,8192]{1,0:T(8,128)(2,1)}, u32[]{:S(2)}) copy-start(bf16[48,8192]{1,0:T(8,128)(2,1)} %o_ref.3) | copy-start | bytes 2359300
  8.3 23.0 %copy-start.1 = (bf16[48,8192]{1,0:T(8,128)(2,1)S(1)}, bf16[48,8192]{1,0:T(8,128)(2,1)}, u32[]{:S(2)}) copy-start(bf16[48,8192]{1,0:T(8,128)(2,1)} %q_ref.3) | copy-start | bytes 2359300
  8.3 23.0 %copy-start.3 = (bf16[48,8192]{1,0:T(8,128)(2,1)S(1)}, bf16[48,8192]{1,0:T(8,128)(2,1)}, u32[]{:S(2)}) copy-start(bf16[48,8192]{1,0:T(8,128)(2,1)} %o_ref.3) | copy-start | bytes 2359300
  9.2 12.6 %collective-permute-start.12 = (bf16[96,2048]{1,0:T(8,128)(2,1)S(1)}, bf16[96,2048]{1,0:T(8,128)(2,1)S(1)}, u32[]{:S(2)}, u32[]{:S(2)}) collective-permute-start(bf16[96,2048]{1,0:T(8,128)(2,1)S(1)} %gate.6), channel_id=1, source_target_pairs={{0,1},{1,0},{2,3},{3,2},{4,5},{5,4},{6,7},{7,6},{8,9},{9,8},{10,11... | collective-permute-start | bytes 1179656 | tf_op jit(solution)/shard_map/ppermute | solution.py:297
  9.4 16.6 %collective-permute-start.10 = (bf16[96,2048]{1,0:T(8,128)(2,1)S(1)}, bf16[96,2048]{1,0:T(8,128)(2,1)S(1)}, u32[]{:S(2)}, u32[]{:S(2)}) collective-permute-start(bf16[96,2048]{1,0:T(8,128)(2,1)S(1)} %gate.4), channel_id=1, source_target_pairs={{0,2},{1,3},{2,0},{3,1},{4,6},{5,7},{6,4},{7,5},{8,10},{9,11},{10,... | collective-permute-start | bytes 1179656 | tf_op jit(solution)/shard_map/ppermute | solution.py:297
  10.8 5.7 %collective-permute-start.4 = (bf16[96,512]{1,0:T(8,128)(2,1)S(1)}, bf16[96,512]{1,0:T(8,128)(2,1)S(1)}, u32[]{:S(2)}, u32[]{:S(2)}) collective-permute-start(bf16[96,512]{1,0:T(8,128)(2,1)S(1)} %get-tuple-element.40.refs_4_), channel_id=1, source_target_pairs={{0,8},{4,12},{8,0},{12,4},{16,24},{20,28},{24,16},{28,20},{1,9},{5... | collective-permute-start | bytes 294920 | tf_op jit(solution)/shard_map/ppermute | solution.py:297
  12.4 7.4 %collective-permute-start.3 = (bf16[96,512]{1,0:T(8,128)(2,1)S(1)}, bf16[96,512]{1,0:T(8,128)(2,1)S(1)}, u32[]{:S(2)}, u32[]{:S(2)}) collective-permute-start(bf16[96,512]{1,0:T(8,128)(2,1)S(1)} %get-tuple-element.40.refs_4_), channel_id=1, source_target_pairs={{0,16},{4,20},{8,24},{12,28},{16,0},{20,4},{24,8},{28,12},{1,17},{... | collective-permute-start | bytes 294920 | tf_op jit(solution)/shard_map/ppermute | solution.py:297
  15.0 6.4 %collective-permute-start.6 = (bf16[96,512]{1,0:T(8,128)(2,1)S(1)}, bf16[96,512]{1,0:T(8,128)(2,1)S(1)}, u32[]{:S(2)}, u32[]{:S(2)}) collective-permute-start(bf16[96,512]{1,0:T(8,128)(2,1)S(1)} %get-tuple-element.40.refs_4_), channel_id=1, source_target_pairs={{0,4},{4,0},{8,12},{12,8},{16,20},{20,16},{24,28},{28,24},{1,5},{5... | collective-permute-start | bytes 294920 | tf_op jit(solution)/shard_map/ppermute | solution.py:297
  16.5 6.3 %collective-permute-start.8 = (bf16[96,512]{1,0:T(8,128)(2,1)S(1)}, bf16[96,512]{1,0:T(8,128)(2,1)S(1)}, u32[]{:S(2)}, u32[]{:S(2)}) collective-permute-start(bf16[96,512]{1,0:T(8,128)(2,1)S(1)} %collective-permute-done.4.refs_2_.refs_6_), channel_id=1, source_target_pairs={{0,4},{4,0},{8,12},{12,8},{16,20},{20,16},{24,28},{28,24},{1,5},{5... | collective-permute-start | bytes 294920 | tf_op jit(solution)/shard_map/ppermute | solution.py:297
  19.8 4.6 %collective-permute-start.7 = (bf16[96,512]{1,0:T(8,128)(2,1)S(1)}, bf16[96,512]{1,0:T(8,128)(2,1)S(1)}, u32[]{:S(2)}, u32[]{:S(2)}) collective-permute-start(bf16[96,512]{1,0:T(8,128)(2,1)S(1)} %collective-permute-done.3.refs_4_.refs_5_), channel_id=1, source_target_pairs={{0,4},{4,0},{8,12},{12,8},{16,20},{20,16},{24,28},{28,24},{1,5},{5... | collective-permute-start | bytes 294920 | tf_op jit(solution)/shard_map/ppermute | solution.py:297
  21.4 4.6 %collective-permute-start.5 = (bf16[96,512]{1,0:T(8,128)(2,1)S(1)}, bf16[96,512]{1,0:T(8,128)(2,1)S(1)}, u32[]{:S(2)}, u32[]{:S(2)}) collective-permute-start(bf16[96,512]{1,0:T(8,128)(2,1)S(1)} %collective-permute-done.3.refs_4_.refs_5_), channel_id=1, source_target_pairs={{0,8},{4,12},{8,0},{12,4},{16,24},{20,28},{24,16},{28,20},{1,9},{5... | collective-permute-start | bytes 294920 | tf_op jit(solution)/shard_map/ppermute | solution.py:297
  21.8 9.5 %collective-permute-start.13 = (bf16[96,2048]{1,0:T(8,128)(2,1)S(1)}, bf16[96,2048]{1,0:T(8,128)(2,1)S(1)}, u32[]{:S(2)}, u32[]{:S(2)}) collective-permute-start(bf16[96,2048]{1,0:T(8,128)(2,1)S(1)} %collective-permute-done.12), channel_id=1, source_target_pairs={{0,2},{1,3},{2,0},{3,1},{4,6},{5,7},{6,4},{7,5},{8,10},{9,11},{10,... | collective-permute-start | bytes 1179656 | tf_op jit(solution)/shard_map/ppermute | solution.py:297
  26.0 5.3 %collective-permute-start.11 = (bf16[96,2048]{1,0:T(8,128)(2,1)S(1)}, bf16[96,2048]{1,0:T(8,128)(2,1)S(1)}, u32[]{:S(2)}, u32[]{:S(2)}) collective-permute-start(bf16[96,2048]{1,0:T(8,128)(2,1)S(1)} %gate.5), channel_id=1, source_target_pairs={{0,1},{1,0},{2,3},{3,2},{4,5},{5,4},{6,7},{7,6},{8,9},{9,8},{10,11... | collective-permute-start | bytes 1179656 | tf_op jit(solution)/shard_map/ppermute | solution.py:297
  26.0 5.3 %collective-permute-start.9 = (bf16[96,512]{1,0:T(8,128)(2,1)S(1)}, bf16[96,512]{1,0:T(8,128)(2,1)S(1)}, u32[]{:S(2)}, u32[]{:S(2)}) collective-permute-start(bf16[96,512]{1,0:T(8,128)(2,1)S(1)} %collective-permute-done.5.refs_6_.refs_7_), channel_id=1, source_target_pairs={{0,4},{4,0},{8,12},{12,8},{16,20},{20,16},{24,28},{28,24},{1,5},{5... | collective-permute-start | bytes 294920 | tf_op jit(solution)/shard_map/ppermute | solution.py:297
  35.8 11.0 %collective-permute-start.14 = (bf16[384,256]{1,0:T(8,128)(2,1)S(1)}, bf16[384,256]{1,0:T(8,128)(2,1)S(1)}, u32[]{:S(2)}, u32[]{:S(2)}) collective-permute-start(bf16[384,256]{1,0:T(8,128)(2,1)S(1)} %get-tuple-element.56), channel_id=1, source_target_pairs={{0,4},{4,0},{8,12},{12,8},{16,20},{20,16},{24,28},{28,24},{1,5},{5... | collective-permute-start | bytes 589832 | tf_op jit(solution)/shard_map/ppermute | solution.py:297
  41.3 5.2 %collective-permute-start.18 = (bf16[192,256]{1,0:T(8,128)(2,1)S(1)}, bf16[192,256]{1,0:T(8,128)(2,1)S(1)}, u32[]{:S(2)}, u32[]{:S(2)}) collective-permute-start(bf16[192,256]{1,0:T(8,128)(2,1)S(1)} %get-tuple-element.63), channel_id=1, source_target_pairs={{0,4},{4,0},{8,12},{12,8},{16,20},{20,16},{24,28},{28,24},{1,5},{5... | collective-permute-start | bytes 294920 | tf_op jit(solution)/shard_map/ppermute | solution.py:297
  42.6 6.1 %collective-permute-start.17 = (bf16[192,256]{1,0:T(8,128)(2,1)S(1)}, bf16[192,256]{1,0:T(8,128)(2,1)S(1)}, u32[]{:S(2)}, u32[]{:S(2)}) collective-permute-start(bf16[192,256]{1,0:T(8,128)(2,1)S(1)} %get-tuple-element.62), channel_id=1, source_target_pairs={{0,4},{4,0},{8,12},{12,8},{16,20},{20,16},{24,28},{28,24},{1,5},{5... | collective-permute-start | bytes 294920 | tf_op jit(solution)/shard_map/ppermute | solution.py:297
  46.5 4.7 %collective-permute-start.19 = (bf16[192,256]{1,0:T(8,128)(2,1)S(1)}, bf16[192,256]{1,0:T(8,128)(2,1)S(1)}, u32[]{:S(2)}, u32[]{:S(2)}) collective-permute-start(bf16[192,256]{1,0:T(8,128)(2,1)S(1)} %add.6), channel_id=1, source_target_pairs={{0,8},{4,12},{8,0},{12,4},{16,24},{20,28},{24,16},{28,20},{1,9},{5... | collective-permute-start | bytes 294920 | tf_op jit(solution)/shard_map/ppermute | solution.py:297
  46.8 6.5 %collective-permute-start.15 = (bf16[192,256]{1,0:T(8,128)(2,1)S(1)}, bf16[192,256]{1,0:T(8,128)(2,1)S(1)}, u32[]{:S(2)}, u32[]{:S(2)}) collective-permute-start(bf16[192,256]{1,0:T(8,128)(2,1)S(1)} %add.4), channel_id=1, source_target_pairs={{0,8},{4,12},{8,0},{12,4},{16,24},{20,28},{24,16},{28,20},{1,9},{5... | collective-permute-start | bytes 294920 | tf_op jit(solution)/shard_map/ppermute | solution.py:297
  51.2 5.5 %collective-permute-start.20 = (bf16[96,256]{1,0:T(8,128)(2,1)S(1)}, bf16[96,256]{1,0:T(8,128)(2,1)S(1)}, u32[]{:S(2)}, u32[]{:S(2)}) collective-permute-start(bf16[96,256]{1,0:T(8,128)(2,1)S(1)} %add.7), channel_id=1, source_target_pairs={{0,16},{4,20},{8,24},{12,28},{16,0},{20,4},{24,8},{28,12},{1,17},{... | collective-permute-start | bytes 147464 | tf_op jit(solution)/shard_map/ppermute | solution.py:297
  53.3 5.6 %collective-permute-start.16 = (bf16[96,256]{1,0:T(8,128)(2,1)S(1)}, bf16[96,256]{1,0:T(8,128)(2,1)S(1)}, u32[]{:S(2)}, u32[]{:S(2)}) collective-permute-start(bf16[96,256]{1,0:T(8,128)(2,1)S(1)} %add.5), channel_id=1, source_target_pairs={{0,16},{4,20},{8,24},{12,28},{16,0},{20,4},{24,8},{28,12},{1,17},{... | collective-permute-start | bytes 147464 | tf_op jit(solution)/shard_map/ppermute | solution.py:297

commit v12 on v11

--- a/solution.py
+++ b/solution.py
@@ -428,7 +428,12 @@
             *([saved[-1][2]] if g else []),
         )
         saved.append(outs)
-    far = [[swap(part, "ctx", shards, 1) for part in outs[7:]] for outs in saved]
+    far = []
+    for outs in saved:
+        received = [swap(outs[7], "ctx", shards, 1)]
+        for part in outs[8:]:
+            received.append(swap(gate(part, received), "ctx", shards, 1))
+        far.append(received)
     near = []
     own = []
     for g in range(kv_heads):
@@ -461,6 +466,7 @@
     )(*kv, *[x for outs in saved for x in (outs[1], outs[3], outs[6])])
 
     spread_args = []
+    before = {}
     for g in range(kv_heads):
         rows_left, step = half // 2, 2
         first, rest = far[g][0], far[g][-1]
@@ -470,12 +476,13 @@
             send = pl.pallas_call(
                 functools.partial(add_kernel, [start for _, start in terms]),
                 out_shape=shape(rows_left, 2 * HD),
-                in_specs=in_vmem(len(terms)),
+                in_specs=in_vmem(len(terms)) + anywhere(step in before),
                 out_specs=in_vmem(1)[0],
                 compiler_params=params(8),
                 name="add",
-            )(*[term for term, _ in terms])
+            )(*[term for term, _ in terms], *[before[s] for s in [step] if s in before])
             kept.append(swap(send, "ctx", shards, step))
+            before[step] = send if step == 2 else kept[-2]
             rows_left //= 2
             step *= 2
             terms = [(term, rows_left) for term in kept]

time: 60.2 us -> 60 us (level)
  waiting for transfers between devices: 18 us -> 15.5 us
  starting transfers between devices: 22.2 us -> 24.5 us
    ppermute x21, waiting for transfers between devices: 18 us -> 15.5 us  [swap(): return lax.ppermute(x, axis, [(i, i ^ m) for i in range(size)])]
    ppermute x21, starting transfers between devices: 22.2 us -> 24.5 us  [swap(): return lax.ppermute(x, axis, [(i, i ^ m) for i in range(size)])]
  transfers between devices with their start and end apart: 21 -> 21, of which waited for: 9 -> 8; matrix products, arithmetic and copies ran while one was open for 0% -> 0% of each run, Pallas kernels for 16% -> 16%
where the time goes in v12:
time: 60 us; the launch traced here: 59.7 us
  starting transfers between devices  24.5 us (41%)
  waiting for transfers between devices  15.5 us (26%)
  Pallas kernels  14.9 us (25%)
  local copies, waits for them, and re-layouts  4.06 us (7%)
  between operations  0.77 us (1%)
    ppermute x21, starting transfers between devices, swap(): return lax.ppermute(x, axis, [(i, i ^ m) for i in range(size)])  24.5 us
    ppermute x21, waiting for transfers between devices, swap(): return lax.ppermute(x, axis, [(i, i ^ m) for i in range(size)])  15.5 us
    pallas_call x2, Pallas kernels, local(): pl.pallas_call(functools.partial(attend_kernel, g, order, far_parts), out...  9.13 us
    unnamed x14, local copies, waits for them, and re-layouts  4.06 us
    pallas_call x1, Pallas kernels, local(): pl.pallas_call(functools.partial(queries_kernel, heads), out_shape=shape(...  2.2 us
    pallas_call x2, Pallas kernels, local(): pl.pallas_call(functools.partial(terms_kernel, heads), out_shape=[shape(h...  1.8 us
  transfers between devices with their start and end apart: 21, of which 8 were waited for; matrix products, arithmetic and copies ran while one was open for 0% of the time, Pallas kernels for 16%

profile of v12, /device:TPU:0, one launch (start us, length us, event | category | flops | bytes accessed | tf_op | source)
XLA Modules:
  0.0 59.7 jit_solution(9111547682973837106)
XLA Ops:
  0.6 0.9 %copy-done.4 = bf16[48,1024]{1,0:T(8,128)(2,1)S(1)} copy-done((bf16[48,1024]{1,0:T(8,128)(2,1)S(1)}, bf16[48,1024]{1,0:T(8,128)(2,1)}, u32[]{:S(2)}) %copy-start.4) | copy-done | bytes 98328
  1.5 0.9 %copy-done.5 = bf16[48,1024]{1,0:T(8,128)(2,1)S(1)} copy-done((bf16[48,1024]{1,0:T(8,128)(2,1)S(1)}, bf16[48,1024]{1,0:T(8,128)(2,1)}, u32[]{:S(2)}) %copy-start.5) | copy-done | bytes 98328
  3.0 2.6 %collective-permute-start.1 = (bf16[48,512]{1,0:T(8,128)(2,1)S(1)}, bf16[48,512]{1,0:T(8,128)(2,1)S(1)}, u32[]{:S(2)}, u32[]{:S(2)}) collective-permute-start(bf16[48,512]{1,0:T(8,128)(2,1)S(1)} %get-tuple-element.37), channel_id=1, source_target_pairs={{0,2},{1,3},{2,0},{3,1},{4,6},{5,7},{6,4},{7,5},{8,10},{9,11},{10,... | collective-permute-start | bytes 147464 | tf_op jit(solution)/shard_map/ppermute | solution.py:297
  5.6 1.1 %copy-done = bf16[48,8192]{1,0:T(8,128)(2,1)S(1)} copy-done((bf16[48,8192]{1,0:T(8,128)(2,1)S(1)}, bf16[48,8192]{1,0:T(8,128)(2,1)}, u32[]{:S(2)}) %copy-start) | copy-done | bytes 786456
  6.7 1.1 %copy-done.2 = bf16[48,8192]{1,0:T(8,128)(2,1)S(1)} copy-done((bf16[48,8192]{1,0:T(8,128)(2,1)S(1)}, bf16[48,8192]{1,0:T(8,128)(2,1)}, u32[]{:S(2)}) %copy-start.2) | copy-done | bytes 786456
  8.3 0.9 %collective-permute-done.2.refs_3_ = bf16[48,512]{1,0:T(8,128)(2,1)S(1)} collective-permute-done((bf16[48,512]{1,0:T(8,128)(2,1)S(1)}, bf16[48,512]{1,0:T(8,128)(2,1)S(1)}, u32[]{:S(2)}, u32[]{:S(2)}) %collective-permute-start.2) | collective-permute-done | bytes 49184 | tf_op jit(solution)/shard_map/ppermute | solution.py:297
  9.4 1.1 %collective-permute-start.10 = (bf16[96,2048]{1,0:T(8,128)(2,1)S(1)}, bf16[96,2048]{1,0:T(8,128)(2,1)S(1)}, u32[]{:S(2)}, u32[]{:S(2)}) collective-permute-start(bf16[96,2048]{1,0:T(8,128)(2,1)S(1)} %gate.5), channel_id=1, source_target_pairs={{0,2},{1,3},{2,0},{3,1},{4,6},{5,7},{6,4},{7,5},{8,10},{9,11},{10,... | collective-permute-start | bytes 1179656 | tf_op jit(solution)/shard_map/ppermute | solution.py:297
  10.8 1.6 %collective-permute-start.4 = (bf16[96,512]{1,0:T(8,128)(2,1)S(1)}, bf16[96,512]{1,0:T(8,128)(2,1)S(1)}, u32[]{:S(2)}, u32[]{:S(2)}) collective-permute-start(bf16[96,512]{1,0:T(8,128)(2,1)S(1)} %get-tuple-element.40.refs_4_), channel_id=1, source_target_pairs={{0,8},{4,12},{8,0},{12,4},{16,24},{20,28},{24,16},{28,20},{1,9},{5... | collective-permute-start | bytes 294920 | tf_op jit(solution)/shard_map/ppermute | solution.py:297
  12.4 2.6 %collective-permute-start.3 = (bf16[96,512]{1,0:T(8,128)(2,1)S(1)}, bf16[96,512]{1,0:T(8,128)(2,1)S(1)}, u32[]{:S(2)}, u32[]{:S(2)}) collective-permute-start(bf16[96,512]{1,0:T(8,128)(2,1)S(1)} %get-tuple-element.40.refs_4_), channel_id=1, source_target_pairs={{0,16},{4,20},{8,24},{12,28},{16,0},{20,4},{24,8},{28,12},{1,17},{... | collective-permute-start | bytes 294920 | tf_op jit(solution)/shard_map/ppermute | solution.py:297
  15.0 1.5 %collective-permute-start.6 = (bf16[96,512]{1,0:T(8,128)(2,1)S(1)}, bf16[96,512]{1,0:T(8,128)(2,1)S(1)}, u32[]{:S(2)}, u32[]{:S(2)}) collective-permute-start(bf16[96,512]{1,0:T(8,128)(2,1)S(1)} %get-tuple-element.40.refs_4_), channel_id=1, source_target_pairs={{0,4},{4,0},{8,12},{12,8},{16,20},{20,16},{24,28},{28,24},{1,5},{5... | collective-permute-start | bytes 294920 | tf_op jit(solution)/shard_map/ppermute | solution.py:297
  17.0 2.8 %collective-permute-done.3.refs_4_.refs_5_ = bf16[96,512]{1,0:T(8,128)(2,1)S(1)} collective-permute-done((bf16[96,512]{1,0:T(8,128)(2,1)S(1)}, bf16[96,512]{1,0:T(8,128)(2,1)S(1)}, u32[]{:S(2)}, u32[]{:S(2)}) %collective-permute-start.3) | collective-permute-done | bytes 98336 | tf_op jit(solution)/shard_map/ppermute | solution.py:297
  19.8 1.5 %collective-permute-start.7 = (bf16[96,512]{1,0:T(8,128)(2,1)S(1)}, bf16[96,512]{1,0:T(8,128)(2,1)S(1)}, u32[]{:S(2)}, u32[]{:S(2)}) collective-permute-start(bf16[96,512]{1,0:T(8,128)(2,1)S(1)} %collective-permute-done.3.refs_4_.refs_5_), channel_id=1, source_target_pairs={{0,4},{4,0},{8,12},{12,8},{16,20},{20,16},{24,28},{28,24},{1,5},{5... | collective-permute-start | bytes 294920 | tf_op jit(solution)/shard_map/ppermute | solution.py:297
  21.8 1.0 %collective-permute-start.13 = (bf16[96,2048]{1,0:T(8,128)(2,1)S(1)}, bf16[96,2048]{1,0:T(8,128)(2,1)S(1)}, u32[]{:S(2)}, u32[]{:S(2)}) collective-permute-start(bf16[96,2048]{1,0:T(8,128)(2,1)S(1)} %collective-permute-done.12), channel_id=1, source_target_pairs={{0,2},{1,3},{2,0},{3,1},{4,6},{5,7},{6,4},{7,5},{8,10},{9,11},{10,... | collective-permute-start | bytes 1179656 | tf_op jit(solution)/shard_map/ppermute | solution.py:297
  22.8 1.6 %collective-permute-done.7.refs_5_.refs_9_ = bf16[96,512]{1,0:T(8,128)(2,1)S(1)} collective-permute-done((bf16[96,512]{1,0:T(8,128)(2,1)S(1)}, bf16[96,512]{1,0:T(8,128)(2,1)S(1)}, u32[]{:S(2)}, u32[]{:S(2)}) %collective-permute-start.7) | collective-permute-done | bytes 98336 | tf_op jit(solution)/shard_map/ppermute | solution.py:297
  24.4 1.5 %collective-permute-done.5.refs_6_.refs_7_ = bf16[96,512]{1,0:T(8,128)(2,1)S(1)} collective-permute-done((bf16[96,512]{1,0:T(8,128)(2,1)S(1)}, bf16[96,512]{1,0:T(8,128)(2,1)S(1)}, u32[]{:S(2)}, u32[]{:S(2)}) %collective-permute-start.5) | collective-permute-done | bytes 98336 | tf_op jit(solution)/shard_map/ppermute | solution.py:297
  26.0 0.9 %collective-permute-start.9 = (bf16[96,512]{1,0:T(8,128)(2,1)S(1)}, bf16[96,512]{1,0:T(8,128)(2,1)S(1)}, u32[]{:S(2)}, u32[]{:S(2)}) collective-permute-start(bf16[96,512]{1,0:T(8,128)(2,1)S(1)} %collective-permute-done.5.refs_6_.refs_7_), channel_id=1, source_target_pairs={{0,4},{4,0},{8,12},{12,8},{16,20},{20,16},{24,28},{28,24},{1,5},{5... | collective-permute-start | bytes 294920 | tf_op jit(solution)/shard_map/ppermute | solution.py:297
  26.9 4.3 %collective-permute-done.13.refs_0_ = bf16[96,2048]{1,0:T(8,128)(2,1)S(1)} collective-permute-done((bf16[96,2048]{1,0:T(8,128)(2,1)S(1)}, bf16[96,2048]{1,0:T(8,128)(2,1)S(1)}, u32[]{:S(2)}, u32[]{:S(2)}) %collective-permute-start.13) | collective-permute-done | bytes 393248 | tf_op jit(solution)/shard_map/ppermute | solution.py:297
  31.3 4.5 %attend.2 = (bf16[768,1536]{1,0:T(8,128)(2,1)S(1)}, bf16[768,1536]{1,0:T(8,128)(2,1)S(1)}, bf16[48,1536]{1,0:T(8,128)(2,1)S(1)}, bf16[48,1536]{1,0:T(8,128)(2,1)...) custom-call(bf16[48,8192]{1,0:T(8,128)(2,1)S(1)} %copy-done.1, ...), custom_call_target="tpu_custom_call" | custom-call | flops 962592768 | bytes 8388608 | tf_op jit(solution)/shard_map/attend/pallas_call | solution.py:392
  35.8 0.9 %collective-permute-start.14 = (bf16[384,256]{1,0:T(8,128)(2,1)S(1)}, bf16[384,256]{1,0:T(8,128)(2,1)S(1)}, u32[]{:S(2)}, u32[]{:S(2)}) collective-permute-start(bf16[384,256]{1,0:T(8,128)(2,1)S(1)} %get-tuple-element.56), channel_id=1, source_target_pairs={{0,4},{4,0},{8,12},{12,8},{16,20},{20,16},{24,28},{28,24},{1,5},{5... | collective-permute-start | bytes 589832 | tf_op jit(solution)/shard_map/ppermute | solution.py:297
  36.6 4.6 %attend.3 = (bf16[768,1536]{1,0:T(8,128)(2,1)S(1)}, bf16[768,1536]{1,0:T(8,128)(2,1)S(1)}, bf16[48,1536]{1,0:T(8,128)(2,1)S(1)}, bf16[48,1536]{1,0:T(8,128)(2,1)...) custom-call(bf16[48,8192]{1,0:T(8,128)(2,1)S(1)} %copy-done.1, ...), custom_call_target="tpu_custom_call" | custom-call | flops 962592768 | bytes 8388608 | tf_op jit(solution)/shard_map/attend/pallas_call | solution.py:392
  41.3 1.3 %collective-permute-start.17 = (bf16[192,256]{1,0:T(8,128)(2,1)S(1)}, bf16[192,256]{1,0:T(8,128)(2,1)S(1)}, u32[]{:S(2)}, u32[]{:S(2)}) collective-permute-start(bf16[192,256]{1,0:T(8,128)(2,1)S(1)} %get-tuple-element.63), channel_id=1, source_target_pairs={{0,4},{4,0},{8,12},{12,8},{16,20},{20,16},{24,28},{28,24},{1,5},{5... | collective-permute-start | bytes 294920 | tf_op jit(solution)/shard_map/ppermute | solution.py:297
  42.6 0.9 %terms.2 = (f32[384,256]{1,0:T(8,128)S(1)}, f32[192,256]{1,0:T(8,128)S(1)}) custom-call(bf16[768,1536]{1,0:T(8,128)(2,1)S(1)} %get-tuple-element.51.p_ref, bf16[768,1536]{1,0:T(8,128)(2,1)S(1)} %get-tuple-element.44.refs_4_.ds_ref, bf16[48,1536]{1,0:T(8,128)(2,1)S(1)} %get-tuple-element.47.refs_15_.own_p_ref, ...), custom_call_target="tpu_custom_call" | custom-call | flops 301989888 | bytes 1048576 | tf_op jit(solution)/shard_map/terms/pallas_call | solution.py:440
  43.5 0.9 %terms.3 = (f32[384,256]{1,0:T(8,128)S(1)}, f32[192,256]{1,0:T(8,128)S(1)}) custom-call(bf16[768,1536]{1,0:T(8,128)(2,1)S(1)} %get-tuple-element.58.p_ref, bf16[768,1536]{1,0:T(8,128)(2,1)S(1)} %get-tuple-element.48.refs_7_.ds_ref, bf16[48,1536]{1,0:T(8,128)(2,1)S(1)} %get-tuple-element.54.after_ref.own_p_ref, ...), custom_call_target="tpu_custom_call" | custom-call | flops 301989888 | bytes 1048576 | tf_op jit(solution)/shard_map/terms/pallas_call | solution.py:440
  44.4 1.6 %collective-permute-done.17.refs_1_ = bf16[192,256]{1,0:T(8,128)(2,1)S(1)} collective-permute-done((bf16[192,256]{1,0:T(8,128)(2,1)S(1)}, bf16[192,256]{1,0:T(8,128)(2,1)S(1)}, u32[]{:S(2)}, u32[]{:S(2)}) %collective-permute-start.17) | collective-permute-done | bytes 98336 | tf_op jit(solution)/shard_map/ppermute | solution.py:297
  46.4 1.2 %collective-permute-start.18 = (bf16[192,256]{1,0:T(8,128)(2,1)S(1)}, bf16[192,256]{1,0:T(8,128)(2,1)S(1)}, u32[]{:S(2)}, u32[]{:S(2)}) collective-permute-start(bf16[192,256]{1,0:T(8,128)(2,1)S(1)} %gate.9), channel_id=1, source_target_pairs={{0,4},{4,0},{8,12},{12,8},{16,20},{20,16},{24,28},{28,24},{1,5},{5... | collective-permute-start | bytes 294920 | tf_op jit(solution)/shard_map/ppermute | solution.py:297
  47.7 1.7 %collective-permute-start.19 = (bf16[192,256]{1,0:T(8,128)(2,1)S(1)}, bf16[192,256]{1,0:T(8,128)(2,1)S(1)}, u32[]{:S(2)}, u32[]{:S(2)}) collective-permute-start(bf16[192,256]{1,0:T(8,128)(2,1)S(1)} %add.6), channel_id=1, source_target_pairs={{0,8},{4,12},{8,0},{12,4},{16,24},{20,28},{24,16},{28,20},{1,9},{5... | collective-permute-start | bytes 294920 | tf_op jit(solution)/shard_map/ppermute | solution.py:297
  49.4 1.3 %collective-permute-done.15.refs_2_.refs_3_ = bf16[192,256]{1,0:T(8,128)(2,1)S(1)} collective-permute-done((bf16[192,256]{1,0:T(8,128)(2,1)S(1)}, bf16[192,256]{1,0:T(8,128)(2,1)S(1)}, u32[]{:S(2)}, u32[]{:S(2)}) %collective-permute-start.15) | collective-permute-done | bytes 98336 | tf_op jit(solution)/shard_map/ppermute | solution.py:297
  50.7 2.4 %collective-permute-start.16 = (bf16[96,256]{1,0:T(8,128)(2,1)S(1)}, bf16[96,256]{1,0:T(8,128)(2,1)S(1)}, u32[]{:S(2)}, u32[]{:S(2)}) collective-permute-start(bf16[96,256]{1,0:T(8,128)(2,1)S(1)} %add.5), channel_id=1, source_target_pairs={{0,16},{4,20},{8,24},{12,28},{16,0},{20,4},{24,8},{28,12},{1,17},{... | collective-permute-start | bytes 147464 | tf_op jit(solution)/shard_map/ppermute | solution.py:297
  53.1 1.9 %collective-permute-start.20 = (bf16[96,256]{1,0:T(8,128)(2,1)S(1)}, bf16[96,256]{1,0:T(8,128)(2,1)S(1)}, u32[]{:S(2)}, u32[]{:S(2)}) collective-permute-start(bf16[96,256]{1,0:T(8,128)(2,1)S(1)} %add.7), channel_id=1, source_target_pairs={{0,16},{4,20},{8,24},{12,28},{16,0},{20,4},{24,8},{28,12},{1,17},{... | collective-permute-start | bytes 147464 | tf_op jit(solution)/shard_map/ppermute | solution.py:297
  55.0 2.2 %queries.1 = bf16[192,2048]{1,0:T(8,128)(2,1)} custom-call(bf16[48,512]{1,0:T(8,128)(2,1)S(1)} %get-tuple-element.35.refs_0_.refs_2_, bf16[48,512]{1,0:T(8,128)(2,1)S(1)} %collective-permute-done.refs_1_, bf16[48,512]{1,0:T(8,128)(2,1)S(1)} %collective-permute-done.1.refs_2_, bf16[48,512]{1,0:T(8,128)(2,1)S(1)} %collective-permute-done.2.refs_3_, ...), custom_call_target="tpu_custom_call" | custom-call | flops 603979776 | bytes 1048576 | tf_op jit(solution)/shard_map/queries/pallas_call | solution.py:456
  57.2 1.5 %collective-permute-done.20.refs_8_ = bf16[96,256]{1,0:T(8,128)(2,1)S(1)} collective-permute-done((bf16[96,256]{1,0:T(8,128)(2,1)S(1)}, bf16[96,256]{1,0:T(8,128)(2,1)S(1)}, u32[]{:S(2)}, u32[]{:S(2)}) %collective-permute-start.20) | collective-permute-done | bytes 49184 | tf_op jit(solution)/shard_map/ppermute | solution.py:297
  58.7 1.0 %spread.1 = (bf16[192,256]{1,0:T(8,128)(2,1)}, bf16[192,256]{1,0:T(8,128)(2,1)}) custom-call(s32[2,192]{1,0:T(2,128)S(1)} %copy-done.6, f32[384,256]{1,0:T(8,128)S(1)} %get-tuple-element.55.refs_0_, bf16[384,256]{1,0:T(8,128)(2,1)S(1)} %collective-permute-done.14.refs_1_, bf16[192,256]{1,0:T(8,128)(2,1)S(1)} %collective-permute-done.15.refs_2_.refs_3_, ...), custom_call_target="tpu_custom_call" | custom-call | tf_op jit(solution)/shard_map/spread/pallas_call | solution.py:492
  (42 shorter events, 2.9 us)
Async XLA Ops:
  0.6 0.9 %copy-start.4 = (bf16[48,1024]{1,0:T(8,128)(2,1)S(1)}, bf16[48,1024]{1,0:T(8,128)(2,1)}, u32[]{:S(2)}) copy-start(bf16[48,1024]{1,0:T(8,128)(2,1)} %key_ref.1) | copy-start | bytes 294916
  1.5 0.9 %copy-start.5 = (bf16[48,1024]{1,0:T(8,128)(2,1)S(1)}, bf16[48,1024]{1,0:T(8,128)(2,1)}, u32[]{:S(2)}) copy-start(bf16[48,1024]{1,0:T(8,128)(2,1)} %value_ref.1) | copy-start | bytes 294916
  2.4 8.1 %copy-start.6 = (s32[2,192]{1,0:T(2,128)S(1)}, s32[2,192]{1,0:T(2,128)}, u32[]{:S(2)}) copy-start(s32[2,192]{1,0:T(2,128)} %seg_ref.3) | copy-start | bytes 4612
  2.4 5.8 %collective-permute-start = (bf16[48,512]{1,0:T(8,128)(2,1)S(1)}, bf16[48,512]{1,0:T(8,128)(2,1)S(1)}, u32[]{:S(2)}, u32[]{:S(2)}) collective-permute-start(bf16[48,512]{1,0:T(8,128)(2,1)S(1)} %get-tuple-element.36), channel_id=1, source_target_pairs={{0,1},{1,0},{2,3},{3,2},{4,5},{5,4},{6,7},{7,6},{8,9},{9,8},{10,11... | collective-permute-start | bytes 147464 | tf_op jit(solution)/shard_map/ppermute | solution.py:297
  3.0 5.3 %collective-permute-start.1 = (bf16[48,512]{1,0:T(8,128)(2,1)S(1)}, bf16[48,512]{1,0:T(8,128)(2,1)S(1)}, u32[]{:S(2)}, u32[]{:S(2)}) collective-permute-start(bf16[48,512]{1,0:T(8,128)(2,1)S(1)} %get-tuple-element.37), channel_id=1, source_target_pairs={{0,2},{1,3},{2,0},{3,1},{4,6},{5,7},{6,4},{7,5},{8,10},{9,11},{10,... | collective-permute-start | bytes 147464 | tf_op jit(solution)/shard_map/ppermute | solution.py:297
  5.5 3.7 %collective-permute-start.2 = (bf16[48,512]{1,0:T(8,128)(2,1)S(1)}, bf16[48,512]{1,0:T(8,128)(2,1)S(1)}, u32[]{:S(2)}, u32[]{:S(2)}) collective-permute-start(bf16[48,512]{1,0:T(8,128)(2,1)S(1)} %get-tuple-element.38), channel_id=1, source_target_pairs={{0,3},{1,2},{2,1},{3,0},{4,7},{5,6},{6,5},{7,4},{8,11},{9,10},{10,... | collective-permute-start | bytes 147464 | tf_op jit(solution)/shard_map/ppermute | solution.py:297
  5.6 1.1 %copy-start = (bf16[48,8192]{1,0:T(8,128)(2,1)S(1)}, bf16[48,8192]{1,0:T(8,128)(2,1)}, u32[]{:S(2)}) copy-start(bf16[48,8192]{1,0:T(8,128)(2,1)} %q_ref.3) | copy-start | bytes 2359300
  6.7 1.1 %copy-start.2 = (bf16[48,8192]{1,0:T(8,128)(2,1)S(1)}, bf16[48,8192]{1,0:T(8,128)(2,1)}, u32[]{:S(2)}) copy-start(bf16[48,8192]{1,0:T(8,128)(2,1)} %o_ref.3) | copy-start | bytes 2359300
  8.3 23.0 %copy-start.1 = (bf16[48,8192]{1,0:T(8,128)(2,1)S(1)}, bf16[48,8192]{1,0:T(8,128)(2,1)}, u32[]{:S(2)}) copy-start(bf16[48,8192]{1,0:T(8,128)(2,1)} %q_ref.3) | copy-start | bytes 2359300
  8.3 23.0 %copy-start.3 = (bf16[48,8192]{1,0:T(8,128)(2,1)S(1)}, bf16[48,8192]{1,0:T(8,128)(2,1)}, u32[]{:S(2)}) copy-start(bf16[48,8192]{1,0:T(8,128)(2,1)} %o_ref.3) | copy-start | bytes 2359300
  9.2 12.6 %collective-permute-start.12 = (bf16[96,2048]{1,0:T(8,128)(2,1)S(1)}, bf16[96,2048]{1,0:T(8,128)(2,1)S(1)}, u32[]{:S(2)}, u32[]{:S(2)}) collective-permute-start(bf16[96,2048]{1,0:T(8,128)(2,1)S(1)} %gate.7), channel_id=1, source_target_pairs={{0,1},{1,0},{2,3},{3,2},{4,5},{5,4},{6,7},{7,6},{8,9},{9,8},{10,11... | collective-permute-start | bytes 1179656 | tf_op jit(solution)/shard_map/ppermute | solution.py:297
  9.4 16.6 %collective-permute-start.10 = (bf16[96,2048]{1,0:T(8,128)(2,1)S(1)}, bf16[96,2048]{1,0:T(8,128)(2,1)S(1)}, u32[]{:S(2)}, u32[]{:S(2)}) collective-permute-start(bf16[96,2048]{1,0:T(8,128)(2,1)S(1)} %gate.5), channel_id=1, source_target_pairs={{0,2},{1,3},{2,0},{3,1},{4,6},{5,7},{6,4},{7,5},{8,10},{9,11},{10,... | collective-permute-start | bytes 1179656 | tf_op jit(solution)/shard_map/ppermute | solution.py:297
  10.8 5.7 %collective-permute-start.4 = (bf16[96,512]{1,0:T(8,128)(2,1)S(1)}, bf16[96,512]{1,0:T(8,128)(2,1)S(1)}, u32[]{:S(2)}, u32[]{:S(2)}) collective-permute-start(bf16[96,512]{1,0:T(8,128)(2,1)S(1)} %get-tuple-element.40.refs_4_), channel_id=1, source_target_pairs={{0,8},{4,12},{8,0},{12,4},{16,24},{20,28},{24,16},{28,20},{1,9},{5... | collective-permute-start | bytes 294920 | tf_op jit(solution)/shard_map/ppermute | solution.py:297
  12.4 7.4 %collective-permute-start.3 = (bf16[96,512]{1,0:T(8,128)(2,1)S(1)}, bf16[96,512]{1,0:T(8,128)(2,1)S(1)}, u32[]{:S(2)}, u32[]{:S(2)}) collective-permute-start(bf16[96,512]{1,0:T(8,128)(2,1)S(1)} %get-tuple-element.40.refs_4_), channel_id=1, source_target_pairs={{0,16},{4,20},{8,24},{12,28},{16,0},{20,4},{24,8},{28,12},{1,17},{... | collective-permute-start | bytes 294920 | tf_op jit(solution)/shard_map/ppermute | solution.py:297
  15.0 6.4 %collective-permute-start.6 = (bf16[96,512]{1,0:T(8,128)(2,1)S(1)}, bf16[96,512]{1,0:T(8,128)(2,1)S(1)}, u32[]{:S(2)}, u32[]{:S(2)}) collective-permute-start(bf16[96,512]{1,0:T(8,128)(2,1)S(1)} %get-tuple-element.40.refs_4_), channel_id=1, source_target_pairs={{0,4},{4,0},{8,12},{12,8},{16,20},{20,16},{24,28},{28,24},{1,5},{5... | collective-permute-start | bytes 294920 | tf_op jit(solution)/shard_map/ppermute | solution.py:297
  16.5 6.3 %collective-permute-start.8 = (bf16[96,512]{1,0:T(8,128)(2,1)S(1)}, bf16[96,512]{1,0:T(8,128)(2,1)S(1)}, u32[]{:S(2)}, u32[]{:S(2)}) collective-permute-start(bf16[96,512]{1,0:T(8,128)(2,1)S(1)} %collective-permute-done.4.refs_2_.refs_6_), channel_id=1, source_target_pairs={{0,4},{4,0},{8,12},{12,8},{16,20},{20,16},{24,28},{28,24},{1,5},{5... | collective-permute-start | bytes 294920 | tf_op jit(solution)/shard_map/ppermute | solution.py:297
  19.8 4.6 %collective-permute-start.7 = (bf16[96,512]{1,0:T(8,128)(2,1)S(1)}, bf16[96,512]{1,0:T(8,128)(2,1)S(1)}, u32[]{:S(2)}, u32[]{:S(2)}) collective-permute-start(bf16[96,512]{1,0:T(8,128)(2,1)S(1)} %collective-permute-done.3.refs_4_.refs_5_), channel_id=1, source_target_pairs={{0,4},{4,0},{8,12},{12,8},{16,20},{20,16},{24,28},{28,24},{1,5},{5... | collective-permute-start | bytes 294920 | tf_op jit(solution)/shard_map/ppermute | solution.py:297
  21.4 4.6 %collective-permute-start.5 = (bf16[96,512]{1,0:T(8,128)(2,1)S(1)}, bf16[96,512]{1,0:T(8,128)(2,1)S(1)}, u32[]{:S(2)}, u32[]{:S(2)}) collective-permute-start(bf16[96,512]{1,0:T(8,128)(2,1)S(1)} %collective-permute-done.3.refs_4_.refs_5_), channel_id=1, source_target_pairs={{0,8},{4,12},{8,0},{12,4},{16,24},{20,28},{24,16},{28,20},{1,9},{5... | collective-permute-start | bytes 294920 | tf_op jit(solution)/shard_map/ppermute | solution.py:297
  21.8 9.5 %collective-permute-start.13 = (bf16[96,2048]{1,0:T(8,128)(2,1)S(1)}, bf16[96,2048]{1,0:T(8,128)(2,1)S(1)}, u32[]{:S(2)}, u32[]{:S(2)}) collective-permute-start(bf16[96,2048]{1,0:T(8,128)(2,1)S(1)} %collective-permute-done.12), channel_id=1, source_target_pairs={{0,2},{1,3},{2,0},{3,1},{4,6},{5,7},{6,4},{7,5},{8,10},{9,11},{10,... | collective-permute-start | bytes 1179656 | tf_op jit(solution)/shard_map/ppermute | solution.py:297
  26.0 5.3 %collective-permute-start.11 = (bf16[96,2048]{1,0:T(8,128)(2,1)S(1)}, bf16[96,2048]{1,0:T(8,128)(2,1)S(1)}, u32[]{:S(2)}, u32[]{:S(2)}) collective-permute-start(bf16[96,2048]{1,0:T(8,128)(2,1)S(1)} %gate.6), channel_id=1, source_target_pairs={{0,1},{1,0},{2,3},{3,2},{4,5},{5,4},{6,7},{7,6},{8,9},{9,8},{10,11... | collective-permute-start | bytes 1179656 | tf_op jit(solution)/shard_map/ppermute | solution.py:297
  26.0 5.3 %collective-permute-start.9 = (bf16[96,512]{1,0:T(8,128)(2,1)S(1)}, bf16[96,512]{1,0:T(8,128)(2,1)S(1)}, u32[]{:S(2)}, u32[]{:S(2)}) collective-permute-start(bf16[96,512]{1,0:T(8,128)(2,1)S(1)} %collective-permute-done.5.refs_6_.refs_7_), channel_id=1, source_target_pairs={{0,4},{4,0},{8,12},{12,8},{16,20},{20,16},{24,28},{28,24},{1,5},{5... | collective-permute-start | bytes 294920 | tf_op jit(solution)/shard_map/ppermute | solution.py:297
  35.8 10.2 %collective-permute-start.14 = (bf16[384,256]{1,0:T(8,128)(2,1)S(1)}, bf16[384,256]{1,0:T(8,128)(2,1)S(1)}, u32[]{:S(2)}, u32[]{:S(2)}) collective-permute-start(bf16[384,256]{1,0:T(8,128)(2,1)S(1)} %get-tuple-element.56), channel_id=1, source_target_pairs={{0,4},{4,0},{8,12},{12,8},{16,20},{20,16},{24,28},{28,24},{1,5},{5... | collective-permute-start | bytes 589832 | tf_op jit(solution)/shard_map/ppermute | solution.py:297
  41.3 4.7 %collective-permute-start.17 = (bf16[192,256]{1,0:T(8,128)(2,1)S(1)}, bf16[192,256]{1,0:T(8,128)(2,1)S(1)}, u32[]{:S(2)}, u32[]{:S(2)}) collective-permute-start(bf16[192,256]{1,0:T(8,128)(2,1)S(1)} %get-tuple-element.63), channel_id=1, source_target_pairs={{0,4},{4,0},{8,12},{12,8},{16,20},{20,16},{24,28},{28,24},{1,5},{5... | collective-permute-start | bytes 294920 | tf_op jit(solution)/shard_map/ppermute | solution.py:297
  46.0 4.7 %collective-permute-start.15 = (bf16[192,256]{1,0:T(8,128)(2,1)S(1)}, bf16[192,256]{1,0:T(8,128)(2,1)S(1)}, u32[]{:S(2)}, u32[]{:S(2)}) collective-permute-start(bf16[192,256]{1,0:T(8,128)(2,1)S(1)} %add.4.refs_2_), channel_id=1, source_target_pairs={{0,8},{4,12},{8,0},{12,4},{16,24},{20,28},{24,16},{28,20},{1,9},{5... | collective-permute-start | bytes 294920 | tf_op jit(solution)/shard_map/ppermute | solution.py:297
  46.4 6.6 %collective-permute-start.18 = (bf16[192,256]{1,0:T(8,128)(2,1)S(1)}, bf16[192,256]{1,0:T(8,128)(2,1)S(1)}, u32[]{:S(2)}, u32[]{:S(2)}) collective-permute-start(bf16[192,256]{1,0:T(8,128)(2,1)S(1)} %gate.9), channel_id=1, source_target_pairs={{0,4},{4,0},{8,12},{12,8},{16,20},{20,16},{24,28},{28,24},{1,5},{5... | collective-permute-start | bytes 294920 | tf_op jit(solution)/shard_map/ppermute | solution.py:297
  47.7 5.4 %collective-permute-start.19 = (bf16[192,256]{1,0:T(8,128)(2,1)S(1)}, bf16[192,256]{1,0:T(8,128)(2,1)S(1)}, u32[]{:S(2)}, u32[]{:S(2)}) collective-permute-start(bf16[192,256]{1,0:T(8,128)(2,1)S(1)} %add.6), channel_id=1, source_target_pairs={{0,8},{4,12},{8,0},{12,4},{16,24},{20,28},{24,16},{28,20},{1,9},{5... | collective-permute-start | bytes 294920 | tf_op jit(solution)/shard_map/ppermute | solution.py:297
  50.7 6.5 %collective-permute-start.16 = (bf16[96,256]{1,0:T(8,128)(2,1)S(1)}, bf16[96,256]{1,0:T(8,128)(2,1)S(1)}, u32[]{:S(2)}, u32[]{:S(2)}) collective-permute-start(bf16[96,256]{1,0:T(8,128)(2,1)S(1)} %add.5), channel_id=1, source_target_pairs={{0,16},{4,20},{8,24},{12,28},{16,0},{20,4},{24,8},{28,12},{1,17},{... | collective-permute-start | bytes 147464 | tf_op jit(solution)/shard_map/ppermute | solution.py:297
  53.1 5.6 %collective-permute-start.20 = (bf16[96,256]{1,0:T(8,128)(2,1)S(1)}, bf16[96,256]{1,0:T(8,128)(2,1)S(1)}, u32[]{:S(2)}, u32[]{:S(2)}) collective-permute-start(bf16[96,256]{1,0:T(8,128)(2,1)S(1)} %add.7), channel_id=1, source_target_pairs={{0,16},{4,20},{8,24},{12,28},{16,0},{20,4},{24,8},{28,12},{1,17},{... | collective-permute-start | bytes 147464 | tf_op jit(solution)/shard_map/ppermute | solution.py:297

commit v13 on v10

--- a/solution.py
+++ b/solution.py
@@ -17,6 +17,8 @@
 LOG2E = 1.4426950408889634
 DEAD = 1024.0
 HIDDEN = 2.0**96
+PAIR = 2
+PART = 48
 
 
 def nt(a, b):
@@ -127,7 +129,7 @@
     kv_pieces, blocks, refs = refs[:heads], refs[heads : heads + shards], refs[heads + shards :]
     qo_pieces = refs[: heads - 1]
     (
-        p_ref, ds_ref, own_p_ref, own_ds_ref, qs_ref, os_ref, kt_ref, far_ref,
+        p_ref, ds_ref, own_p_ref, own_ds_ref, qs_ref, os_ref, key_ref, far_ref,
         kx, vx, mine, s_ref, g_ref, sems,
     ) = refs[-14:]
     rows = q_ref.shape[0]
@@ -159,36 +161,50 @@
             extra = jnp.where(hide & (lane >= SLOT_DEV), -HIDDEN, 0.0)
         kx[at, 0:HD] = jnp.where(key > 100.0, 0.0, key).astype(jnp.bfloat16)
         kx[at, HD : 2 * HD] = extra.astype(jnp.bfloat16)
-    kx[slots : slots + rows, HD : 2 * HD] = jnp.zeros((rows, HD), jnp.bfloat16)
+    kx[slots:, HD : 2 * HD] = jnp.zeros((PAIR * rows, HD), jnp.bfloat16)
 
     width = GROUP * rows
-    eye_row = lax.broadcasted_iota(jnp.int32, (rows, width), 0)
-    eye_lane = lax.broadcasted_iota(jnp.int32, (rows, width), 1)
-    eye = eye_row == lax.rem(eye_lane, rows)
+    span = PAIR * width
+    eye_row = lax.broadcasted_iota(jnp.int32, (PAIR * rows, span), 0)
+    eye_lane = lax.broadcasted_iota(jnp.int32, (PAIR * rows, span), 1)
+    eye = (eye_row // rows == eye_lane // width) & (eye_row % rows == eye_lane % rows)
     factor = SCALE * LOG2E
 
-    for m in list(range(1, heads)) + [0]:
-        if m == 0:
+    turns = list(range(1, heads)) + [0]
+    for turn in range(0, heads, PAIR):
+        pair = turns[turn : turn + PAIR]
+        if 0 in pair:
             wait_copies(copies)
-        qo, part = (qo_pieces[m - 1], g) if m else (mine, 0)
-        span = slice(part * rows, (part + 1) * rows)
-        at = pl.ds(pl.multiple_of(lax.bitwise_xor(me, m) * rows, 16), rows)
-        chunk = slice(m * width, (m + 1) * width)
-        kx[slots : slots + rows, 0:HD] = kv_pieces[m][:, key_at]
-        vx[slots : slots + rows, :] = kv_pieces[m][:, value_at]
-        q2 = jnp.concatenate([qo[span, h * HD : (h + 1) * HD] for h in range(GROUP)], axis=0)
-        o2 = jnp.concatenate(
-            [qo[span, GW + h * HD : GW + (h + 1) * HD] for h in range(GROUP)], axis=0
+        queries = []
+        cotangents = []
+        hides = []
+        for i, m in enumerate(pair):
+            qo, part = (qo_pieces[m - 1], g) if m else (mine, 0)
+            at = slice(part * rows, (part + 1) * rows)
+            here = slice(slots + i * rows, slots + (i + 1) * rows)
+            kx[here, 0:HD] = kv_pieces[m][:, key_at]
+            vx[here, :] = kv_pieces[m][:, value_at]
+            q2 = jnp.concatenate([qo[at, h * HD : (h + 1) * HD] for h in range(GROUP)], axis=0)
+            o2 = jnp.concatenate(
+                [qo[at, GW + h * HD : GW + (h + 1) * HD] for h in range(GROUP)], axis=0
+            )
+            chunk = slice(m * width, (m + 1) * width)
+            qs_ref[chunk, :] = q2
+            os_ref[chunk, :] = o2
+            queries.append(q2)
+            cotangents.append(o2)
+            tokens_at = pl.ds(pl.multiple_of(lax.bitwise_xor(me, m) * rows, 16), rows)
+            hides += [hide_ref[g, tokens_at, :]] * GROUP
+        qx = jnp.concatenate(
+            [jnp.concatenate(queries, axis=0), jnp.concatenate(hides, axis=0)], axis=1
         )
-        qs_ref[chunk, :] = q2
-        os_ref[chunk, :] = o2
-        qx = jnp.concatenate([q2, jnp.concatenate([hide_ref[g, at, :]] * GROUP, axis=0)], axis=1)
-        s_at, g_at = s_ref.at[m % 2], g_ref.at[m % 2]
+        held = turn // PAIR % s_ref.shape[0]
+        s_at, g_at = s_ref.at[held], g_ref.at[held]
         s_at[...] = nt(kx[...], qx)
-        g_at[...] = nt(vx[...], o2)
+        g_at[...] = nt(vx[...], jnp.concatenate(cotangents, axis=0))
         own_score = jnp.sum(jnp.where(eye, s_at[slots:, :], 0.0), axis=0, keepdims=True)
         own_grad_prob = jnp.sum(jnp.where(eye, g_at[slots:, :], 0.0), axis=0, keepdims=True)
-        parts = [slice(r * SLOT_DEV, (r + 1) * SLOT_DEV) for r in range(shards)]
+        parts = [slice(r, r + PART) for r in range(0, slots, PART)]
         top = folded(functools.reduce(jnp.maximum, [s_at[part, :] for part in parts]), jnp.max)
         top = jnp.maximum(jnp.max(top, axis=0, keepdims=True), own_score)
         total = 0.0
@@ -205,15 +221,22 @@
         log_total = jnp.log2(total)
         for part in parts:
             probs = jnp.exp2((s_at[part, :] - top) * factor - log_total)
-            p_ref[part, chunk] = probs.astype(jnp.bfloat16)
-            ds_ref[part, chunk] = (probs * (g_at[part, :] - delta)).astype(jnp.bfloat16)
+            low_probs = probs.astype(jnp.bfloat16)
+            low_grads = (probs * (g_at[part, :] - delta)).astype(jnp.bfloat16)
+            for i, m in enumerate(pair):
+                p_ref[part, m * width : (m + 1) * width] = low_probs[:, i * width : (i + 1) * width]
+                ds_ref[part, m * width : (m + 1) * width] = low_grads[:, i * width : (i + 1) * width]
         own_grad_score = own_prob * (own_grad_prob - delta)
-        own_p_ref[:, chunk] = jnp.where(eye, own_prob, 0.0).astype(jnp.bfloat16)
-        own_ds_ref[:, chunk] = jnp.where(eye, own_grad_score, 0.0).astype(jnp.bfloat16)
+        for i, m in enumerate(pair):
+            chunk = slice(m * width, (m + 1) * width)
+            here = slice(i * width, (i + 1) * width)
+            one = eye[0:rows, 0:width]
+            own_p_ref[:, chunk] = jnp.where(one, own_prob[:, here], 0.0).astype(jnp.bfloat16)
+            own_ds_ref[:, chunk] = jnp.where(one, own_grad_score[:, here], 0.0).astype(jnp.bfloat16)
     far = slice(slots // 2, slots)
     far_ref[:, 0:HD] = (SCALE * nn(ds_ref[far, :], qs_ref[...])).astype(far_ref.dtype)
     far_ref[:, HD : 2 * HD] = nn(p_ref[far, :], os_ref[...]).astype(far_ref.dtype)
-    kt_ref[...] = kx[0:slots, 0:HD].astype(jnp.float32).T.astype(jnp.bfloat16)
+    key_ref[...] = kx[0:slots, 0:HD]
 
 
 def terms_kernel(heads, p_ref, ds_ref, own_p_ref, own_ds_ref, qs_ref, os_ref, after_ref, near_ref, own_ref):
@@ -234,14 +257,15 @@
     kv_pieces, refs, dq_ref = refs[:heads], refs[heads:-1], refs[-1]
     me = place()[1]
     for g in range(len(refs) // 3):
-        ds_ref, own_ds_ref, kt_ref = refs[3 * g : 3 * g + 3]
+        ds_ref, own_ds_ref, key_ref = refs[3 * g : 3 * g + 3]
+        turned = key_ref[...].astype(jnp.float32).T.astype(jnp.bfloat16)
         rows = own_ds_ref.shape[0]
         width = GROUP * rows
         for m in range(heads):
             at = pl.ds(pl.multiple_of(lax.bitwise_xor(me, m) * rows, 16), rows)
             chunk = slice(m * width, (m + 1) * width)
             own_key = kv_pieces[m][:, g * HD : (g + 1) * HD]
-            dq = nn(kt_ref[...], ds_ref[:, chunk]) + tn(own_key, own_ds_ref[:, chunk])
+            dq = nn(turned, ds_ref[:, chunk]) + tn(own_key, own_ds_ref[:, chunk])
             dq = (SCALE * dq).T.astype(jnp.bfloat16)
             for h in range(GROUP):
                 column = (g * GROUP + h) * HD
@@ -384,6 +408,7 @@
 
     all_rows = tokens * GROUP
     saved = []
+    buffers = 2 if slots <= 1024 else 1
     for g in range(kv_heads):
         outs = pl.pallas_call(
             functools.partial(attend_kernel, g, order),
@@ -394,17 +419,17 @@
                 shape(rows, all_rows),
                 shape(all_rows, HD),
                 shape(all_rows, HD),
-                shape(HD, slots),
+                shape(slots, HD),
                 shape(half, 2 * HD),
             ],
             in_specs=anywhere(2) + in_vmem(heads + heads + shards) + anywhere(g > 0),
             out_specs=in_vmem(8),
             scratch_shapes=[
-                pltpu.VMEM((slots + rows, 2 * HD), jnp.bfloat16),
-                pltpu.VMEM((slots + rows, HD), jnp.bfloat16),
+                pltpu.VMEM((slots + PAIR * rows, 2 * HD), jnp.bfloat16),
+                pltpu.VMEM((slots + PAIR * rows, HD), jnp.bfloat16),
                 pltpu.VMEM((rows, 2 * GW), jnp.bfloat16),
-                pltpu.VMEM((2, slots + rows, GROUP * rows), jnp.float32),
-                pltpu.VMEM((2, slots + rows, GROUP * rows), jnp.float32),
+                pltpu.VMEM((buffers, slots + PAIR * rows, PAIR * GROUP * rows), jnp.float32),
+                pltpu.VMEM((buffers, slots + PAIR * rows, PAIR * GROUP * rows), jnp.float32),
                 pltpu.SemaphoreType.DMA((2,)),
             ],
             compiler_params=params(24),

time: 59.4 us -> 59.4 us (level)
  no operation moved by 1% of the time
where the time goes in v13:
time: 59.4 us; the launch traced here: 59.2 us
  waiting for transfers between devices  20.5 us (35%)
  starting transfers between devices  18.9 us (32%)
  Pallas kernels  15 us (25%)
  local copies, waits for them, and re-layouts  4.06 us (7%)
  between operations  0.78 us (1%)
    ppermute x20, waiting for transfers between devices, swap(): return lax.ppermute(x, axis, [(i, i ^ m) for i in range(size)])  20.5 us
    ppermute x20, starting transfers between devices, swap(): return lax.ppermute(x, axis, [(i, i ^ m) for i in range(size)])  18.9 us
    pallas_call x2, Pallas kernels, local(): pl.pallas_call(functools.partial(attend_kernel, g, order), out_shape=[sha...  9.17 us
    unnamed x14, local copies, waits for them, and re-layouts  4.06 us
    pallas_call x1, Pallas kernels, local(): pl.pallas_call(functools.partial(queries_kernel, heads), out_shape=shape(...  2.2 us
    pallas_call x2, Pallas kernels, local(): pl.pallas_call(functools.partial(terms_kernel, heads), out_shape=[shape(h...  1.8 us
  transfers between devices with their start and end apart: 20, of which 10 were waited for; matrix products, arithmetic and copies ran while one was open for 0% of the time, Pallas kernels for 16%

profile of v13, /device:TPU:0, one launch (start us, length us, event | category | flops | bytes accessed | tf_op | source)
XLA Modules:
  0.0 59.2 jit_solution(12355117554009668912)
XLA Ops:
  0.6 0.9 %copy-done.4 = bf16[48,1024]{1,0:T(8,128)(2,1)S(1)} copy-done((bf16[48,1024]{1,0:T(8,128)(2,1)S(1)}, bf16[48,1024]{1,0:T(8,128)(2,1)}, u32[]{:S(2)}) %copy-start.4) | copy-done | bytes 98328
  1.5 0.9 %copy-done.5 = bf16[48,1024]{1,0:T(8,128)(2,1)S(1)} copy-done((bf16[48,1024]{1,0:T(8,128)(2,1)S(1)}, bf16[48,1024]{1,0:T(8,128)(2,1)}, u32[]{:S(2)}) %copy-start.5) | copy-done | bytes 98328
  2.4 0.5 collective-permute-start
  3.0 2.6 %collective-permute-start.1 = (bf16[48,512]{1,0:T(8,128)(2,1)S(1)}, bf16[48,512]{1,0:T(8,128)(2,1)S(1)}, u32[]{:S(2)}, u32[]{:S(2)}) collective-permute-start(bf16[48,512]{1,0:T(8,128)(2,1)S(1)} %get-tuple-element.44), channel_id=1, source_target_pairs={{0,2},{1,3},{2,0},{3,1},{4,6},{5,7},{6,4},{7,5},{8,10},{9,11},{10,... | collective-permute-start | bytes 147464 | tf_op jit(solution)/shard_map/ppermute | solution.py:318
  5.6 1.1 %copy-done = bf16[48,8192]{1,0:T(8,128)(2,1)S(1)} copy-done((bf16[48,8192]{1,0:T(8,128)(2,1)S(1)}, bf16[48,8192]{1,0:T(8,128)(2,1)}, u32[]{:S(2)}) %copy-start) | copy-done | bytes 786456
  6.7 1.1 %copy-done.2 = bf16[48,8192]{1,0:T(8,128)(2,1)S(1)} copy-done((bf16[48,8192]{1,0:T(8,128)(2,1)S(1)}, bf16[48,8192]{1,0:T(8,128)(2,1)}, u32[]{:S(2)}) %copy-start.2) | copy-done | bytes 786456
  8.3 0.9 %collective-permute-done.2.refs_3_ = bf16[48,512]{1,0:T(8,128)(2,1)S(1)} collective-permute-done((bf16[48,512]{1,0:T(8,128)(2,1)S(1)}, bf16[48,512]{1,0:T(8,128)(2,1)S(1)}, u32[]{:S(2)}, u32[]{:S(2)}) %collective-permute-start.2) | collective-permute-done | bytes 49184 | tf_op jit(solution)/shard_map/ppermute | solution.py:318
  9.4 1.1 %collective-permute-start.10 = (bf16[96,2048]{1,0:T(8,128)(2,1)S(1)}, bf16[96,2048]{1,0:T(8,128)(2,1)S(1)}, u32[]{:S(2)}, u32[]{:S(2)}) collective-permute-start(bf16[96,2048]{1,0:T(8,128)(2,1)S(1)} %gate.4), channel_id=1, source_target_pairs={{0,2},{1,3},{2,0},{3,1},{4,6},{5,7},{6,4},{7,5},{8,10},{9,11},{10,... | collective-permute-start | bytes 1179656 | tf_op jit(solution)/shard_map/ppermute | solution.py:318
  10.8 1.6 %collective-permute-start.4 = (bf16[96,512]{1,0:T(8,128)(2,1)S(1)}, bf16[96,512]{1,0:T(8,128)(2,1)S(1)}, u32[]{:S(2)}, u32[]{:S(2)}) collective-permute-start(bf16[96,512]{1,0:T(8,128)(2,1)S(1)} %get-tuple-element.47.refs_4_), channel_id=1, source_target_pairs={{0,8},{4,12},{8,0},{12,4},{16,24},{20,28},{24,16},{28,20},{1,9},{5... | collective-permute-start | bytes 294920 | tf_op jit(solution)/shard_map/ppermute | solution.py:318
  12.4 2.6 %collective-permute-start.3 = (bf16[96,512]{1,0:T(8,128)(2,1)S(1)}, bf16[96,512]{1,0:T(8,128)(2,1)S(1)}, u32[]{:S(2)}, u32[]{:S(2)}) collective-permute-start(bf16[96,512]{1,0:T(8,128)(2,1)S(1)} %get-tuple-element.47.refs_4_), channel_id=1, source_target_pairs={{0,16},{4,20},{8,24},{12,28},{16,0},{20,4},{24,8},{28,12},{1,17},{... | collective-permute-start | bytes 294920 | tf_op jit(solution)/shard_map/ppermute | solution.py:318
  15.0 1.5 %collective-permute-start.6 = (bf16[96,512]{1,0:T(8,128)(2,1)S(1)}, bf16[96,512]{1,0:T(8,128)(2,1)S(1)}, u32[]{:S(2)}, u32[]{:S(2)}) collective-permute-start(bf16[96,512]{1,0:T(8,128)(2,1)S(1)} %get-tuple-element.47.refs_4_), channel_id=1, source_target_pairs={{0,4},{4,0},{8,12},{12,8},{16,20},{20,16},{24,28},{28,24},{1,5},{5... | collective-permute-start | bytes 294920 | tf_op jit(solution)/shard_map/ppermute | solution.py:318
  16.5 0.5 collective-permute-start.8
  17.0 2.8 %collective-permute-done.3.refs_4_.refs_5_ = bf16[96,512]{1,0:T(8,128)(2,1)S(1)} collective-permute-done((bf16[96,512]{1,0:T(8,128)(2,1)S(1)}, bf16[96,512]{1,0:T(8,128)(2,1)S(1)}, u32[]{:S(2)}, u32[]{:S(2)}) %collective-permute-start.3) | collective-permute-done | bytes 98336 | tf_op jit(solution)/shard_map/ppermute | solution.py:318
  19.8 1.5 %collective-permute-start.7 = (bf16[96,512]{1,0:T(8,128)(2,1)S(1)}, bf16[96,512]{1,0:T(8,128)(2,1)S(1)}, u32[]{:S(2)}, u32[]{:S(2)}) collective-permute-start(bf16[96,512]{1,0:T(8,128)(2,1)S(1)} %collective-permute-done.3.refs_4_.refs_5_), channel_id=1, source_target_pairs={{0,4},{4,0},{8,12},{12,8},{16,20},{20,16},{24,28},{28,24},{1,5},{5... | collective-permute-start | bytes 294920 | tf_op jit(solution)/shard_map/ppermute | solution.py:318
  21.8 1.0 %collective-permute-start.13 = (bf16[96,2048]{1,0:T(8,128)(2,1)S(1)}, bf16[96,2048]{1,0:T(8,128)(2,1)S(1)}, u32[]{:S(2)}, u32[]{:S(2)}) collective-permute-start(bf16[96,2048]{1,0:T(8,128)(2,1)S(1)} %collective-permute-done.12), channel_id=1, source_target_pairs={{0,2},{1,3},{2,0},{3,1},{4,6},{5,7},{6,4},{7,5},{8,10},{9,11},{10,... | collective-permute-start | bytes 1179656 | tf_op jit(solution)/shard_map/ppermute | solution.py:318
  22.8 1.6 %collective-permute-done.7.refs_5_.refs_9_ = bf16[96,512]{1,0:T(8,128)(2,1)S(1)} collective-permute-done((bf16[96,512]{1,0:T(8,128)(2,1)S(1)}, bf16[96,512]{1,0:T(8,128)(2,1)S(1)}, u32[]{:S(2)}, u32[]{:S(2)}) %collective-permute-start.7) | collective-permute-done | bytes 98336 | tf_op jit(solution)/shard_map/ppermute | solution.py:318
  24.4 1.5 %collective-permute-done.5.refs_6_.refs_7_ = bf16[96,512]{1,0:T(8,128)(2,1)S(1)} collective-permute-done((bf16[96,512]{1,0:T(8,128)(2,1)S(1)}, bf16[96,512]{1,0:T(8,128)(2,1)S(1)}, u32[]{:S(2)}, u32[]{:S(2)}) %collective-permute-start.5) | collective-permute-done | bytes 98336 | tf_op jit(solution)/shard_map/ppermute | solution.py:318
  26.0 0.9 %collective-permute-start.9 = (bf16[96,512]{1,0:T(8,128)(2,1)S(1)}, bf16[96,512]{1,0:T(8,128)(2,1)S(1)}, u32[]{:S(2)}, u32[]{:S(2)}) collective-permute-start(bf16[96,512]{1,0:T(8,128)(2,1)S(1)} %collective-permute-done.5.refs_6_.refs_7_), channel_id=1, source_target_pairs={{0,4},{4,0},{8,12},{12,8},{16,20},{20,16},{24,28},{28,24},{1,5},{5... | collective-permute-start | bytes 294920 | tf_op jit(solution)/shard_map/ppermute | solution.py:318
  26.9 4.3 %collective-permute-done.13.refs_0_ = bf16[96,2048]{1,0:T(8,128)(2,1)S(1)} collective-permute-done((bf16[96,2048]{1,0:T(8,128)(2,1)S(1)}, bf16[96,2048]{1,0:T(8,128)(2,1)S(1)}, u32[]{:S(2)}, u32[]{:S(2)}) %collective-permute-start.13) | collective-permute-done | bytes 393248 | tf_op jit(solution)/shard_map/ppermute | solution.py:318
  31.3 4.5 %attend.2 = (bf16[768,1536]{1,0:T(8,128)(2,1)S(1)}, bf16[768,1536]{1,0:T(8,128)(2,1)S(1)}, bf16[48,1536]{1,0:T(8,128)(2,1)S(1)}, bf16[48,1536]{1,0:T(8,128)(2,1)...) custom-call(bf16[48,8192]{1,0:T(8,128)(2,1)S(1)} %copy-done.1, ...), custom_call_target="tpu_custom_call" | custom-call | flops 962592768 | bytes 8388608 | tf_op jit(solution)/shard_map/attend/pallas_call | solution.py:413
  35.8 0.9 %collective-permute-start.14 = (bf16[384,256]{1,0:T(8,128)(2,1)S(1)}, bf16[384,256]{1,0:T(8,128)(2,1)S(1)}, u32[]{:S(2)}, u32[]{:S(2)}) collective-permute-start(bf16[384,256]{1,0:T(8,128)(2,1)S(1)} %get-tuple-element.63), channel_id=1, source_target_pairs={{0,4},{4,0},{8,12},{12,8},{16,20},{20,16},{24,28},{28,24},{1,5},{5... | collective-permute-start | bytes 589832 | tf_op jit(solution)/shard_map/ppermute | solution.py:318
  36.7 4.7 %attend.3 = (bf16[768,1536]{1,0:T(8,128)(2,1)S(1)}, bf16[768,1536]{1,0:T(8,128)(2,1)S(1)}, bf16[48,1536]{1,0:T(8,128)(2,1)S(1)}, bf16[48,1536]{1,0:T(8,128)(2,1)...) custom-call(bf16[48,8192]{1,0:T(8,128)(2,1)S(1)} %copy-done.1, ...), custom_call_target="tpu_custom_call" | custom-call | flops 962592768 | bytes 8388608 | tf_op jit(solution)/shard_map/attend/pallas_call | solution.py:413
  41.3 1.3 %collective-permute-start.17 = (bf16[384,256]{1,0:T(8,128)(2,1)S(1)}, bf16[384,256]{1,0:T(8,128)(2,1)S(1)}, u32[]{:S(2)}, u32[]{:S(2)}) collective-permute-start(bf16[384,256]{1,0:T(8,128)(2,1)S(1)} %get-tuple-element.73), channel_id=1, source_target_pairs={{0,4},{4,0},{8,12},{12,8},{16,20},{20,16},{24,28},{28,24},{1,5},{5... | collective-permute-start | bytes 589832 | tf_op jit(solution)/shard_map/ppermute | solution.py:318
  42.6 0.9 %terms.2 = (f32[384,256]{1,0:T(8,128)S(1)}, f32[192,256]{1,0:T(8,128)S(1)}) custom-call(bf16[768,1536]{1,0:T(8,128)(2,1)S(1)} %get-tuple-element.58.p_ref, bf16[768,1536]{1,0:T(8,128)(2,1)S(1)} %get-tuple-element.51.refs_4_.ds_ref, bf16[48,1536]{1,0:T(8,128)(2,1)S(1)} %get-tuple-element.54.refs_15_.own_p_ref, ...), custom_call_target="tpu_custom_call" | custom-call | flops 301989888 | bytes 1048576 | tf_op jit(solution)/shard_map/terms/pallas_call | solution.py:456
  43.5 0.9 %terms.3 = (f32[384,256]{1,0:T(8,128)S(1)}, f32[192,256]{1,0:T(8,128)S(1)}) custom-call(bf16[768,1536]{1,0:T(8,128)(2,1)S(1)} %get-tuple-element.69.p_ref, bf16[768,1536]{1,0:T(8,128)(2,1)S(1)} %get-tuple-element.55.refs_7_.ds_ref, bf16[48,1536]{1,0:T(8,128)(2,1)S(1)} %get-tuple-element.61.after_ref.own_p_ref, ...), custom_call_target="tpu_custom_call" | custom-call | flops 301989888 | bytes 1048576 | tf_op jit(solution)/shard_map/terms/pallas_call | solution.py:456
  44.9 2.7 %collective-permute-done.17.far_ref = bf16[384,256]{1,0:T(8,128)(2,1)S(1)} collective-permute-done((bf16[384,256]{1,0:T(8,128)(2,1)S(1)}, bf16[384,256]{1,0:T(8,128)(2,1)S(1)}, u32[]{:S(2)}, u32[]{:S(2)}) %collective-permute-start.17) | collective-permute-done | bytes 196640 | tf_op jit(solution)/shard_map/ppermute | solution.py:318
  47.8 1.8 %collective-permute-done.15.far_ref = bf16[192,256]{1,0:T(8,128)(2,1)S(1)} collective-permute-done((bf16[192,256]{1,0:T(8,128)(2,1)S(1)}, bf16[192,256]{1,0:T(8,128)(2,1)S(1)}, u32[]{:S(2)}, u32[]{:S(2)}) %collective-permute-start.15) | collective-permute-done | bytes 98336 | tf_op jit(solution)/shard_map/ppermute | solution.py:318
  49.7 1.2 %collective-permute-start.16 = (bf16[96,256]{1,0:T(8,128)(2,1)S(1)}, bf16[96,256]{1,0:T(8,128)(2,1)S(1)}, u32[]{:S(2)}, u32[]{:S(2)}) collective-permute-start(bf16[96,256]{1,0:T(8,128)(2,1)S(1)} %get-tuple-element.67), channel_id=1, source_target_pairs={{0,16},{4,20},{8,24},{12,28},{16,0},{20,4},{24,8},{28,12},{1,17},{... | collective-permute-start | bytes 147464 | tf_op jit(solution)/shard_map/ppermute | solution.py:318
  50.9 1.9 %collective-permute-done.18.far_ref = bf16[192,256]{1,0:T(8,128)(2,1)S(1)} collective-permute-done((bf16[192,256]{1,0:T(8,128)(2,1)S(1)}, bf16[192,256]{1,0:T(8,128)(2,1)S(1)}, u32[]{:S(2)}, u32[]{:S(2)}) %collective-permute-start.18) | collective-permute-done | bytes 98336 | tf_op jit(solution)/shard_map/ppermute | solution.py:318
  53.1 2.2 %queries.1 = bf16[192,2048]{1,0:T(8,128)(2,1)} custom-call(bf16[48,512]{1,0:T(8,128)(2,1)S(1)} %get-tuple-element.42.refs_0_.refs_2_, bf16[48,512]{1,0:T(8,128)(2,1)S(1)} %collective-permute-done.refs_1_, bf16[48,512]{1,0:T(8,128)(2,1)S(1)} %collective-permute-done.1.refs_2_, bf16[48,512]{1,0:T(8,128)(2,1)S(1)} %collective-permute-done.2.refs_3_, ...), custom_call_target="tpu_custom_call" | custom-call | flops 603979776 | bytes 1048576 | tf_op jit(solution)/shard_map/queries/pallas_call | solution.py:472
  55.6 2.5 %collective-permute-done.19.refs_4_ = bf16[96,256]{1,0:T(8,128)(2,1)S(1)} collective-permute-done((bf16[96,256]{1,0:T(8,128)(2,1)S(1)}, bf16[96,256]{1,0:T(8,128)(2,1)S(1)}, u32[]{:S(2)}, u32[]{:S(2)}) %collective-permute-start.19) | collective-permute-done | bytes 49184 | tf_op jit(solution)/shard_map/ppermute | solution.py:318
  58.2 1.0 %spread.1 = (bf16[192,256]{1,0:T(8,128)(2,1)}, bf16[192,256]{1,0:T(8,128)(2,1)}) custom-call(s32[2,192]{1,0:T(2,128)S(1)} %copy-done.6, f32[96,256]{1,0:T(8,128)S(1)} %get-tuple-element.66.refs_0_, bf16[96,256]{1,0:T(8,128)(2,1)S(1)} %collective-permute-done.16.refs_1_, f32[192,256]{1,0:T(8,128)S(1)} %get-tuple-element.68.refs_2_, ...), custom_call_target="tpu_custom_call" | custom-call | tf_op jit(solution)/shard_map/spread/pallas_call | solution.py:501
  (39 shorter events, 2.7 us)
Async XLA Ops:
  0.6 0.9 %copy-start.4 = (bf16[48,1024]{1,0:T(8,128)(2,1)S(1)}, bf16[48,1024]{1,0:T(8,128)(2,1)}, u32[]{:S(2)}) copy-start(bf16[48,1024]{1,0:T(8,128)(2,1)} %key_ref.1) | copy-start | bytes 294916
  1.5 0.9 %copy-start.5 = (bf16[48,1024]{1,0:T(8,128)(2,1)S(1)}, bf16[48,1024]{1,0:T(8,128)(2,1)}, u32[]{:S(2)}) copy-start(bf16[48,1024]{1,0:T(8,128)(2,1)} %value_ref.1) | copy-start | bytes 294916
  2.4 8.1 %copy-start.6 = (s32[2,192]{1,0:T(2,128)S(1)}, s32[2,192]{1,0:T(2,128)}, u32[]{:S(2)}) copy-start(s32[2,192]{1,0:T(2,128)} %seg_ref.3) | copy-start | bytes 4612
  2.4 5.8 %collective-permute-start = (bf16[48,512]{1,0:T(8,128)(2,1)S(1)}, bf16[48,512]{1,0:T(8,128)(2,1)S(1)}, u32[]{:S(2)}, u32[]{:S(2)}) collective-permute-start(bf16[48,512]{1,0:T(8,128)(2,1)S(1)} %get-tuple-element.43), channel_id=1, source_target_pairs={{0,1},{1,0},{2,3},{3,2},{4,5},{5,4},{6,7},{7,6},{8,9},{9,8},{10,11... | collective-permute-start | bytes 147464 | tf_op jit(solution)/shard_map/ppermute | solution.py:318
  3.0 5.3 %collective-permute-start.1 = (bf16[48,512]{1,0:T(8,128)(2,1)S(1)}, bf16[48,512]{1,0:T(8,128)(2,1)S(1)}, u32[]{:S(2)}, u32[]{:S(2)}) collective-permute-start(bf16[48,512]{1,0:T(8,128)(2,1)S(1)} %get-tuple-element.44), channel_id=1, source_target_pairs={{0,2},{1,3},{2,0},{3,1},{4,6},{5,7},{6,4},{7,5},{8,10},{9,11},{10,... | collective-permute-start | bytes 147464 | tf_op jit(solution)/shard_map/ppermute | solution.py:318
  5.5 3.7 %collective-permute-start.2 = (bf16[48,512]{1,0:T(8,128)(2,1)S(1)}, bf16[48,512]{1,0:T(8,128)(2,1)S(1)}, u32[]{:S(2)}, u32[]{:S(2)}) collective-permute-start(bf16[48,512]{1,0:T(8,128)(2,1)S(1)} %get-tuple-element.45), channel_id=1, source_target_pairs={{0,3},{1,2},{2,1},{3,0},{4,7},{5,6},{6,5},{7,4},{8,11},{9,10},{10,... | collective-permute-start | bytes 147464 | tf_op jit(solution)/shard_map/ppermute | solution.py:318
  5.6 1.1 %copy-start = (bf16[48,8192]{1,0:T(8,128)(2,1)S(1)}, bf16[48,8192]{1,0:T(8,128)(2,1)}, u32[]{:S(2)}) copy-start(bf16[48,8192]{1,0:T(8,128)(2,1)} %q_ref.3) | copy-start | bytes 2359300
  6.7 1.1 %copy-start.2 = (bf16[48,8192]{1,0:T(8,128)(2,1)S(1)}, bf16[48,8192]{1,0:T(8,128)(2,1)}, u32[]{:S(2)}) copy-start(bf16[48,8192]{1,0:T(8,128)(2,1)} %o_ref.3) | copy-start | bytes 2359300
  8.3 23.0 %copy-start.1 = (bf16[48,8192]{1,0:T(8,128)(2,1)S(1)}, bf16[48,8192]{1,0:T(8,128)(2,1)}, u32[]{:S(2)}) copy-start(bf16[48,8192]{1,0:T(8,128)(2,1)} %q_ref.3) | copy-start | bytes 2359300
  8.3 23.0 %copy-start.3 = (bf16[48,8192]{1,0:T(8,128)(2,1)S(1)}, bf16[48,8192]{1,0:T(8,128)(2,1)}, u32[]{:S(2)}) copy-start(bf16[48,8192]{1,0:T(8,128)(2,1)} %o_ref.3) | copy-start | bytes 2359300
  9.2 12.6 %collective-permute-start.12 = (bf16[96,2048]{1,0:T(8,128)(2,1)S(1)}, bf16[96,2048]{1,0:T(8,128)(2,1)S(1)}, u32[]{:S(2)}, u32[]{:S(2)}) collective-permute-start(bf16[96,2048]{1,0:T(8,128)(2,1)S(1)} %gate.6), channel_id=1, source_target_pairs={{0,1},{1,0},{2,3},{3,2},{4,5},{5,4},{6,7},{7,6},{8,9},{9,8},{10,11... | collective-permute-start | bytes 1179656 | tf_op jit(solution)/shard_map/ppermute | solution.py:318
  9.4 16.6 %collective-permute-start.10 = (bf16[96,2048]{1,0:T(8,128)(2,1)S(1)}, bf16[96,2048]{1,0:T(8,128)(2,1)S(1)}, u32[]{:S(2)}, u32[]{:S(2)}) collective-permute-start(bf16[96,2048]{1,0:T(8,128)(2,1)S(1)} %gate.4), channel_id=1, source_target_pairs={{0,2},{1,3},{2,0},{3,1},{4,6},{5,7},{6,4},{7,5},{8,10},{9,11},{10,... | collective-permute-start | bytes 1179656 | tf_op jit(solution)/shard_map/ppermute | solution.py:318
  10.8 5.7 %collective-permute-start.4 = (bf16[96,512]{1,0:T(8,128)(2,1)S(1)}, bf16[96,512]{1,0:T(8,128)(2,1)S(1)}, u32[]{:S(2)}, u32[]{:S(2)}) collective-permute-start(bf16[96,512]{1,0:T(8,128)(2,1)S(1)} %get-tuple-element.47.refs_4_), channel_id=1, source_target_pairs={{0,8},{4,12},{8,0},{12,4},{16,24},{20,28},{24,16},{28,20},{1,9},{5... | collective-permute-start | bytes 294920 | tf_op jit(solution)/shard_map/ppermute | solution.py:318
  12.4 7.4 %collective-permute-start.3 = (bf16[96,512]{1,0:T(8,128)(2,1)S(1)}, bf16[96,512]{1,0:T(8,128)(2,1)S(1)}, u32[]{:S(2)}, u32[]{:S(2)}) collective-permute-start(bf16[96,512]{1,0:T(8,128)(2,1)S(1)} %get-tuple-element.47.refs_4_), channel_id=1, source_target_pairs={{0,16},{4,20},{8,24},{12,28},{16,0},{20,4},{24,8},{28,12},{1,17},{... | collective-permute-start | bytes 294920 | tf_op jit(solution)/shard_map/ppermute | solution.py:318
  15.0 6.4 %collective-permute-start.6 = (bf16[96,512]{1,0:T(8,128)(2,1)S(1)}, bf16[96,512]{1,0:T(8,128)(2,1)S(1)}, u32[]{:S(2)}, u32[]{:S(2)}) collective-permute-start(bf16[96,512]{1,0:T(8,128)(2,1)S(1)} %get-tuple-element.47.refs_4_), channel_id=1, source_target_pairs={{0,4},{4,0},{8,12},{12,8},{16,20},{20,16},{24,28},{28,24},{1,5},{5... | collective-permute-start | bytes 294920 | tf_op jit(solution)/shard_map/ppermute | solution.py:318
  16.5 6.3 %collective-permute-start.8 = (bf16[96,512]{1,0:T(8,128)(2,1)S(1)}, bf16[96,512]{1,0:T(8,128)(2,1)S(1)}, u32[]{:S(2)}, u32[]{:S(2)}) collective-permute-start(bf16[96,512]{1,0:T(8,128)(2,1)S(1)} %collective-permute-done.4.refs_2_.refs_6_), channel_id=1, source_target_pairs={{0,4},{4,0},{8,12},{12,8},{16,20},{20,16},{24,28},{28,24},{1,5},{5... | collective-permute-start | bytes 294920 | tf_op jit(solution)/shard_map/ppermute | solution.py:318
  19.8 4.6 %collective-permute-start.7 = (bf16[96,512]{1,0:T(8,128)(2,1)S(1)}, bf16[96,512]{1,0:T(8,128)(2,1)S(1)}, u32[]{:S(2)}, u32[]{:S(2)}) collective-permute-start(bf16[96,512]{1,0:T(8,128)(2,1)S(1)} %collective-permute-done.3.refs_4_.refs_5_), channel_id=1, source_target_pairs={{0,4},{4,0},{8,12},{12,8},{16,20},{20,16},{24,28},{28,24},{1,5},{5... | collective-permute-start | bytes 294920 | tf_op jit(solution)/shard_map/ppermute | solution.py:318
  21.4 4.6 %collective-permute-start.5 = (bf16[96,512]{1,0:T(8,128)(2,1)S(1)}, bf16[96,512]{1,0:T(8,128)(2,1)S(1)}, u32[]{:S(2)}, u32[]{:S(2)}) collective-permute-start(bf16[96,512]{1,0:T(8,128)(2,1)S(1)} %collective-permute-done.3.refs_4_.refs_5_), channel_id=1, source_target_pairs={{0,8},{4,12},{8,0},{12,4},{16,24},{20,28},{24,16},{28,20},{1,9},{5... | collective-permute-start | bytes 294920 | tf_op jit(solution)/shard_map/ppermute | solution.py:318
  21.8 9.5 %collective-permute-start.13 = (bf16[96,2048]{1,0:T(8,128)(2,1)S(1)}, bf16[96,2048]{1,0:T(8,128)(2,1)S(1)}, u32[]{:S(2)}, u32[]{:S(2)}) collective-permute-start(bf16[96,2048]{1,0:T(8,128)(2,1)S(1)} %collective-permute-done.12), channel_id=1, source_target_pairs={{0,2},{1,3},{2,0},{3,1},{4,6},{5,7},{6,4},{7,5},{8,10},{9,11},{10,... | collective-permute-start | bytes 1179656 | tf_op jit(solution)/shard_map/ppermute | solution.py:318
  26.0 5.3 %collective-permute-start.11 = (bf16[96,2048]{1,0:T(8,128)(2,1)S(1)}, bf16[96,2048]{1,0:T(8,128)(2,1)S(1)}, u32[]{:S(2)}, u32[]{:S(2)}) collective-permute-start(bf16[96,2048]{1,0:T(8,128)(2,1)S(1)} %gate.5), channel_id=1, source_target_pairs={{0,1},{1,0},{2,3},{3,2},{4,5},{5,4},{6,7},{7,6},{8,9},{9,8},{10,11... | collective-permute-start | bytes 1179656 | tf_op jit(solution)/shard_map/ppermute | solution.py:318
  26.0 5.3 %collective-permute-start.9 = (bf16[96,512]{1,0:T(8,128)(2,1)S(1)}, bf16[96,512]{1,0:T(8,128)(2,1)S(1)}, u32[]{:S(2)}, u32[]{:S(2)}) collective-permute-start(bf16[96,512]{1,0:T(8,128)(2,1)S(1)} %collective-permute-done.5.refs_6_.refs_7_), channel_id=1, source_target_pairs={{0,4},{4,0},{8,12},{12,8},{16,20},{20,16},{24,28},{28,24},{1,5},{5... | collective-permute-start | bytes 294920 | tf_op jit(solution)/shard_map/ppermute | solution.py:318
  35.8 8.6 %collective-permute-start.14 = (bf16[384,256]{1,0:T(8,128)(2,1)S(1)}, bf16[384,256]{1,0:T(8,128)(2,1)S(1)}, u32[]{:S(2)}, u32[]{:S(2)}) collective-permute-start(bf16[384,256]{1,0:T(8,128)(2,1)S(1)} %get-tuple-element.63), channel_id=1, source_target_pairs={{0,4},{4,0},{8,12},{12,8},{16,20},{20,16},{24,28},{28,24},{1,5},{5... | collective-permute-start | bytes 589832 | tf_op jit(solution)/shard_map/ppermute | solution.py:318
  41.3 6.3 %collective-permute-start.17 = (bf16[384,256]{1,0:T(8,128)(2,1)S(1)}, bf16[384,256]{1,0:T(8,128)(2,1)S(1)}, u32[]{:S(2)}, u32[]{:S(2)}) collective-permute-start(bf16[384,256]{1,0:T(8,128)(2,1)S(1)} %get-tuple-element.73), channel_id=1, source_target_pairs={{0,4},{4,0},{8,12},{12,8},{16,20},{20,16},{24,28},{28,24},{1,5},{5... | collective-permute-start | bytes 589832 | tf_op jit(solution)/shard_map/ppermute | solution.py:318
  44.5 5.2 %collective-permute-start.15 = (bf16[192,256]{1,0:T(8,128)(2,1)S(1)}, bf16[192,256]{1,0:T(8,128)(2,1)S(1)}, u32[]{:S(2)}, u32[]{:S(2)}) collective-permute-start(bf16[192,256]{1,0:T(8,128)(2,1)S(1)} %get-tuple-element.65), channel_id=1, source_target_pairs={{0,8},{4,12},{8,0},{12,4},{16,24},{20,28},{24,16},{28,20},{1,9},{5... | collective-permute-start | bytes 294920 | tf_op jit(solution)/shard_map/ppermute | solution.py:318
  47.6 5.2 %collective-permute-start.18 = (bf16[192,256]{1,0:T(8,128)(2,1)S(1)}, bf16[192,256]{1,0:T(8,128)(2,1)S(1)}, u32[]{:S(2)}, u32[]{:S(2)}) collective-permute-start(bf16[192,256]{1,0:T(8,128)(2,1)S(1)} %get-tuple-element.75), channel_id=1, source_target_pairs={{0,8},{4,12},{8,0},{12,4},{16,24},{20,28},{24,16},{28,20},{1,9},{5... | collective-permute-start | bytes 294920 | tf_op jit(solution)/shard_map/ppermute | solution.py:318
  49.7 6.0 %collective-permute-start.16 = (bf16[96,256]{1,0:T(8,128)(2,1)S(1)}, bf16[96,256]{1,0:T(8,128)(2,1)S(1)}, u32[]{:S(2)}, u32[]{:S(2)}) collective-permute-start(bf16[96,256]{1,0:T(8,128)(2,1)S(1)} %get-tuple-element.67), channel_id=1, source_target_pairs={{0,16},{4,20},{8,24},{12,28},{16,0},{20,4},{24,8},{28,12},{1,17},{... | collective-permute-start | bytes 147464 | tf_op jit(solution)/shard_map/ppermute | solution.py:318
  52.8 5.3 %collective-permute-start.19 = (bf16[96,256]{1,0:T(8,128)(2,1)S(1)}, bf16[96,256]{1,0:T(8,128)(2,1)S(1)}, u32[]{:S(2)}, u32[]{:S(2)}) collective-permute-start(bf16[96,256]{1,0:T(8,128)(2,1)S(1)} %get-tuple-element.77), channel_id=1, source_target_pairs={{0,16},{4,20},{8,24},{12,28},{16,0},{20,4},{24,8},{28,12},{1,17},{... | collective-permute-start | bytes 147464 | tf_op jit(solution)/shard_map/ppermute | solution.py:318

commit v14 on v13

--- a/solution.py
+++ b/solution.py
@@ -211,6 +211,7 @@
         delta = 0.0
         for part in parts:
             weights = jnp.exp2((s_at[part, :] - top) * factor)
+            s_at[part, :] = weights
             total = total + folded(weights, jnp.sum)
             delta = delta + folded(weights * g_at[part, :], jnp.sum)
         own_weight = jnp.exp2((own_score - top) * factor)
@@ -218,9 +219,9 @@
         delta = jnp.sum(delta, axis=0, keepdims=True) + own_weight * own_grad_prob
         delta = delta / total
         own_prob = own_weight / total
-        log_total = jnp.log2(total)
+        inverse = 1.0 / total
         for part in parts:
-            probs = jnp.exp2((s_at[part, :] - top) * factor - log_total)
+            probs = s_at[part, :] * inverse
             low_probs = probs.astype(jnp.bfloat16)
             low_grads = (probs * (g_at[part, :] - delta)).astype(jnp.bfloat16)
             for i, m in enumerate(pair):

time: 59.4 us -> 58.8 us (0.990)
  Pallas kernels: 15 us -> 14.4 us
    pallas_call x2, Pallas kernels: 9.17 us -> 8.54 us  [local(): pl.pallas_call(functools.partial(attend_kernel, g, order), out_shape=[sha...]
where the time goes in v14:
time: 58.8 us; the launch traced here: 58.6 us
  waiting for transfers between devices  20.4 us (35%)
  starting transfers between devices  19 us (32%)
  Pallas kernels  14.4 us (24%)
  local copies, waits for them, and re-layouts  4.06 us (7%)
  between operations  0.78 us (1%)
    ppermute x20, waiting for transfers between devices, swap(): return lax.ppermute(x, axis, [(i, i ^ m) for i in range(size)])  20.4 us
    ppermute x20, starting transfers between devices, swap(): return lax.ppermute(x, axis, [(i, i ^ m) for i in range(size)])  19 us
    pallas_call x2, Pallas kernels, local(): pl.pallas_call(functools.partial(attend_kernel, g, order), out_shape=[sha...  8.54 us
    unnamed x14, local copies, waits for them, and re-layouts  4.06 us
    pallas_call x1, Pallas kernels, local(): pl.pallas_call(functools.partial(queries_kernel, heads), out_shape=shape(...  2.2 us
    pallas_call x2, Pallas kernels, local(): pl.pallas_call(functools.partial(terms_kernel, heads), out_shape=[shape(h...  1.8 us
  transfers between devices with their start and end apart: 20, of which 10 were waited for; matrix products, arithmetic and copies ran while one was open for 0% of the time, Pallas kernels for 16%

profile of v14, /device:TPU:0, one launch (start us, length us, event | category | flops | bytes accessed | tf_op | source)
XLA Modules:
  0.0 58.6 jit_solution(8367079962881507177)
XLA Ops:
  0.6 0.9 %copy-done.4 = bf16[48,1024]{1,0:T(8,128)(2,1)S(1)} copy-done((bf16[48,1024]{1,0:T(8,128)(2,1)S(1)}, bf16[48,1024]{1,0:T(8,128)(2,1)}, u32[]{:S(2)}) %copy-start.4) | copy-done | bytes 98328
  1.5 0.9 %copy-done.5 = bf16[48,1024]{1,0:T(8,128)(2,1)S(1)} copy-done((bf16[48,1024]{1,0:T(8,128)(2,1)S(1)}, bf16[48,1024]{1,0:T(8,128)(2,1)}, u32[]{:S(2)}) %copy-start.5) | copy-done | bytes 98328
  2.4 0.5 collective-permute-start
  3.0 2.6 %collective-permute-start.1 = (bf16[48,512]{1,0:T(8,128)(2,1)S(1)}, bf16[48,512]{1,0:T(8,128)(2,1)S(1)}, u32[]{:S(2)}, u32[]{:S(2)}) collective-permute-start(bf16[48,512]{1,0:T(8,128)(2,1)S(1)} %get-tuple-element.44), channel_id=1, source_target_pairs={{0,2},{1,3},{2,0},{3,1},{4,6},{5,7},{6,4},{7,5},{8,10},{9,11},{10,... | collective-permute-start | bytes 147464 | tf_op jit(solution)/shard_map/ppermute | solution.py:319
  5.6 1.1 %copy-done = bf16[48,8192]{1,0:T(8,128)(2,1)S(1)} copy-done((bf16[48,8192]{1,0:T(8,128)(2,1)S(1)}, bf16[48,8192]{1,0:T(8,128)(2,1)}, u32[]{:S(2)}) %copy-start) | copy-done | bytes 786456
  6.7 1.1 %copy-done.2 = bf16[48,8192]{1,0:T(8,128)(2,1)S(1)} copy-done((bf16[48,8192]{1,0:T(8,128)(2,1)S(1)}, bf16[48,8192]{1,0:T(8,128)(2,1)}, u32[]{:S(2)}) %copy-start.2) | copy-done | bytes 786456
  8.3 0.9 %collective-permute-done.2.refs_3_ = bf16[48,512]{1,0:T(8,128)(2,1)S(1)} collective-permute-done((bf16[48,512]{1,0:T(8,128)(2,1)S(1)}, bf16[48,512]{1,0:T(8,128)(2,1)S(1)}, u32[]{:S(2)}, u32[]{:S(2)}) %collective-permute-start.2) | collective-permute-done | bytes 49184 | tf_op jit(solution)/shard_map/ppermute | solution.py:319
  9.4 1.1 %collective-permute-start.10 = (bf16[96,2048]{1,0:T(8,128)(2,1)S(1)}, bf16[96,2048]{1,0:T(8,128)(2,1)S(1)}, u32[]{:S(2)}, u32[]{:S(2)}) collective-permute-start(bf16[96,2048]{1,0:T(8,128)(2,1)S(1)} %gate.4), channel_id=1, source_target_pairs={{0,2},{1,3},{2,0},{3,1},{4,6},{5,7},{6,4},{7,5},{8,10},{9,11},{10,... | collective-permute-start | bytes 1179656 | tf_op jit(solution)/shard_map/ppermute | solution.py:319
  10.8 1.6 %collective-permute-start.4 = (bf16[96,512]{1,0:T(8,128)(2,1)S(1)}, bf16[96,512]{1,0:T(8,128)(2,1)S(1)}, u32[]{:S(2)}, u32[]{:S(2)}) collective-permute-start(bf16[96,512]{1,0:T(8,128)(2,1)S(1)} %get-tuple-element.47.refs_4_), channel_id=1, source_target_pairs={{0,8},{4,12},{8,0},{12,4},{16,24},{20,28},{24,16},{28,20},{1,9},{5... | collective-permute-start | bytes 294920 | tf_op jit(solution)/shard_map/ppermute | solution.py:319
  12.4 2.6 %collective-permute-start.3 = (bf16[96,512]{1,0:T(8,128)(2,1)S(1)}, bf16[96,512]{1,0:T(8,128)(2,1)S(1)}, u32[]{:S(2)}, u32[]{:S(2)}) collective-permute-start(bf16[96,512]{1,0:T(8,128)(2,1)S(1)} %get-tuple-element.47.refs_4_), channel_id=1, source_target_pairs={{0,16},{4,20},{8,24},{12,28},{16,0},{20,4},{24,8},{28,12},{1,17},{... | collective-permute-start | bytes 294920 | tf_op jit(solution)/shard_map/ppermute | solution.py:319
  15.0 1.5 %collective-permute-start.6 = (bf16[96,512]{1,0:T(8,128)(2,1)S(1)}, bf16[96,512]{1,0:T(8,128)(2,1)S(1)}, u32[]{:S(2)}, u32[]{:S(2)}) collective-permute-start(bf16[96,512]{1,0:T(8,128)(2,1)S(1)} %get-tuple-element.47.refs_4_), channel_id=1, source_target_pairs={{0,4},{4,0},{8,12},{12,8},{16,20},{20,16},{24,28},{28,24},{1,5},{5... | collective-permute-start | bytes 294920 | tf_op jit(solution)/shard_map/ppermute | solution.py:319
  16.5 0.5 collective-permute-start.8
  17.0 2.8 %collective-permute-done.3.refs_4_.refs_5_ = bf16[96,512]{1,0:T(8,128)(2,1)S(1)} collective-permute-done((bf16[96,512]{1,0:T(8,128)(2,1)S(1)}, bf16[96,512]{1,0:T(8,128)(2,1)S(1)}, u32[]{:S(2)}, u32[]{:S(2)}) %collective-permute-start.3) | collective-permute-done | bytes 98336 | tf_op jit(solution)/shard_map/ppermute | solution.py:319
  19.8 1.5 %collective-permute-start.7 = (bf16[96,512]{1,0:T(8,128)(2,1)S(1)}, bf16[96,512]{1,0:T(8,128)(2,1)S(1)}, u32[]{:S(2)}, u32[]{:S(2)}) collective-permute-start(bf16[96,512]{1,0:T(8,128)(2,1)S(1)} %collective-permute-done.3.refs_4_.refs_5_), channel_id=1, source_target_pairs={{0,4},{4,0},{8,12},{12,8},{16,20},{20,16},{24,28},{28,24},{1,5},{5... | collective-permute-start | bytes 294920 | tf_op jit(solution)/shard_map/ppermute | solution.py:319
  21.8 1.0 %collective-permute-start.13 = (bf16[96,2048]{1,0:T(8,128)(2,1)S(1)}, bf16[96,2048]{1,0:T(8,128)(2,1)S(1)}, u32[]{:S(2)}, u32[]{:S(2)}) collective-permute-start(bf16[96,2048]{1,0:T(8,128)(2,1)S(1)} %collective-permute-done.12), channel_id=1, source_target_pairs={{0,2},{1,3},{2,0},{3,1},{4,6},{5,7},{6,4},{7,5},{8,10},{9,11},{10,... | collective-permute-start | bytes 1179656 | tf_op jit(solution)/shard_map/ppermute | solution.py:319
  22.8 1.6 %collective-permute-done.7.refs_5_.refs_9_ = bf16[96,512]{1,0:T(8,128)(2,1)S(1)} collective-permute-done((bf16[96,512]{1,0:T(8,128)(2,1)S(1)}, bf16[96,512]{1,0:T(8,128)(2,1)S(1)}, u32[]{:S(2)}, u32[]{:S(2)}) %collective-permute-start.7) | collective-permute-done | bytes 98336 | tf_op jit(solution)/shard_map/ppermute | solution.py:319
  24.4 1.5 %collective-permute-done.5.refs_6_.refs_7_ = bf16[96,512]{1,0:T(8,128)(2,1)S(1)} collective-permute-done((bf16[96,512]{1,0:T(8,128)(2,1)S(1)}, bf16[96,512]{1,0:T(8,128)(2,1)S(1)}, u32[]{:S(2)}, u32[]{:S(2)}) %collective-permute-start.5) | collective-permute-done | bytes 98336 | tf_op jit(solution)/shard_map/ppermute | solution.py:319
  26.0 0.9 %collective-permute-start.9 = (bf16[96,512]{1,0:T(8,128)(2,1)S(1)}, bf16[96,512]{1,0:T(8,128)(2,1)S(1)}, u32[]{:S(2)}, u32[]{:S(2)}) collective-permute-start(bf16[96,512]{1,0:T(8,128)(2,1)S(1)} %collective-permute-done.5.refs_6_.refs_7_), channel_id=1, source_target_pairs={{0,4},{4,0},{8,12},{12,8},{16,20},{20,16},{24,28},{28,24},{1,5},{5... | collective-permute-start | bytes 294920 | tf_op jit(solution)/shard_map/ppermute | solution.py:319
  26.9 4.3 %collective-permute-done.13.refs_0_ = bf16[96,2048]{1,0:T(8,128)(2,1)S(1)} collective-permute-done((bf16[96,2048]{1,0:T(8,128)(2,1)S(1)}, bf16[96,2048]{1,0:T(8,128)(2,1)S(1)}, u32[]{:S(2)}, u32[]{:S(2)}) %collective-permute-start.13) | collective-permute-done | bytes 393248 | tf_op jit(solution)/shard_map/ppermute | solution.py:319
  31.3 4.2 %attend.2 = (bf16[768,1536]{1,0:T(8,128)(2,1)S(1)}, bf16[768,1536]{1,0:T(8,128)(2,1)S(1)}, bf16[48,1536]{1,0:T(8,128)(2,1)S(1)}, bf16[48,1536]{1,0:T(8,128)(2,1)...) custom-call(bf16[48,8192]{1,0:T(8,128)(2,1)S(1)} %copy-done.1, ...), custom_call_target="tpu_custom_call" | custom-call | flops 962592768 | bytes 8388608 | tf_op jit(solution)/shard_map/attend/pallas_call | solution.py:414
  35.5 0.9 %collective-permute-start.14 = (bf16[384,256]{1,0:T(8,128)(2,1)S(1)}, bf16[384,256]{1,0:T(8,128)(2,1)S(1)}, u32[]{:S(2)}, u32[]{:S(2)}) collective-permute-start(bf16[384,256]{1,0:T(8,128)(2,1)S(1)} %get-tuple-element.63), channel_id=1, source_target_pairs={{0,4},{4,0},{8,12},{12,8},{16,20},{20,16},{24,28},{28,24},{1,5},{5... | collective-permute-start | bytes 589832 | tf_op jit(solution)/shard_map/ppermute | solution.py:319
  36.3 4.4 %attend.3 = (bf16[768,1536]{1,0:T(8,128)(2,1)S(1)}, bf16[768,1536]{1,0:T(8,128)(2,1)S(1)}, bf16[48,1536]{1,0:T(8,128)(2,1)S(1)}, bf16[48,1536]{1,0:T(8,128)(2,1)...) custom-call(bf16[48,8192]{1,0:T(8,128)(2,1)S(1)} %copy-done.1, ...), custom_call_target="tpu_custom_call" | custom-call | flops 962592768 | bytes 8388608 | tf_op jit(solution)/shard_map/attend/pallas_call | solution.py:414
  40.7 1.3 %collective-permute-start.17 = (bf16[384,256]{1,0:T(8,128)(2,1)S(1)}, bf16[384,256]{1,0:T(8,128)(2,1)S(1)}, u32[]{:S(2)}, u32[]{:S(2)}) collective-permute-start(bf16[384,256]{1,0:T(8,128)(2,1)S(1)} %get-tuple-element.73), channel_id=1, source_target_pairs={{0,4},{4,0},{8,12},{12,8},{16,20},{20,16},{24,28},{28,24},{1,5},{5... | collective-permute-start | bytes 589832 | tf_op jit(solution)/shard_map/ppermute | solution.py:319
  42.0 0.9 %terms.2 = (f32[384,256]{1,0:T(8,128)S(1)}, f32[192,256]{1,0:T(8,128)S(1)}) custom-call(bf16[768,1536]{1,0:T(8,128)(2,1)S(1)} %get-tuple-element.58.p_ref, bf16[768,1536]{1,0:T(8,128)(2,1)S(1)} %get-tuple-element.51.refs_4_.ds_ref, bf16[48,1536]{1,0:T(8,128)(2,1)S(1)} %get-tuple-element.54.refs_15_.own_p_ref, ...), custom_call_target="tpu_custom_call" | custom-call | flops 301989888 | bytes 1048576 | tf_op jit(solution)/shard_map/terms/pallas_call | solution.py:457
  42.9 0.9 %terms.3 = (f32[384,256]{1,0:T(8,128)S(1)}, f32[192,256]{1,0:T(8,128)S(1)}) custom-call(bf16[768,1536]{1,0:T(8,128)(2,1)S(1)} %get-tuple-element.69.p_ref, bf16[768,1536]{1,0:T(8,128)(2,1)S(1)} %get-tuple-element.55.refs_7_.ds_ref, bf16[48,1536]{1,0:T(8,128)(2,1)S(1)} %get-tuple-element.61.after_ref.own_p_ref, ...), custom_call_target="tpu_custom_call" | custom-call | flops 301989888 | bytes 1048576 | tf_op jit(solution)/shard_map/terms/pallas_call | solution.py:457
  44.3 2.7 %collective-permute-done.17.far_ref = bf16[384,256]{1,0:T(8,128)(2,1)S(1)} collective-permute-done((bf16[384,256]{1,0:T(8,128)(2,1)S(1)}, bf16[384,256]{1,0:T(8,128)(2,1)S(1)}, u32[]{:S(2)}, u32[]{:S(2)}) %collective-permute-start.17) | collective-permute-done | bytes 196640 | tf_op jit(solution)/shard_map/ppermute | solution.py:319
  47.2 1.8 %collective-permute-done.15.far_ref = bf16[192,256]{1,0:T(8,128)(2,1)S(1)} collective-permute-done((bf16[192,256]{1,0:T(8,128)(2,1)S(1)}, bf16[192,256]{1,0:T(8,128)(2,1)S(1)}, u32[]{:S(2)}, u32[]{:S(2)}) %collective-permute-start.15) | collective-permute-done | bytes 98336 | tf_op jit(solution)/shard_map/ppermute | solution.py:319
  49.0 1.2 %collective-permute-start.16 = (bf16[96,256]{1,0:T(8,128)(2,1)S(1)}, bf16[96,256]{1,0:T(8,128)(2,1)S(1)}, u32[]{:S(2)}, u32[]{:S(2)}) collective-permute-start(bf16[96,256]{1,0:T(8,128)(2,1)S(1)} %get-tuple-element.67), channel_id=1, source_target_pairs={{0,16},{4,20},{8,24},{12,28},{16,0},{20,4},{24,8},{28,12},{1,17},{... | collective-permute-start | bytes 147464 | tf_op jit(solution)/shard_map/ppermute | solution.py:319
  50.3 1.8 %collective-permute-done.18.far_ref = bf16[192,256]{1,0:T(8,128)(2,1)S(1)} collective-permute-done((bf16[192,256]{1,0:T(8,128)(2,1)S(1)}, bf16[192,256]{1,0:T(8,128)(2,1)S(1)}, u32[]{:S(2)}, u32[]{:S(2)}) %collective-permute-start.18) | collective-permute-done | bytes 98336 | tf_op jit(solution)/shard_map/ppermute | solution.py:319
  52.5 2.2 %queries.1 = bf16[192,2048]{1,0:T(8,128)(2,1)} custom-call(bf16[48,512]{1,0:T(8,128)(2,1)S(1)} %get-tuple-element.42.refs_0_.refs_2_, bf16[48,512]{1,0:T(8,128)(2,1)S(1)} %collective-permute-done.refs_1_, bf16[48,512]{1,0:T(8,128)(2,1)S(1)} %collective-permute-done.1.refs_2_, bf16[48,512]{1,0:T(8,128)(2,1)S(1)} %collective-permute-done.2.refs_3_, ...), custom_call_target="tpu_custom_call" | custom-call | flops 603979776 | bytes 1048576 | tf_op jit(solution)/shard_map/queries/pallas_call | solution.py:473
  55.0 2.5 %collective-permute-done.19.refs_4_ = bf16[96,256]{1,0:T(8,128)(2,1)S(1)} collective-permute-done((bf16[96,256]{1,0:T(8,128)(2,1)S(1)}, bf16[96,256]{1,0:T(8,128)(2,1)S(1)}, u32[]{:S(2)}, u32[]{:S(2)}) %collective-permute-start.19) | collective-permute-done | bytes 49184 | tf_op jit(solution)/shard_map/ppermute | solution.py:319
  57.5 1.0 %spread.1 = (bf16[192,256]{1,0:T(8,128)(2,1)}, bf16[192,256]{1,0:T(8,128)(2,1)}) custom-call(s32[2,192]{1,0:T(2,128)S(1)} %copy-done.6, f32[96,256]{1,0:T(8,128)S(1)} %get-tuple-element.66.refs_0_, bf16[96,256]{1,0:T(8,128)(2,1)S(1)} %collective-permute-done.16.refs_1_, f32[192,256]{1,0:T(8,128)S(1)} %get-tuple-element.68.refs_2_, ...), custom_call_target="tpu_custom_call" | custom-call | tf_op jit(solution)/shard_map/spread/pallas_call | solution.py:502
  (39 shorter events, 2.8 us)
Async XLA Ops:
  0.6 0.9 %copy-start.4 = (bf16[48,1024]{1,0:T(8,128)(2,1)S(1)}, bf16[48,1024]{1,0:T(8,128)(2,1)}, u32[]{:S(2)}) copy-start(bf16[48,1024]{1,0:T(8,128)(2,1)} %key_ref.1) | copy-start | bytes 294916
  1.5 0.9 %copy-start.5 = (bf16[48,1024]{1,0:T(8,128)(2,1)S(1)}, bf16[48,1024]{1,0:T(8,128)(2,1)}, u32[]{:S(2)}) copy-start(bf16[48,1024]{1,0:T(8,128)(2,1)} %value_ref.1) | copy-start | bytes 294916
  2.4 8.1 %copy-start.6 = (s32[2,192]{1,0:T(2,128)S(1)}, s32[2,192]{1,0:T(2,128)}, u32[]{:S(2)}) copy-start(s32[2,192]{1,0:T(2,128)} %seg_ref.3) | copy-start | bytes 4612
  2.4 5.8 %collective-permute-start = (bf16[48,512]{1,0:T(8,128)(2,1)S(1)}, bf16[48,512]{1,0:T(8,128)(2,1)S(1)}, u32[]{:S(2)}, u32[]{:S(2)}) collective-permute-start(bf16[48,512]{1,0:T(8,128)(2,1)S(1)} %get-tuple-element.43), channel_id=1, source_target_pairs={{0,1},{1,0},{2,3},{3,2},{4,5},{5,4},{6,7},{7,6},{8,9},{9,8},{10,11... | collective-permute-start | bytes 147464 | tf_op jit(solution)/shard_map/ppermute | solution.py:319
  3.0 5.3 %collective-permute-start.1 = (bf16[48,512]{1,0:T(8,128)(2,1)S(1)}, bf16[48,512]{1,0:T(8,128)(2,1)S(1)}, u32[]{:S(2)}, u32[]{:S(2)}) collective-permute-start(bf16[48,512]{1,0:T(8,128)(2,1)S(1)} %get-tuple-element.44), channel_id=1, source_target_pairs={{0,2},{1,3},{2,0},{3,1},{4,6},{5,7},{6,4},{7,5},{8,10},{9,11},{10,... | collective-permute-start | bytes 147464 | tf_op jit(solution)/shard_map/ppermute | solution.py:319
  5.5 3.7 %collective-permute-start.2 = (bf16[48,512]{1,0:T(8,128)(2,1)S(1)}, bf16[48,512]{1,0:T(8,128)(2,1)S(1)}, u32[]{:S(2)}, u32[]{:S(2)}) collective-permute-start(bf16[48,512]{1,0:T(8,128)(2,1)S(1)} %get-tuple-element.45), channel_id=1, source_target_pairs={{0,3},{1,2},{2,1},{3,0},{4,7},{5,6},{6,5},{7,4},{8,11},{9,10},{10,... | collective-permute-start | bytes 147464 | tf_op jit(solution)/shard_map/ppermute | solution.py:319
  5.6 1.1 %copy-start = (bf16[48,8192]{1,0:T(8,128)(2,1)S(1)}, bf16[48,8192]{1,0:T(8,128)(2,1)}, u32[]{:S(2)}) copy-start(bf16[48,8192]{1,0:T(8,128)(2,1)} %q_ref.3) | copy-start | bytes 2359300
  6.7 1.1 %copy-start.2 = (bf16[48,8192]{1,0:T(8,128)(2,1)S(1)}, bf16[48,8192]{1,0:T(8,128)(2,1)}, u32[]{:S(2)}) copy-start(bf16[48,8192]{1,0:T(8,128)(2,1)} %o_ref.3) | copy-start | bytes 2359300
  8.3 23.0 %copy-start.1 = (bf16[48,8192]{1,0:T(8,128)(2,1)S(1)}, bf16[48,8192]{1,0:T(8,128)(2,1)}, u32[]{:S(2)}) copy-start(bf16[48,8192]{1,0:T(8,128)(2,1)} %q_ref.3) | copy-start | bytes 2359300
  8.3 23.0 %copy-start.3 = (bf16[48,8192]{1,0:T(8,128)(2,1)S(1)}, bf16[48,8192]{1,0:T(8,128)(2,1)}, u32[]{:S(2)}) copy-start(bf16[48,8192]{1,0:T(8,128)(2,1)} %o_ref.3) | copy-start | bytes 2359300
  9.2 12.6 %collective-permute-start.12 = (bf16[96,2048]{1,0:T(8,128)(2,1)S(1)}, bf16[96,2048]{1,0:T(8,128)(2,1)S(1)}, u32[]{:S(2)}, u32[]{:S(2)}) collective-permute-start(bf16[96,2048]{1,0:T(8,128)(2,1)S(1)} %gate.6), channel_id=1, source_target_pairs={{0,1},{1,0},{2,3},{3,2},{4,5},{5,4},{6,7},{7,6},{8,9},{9,8},{10,11... | collective-permute-start | bytes 1179656 | tf_op jit(solution)/shard_map/ppermute | solution.py:319
  9.4 16.6 %collective-permute-start.10 = (bf16[96,2048]{1,0:T(8,128)(2,1)S(1)}, bf16[96,2048]{1,0:T(8,128)(2,1)S(1)}, u32[]{:S(2)}, u32[]{:S(2)}) collective-permute-start(bf16[96,2048]{1,0:T(8,128)(2,1)S(1)} %gate.4), channel_id=1, source_target_pairs={{0,2},{1,3},{2,0},{3,1},{4,6},{5,7},{6,4},{7,5},{8,10},{9,11},{10,... | collective-permute-start | bytes 1179656 | tf_op jit(solution)/shard_map/ppermute | solution.py:319
  10.8 5.7 %collective-permute-start.4 = (bf16[96,512]{1,0:T(8,128)(2,1)S(1)}, bf16[96,512]{1,0:T(8,128)(2,1)S(1)}, u32[]{:S(2)}, u32[]{:S(2)}) collective-permute-start(bf16[96,512]{1,0:T(8,128)(2,1)S(1)} %get-tuple-element.47.refs_4_), channel_id=1, source_target_pairs={{0,8},{4,12},{8,0},{12,4},{16,24},{20,28},{24,16},{28,20},{1,9},{5... | collective-permute-start | bytes 294920 | tf_op jit(solution)/shard_map/ppermute | solution.py:319
  12.4 7.4 %collective-permute-start.3 = (bf16[96,512]{1,0:T(8,128)(2,1)S(1)}, bf16[96,512]{1,0:T(8,128)(2,1)S(1)}, u32[]{:S(2)}, u32[]{:S(2)}) collective-permute-start(bf16[96,512]{1,0:T(8,128)(2,1)S(1)} %get-tuple-element.47.refs_4_), channel_id=1, source_target_pairs={{0,16},{4,20},{8,24},{12,28},{16,0},{20,4},{24,8},{28,12},{1,17},{... | collective-permute-start | bytes 294920 | tf_op jit(solution)/shard_map/ppermute | solution.py:319
  15.0 6.4 %collective-permute-start.6 = (bf16[96,512]{1,0:T(8,128)(2,1)S(1)}, bf16[96,512]{1,0:T(8,128)(2,1)S(1)}, u32[]{:S(2)}, u32[]{:S(2)}) collective-permute-start(bf16[96,512]{1,0:T(8,128)(2,1)S(1)} %get-tuple-element.47.refs_4_), channel_id=1, source_target_pairs={{0,4},{4,0},{8,12},{12,8},{16,20},{20,16},{24,28},{28,24},{1,5},{5... | collective-permute-start | bytes 294920 | tf_op jit(solution)/shard_map/ppermute | solution.py:319
  16.5 6.3 %collective-permute-start.8 = (bf16[96,512]{1,0:T(8,128)(2,1)S(1)}, bf16[96,512]{1,0:T(8,128)(2,1)S(1)}, u32[]{:S(2)}, u32[]{:S(2)}) collective-permute-start(bf16[96,512]{1,0:T(8,128)(2,1)S(1)} %collective-permute-done.4.refs_2_.refs_6_), channel_id=1, source_target_pairs={{0,4},{4,0},{8,12},{12,8},{16,20},{20,16},{24,28},{28,24},{1,5},{5... | collective-permute-start | bytes 294920 | tf_op jit(solution)/shard_map/ppermute | solution.py:319
  19.8 4.6 %collective-permute-start.7 = (bf16[96,512]{1,0:T(8,128)(2,1)S(1)}, bf16[96,512]{1,0:T(8,128)(2,1)S(1)}, u32[]{:S(2)}, u32[]{:S(2)}) collective-permute-start(bf16[96,512]{1,0:T(8,128)(2,1)S(1)} %collective-permute-done.3.refs_4_.refs_5_), channel_id=1, source_target_pairs={{0,4},{4,0},{8,12},{12,8},{16,20},{20,16},{24,28},{28,24},{1,5},{5... | collective-permute-start | bytes 294920 | tf_op jit(solution)/shard_map/ppermute | solution.py:319
  21.4 4.6 %collective-permute-start.5 = (bf16[96,512]{1,0:T(8,128)(2,1)S(1)}, bf16[96,512]{1,0:T(8,128)(2,1)S(1)}, u32[]{:S(2)}, u32[]{:S(2)}) collective-permute-start(bf16[96,512]{1,0:T(8,128)(2,1)S(1)} %collective-permute-done.3.refs_4_.refs_5_), channel_id=1, source_target_pairs={{0,8},{4,12},{8,0},{12,4},{16,24},{20,28},{24,16},{28,20},{1,9},{5... | collective-permute-start | bytes 294920 | tf_op jit(solution)/shard_map/ppermute | solution.py:319
  21.8 9.5 %collective-permute-start.13 = (bf16[96,2048]{1,0:T(8,128)(2,1)S(1)}, bf16[96,2048]{1,0:T(8,128)(2,1)S(1)}, u32[]{:S(2)}, u32[]{:S(2)}) collective-permute-start(bf16[96,2048]{1,0:T(8,128)(2,1)S(1)} %collective-permute-done.12), channel_id=1, source_target_pairs={{0,2},{1,3},{2,0},{3,1},{4,6},{5,7},{6,4},{7,5},{8,10},{9,11},{10,... | collective-permute-start | bytes 1179656 | tf_op jit(solution)/shard_map/ppermute | solution.py:319
  26.0 5.3 %collective-permute-start.11 = (bf16[96,2048]{1,0:T(8,128)(2,1)S(1)}, bf16[96,2048]{1,0:T(8,128)(2,1)S(1)}, u32[]{:S(2)}, u32[]{:S(2)}) collective-permute-start(bf16[96,2048]{1,0:T(8,128)(2,1)S(1)} %gate.5), channel_id=1, source_target_pairs={{0,1},{1,0},{2,3},{3,2},{4,5},{5,4},{6,7},{7,6},{8,9},{9,8},{10,11... | collective-permute-start | bytes 1179656 | tf_op jit(solution)/shard_map/ppermute | solution.py:319
  26.0 5.3 %collective-permute-start.9 = (bf16[96,512]{1,0:T(8,128)(2,1)S(1)}, bf16[96,512]{1,0:T(8,128)(2,1)S(1)}, u32[]{:S(2)}, u32[]{:S(2)}) collective-permute-start(bf16[96,512]{1,0:T(8,128)(2,1)S(1)} %collective-permute-done.5.refs_6_.refs_7_), channel_id=1, source_target_pairs={{0,4},{4,0},{8,12},{12,8},{16,20},{20,16},{24,28},{28,24},{1,5},{5... | collective-permute-start | bytes 294920 | tf_op jit(solution)/shard_map/ppermute | solution.py:319
  35.5 8.3 %collective-permute-start.14 = (bf16[384,256]{1,0:T(8,128)(2,1)S(1)}, bf16[384,256]{1,0:T(8,128)(2,1)S(1)}, u32[]{:S(2)}, u32[]{:S(2)}) collective-permute-start(bf16[384,256]{1,0:T(8,128)(2,1)S(1)} %get-tuple-element.63), channel_id=1, source_target_pairs={{0,4},{4,0},{8,12},{12,8},{16,20},{20,16},{24,28},{28,24},{1,5},{5... | collective-permute-start | bytes 589832 | tf_op jit(solution)/shard_map/ppermute | solution.py:319
  40.7 6.3 %collective-permute-start.17 = (bf16[384,256]{1,0:T(8,128)(2,1)S(1)}, bf16[384,256]{1,0:T(8,128)(2,1)S(1)}, u32[]{:S(2)}, u32[]{:S(2)}) collective-permute-start(bf16[384,256]{1,0:T(8,128)(2,1)S(1)} %get-tuple-element.73), channel_id=1, source_target_pairs={{0,4},{4,0},{8,12},{12,8},{16,20},{20,16},{24,28},{28,24},{1,5},{5... | collective-permute-start | bytes 589832 | tf_op jit(solution)/shard_map/ppermute | solution.py:319
  43.9 5.2 %collective-permute-start.15 = (bf16[192,256]{1,0:T(8,128)(2,1)S(1)}, bf16[192,256]{1,0:T(8,128)(2,1)S(1)}, u32[]{:S(2)}, u32[]{:S(2)}) collective-permute-start(bf16[192,256]{1,0:T(8,128)(2,1)S(1)} %get-tuple-element.65), channel_id=1, source_target_pairs={{0,8},{4,12},{8,0},{12,4},{16,24},{20,28},{24,16},{28,20},{1,9},{5... | collective-permute-start | bytes 294920 | tf_op jit(solution)/shard_map/ppermute | solution.py:319
  47.0 5.1 %collective-permute-start.18 = (bf16[192,256]{1,0:T(8,128)(2,1)S(1)}, bf16[192,256]{1,0:T(8,128)(2,1)S(1)}, u32[]{:S(2)}, u32[]{:S(2)}) collective-permute-start(bf16[192,256]{1,0:T(8,128)(2,1)S(1)} %get-tuple-element.75), channel_id=1, source_target_pairs={{0,8},{4,12},{8,0},{12,4},{16,24},{20,28},{24,16},{28,20},{1,9},{5... | collective-permute-start | bytes 294920 | tf_op jit(solution)/shard_map/ppermute | solution.py:319
  49.0 6.0 %collective-permute-start.16 = (bf16[96,256]{1,0:T(8,128)(2,1)S(1)}, bf16[96,256]{1,0:T(8,128)(2,1)S(1)}, u32[]{:S(2)}, u32[]{:S(2)}) collective-permute-start(bf16[96,256]{1,0:T(8,128)(2,1)S(1)} %get-tuple-element.67), channel_id=1, source_target_pairs={{0,16},{4,20},{8,24},{12,28},{16,0},{20,4},{24,8},{28,12},{1,17},{... | collective-permute-start | bytes 147464 | tf_op jit(solution)/shard_map/ppermute | solution.py:319
  52.1 5.4 %collective-permute-start.19 = (bf16[96,256]{1,0:T(8,128)(2,1)S(1)}, bf16[96,256]{1,0:T(8,128)(2,1)S(1)}, u32[]{:S(2)}, u32[]{:S(2)}) collective-permute-start(bf16[96,256]{1,0:T(8,128)(2,1)S(1)} %get-tuple-element.77), channel_id=1, source_target_pairs={{0,16},{4,20},{8,24},{12,28},{16,0},{20,4},{24,8},{28,12},{1,17},{... | collective-permute-start | bytes 147464 | tf_op jit(solution)/shard_map/ppermute | solution.py:319

commit v15 on v14

--- a/solution.py
+++ b/solution.py
@@ -18,7 +18,7 @@
 DEAD = 1024.0
 HIDDEN = 2.0**96
 PAIR = 2
-PART = 48
+PART = 16
 
 
 def nt(a, b):

time: 58.8 us -> 58.7 us (level)
  no operation moved by 1% of the time
where the time goes in v15:
time: 58.7 us; the launch traced here: 58.5 us
  waiting for transfers between devices  20.3 us (35%)
  starting transfers between devices  19.1 us (33%)
  Pallas kernels  14.3 us (24%)
  local copies, waits for them, and re-layouts  4.06 us (7%)
  between operations  0.78 us (1%)
    ppermute x20, waiting for transfers between devices, swap(): return lax.ppermute(x, axis, [(i, i ^ m) for i in range(size)])  20.3 us
    ppermute x20, starting transfers between devices, swap(): return lax.ppermute(x, axis, [(i, i ^ m) for i in range(size)])  19.1 us
    pallas_call x2, Pallas kernels, local(): pl.pallas_call(functools.partial(attend_kernel, g, order), out_shape=[sha...  8.49 us
    unnamed x14, local copies, waits for them, and re-layouts  4.06 us
    pallas_call x1, Pallas kernels, local(): pl.pallas_call(functools.partial(queries_kernel, heads), out_shape=shape(...  2.2 us
    pallas_call x2, Pallas kernels, local(): pl.pallas_call(functools.partial(terms_kernel, heads), out_shape=[shape(h...  1.8 us
  transfers between devices with their start and end apart: 20, of which 10 were waited for; matrix products, arithmetic and copies ran while one was open for 0% of the time, Pallas kernels for 16%

profile of v15, /device:TPU:0, one launch (start us, length us, event | category | flops | bytes accessed | tf_op | source)
XLA Modules:
  0.0 58.5 jit_solution(11424616041071498215)
XLA Ops:
  0.6 0.9 %copy-done.4 = bf16[48,1024]{1,0:T(8,128)(2,1)S(1)} copy-done((bf16[48,1024]{1,0:T(8,128)(2,1)S(1)}, bf16[48,1024]{1,0:T(8,128)(2,1)}, u32[]{:S(2)}) %copy-start.4) | copy-done | bytes 98328
  1.5 0.9 %copy-done.5 = bf16[48,1024]{1,0:T(8,128)(2,1)S(1)} copy-done((bf16[48,1024]{1,0:T(8,128)(2,1)S(1)}, bf16[48,1024]{1,0:T(8,128)(2,1)}, u32[]{:S(2)}) %copy-start.5) | copy-done | bytes 98328
  2.4 0.5 collective-permute-start
  3.0 2.6 %collective-permute-start.1 = (bf16[48,512]{1,0:T(8,128)(2,1)S(1)}, bf16[48,512]{1,0:T(8,128)(2,1)S(1)}, u32[]{:S(2)}, u32[]{:S(2)}) collective-permute-start(bf16[48,512]{1,0:T(8,128)(2,1)S(1)} %get-tuple-element.44), channel_id=1, source_target_pairs={{0,2},{1,3},{2,0},{3,1},{4,6},{5,7},{6,4},{7,5},{8,10},{9,11},{10,... | collective-permute-start | bytes 147464 | tf_op jit(solution)/shard_map/ppermute | solution.py:319
  5.6 1.1 %copy-done = bf16[48,8192]{1,0:T(8,128)(2,1)S(1)} copy-done((bf16[48,8192]{1,0:T(8,128)(2,1)S(1)}, bf16[48,8192]{1,0:T(8,128)(2,1)}, u32[]{:S(2)}) %copy-start) | copy-done | bytes 786456
  6.7 1.1 %copy-done.2 = bf16[48,8192]{1,0:T(8,128)(2,1)S(1)} copy-done((bf16[48,8192]{1,0:T(8,128)(2,1)S(1)}, bf16[48,8192]{1,0:T(8,128)(2,1)}, u32[]{:S(2)}) %copy-start.2) | copy-done | bytes 786456
  8.3 0.9 %collective-permute-done.2.refs_3_ = bf16[48,512]{1,0:T(8,128)(2,1)S(1)} collective-permute-done((bf16[48,512]{1,0:T(8,128)(2,1)S(1)}, bf16[48,512]{1,0:T(8,128)(2,1)S(1)}, u32[]{:S(2)}, u32[]{:S(2)}) %collective-permute-start.2) | collective-permute-done | bytes 49184 | tf_op jit(solution)/shard_map/ppermute | solution.py:319
  9.4 1.1 %collective-permute-start.10 = (bf16[96,2048]{1,0:T(8,128)(2,1)S(1)}, bf16[96,2048]{1,0:T(8,128)(2,1)S(1)}, u32[]{:S(2)}, u32[]{:S(2)}) collective-permute-start(bf16[96,2048]{1,0:T(8,128)(2,1)S(1)} %gate.4), channel_id=1, source_target_pairs={{0,2},{1,3},{2,0},{3,1},{4,6},{5,7},{6,4},{7,5},{8,10},{9,11},{10,... | collective-permute-start | bytes 1179656 | tf_op jit(solution)/shard_map/ppermute | solution.py:319
  10.8 1.6 %collective-permute-start.4 = (bf16[96,512]{1,0:T(8,128)(2,1)S(1)}, bf16[96,512]{1,0:T(8,128)(2,1)S(1)}, u32[]{:S(2)}, u32[]{:S(2)}) collective-permute-start(bf16[96,512]{1,0:T(8,128)(2,1)S(1)} %get-tuple-element.47.refs_4_), channel_id=1, source_target_pairs={{0,8},{4,12},{8,0},{12,4},{16,24},{20,28},{24,16},{28,20},{1,9},{5... | collective-permute-start | bytes 294920 | tf_op jit(solution)/shard_map/ppermute | solution.py:319
  12.4 2.6 %collective-permute-start.3 = (bf16[96,512]{1,0:T(8,128)(2,1)S(1)}, bf16[96,512]{1,0:T(8,128)(2,1)S(1)}, u32[]{:S(2)}, u32[]{:S(2)}) collective-permute-start(bf16[96,512]{1,0:T(8,128)(2,1)S(1)} %get-tuple-element.47.refs_4_), channel_id=1, source_target_pairs={{0,16},{4,20},{8,24},{12,28},{16,0},{20,4},{24,8},{28,12},{1,17},{... | collective-permute-start | bytes 294920 | tf_op jit(solution)/shard_map/ppermute | solution.py:319
  15.0 1.5 %collective-permute-start.6 = (bf16[96,512]{1,0:T(8,128)(2,1)S(1)}, bf16[96,512]{1,0:T(8,128)(2,1)S(1)}, u32[]{:S(2)}, u32[]{:S(2)}) collective-permute-start(bf16[96,512]{1,0:T(8,128)(2,1)S(1)} %get-tuple-element.47.refs_4_), channel_id=1, source_target_pairs={{0,4},{4,0},{8,12},{12,8},{16,20},{20,16},{24,28},{28,24},{1,5},{5... | collective-permute-start | bytes 294920 | tf_op jit(solution)/shard_map/ppermute | solution.py:319
  16.5 0.5 collective-permute-start.8
  17.0 2.8 %collective-permute-done.3.refs_4_.refs_5_ = bf16[96,512]{1,0:T(8,128)(2,1)S(1)} collective-permute-done((bf16[96,512]{1,0:T(8,128)(2,1)S(1)}, bf16[96,512]{1,0:T(8,128)(2,1)S(1)}, u32[]{:S(2)}, u32[]{:S(2)}) %collective-permute-start.3) | collective-permute-done | bytes 98336 | tf_op jit(solution)/shard_map/ppermute | solution.py:319
  19.8 1.5 %collective-permute-start.7 = (bf16[96,512]{1,0:T(8,128)(2,1)S(1)}, bf16[96,512]{1,0:T(8,128)(2,1)S(1)}, u32[]{:S(2)}, u32[]{:S(2)}) collective-permute-start(bf16[96,512]{1,0:T(8,128)(2,1)S(1)} %collective-permute-done.3.refs_4_.refs_5_), channel_id=1, source_target_pairs={{0,4},{4,0},{8,12},{12,8},{16,20},{20,16},{24,28},{28,24},{1,5},{5... | collective-permute-start | bytes 294920 | tf_op jit(solution)/shard_map/ppermute | solution.py:319
  21.8 1.0 %collective-permute-start.13 = (bf16[96,2048]{1,0:T(8,128)(2,1)S(1)}, bf16[96,2048]{1,0:T(8,128)(2,1)S(1)}, u32[]{:S(2)}, u32[]{:S(2)}) collective-permute-start(bf16[96,2048]{1,0:T(8,128)(2,1)S(1)} %collective-permute-done.12), channel_id=1, source_target_pairs={{0,2},{1,3},{2,0},{3,1},{4,6},{5,7},{6,4},{7,5},{8,10},{9,11},{10,... | collective-permute-start | bytes 1179656 | tf_op jit(solution)/shard_map/ppermute | solution.py:319
  22.8 1.6 %collective-permute-done.7.refs_5_.refs_9_ = bf16[96,512]{1,0:T(8,128)(2,1)S(1)} collective-permute-done((bf16[96,512]{1,0:T(8,128)(2,1)S(1)}, bf16[96,512]{1,0:T(8,128)(2,1)S(1)}, u32[]{:S(2)}, u32[]{:S(2)}) %collective-permute-start.7) | collective-permute-done | bytes 98336 | tf_op jit(solution)/shard_map/ppermute | solution.py:319
  24.4 1.5 %collective-permute-done.5.refs_6_.refs_7_ = bf16[96,512]{1,0:T(8,128)(2,1)S(1)} collective-permute-done((bf16[96,512]{1,0:T(8,128)(2,1)S(1)}, bf16[96,512]{1,0:T(8,128)(2,1)S(1)}, u32[]{:S(2)}, u32[]{:S(2)}) %collective-permute-start.5) | collective-permute-done | bytes 98336 | tf_op jit(solution)/shard_map/ppermute | solution.py:319
  26.0 0.9 %collective-permute-start.9 = (bf16[96,512]{1,0:T(8,128)(2,1)S(1)}, bf16[96,512]{1,0:T(8,128)(2,1)S(1)}, u32[]{:S(2)}, u32[]{:S(2)}) collective-permute-start(bf16[96,512]{1,0:T(8,128)(2,1)S(1)} %collective-permute-done.5.refs_6_.refs_7_), channel_id=1, source_target_pairs={{0,4},{4,0},{8,12},{12,8},{16,20},{20,16},{24,28},{28,24},{1,5},{5... | collective-permute-start | bytes 294920 | tf_op jit(solution)/shard_map/ppermute | solution.py:319
  26.9 4.3 %collective-permute-done.13.refs_0_ = bf16[96,2048]{1,0:T(8,128)(2,1)S(1)} collective-permute-done((bf16[96,2048]{1,0:T(8,128)(2,1)S(1)}, bf16[96,2048]{1,0:T(8,128)(2,1)S(1)}, u32[]{:S(2)}, u32[]{:S(2)}) %collective-permute-start.13) | collective-permute-done | bytes 393248 | tf_op jit(solution)/shard_map/ppermute | solution.py:319
  31.3 4.2 %attend.2 = (bf16[768,1536]{1,0:T(8,128)(2,1)S(1)}, bf16[768,1536]{1,0:T(8,128)(2,1)S(1)}, bf16[48,1536]{1,0:T(8,128)(2,1)S(1)}, bf16[48,1536]{1,0:T(8,128)(2,1)...) custom-call(bf16[48,8192]{1,0:T(8,128)(2,1)S(1)} %copy-done.1, ...), custom_call_target="tpu_custom_call" | custom-call | flops 962592768 | bytes 8388608 | tf_op jit(solution)/shard_map/attend/pallas_call | solution.py:414
  35.4 0.9 %collective-permute-start.14 = (bf16[384,256]{1,0:T(8,128)(2,1)S(1)}, bf16[384,256]{1,0:T(8,128)(2,1)S(1)}, u32[]{:S(2)}, u32[]{:S(2)}) collective-permute-start(bf16[384,256]{1,0:T(8,128)(2,1)S(1)} %get-tuple-element.63), channel_id=1, source_target_pairs={{0,4},{4,0},{8,12},{12,8},{16,20},{20,16},{24,28},{28,24},{1,5},{5... | collective-permute-start | bytes 589832 | tf_op jit(solution)/shard_map/ppermute | solution.py:319
  36.3 4.3 %attend.3 = (bf16[768,1536]{1,0:T(8,128)(2,1)S(1)}, bf16[768,1536]{1,0:T(8,128)(2,1)S(1)}, bf16[48,1536]{1,0:T(8,128)(2,1)S(1)}, bf16[48,1536]{1,0:T(8,128)(2,1)...) custom-call(bf16[48,8192]{1,0:T(8,128)(2,1)S(1)} %copy-done.1, ...), custom_call_target="tpu_custom_call" | custom-call | flops 962592768 | bytes 8388608 | tf_op jit(solution)/shard_map/attend/pallas_call | solution.py:414
  40.6 1.3 %collective-permute-start.17 = (bf16[384,256]{1,0:T(8,128)(2,1)S(1)}, bf16[384,256]{1,0:T(8,128)(2,1)S(1)}, u32[]{:S(2)}, u32[]{:S(2)}) collective-permute-start(bf16[384,256]{1,0:T(8,128)(2,1)S(1)} %get-tuple-element.73), channel_id=1, source_target_pairs={{0,4},{4,0},{8,12},{12,8},{16,20},{20,16},{24,28},{28,24},{1,5},{5... | collective-permute-start | bytes 589832 | tf_op jit(solution)/shard_map/ppermute | solution.py:319
  41.9 0.9 %terms.2 = (f32[384,256]{1,0:T(8,128)S(1)}, f32[192,256]{1,0:T(8,128)S(1)}) custom-call(bf16[768,1536]{1,0:T(8,128)(2,1)S(1)} %get-tuple-element.58.p_ref, bf16[768,1536]{1,0:T(8,128)(2,1)S(1)} %get-tuple-element.51.refs_4_.ds_ref, bf16[48,1536]{1,0:T(8,128)(2,1)S(1)} %get-tuple-element.54.refs_15_.own_p_ref, ...), custom_call_target="tpu_custom_call" | custom-call | flops 301989888 | bytes 1048576 | tf_op jit(solution)/shard_map/terms/pallas_call | solution.py:457
  42.8 0.9 %terms.3 = (f32[384,256]{1,0:T(8,128)S(1)}, f32[192,256]{1,0:T(8,128)S(1)}) custom-call(bf16[768,1536]{1,0:T(8,128)(2,1)S(1)} %get-tuple-element.69.p_ref, bf16[768,1536]{1,0:T(8,128)(2,1)S(1)} %get-tuple-element.55.refs_7_.ds_ref, bf16[48,1536]{1,0:T(8,128)(2,1)S(1)} %get-tuple-element.61.after_ref.own_p_ref, ...), custom_call_target="tpu_custom_call" | custom-call | flops 301989888 | bytes 1048576 | tf_op jit(solution)/shard_map/terms/pallas_call | solution.py:457
  44.2 2.7 %collective-permute-done.17.far_ref = bf16[384,256]{1,0:T(8,128)(2,1)S(1)} collective-permute-done((bf16[384,256]{1,0:T(8,128)(2,1)S(1)}, bf16[384,256]{1,0:T(8,128)(2,1)S(1)}, u32[]{:S(2)}, u32[]{:S(2)}) %collective-permute-start.17) | collective-permute-done | bytes 196640 | tf_op jit(solution)/shard_map/ppermute | solution.py:319
  47.1 1.8 %collective-permute-done.15.far_ref = bf16[192,256]{1,0:T(8,128)(2,1)S(1)} collective-permute-done((bf16[192,256]{1,0:T(8,128)(2,1)S(1)}, bf16[192,256]{1,0:T(8,128)(2,1)S(1)}, u32[]{:S(2)}, u32[]{:S(2)}) %collective-permute-start.15) | collective-permute-done | bytes 98336 | tf_op jit(solution)/shard_map/ppermute | solution.py:319
  48.9 1.2 %collective-permute-start.16 = (bf16[96,256]{1,0:T(8,128)(2,1)S(1)}, bf16[96,256]{1,0:T(8,128)(2,1)S(1)}, u32[]{:S(2)}, u32[]{:S(2)}) collective-permute-start(bf16[96,256]{1,0:T(8,128)(2,1)S(1)} %get-tuple-element.67), channel_id=1, source_target_pairs={{0,16},{4,20},{8,24},{12,28},{16,0},{20,4},{24,8},{28,12},{1,17},{... | collective-permute-start | bytes 147464 | tf_op jit(solution)/shard_map/ppermute | solution.py:319
  50.2 1.9 %collective-permute-done.18.far_ref = bf16[192,256]{1,0:T(8,128)(2,1)S(1)} collective-permute-done((bf16[192,256]{1,0:T(8,128)(2,1)S(1)}, bf16[192,256]{1,0:T(8,128)(2,1)S(1)}, u32[]{:S(2)}, u32[]{:S(2)}) %collective-permute-start.18) | collective-permute-done | bytes 98336 | tf_op jit(solution)/shard_map/ppermute | solution.py:319
  52.5 2.2 %queries.1 = bf16[192,2048]{1,0:T(8,128)(2,1)} custom-call(bf16[48,512]{1,0:T(8,128)(2,1)S(1)} %get-tuple-element.42.refs_0_.refs_2_, bf16[48,512]{1,0:T(8,128)(2,1)S(1)} %collective-permute-done.refs_1_, bf16[48,512]{1,0:T(8,128)(2,1)S(1)} %collective-permute-done.1.refs_2_, bf16[48,512]{1,0:T(8,128)(2,1)S(1)} %collective-permute-done.2.refs_3_, ...), custom_call_target="tpu_custom_call" | custom-call | flops 603979776 | bytes 1048576 | tf_op jit(solution)/shard_map/queries/pallas_call | solution.py:473
  54.9 2.5 %collective-permute-done.19.refs_4_ = bf16[96,256]{1,0:T(8,128)(2,1)S(1)} collective-permute-done((bf16[96,256]{1,0:T(8,128)(2,1)S(1)}, bf16[96,256]{1,0:T(8,128)(2,1)S(1)}, u32[]{:S(2)}, u32[]{:S(2)}) %collective-permute-start.19) | collective-permute-done | bytes 49184 | tf_op jit(solution)/shard_map/ppermute | solution.py:319
  57.4 1.0 %spread.1 = (bf16[192,256]{1,0:T(8,128)(2,1)}, bf16[192,256]{1,0:T(8,128)(2,1)}) custom-call(s32[2,192]{1,0:T(2,128)S(1)} %copy-done.6, f32[96,256]{1,0:T(8,128)S(1)} %get-tuple-element.66.refs_0_, bf16[96,256]{1,0:T(8,128)(2,1)S(1)} %collective-permute-done.16.refs_1_, f32[192,256]{1,0:T(8,128)S(1)} %get-tuple-element.68.refs_2_, ...), custom_call_target="tpu_custom_call" | custom-call | tf_op jit(solution)/shard_map/spread/pallas_call | solution.py:502
  (39 shorter events, 2.8 us)
Async XLA Ops:
  0.6 0.9 %copy-start.4 = (bf16[48,1024]{1,0:T(8,128)(2,1)S(1)}, bf16[48,1024]{1,0:T(8,128)(2,1)}, u32[]{:S(2)}) copy-start(bf16[48,1024]{1,0:T(8,128)(2,1)} %key_ref.1) | copy-start | bytes 294916
  1.5 0.9 %copy-start.5 = (bf16[48,1024]{1,0:T(8,128)(2,1)S(1)}, bf16[48,1024]{1,0:T(8,128)(2,1)}, u32[]{:S(2)}) copy-start(bf16[48,1024]{1,0:T(8,128)(2,1)} %value_ref.1) | copy-start | bytes 294916
  2.4 8.1 %copy-start.6 = (s32[2,192]{1,0:T(2,128)S(1)}, s32[2,192]{1,0:T(2,128)}, u32[]{:S(2)}) copy-start(s32[2,192]{1,0:T(2,128)} %seg_ref.3) | copy-start | bytes 4612
  2.4 5.8 %collective-permute-start = (bf16[48,512]{1,0:T(8,128)(2,1)S(1)}, bf16[48,512]{1,0:T(8,128)(2,1)S(1)}, u32[]{:S(2)}, u32[]{:S(2)}) collective-permute-start(bf16[48,512]{1,0:T(8,128)(2,1)S(1)} %get-tuple-element.43), channel_id=1, source_target_pairs={{0,1},{1,0},{2,3},{3,2},{4,5},{5,4},{6,7},{7,6},{8,9},{9,8},{10,11... | collective-permute-start | bytes 147464 | tf_op jit(solution)/shard_map/ppermute | solution.py:319
  3.0 5.3 %collective-permute-start.1 = (bf16[48,512]{1,0:T(8,128)(2,1)S(1)}, bf16[48,512]{1,0:T(8,128)(2,1)S(1)}, u32[]{:S(2)}, u32[]{:S(2)}) collective-permute-start(bf16[48,512]{1,0:T(8,128)(2,1)S(1)} %get-tuple-element.44), channel_id=1, source_target_pairs={{0,2},{1,3},{2,0},{3,1},{4,6},{5,7},{6,4},{7,5},{8,10},{9,11},{10,... | collective-permute-start | bytes 147464 | tf_op jit(solution)/shard_map/ppermute | solution.py:319
  5.5 3.7 %collective-permute-start.2 = (bf16[48,512]{1,0:T(8,128)(2,1)S(1)}, bf16[48,512]{1,0:T(8,128)(2,1)S(1)}, u32[]{:S(2)}, u32[]{:S(2)}) collective-permute-start(bf16[48,512]{1,0:T(8,128)(2,1)S(1)} %get-tuple-element.45), channel_id=1, source_target_pairs={{0,3},{1,2},{2,1},{3,0},{4,7},{5,6},{6,5},{7,4},{8,11},{9,10},{10,... | collective-permute-start | bytes 147464 | tf_op jit(solution)/shard_map/ppermute | solution.py:319
  5.6 1.1 %copy-start = (bf16[48,8192]{1,0:T(8,128)(2,1)S(1)}, bf16[48,8192]{1,0:T(8,128)(2,1)}, u32[]{:S(2)}) copy-start(bf16[48,8192]{1,0:T(8,128)(2,1)} %q_ref.3) | copy-start | bytes 2359300
  6.7 1.1 %copy-start.2 = (bf16[48,8192]{1,0:T(8,128)(2,1)S(1)}, bf16[48,8192]{1,0:T(8,128)(2,1)}, u32[]{:S(2)}) copy-start(bf16[48,8192]{1,0:T(8,128)(2,1)} %o_ref.3) | copy-start | bytes 2359300
  8.3 23.0 %copy-start.1 = (bf16[48,8192]{1,0:T(8,128)(2,1)S(1)}, bf16[48,8192]{1,0:T(8,128)(2,1)}, u32[]{:S(2)}) copy-start(bf16[48,8192]{1,0:T(8,128)(2,1)} %q_ref.3) | copy-start | bytes 2359300
  8.3 23.0 %copy-start.3 = (bf16[48,8192]{1,0:T(8,128)(2,1)S(1)}, bf16[48,8192]{1,0:T(8,128)(2,1)}, u32[]{:S(2)}) copy-start(bf16[48,8192]{1,0:T(8,128)(2,1)} %o_ref.3) | copy-start | bytes 2359300
  9.2 12.6 %collective-permute-start.12 = (bf16[96,2048]{1,0:T(8,128)(2,1)S(1)}, bf16[96,2048]{1,0:T(8,128)(2,1)S(1)}, u32[]{:S(2)}, u32[]{:S(2)}) collective-permute-start(bf16[96,2048]{1,0:T(8,128)(2,1)S(1)} %gate.6), channel_id=1, source_target_pairs={{0,1},{1,0},{2,3},{3,2},{4,5},{5,4},{6,7},{7,6},{8,9},{9,8},{10,11... | collective-permute-start | bytes 1179656 | tf_op jit(solution)/shard_map/ppermute | solution.py:319
  9.4 16.6 %collective-permute-start.10 = (bf16[96,2048]{1,0:T(8,128)(2,1)S(1)}, bf16[96,2048]{1,0:T(8,128)(2,1)S(1)}, u32[]{:S(2)}, u32[]{:S(2)}) collective-permute-start(bf16[96,2048]{1,0:T(8,128)(2,1)S(1)} %gate.4), channel_id=1, source_target_pairs={{0,2},{1,3},{2,0},{3,1},{4,6},{5,7},{6,4},{7,5},{8,10},{9,11},{10,... | collective-permute-start | bytes 1179656 | tf_op jit(solution)/shard_map/ppermute | solution.py:319
  10.8 5.7 %collective-permute-start.4 = (bf16[96,512]{1,0:T(8,128)(2,1)S(1)}, bf16[96,512]{1,0:T(8,128)(2,1)S(1)}, u32[]{:S(2)}, u32[]{:S(2)}) collective-permute-start(bf16[96,512]{1,0:T(8,128)(2,1)S(1)} %get-tuple-element.47.refs_4_), channel_id=1, source_target_pairs={{0,8},{4,12},{8,0},{12,4},{16,24},{20,28},{24,16},{28,20},{1,9},{5... | collective-permute-start | bytes 294920 | tf_op jit(solution)/shard_map/ppermute | solution.py:319
  12.4 7.4 %collective-permute-start.3 = (bf16[96,512]{1,0:T(8,128)(2,1)S(1)}, bf16[96,512]{1,0:T(8,128)(2,1)S(1)}, u32[]{:S(2)}, u32[]{:S(2)}) collective-permute-start(bf16[96,512]{1,0:T(8,128)(2,1)S(1)} %get-tuple-element.47.refs_4_), channel_id=1, source_target_pairs={{0,16},{4,20},{8,24},{12,28},{16,0},{20,4},{24,8},{28,12},{1,17},{... | collective-permute-start | bytes 294920 | tf_op jit(solution)/shard_map/ppermute | solution.py:319
  15.0 6.4 %collective-permute-start.6 = (bf16[96,512]{1,0:T(8,128)(2,1)S(1)}, bf16[96,512]{1,0:T(8,128)(2,1)S(1)}, u32[]{:S(2)}, u32[]{:S(2)}) collective-permute-start(bf16[96,512]{1,0:T(8,128)(2,1)S(1)} %get-tuple-element.47.refs_4_), channel_id=1, source_target_pairs={{0,4},{4,0},{8,12},{12,8},{16,20},{20,16},{24,28},{28,24},{1,5},{5... | collective-permute-start | bytes 294920 | tf_op jit(solution)/shard_map/ppermute | solution.py:319
  16.5 6.3 %collective-permute-start.8 = (bf16[96,512]{1,0:T(8,128)(2,1)S(1)}, bf16[96,512]{1,0:T(8,128)(2,1)S(1)}, u32[]{:S(2)}, u32[]{:S(2)}) collective-permute-start(bf16[96,512]{1,0:T(8,128)(2,1)S(1)} %collective-permute-done.4.refs_2_.refs_6_), channel_id=1, source_target_pairs={{0,4},{4,0},{8,12},{12,8},{16,20},{20,16},{24,28},{28,24},{1,5},{5... | collective-permute-start | bytes 294920 | tf_op jit(solution)/shard_map/ppermute | solution.py:319
  19.8 4.6 %collective-permute-start.7 = (bf16[96,512]{1,0:T(8,128)(2,1)S(1)}, bf16[96,512]{1,0:T(8,128)(2,1)S(1)}, u32[]{:S(2)}, u32[]{:S(2)}) collective-permute-start(bf16[96,512]{1,0:T(8,128)(2,1)S(1)} %collective-permute-done.3.refs_4_.refs_5_), channel_id=1, source_target_pairs={{0,4},{4,0},{8,12},{12,8},{16,20},{20,16},{24,28},{28,24},{1,5},{5... | collective-permute-start | bytes 294920 | tf_op jit(solution)/shard_map/ppermute | solution.py:319
  21.4 4.6 %collective-permute-start.5 = (bf16[96,512]{1,0:T(8,128)(2,1)S(1)}, bf16[96,512]{1,0:T(8,128)(2,1)S(1)}, u32[]{:S(2)}, u32[]{:S(2)}) collective-permute-start(bf16[96,512]{1,0:T(8,128)(2,1)S(1)} %collective-permute-done.3.refs_4_.refs_5_), channel_id=1, source_target_pairs={{0,8},{4,12},{8,0},{12,4},{16,24},{20,28},{24,16},{28,20},{1,9},{5... | collective-permute-start | bytes 294920 | tf_op jit(solution)/shard_map/ppermute | solution.py:319
  21.8 9.5 %collective-permute-start.13 = (bf16[96,2048]{1,0:T(8,128)(2,1)S(1)}, bf16[96,2048]{1,0:T(8,128)(2,1)S(1)}, u32[]{:S(2)}, u32[]{:S(2)}) collective-permute-start(bf16[96,2048]{1,0:T(8,128)(2,1)S(1)} %collective-permute-done.12), channel_id=1, source_target_pairs={{0,2},{1,3},{2,0},{3,1},{4,6},{5,7},{6,4},{7,5},{8,10},{9,11},{10,... | collective-permute-start | bytes 1179656 | tf_op jit(solution)/shard_map/ppermute | solution.py:319
  26.0 5.3 %collective-permute-start.11 = (bf16[96,2048]{1,0:T(8,128)(2,1)S(1)}, bf16[96,2048]{1,0:T(8,128)(2,1)S(1)}, u32[]{:S(2)}, u32[]{:S(2)}) collective-permute-start(bf16[96,2048]{1,0:T(8,128)(2,1)S(1)} %gate.5), channel_id=1, source_target_pairs={{0,1},{1,0},{2,3},{3,2},{4,5},{5,4},{6,7},{7,6},{8,9},{9,8},{10,11... | collective-permute-start | bytes 1179656 | tf_op jit(solution)/shard_map/ppermute | solution.py:319
  26.0 5.3 %collective-permute-start.9 = (bf16[96,512]{1,0:T(8,128)(2,1)S(1)}, bf16[96,512]{1,0:T(8,128)(2,1)S(1)}, u32[]{:S(2)}, u32[]{:S(2)}) collective-permute-start(bf16[96,512]{1,0:T(8,128)(2,1)S(1)} %collective-permute-done.5.refs_6_.refs_7_), channel_id=1, source_target_pairs={{0,4},{4,0},{8,12},{12,8},{16,20},{20,16},{24,28},{28,24},{1,5},{5... | collective-permute-start | bytes 294920 | tf_op jit(solution)/shard_map/ppermute | solution.py:319
  35.4 8.3 %collective-permute-start.14 = (bf16[384,256]{1,0:T(8,128)(2,1)S(1)}, bf16[384,256]{1,0:T(8,128)(2,1)S(1)}, u32[]{:S(2)}, u32[]{:S(2)}) collective-permute-start(bf16[384,256]{1,0:T(8,128)(2,1)S(1)} %get-tuple-element.63), channel_id=1, source_target_pairs={{0,4},{4,0},{8,12},{12,8},{16,20},{20,16},{24,28},{28,24},{1,5},{5... | collective-permute-start | bytes 589832 | tf_op jit(solution)/shard_map/ppermute | solution.py:319
  40.6 6.3 %collective-permute-start.17 = (bf16[384,256]{1,0:T(8,128)(2,1)S(1)}, bf16[384,256]{1,0:T(8,128)(2,1)S(1)}, u32[]{:S(2)}, u32[]{:S(2)}) collective-permute-start(bf16[384,256]{1,0:T(8,128)(2,1)S(1)} %get-tuple-element.73), channel_id=1, source_target_pairs={{0,4},{4,0},{8,12},{12,8},{16,20},{20,16},{24,28},{28,24},{1,5},{5... | collective-permute-start | bytes 589832 | tf_op jit(solution)/shard_map/ppermute | solution.py:319
  43.8 5.1 %collective-permute-start.15 = (bf16[192,256]{1,0:T(8,128)(2,1)S(1)}, bf16[192,256]{1,0:T(8,128)(2,1)S(1)}, u32[]{:S(2)}, u32[]{:S(2)}) collective-permute-start(bf16[192,256]{1,0:T(8,128)(2,1)S(1)} %get-tuple-element.65), channel_id=1, source_target_pairs={{0,8},{4,12},{8,0},{12,4},{16,24},{20,28},{24,16},{28,20},{1,9},{5... | collective-permute-start | bytes 294920 | tf_op jit(solution)/shard_map/ppermute | solution.py:319
  47.0 5.1 %collective-permute-start.18 = (bf16[192,256]{1,0:T(8,128)(2,1)S(1)}, bf16[192,256]{1,0:T(8,128)(2,1)S(1)}, u32[]{:S(2)}, u32[]{:S(2)}) collective-permute-start(bf16[192,256]{1,0:T(8,128)(2,1)S(1)} %get-tuple-element.75), channel_id=1, source_target_pairs={{0,8},{4,12},{8,0},{12,4},{16,24},{20,28},{24,16},{28,20},{1,9},{5... | collective-permute-start | bytes 294920 | tf_op jit(solution)/shard_map/ppermute | solution.py:319
  48.9 6.0 %collective-permute-start.16 = (bf16[96,256]{1,0:T(8,128)(2,1)S(1)}, bf16[96,256]{1,0:T(8,128)(2,1)S(1)}, u32[]{:S(2)}, u32[]{:S(2)}) collective-permute-start(bf16[96,256]{1,0:T(8,128)(2,1)S(1)} %get-tuple-element.67), channel_id=1, source_target_pairs={{0,16},{4,20},{8,24},{12,28},{16,0},{20,4},{24,8},{28,12},{1,17},{... | collective-permute-start | bytes 147464 | tf_op jit(solution)/shard_map/ppermute | solution.py:319
  52.1 5.4 %collective-permute-start.19 = (bf16[96,256]{1,0:T(8,128)(2,1)S(1)}, bf16[96,256]{1,0:T(8,128)(2,1)S(1)}, u32[]{:S(2)}, u32[]{:S(2)}) collective-permute-start(bf16[96,256]{1,0:T(8,128)(2,1)S(1)} %get-tuple-element.77), channel_id=1, source_target_pairs={{0,16},{4,20},{8,24},{12,28},{16,0},{20,4},{24,8},{28,12},{1,17},{... | collective-permute-start | bytes 147464 | tf_op jit(solution)/shard_map/ppermute | solution.py:319
